TPU v7x, 32 devices: a whole 2x2x4 slice. The times are simulated.
32 devices in a mesh: fsdp: 8 (over y, x, core), sp: 4 (over z).
Axes of the slice: x: 2, y: 2, z: 4, core: 2. Of those that a mesh axis runs over, the one named last changes fastest.
Arguments:
- tokens: bfloat16 [2, 8, 1024, 2560], P(None, 'fsdp', 'sp'), may hold values from -6 to 6
- doc_starts: int32 [2, 8, 4], P(None, 'fsdp'), may hold values from 0 to 1023, as said below
- cotangent: bfloat16 [2, 8, 1024, 2560], P(None, 'fsdp', 'sp'), may hold values from -6 to 6
- gain_attn: bfloat16 [2560], P('fsdp'), may hold values from 0.25 to 1.75
- gain_ffn: bfloat16 [2560], P('fsdp'), may hold values from 0.25 to 1.75
- w_query: bfloat16 [2560, 2560], P('fsdp'), may hold values from -0.125 to 0.125
- w_key: bfloat16 [2560, 640], P('fsdp'), may hold values from -0.125 to 0.125
- w_value: bfloat16 [2560, 640], P('fsdp'), may hold values from -0.125 to 0.125
- w_out: bfloat16 [2560, 2560], P('fsdp'), may hold values from -0.5 to 0.5
- w_gate: bfloat16 [2560, 7168], P('fsdp'), may hold values from -0.125 to 0.125
- w_up: bfloat16 [2560, 7168], P('fsdp'), may hold values from -0.125 to 0.125
- w_down: bfloat16 [7168, 2560], P('fsdp'), may hold values from -0.0625 to 0.0625
Outputs:
- mixed_out: bfloat16 [2, 8, 1024, 2560], P(None, 'fsdp', 'sp')
- tokens_grad: bfloat16 [2, 8, 1024, 2560], P(None, 'fsdp', 'sp')
- grad_gain_attn: float32 [2560], P('fsdp')
- grad_gain_ffn: float32 [2560], P('fsdp')
- grad_query: float32 [2560, 2560], P('fsdp')
- grad_key: float32 [2560, 640], P('fsdp')
- grad_value: float32 [2560, 640], P('fsdp')
- grad_out: float32 [2560, 2560], P('fsdp')
- grad_gate: float32 [2560, 7168], P('fsdp')
- grad_up: float32 [2560, 7168], P('fsdp')
- grad_down: float32 [7168, 2560], P('fsdp')
Inputs may be any that keep to these rules, and one draw needn't show every extreme that they name: Within each stream the starts rise strictly from doc_starts[m, s, 0] = 0; one document of every stream begins within its first 256 tokens and ends within its last 256.
All inputs are finite; a program needn't handle non-finite values.
Results may differ from a plain program's by a relative error of at most 0.017.
Values may be sent and summed in bfloat16 or wider, within the bound.
No kernel may reach another device: no remote copies, remote signals or barrier semaphores. Data moves between devices by JAX's collectives and lax.ppermute only.
A program may use at most 440 MiB of HBM per device.

v0:
```python
import math

import jax
import jax.numpy as jnp
from jax import lax
from jax.sharding import PartitionSpec as P

D = 2560
HEADS = 32
KV_HEADS = 8
HEAD_DIM = 80
FF = 7168
DOCS = 4


rms_eps = 1e-05
rope_base = 1000000.0


def rms_scale(values):
    return lax.rsqrt(jnp.mean(values * values, axis=-1, keepdims=True) + rms_eps)


def stream_layout(starts, places):
    begun = starts[:, None, :] <= places[None, :, None]
    doc_ids = jnp.sum(begun.astype(jnp.int32), axis=-1) - 1
    first_token = jnp.max(jnp.where(begun, starts[:, None, :], 0), axis=-1)
    return (doc_ids, places[None, :] - first_token)


def rope_tables(place):
    half_dim = HEAD_DIM // 2
    inverse = jnp.exp(
        jnp.arange(half_dim, dtype=jnp.float32) * (-2.0 * math.log(rope_base) / HEAD_DIM)
    )
    angles = place.astype(jnp.float32)[:, None] * inverse[None, :]
    return (jnp.cos(angles)[:, None, :], jnp.sin(angles)[:, None, :])


def rotate(values, cosine, sine):
    half_dim = HEAD_DIM // 2
    first_half = values[..., :half_dim]
    second_half = values[..., half_dim:]
    return jnp.concatenate(
        [first_half * cosine - second_half * sine, second_half * cosine + first_half * sine],
        axis=-1,
    )


def norm_back(grad_normed, gain, normed_x, scale_row, grad_rest):
    scaled = grad_normed * gain
    inner = jnp.mean(scaled * normed_x, axis=-1, keepdims=True)
    return grad_rest + scale_row * (scaled - normed_x * inner)


def trans_dot(left, right):
    return lax.dot_general(
        left, right, (((0,), (0,)), ((), ())), preferred_element_type=jnp.float32
    )


def right_trans(left, right):
    return lax.dot_general(
        left, right, (((1,), (1,)), ((), ())), preferred_element_type=jnp.float32
    )


def block_scores(query_block, keys_head, doc_block, doc_full, row_block, places):
    raw = jnp.einsum(
        "mbkgd,mlkd->mkgbl", query_block, keys_head, preferred_element_type=jnp.float32
    ) * HEAD_DIM ** (-0.5)
    allowed = (doc_block[:, :, None] == doc_full[:, None, :]) & (
        places[None, None, :] <= row_block[None, :, None]
    )
    return jnp.where(allowed[:, None, None], raw, -1e30)


def run_layer(tokens, doc_starts, cotangent, weights):
    gain_attn, gain_ffn, w_query, w_key, w_value, w_out, w_gate, w_up, w_down = weights
    micro = tokens.shape[0]
    rows = tokens.shape[2]
    parts = lax.axis_size("sp")
    length = rows * parts
    count = micro * rows
    kv_local = KV_HEADS // parts
    group_size = HEADS // KV_HEADS
    kv_width = KV_HEADS * HEAD_DIM
    score_scale = HEAD_DIM ** (-0.5)
    block_rows = min(512, length)
    blocks = length // block_rows
    starts = doc_starts.reshape(micro, DOCS)
    gain_one, gain_two, full_query, full_key, full_value, full_out = (
        lax.all_gather(gain_attn, "fsdp", axis=0, tiled=True),
        lax.all_gather(gain_ffn, "fsdp", axis=0, tiled=True),
        lax.all_gather(w_query, "fsdp", axis=0, tiled=True),
        lax.all_gather(w_key, "fsdp", axis=0, tiled=True),
        lax.all_gather(w_value, "fsdp", axis=0, tiled=True),
        lax.all_gather(w_out, "fsdp", axis=0, tiled=True),
    )
    gain_one = gain_one.astype(jnp.float32)
    gain_two = gain_two.astype(jnp.float32)
    inputs = tokens.reshape(count, D).astype(jnp.float32)
    scale_one = rms_scale(inputs)
    normed_x1 = inputs * scale_one
    normed = (normed_x1 * gain_one).astype(jnp.bfloat16)
    query_pre = jnp.dot(normed, full_query, preferred_element_type=jnp.float32)
    key_pre = jnp.dot(normed, full_key, preferred_element_type=jnp.float32)
    value_pre = jnp.dot(normed, full_value, preferred_element_type=jnp.float32)
    own_places = lax.axis_index("sp") * rows + jnp.arange(rows, dtype=jnp.int32)
    own_doc, own_pos = stream_layout(starts, own_places)
    cosine, sine = rope_tables(own_pos.reshape(count))
    queries = rotate(query_pre.reshape(count, HEADS, HEAD_DIM), cosine, sine).astype(jnp.bfloat16)
    keys_rot = rotate(key_pre.reshape(count, KV_HEADS, HEAD_DIM), cosine, sine).astype(jnp.bfloat16)
    values_b = value_pre.astype(jnp.bfloat16)
    query_heads, key_heads, value_heads = (
        lax.all_to_all(
            queries.reshape(micro, rows, parts, -1), "sp", split_axis=2, concat_axis=1, tiled=True
        ),
        lax.all_to_all(
            keys_rot.reshape(micro, rows, parts, -1), "sp", split_axis=2, concat_axis=1, tiled=True
        ),
        lax.all_to_all(
            values_b.reshape(micro, rows, parts, -1), "sp", split_axis=2, concat_axis=1, tiled=True
        ),
    )
    grouped = query_heads.reshape(micro, length, kv_local, group_size, HEAD_DIM)
    keys_head = key_heads.reshape(micro, length, kv_local, HEAD_DIM)
    values_head = value_heads.reshape(micro, length, kv_local, HEAD_DIM)
    places = jnp.arange(length, dtype=jnp.int32)
    doc_full, pos_full = stream_layout(starts, places)

    def attend_forward(block_index):
        start = block_index * block_rows
        query_block = lax.dynamic_slice_in_dim(grouped, start, block_rows, 1)
        doc_block = lax.dynamic_slice_in_dim(doc_full, start, block_rows, 1)
        row_block = start + jnp.arange(block_rows, dtype=jnp.int32)
        scores = block_scores(query_block, keys_head, doc_block, doc_full, row_block, places)
        row_max = jnp.max(scores, axis=-1, keepdims=True)
        weights_exp = jnp.exp(scores - row_max)
        totals = jnp.sum(weights_exp, axis=-1, keepdims=True)
        probabilities = (weights_exp / totals).astype(jnp.bfloat16)
        context_block = jnp.einsum(
            "mkgbl,mlkd->mbkgd", probabilities, values_head, preferred_element_type=jnp.float32
        )
        return (context_block, row_max + jnp.log(totals))

    contexts, log_totals = lax.map(attend_forward, jnp.arange(blocks, dtype=jnp.int32))
    context = jnp.moveaxis(contexts, 0, 1).reshape(micro, length, 1, -1).astype(jnp.bfloat16)
    context_rows = lax.all_to_all(context, "sp", split_axis=1, concat_axis=2, tiled=True).reshape(
        count, D
    )
    mixed = inputs + jnp.dot(context_rows, full_out, preferred_element_type=jnp.float32)
    scale_two = rms_scale(mixed)
    normed_x2 = mixed * scale_two
    normed_ffn = (normed_x2 * gain_two).astype(jnp.bfloat16)
    pieces = (
        lax.all_gather(w_gate, "fsdp", axis=0, tiled=True),
        lax.all_gather(w_up, "fsdp", axis=0, tiled=True),
    )
    columns = normed_ffn
    gate = jnp.dot(columns, pieces[0], preferred_element_type=jnp.float32)
    up_proj = jnp.dot(columns, pieces[1], preferred_element_type=jnp.float32)
    hidden = (jax.nn.silu(gate) * up_proj).astype(jnp.bfloat16)
    columns = hidden
    ffn_out = jnp.dot(
        columns,
        lax.all_gather(w_down, "fsdp", axis=0, tiled=True),
        preferred_element_type=jnp.float32,
    )
    outputs = (mixed + ffn_out).astype(jnp.bfloat16).reshape(tokens.shape)
    grad_low = cotangent.reshape(count, D)
    grad_high = grad_low.astype(jnp.float32)
    hidden_grad = right_trans(grad_low, lax.all_gather(w_down, "fsdp", axis=0, tiled=True))
    sigm = jax.nn.sigmoid(gate)
    gate_grad = (hidden_grad * up_proj * sigm * (1.0 + gate * (1.0 - sigm))).astype(jnp.bfloat16)
    up_grad = (hidden_grad * gate * sigm).astype(jnp.bfloat16)
    pieces = lax.all_gather((w_gate, w_up), "fsdp", axis=0, tiled=True)
    normed_ffn_grad = right_trans(gate_grad, pieces[0]) + right_trans(up_grad, pieces[1])
    gain_two_term = jnp.sum(normed_ffn_grad * normed_x2, axis=0)
    mixed_grad = norm_back(normed_ffn_grad, gain_two, normed_x2, scale_two, grad_high)
    attn_grad = mixed_grad.astype(jnp.bfloat16)
    context_grad = right_trans(attn_grad, full_out).astype(jnp.bfloat16)
    context_heads = lax.all_to_all(
        context_grad.reshape(micro, rows, parts, -1), "sp", split_axis=2, concat_axis=1, tiled=True
    )
    context_heads = context_heads.reshape(micro, length, kv_local, group_size, HEAD_DIM)

    def attend_back(carry, block_index):
        key_grad, value_grad = carry
        start = block_index * block_rows
        query_block = lax.dynamic_slice_in_dim(grouped, start, block_rows, 1)
        doc_block = lax.dynamic_slice_in_dim(doc_full, start, block_rows, 1)
        out_block = lax.dynamic_slice_in_dim(context_heads, start, block_rows, 1)
        row_block = start + jnp.arange(block_rows, dtype=jnp.int32)
        scores = block_scores(query_block, keys_head, doc_block, doc_full, row_block, places)
        probabilities = jnp.exp(scores - log_totals[block_index])
        prob_grad = jnp.einsum(
            "mbkgd,mlkd->mkgbl", out_block, values_head, preferred_element_type=jnp.float32
        )
        inner = jnp.sum(probabilities * prob_grad, axis=-1, keepdims=True)
        score_grad = (probabilities * (prob_grad - inner)).astype(jnp.bfloat16)
        query_grad = (
            jnp.einsum(
                "mkgbl,mlkd->mbkgd", score_grad, keys_head, preferred_element_type=jnp.float32
            )
            * score_scale
        )
        key_grad = (
            key_grad
            + jnp.einsum(
                "mkgbl,mbkgd->mlkd", score_grad, query_block, preferred_element_type=jnp.float32
            )
            * score_scale
        )
        value_grad = value_grad + jnp.einsum(
            "mkgbl,mbkgd->mlkd",
            probabilities.astype(jnp.bfloat16),
            out_block,
            preferred_element_type=jnp.float32,
        )
        return ((key_grad, value_grad), query_grad)

    empty_kv = jnp.zeros((micro, length, kv_local, HEAD_DIM), jnp.float32)
    (key_grad, value_grad), query_grads = lax.scan(
        attend_back, (empty_kv, empty_kv), jnp.arange(blocks, dtype=jnp.int32)
    )
    full_cos, full_sin = rope_tables(pos_full.reshape(micro * length))
    query_grad = jnp.moveaxis(query_grads, 0, 1).reshape(
        micro * length, kv_local * group_size, HEAD_DIM
    )
    query_grad = rotate(query_grad, full_cos, -full_sin).astype(jnp.bfloat16)
    key_grad = rotate(
        key_grad.reshape(micro * length, kv_local, HEAD_DIM), full_cos, -full_sin
    ).astype(jnp.bfloat16)
    value_grad = value_grad.astype(jnp.bfloat16)
    query_rows, key_rows, value_rows = (
        lax.all_to_all(
            query_grad.reshape(micro, length, 1, -1), "sp", split_axis=1, concat_axis=2, tiled=True
        ),
        lax.all_to_all(
            key_grad.reshape(micro, length, 1, -1), "sp", split_axis=1, concat_axis=2, tiled=True
        ),
        lax.all_to_all(
            value_grad.reshape(micro, length, 1, -1), "sp", split_axis=1, concat_axis=2, tiled=True
        ),
    )
    query_rows = query_rows.reshape(count, D)
    key_rows = key_rows.reshape(count, kv_width)
    value_rows = value_rows.reshape(count, kv_width)
    normed_grad = (
        right_trans(query_rows, full_query)
        + right_trans(key_rows, full_key)
        + right_trans(value_rows, full_value)
    )
    gain_one_term = jnp.sum(normed_grad * normed_x1, axis=0)
    input_grad = (
        norm_back(normed_grad, gain_one, normed_x1, scale_one, mixed_grad)
        .astype(jnp.bfloat16)
        .reshape(tokens.shape)
    )
    width_parts = lax.axis_size("fsdp")
    model_slice = D // width_parts
    hidden_slice = FF // width_parts
    normed_own, context_own, normed_ffn_own, hidden_own = (
        lax.all_to_all(
            normed.reshape(count, width_parts, model_slice),
            "fsdp",
            split_axis=1,
            concat_axis=0,
            tiled=True,
        ),
        lax.all_to_all(
            context_rows.reshape(count, width_parts, model_slice),
            "fsdp",
            split_axis=1,
            concat_axis=0,
            tiled=True,
        ),
        lax.all_to_all(
            normed_ffn.reshape(count, width_parts, model_slice),
            "fsdp",
            split_axis=1,
            concat_axis=0,
            tiled=True,
        ),
        lax.all_to_all(
            hidden.reshape(count, width_parts, hidden_slice),
            "fsdp",
            split_axis=1,
            concat_axis=0,
            tiled=True,
        ),
    )
    normed_own = normed_own.reshape(-1, model_slice)
    context_own = context_own.reshape(-1, model_slice)
    normed_ffn_own = normed_ffn_own.reshape(-1, model_slice)
    hidden_own = hidden_own.reshape(-1, hidden_slice)
    pieces = (
        lax.all_gather(query_rows, "fsdp", axis=0, tiled=True),
        lax.all_gather(key_rows, "fsdp", axis=0, tiled=True),
        lax.all_gather(value_rows, "fsdp", axis=0, tiled=True),
        lax.all_gather(attn_grad, "fsdp", axis=0, tiled=True),
        lax.all_gather(gate_grad, "fsdp", axis=0, tiled=True),
        lax.all_gather(up_grad, "fsdp", axis=0, tiled=True),
        lax.all_gather(grad_low, "fsdp", axis=0, tiled=True),
    )
    attn_total = jnp.concatenate(
        [
            trans_dot(normed_own, pieces[0]),
            trans_dot(normed_own, pieces[1]),
            trans_dot(normed_own, pieces[2]),
            trans_dot(context_own, pieces[3]),
        ],
        axis=1,
    )
    ffn_total = jnp.concatenate(
        [trans_dot(normed_ffn_own, pieces[4]), trans_dot(normed_ffn_own, pieces[5])], axis=1
    )
    down_total = trans_dot(hidden_own, pieces[6])
    return (outputs, input_grad, attn_total, ffn_total, down_total, gain_one_term, gain_two_term)


def body(
    tokens,
    doc_starts,
    cotangent,
    gain_attn,
    gain_ffn,
    w_query,
    w_key,
    w_value,
    w_out,
    w_gate,
    w_up,
    w_down,
):
    weights = (gain_attn, gain_ffn, w_query, w_key, w_value, w_out, w_gate, w_up, w_down)
    micro_count = tokens.shape[0]
    results = [
        run_layer(
            tokens[batch_index : batch_index + 1],
            doc_starts[batch_index : batch_index + 1],
            cotangent[batch_index : batch_index + 1],
            weights,
        )
        for batch_index in range(micro_count)
    ]
    outputs = jnp.concatenate([layer_result[0] for layer_result in results], axis=0)
    input_grad = jnp.concatenate([layer_result[1] for layer_result in results], axis=0)
    attn_shard = sum((layer_result[2] for layer_result in results))
    ffn_shard = sum((layer_result[3] for layer_result in results))
    down_shard = sum((layer_result[4] for layer_result in results))
    gain_one_term = sum((layer_result[5] for layer_result in results))
    gain_two_term = sum((layer_result[6] for layer_result in results))
    gain_one_part, gain_two_part = (
        lax.psum_scatter(gain_one_term, "fsdp", scatter_dimension=0, tiled=True),
        lax.psum_scatter(gain_two_term, "fsdp", scatter_dimension=0, tiled=True),
    )
    summed = (
        lax.psum(gain_one_part.astype(jnp.bfloat16), "sp").astype(jnp.float32),
        lax.psum(gain_two_part.astype(jnp.bfloat16), "sp").astype(jnp.float32),
        lax.psum(attn_shard.astype(jnp.bfloat16), "sp").astype(jnp.float32),
        lax.psum(ffn_shard.astype(jnp.bfloat16), "sp").astype(jnp.float32),
        lax.psum(down_shard.astype(jnp.bfloat16), "sp").astype(jnp.float32),
    )
    kv_width = KV_HEADS * HEAD_DIM
    attn_total = summed[2]
    ffn_total = summed[3]
    return (
        outputs,
        input_grad,
        summed[0],
        summed[1],
        attn_total[:, :D],
        attn_total[:, D : D + kv_width],
        attn_total[:, D + kv_width : D + 2 * kv_width],
        attn_total[:, D + 2 * kv_width :],
        ffn_total[:, :FF],
        ffn_total[:, FF:],
        summed[4],
    )


def solution(mesh):
    placed = (
        P(None, "fsdp", "sp", None),
        P(None, "fsdp", None),
        P(None, "fsdp", "sp", None),
        P("fsdp"),
        P("fsdp"),
        P("fsdp", None),
        P("fsdp", None),
        P("fsdp", None),
        P("fsdp", None),
        P("fsdp", None),
        P("fsdp", None),
        P("fsdp", None),
    )
    return jax.shard_map(
        body,
        mesh=mesh,
        in_specs=placed,
        out_specs=(
            P(None, "fsdp", "sp", None),
            P(None, "fsdp", "sp", None),
            P("fsdp"),
            P("fsdp"),
            P("fsdp", None),
            P("fsdp", None),
            P("fsdp", None),
            P("fsdp", None),
            P("fsdp", None),
            P("fsdp", None),
            P("fsdp", None),
        ),
        check_vma=False,
    )
```

profile of v0, /device:TPU:1, one launch (start us, length us, event | category | flops | bytes accessed | tf_op | source)
XLA Modules:
  0.0 3120.4 jit_solution(2860277702329666126)
XLA Ops:
  13.8 22.6 all-reduce.5
  59.4 20.8 all-gather.28.cloned.1.call-done
  110.6 45.8 %all-gather.24.cloned.1.call-done = bf16[2560,2560]{1,0:T(8,128)(2,1)} async-done(((bf16[320,2560]{1,0:T(8,128)(2,1)}), bf16[2560,2560]{1,0:T(8,128)(2,1)}) %all-gather.24.cloned.1.call-update) | async-done | bytes 13107216 | tf_op jit(solution)/shard_map/all_gather | solution.py:95
  156.5 17.9 copy.221
  231.6 31.8 %while.57 = (s32[]{:T(128)}, bf16[2,1,512,2,4,80]{2,5,4,3,1,0:T(8,128)(2,1)S(1)}, f32[2,1,2,4,512,1]{4,3,2,5,1,0:T(4,128)S(1)}, s32[2]{0:T(128)S(1)}, s32[1,1024...) while((s32[]{:T(128)}, ...), condition=%wide.region_14.15_spmd.clone, body=%wide.region_11.14_spmd.clone.sunk | while | flops 1394078208 | bytes 55195848 | solution.py:147
  298.8 31.6 %while.56 = (s32[]{:T(128)}, bf16[2,1,512,2,4,80]{2,5,4,3,1,0:T(8,128)(2,1)S(1)}, f32[2,1,2,4,512,1]{4,3,2,5,1,0:T(4,128)S(1)}, s32[2]{0:T(128)S(1)}, s32[1,1024...) while((s32[]{:T(128)}, ...), condition=%wide.region_6.7_spmd.clone, body=%wide.region_3.0_spmd.clone.sunk | while | flops 1394078208 | bytes 55195848 | solution.py:147
  368.4 23.2 all-to-all-done.3
  419.8 23.1 fusion.215
  442.9 143.7 %all-gather.34.cloned.1.call-done = bf16[2560,7168]{1,0:T(8,128)(2,1)} async-done(((bf16[320,7168]{1,0:T(8,128)(2,1)}), bf16[2560,7168]{1,0:T(8,128)(2,1)}) %all-gather.34.cloned.1.call-update) | async-done | bytes 36700176 | tf_op jit(solution)/shard_map/all_gather | solution.py:158
  586.6 22.5 fusion.216
  609.1 154.7 %all-gather.36.cloned.1.call-done = bf16[7168,2560]{1,0:T(8,128)(2,1)} async-done(((bf16[896,2560]{1,0:T(8,128)(2,1)}), bf16[7168,2560]{1,0:T(8,128)(2,1)}) %all-gather.36.cloned.1.call-update) | async-done | bytes 36700176 | tf_op jit(solution)/shard_map/all_gather | solution.py:167
  763.8 23.3 multiply_convert_fusion.2
  787.1 20.2 fusion.219
  807.3 20.8 multiply_reduce_fusion.1
  828.2 21.4 fusion.217
  849.5 19.9 fusion.218
  869.4 24.0 multiply_convert_fusion
  893.4 18.8 fusion.221
  912.3 21.0 multiply_reduce_fusion
  953.8 31.0 all-to-all-done.8
  990.2 167.4 %while.58 = (s32[]{:T(128)}, f32[1,1024,2,80]{1,3,2,0:T(8,128)}, f32[1,1024,2,80]{1,3,2,0:T(8,128)}, f32[2,1,512,2,4,80]{2,0,5,4,3,1:T(2,128)}, s32[2]{0:T(128)S...) while((s32[]{:T(128)}, f32[1,1024,2,80]{1,3,2,0:T(8,128)}, ...), condition=%wide.region_19.20_spmd.clone, body=%wide.region_17.19_spmd.clone.sunk | while | flops 3421073920 | bytes 226818576 | solution.py:224
  1003.5 14.7 fusion.377
  1020.2 10.8 fusion.378
  1049.5 24.2 dynamic_update_slice.40
  1086.8 14.7 fusion.377
  1103.5 10.8 fusion.378
  1132.9 24.2 dynamic_update_slice.40
  1164.3 11.3 all_to_all.360
  1200.7 21.7 all-to-all-done.12
  1241.7 167.6 %while.59 = (s32[]{:T(128)}, f32[1,1024,2,80]{1,3,2,0:T(8,128)}, f32[1,1024,2,80]{1,3,2,0:T(8,128)}, f32[2,1,512,2,4,80]{2,0,5,4,3,1:T(2,128)}, s32[2]{0:T(128)S...) while((s32[]{:T(128)}, f32[1,1024,2,80]{1,3,2,0:T(8,128)}, ...), condition=%wide.region_25.26_spmd.clone, body=%wide.region_23.25_spmd.clone.sunk | while | flops 3421073920 | bytes 226818576 | solution.py:224
  1255.0 14.7 fusion.392
  1272.1 10.8 fusion.393
  1301.4 24.2 dynamic_update_slice.41
  1338.8 14.7 fusion.392
  1355.5 10.8 fusion.393
  1384.9 24.2 dynamic_update_slice.41
  1416.0 12.4 all_to_all.361
  1436.8 11.9 all_to_all.362
  1481.4 33.4 %all_to_all.363 = bf16[4,2,81920]{2,1,0:T(2,128)(2,1)} all-to-all(bf16[4,2,81920]{2,1,0:T(2,128)(2,1)S(1)} %reshape.1724), channel_id=1, replica_groups=mesh['fsdp'=8,'sp'=4] {'sp'}, dimensions={0} | all-to-all | bytes 2621440 | tf_op jit(solution)/shard_map/all_to_all | solution.py:237
  1545.2 33.3 %all_to_all.364 = bf16[4,2,81920]{2,1,0:T(2,128)(2,1)} all-to-all(bf16[4,2,81920]{2,1,0:T(2,128)(2,1)S(1)} %reshape.1718), channel_id=1, replica_groups=mesh['fsdp'=8,'sp'=4] {'sp'}, dimensions={0} | all-to-all | bytes 2621440 | tf_op jit(solution)/shard_map/all_to_all | solution.py:237
  1600.7 34.1 %all_to_all.365 = bf16[256,8,320]{0,2,1:T(8,128)(2,1)S(1)} all-to-all(bf16[256,8,320]{0,2,1:T(8,128)(2,1)S(1)} %get-tuple-element.525), channel_id=1, replica_groups=mesh['fsdp'=8,'sp'=4] {'fsdp'}, dimensions={1} | all-to-all | bytes 2621440 | tf_op jit(solution)/shard_map/all_to_all | solution.py:265
  1634.9 28.0 all_to_all.366
  1662.9 27.3 all_to_all.367
  1698.5 27.2 all-to-all-done.19
  1735.1 18.4 all-to-all-done.20
  1766.3 15.5 all-to-all-done.21
  1794.8 49.4 %all-to-all-done.23 = bf16[256,8,896]{2,0,1:T(8,128)(2,1)} async-done(((bf16[256,8,896]{2,0,1:T(8,128)(2,1)}), bf16[256,8,896]{2,0,1:T(8,128)(2,1)}, u32[]{:S(2)}, u32[]{:S(2)}) %all-to-all-start.23) | async-done | bytes 3670048 | tf_op jit(solution)/shard_map/all_to_all | solution.py:286
  1862.9 15.8 fusion.129
  1878.6 46.9 %all-to-all-done.22 = bf16[256,8,896]{2,0,1:T(8,128)(2,1)} async-done(((bf16[256,8,896]{2,0,1:T(8,128)(2,1)}), bf16[256,8,896]{2,0,1:T(8,128)(2,1)}, u32[]{:S(2)}, u32[]{:S(2)}) %all-to-all-start.22) | async-done | bytes 3670048 | tf_op jit(solution)/shard_map/all_to_all | solution.py:286
  1925.5 16.7 add_convert_fusion
  1999.5 21.3 all-gather.56.cloned.1.call-done
  2020.7 21.5 fusion.232
  2042.2 123.5 %all-gather.54.cloned.1.call-done = bf16[2048,7168]{1,0:T(8,128)(2,1)} async-done(((bf16[256,7168]{1,0:T(8,128)(2,1)}), bf16[2048,7168]{1,0:T(8,128)(2,1)}) %all-gather.54.cloned.1.call-update) | async-done | bytes 29360144 | tf_op jit(solution)/shard_map/all_gather | solution.py:303
  2165.7 17.9 fusion.231
  2183.7 126.9 %all-gather.60.cloned.1.call-done = bf16[2048,7168]{1,0:T(8,128)(2,1)} async-done(((bf16[256,7168]{1,0:T(8,128)(2,1)}), bf16[2048,7168]{1,0:T(8,128)(2,1)}) %all-gather.60.cloned.1.call-update) | async-done | bytes 29360144 | tf_op jit(solution)/shard_map/all_gather | solution.py:304
  2310.6 17.3 fusion.234
  2327.9 127.7 %all-gather.58.cloned.1.call-done = bf16[2048,7168]{1,0:T(8,128)(2,1)} async-done(((bf16[256,7168]{1,0:T(8,128)(2,1)}), bf16[2048,7168]{1,0:T(8,128)(2,1)}) %all-gather.58.cloned.1.call-update) | async-done | bytes 29360144 | tf_op jit(solution)/shard_map/all_gather | solution.py:303
  2455.6 17.3 fusion.233
  2472.9 13.3 fusion.128
  2486.9 19.5 fusion.138
  2506.5 18.4 fusion.139
  2555.6 21.7 all-reduce.4
  2600.0 485.2 %all-reduce.10.cloned.1.call-done = (bf16[320,6400]{1,0:T(8,128)(2,1)}, bf16[320,14336]{1,0:T(8,128)(2,1)}, bf16[896,2560]{1,0:T(8,128)(2,1)}) async-done(((bf16[320,6400]{1,0:T(8,128)(2,1)}, bf16[320,14336]{1,0:T(8,128)(2,1)}, bf16[896,2560]{1,0:T(8,128)(2,1)}), (bf16[320,6400]{1,0:T(8,128)(2,1)}, bf16[320,14336]{1,0:T(8,128)(2,1)}, bf16[896,2560]{1,0:T(8,128)(2,1)})) %all-reduce.10.cloned.1.call-update) | async-done | bytes 17858576 | tf_op jit(solution)/shard_map/psum | solution.py:362
  3093.2 12.9 fusion.210
  (617 shorter events, 766.9 us)
Async XLA Ops:
  7.2 38.3 %all-gather.26.cloned.1.call-start = ((), (), s32[]{:S(2)}) async-start(), calls=%async_computation.25 | async-start | bytes 3686400 | tf_op jit(solution)/shard_map/all_gather | solution.py:96
  7.9 72.3 %all-gather.28.cloned.1.call-start = ((), (), s32[]{:S(2)}) async-start(), calls=%async_computation.26 | async-start | bytes 3686400 | tf_op jit(solution)/shard_map/all_gather | solution.py:97
  8.7 147.8 %all-gather.24.cloned.1.call-start = ((), (), s32[]{:S(2)}) async-start(), calls=%async_computation.24 | async-start | bytes 14745600 | tf_op jit(solution)/shard_map/all_gather | solution.py:95
  9.4 392.0 %all-gather.30.cloned.1.call-start = ((), (), s32[]{:S(2)}) async-start(), calls=%async_computation.27 | async-start | bytes 14745600 | tf_op jit(solution)/shard_map/all_gather | solution.py:98
  10.0 408.8 %all-gather.32.cloned.1.call-start = ((), (), s32[]{:S(2)}) async-start(), calls=%async_computation.28 | async-start | bytes 41287680 | tf_op jit(solution)/shard_map/all_gather | solution.py:157
  10.6 576.1 %all-gather.34.cloned.1.call-start = ((), (), s32[]{:S(2)}) async-start(), calls=%async_computation.29 | async-start | bytes 41287680 | tf_op jit(solution)/shard_map/all_gather | solution.py:158
  11.2 25.3 copy-start.99
  11.2 25.4 copy-start.7
  11.2 752.6 %all-gather.36.cloned.1.call-start = ((), (), s32[]{:S(2)}) async-start(), calls=%async_computation.30 | async-start | bytes 41287680 | tf_op jit(solution)/shard_map/all_gather | solution.py:167
  36.4 169.2 %copy-start.71 = (f32[2560]{0:T(1024)}, f32[2560]{0:T(1024)S(1)}, u32[]{:S(2)}) copy-start(f32[2560]{0:T(1024)S(1)} %convert_element_type.348) | copy-start | bytes 30724
  37.2 141.6 %copy-start.90 = (f32[256]{0:T(256)}, f32[256]{0:T(256)S(1)}, u32[]{:S(2)}) copy-start(f32[256]{0:T(256)S(1)} %get-tuple-element.552) | copy-start | bytes 3076
  37.2 168.4 %copy-start.87 = (f32[256]{0:T(256)}, f32[256]{0:T(256)S(1)}, u32[]{:S(2)}) copy-start(f32[256]{0:T(256)S(1)} %get-tuple-element.553) | copy-start | bytes 3076
  55.1 29.2 all-to-all-start.5
  84.3 13.1 all-to-all-start.6
  97.4 77.0 %all-to-all-start.1 = ((bf16[1,256,4,160]{1,3,0,2:T(8,128)(2,1)}), bf16[1,256,4,160]{1,3,0,2:T(8,128)(2,1)}, u32[]{:S(2)}, u32[]{:S(2)}) async-start(bf16[1,256,4,160]{1,3,0,2:T(8,128)(2,1)} %bitcast.989), calls=%async_computation.1 | async-start | bytes 655360 | tf_op jit(solution)/shard_map/all_to_all | solution.py:119
  101.5 1761.4 %all-gather.64.cloned.1.call-start = ((), (), s32[]{:S(2)}) async-start(), calls=%async_computation.44 | async-start | bytes 11796480 | tf_op jit(solution)/shard_map/all_gather | solution.py:305
  174.4 13.2 all-to-all-start.2
  187.6 35.5 %all-to-all-start.4 = ((bf16[1,256,4,640]{1,3,0,2:T(8,128)(2,1)}), bf16[1,256,4,640]{1,3,0,2:T(8,128)(2,1)}, u32[]{:S(2)}, u32[]{:S(2)}) async-start(bf16[1,256,4,640]{1,3,0,2:T(8,128)(2,1)} %bitcast.943), calls=%async_computation.4 | async-start | bytes 2621440 | tf_op jit(solution)/shard_map/all_to_all | solution.py:116
  223.0 66.7 %all-to-all-start = ((bf16[1,256,4,640]{1,3,0,2:T(8,128)(2,1)}), bf16[1,256,4,640]{1,3,0,2:T(8,128)(2,1)}, u32[]{:S(2)}, u32[]{:S(2)}) async-start(bf16[1,256,4,640]{1,3,0,2:T(8,128)(2,1)} %bitcast.9), calls=%async_computation | async-start | bytes 2621440 | tf_op jit(solution)/shard_map/all_to_all | solution.py:116
  289.7 66.2 %all-to-all-start.7 = ((bf16[4,2,81920]{2,1,0:T(2,128)(2,1)}), bf16[4,2,81920]{2,1,0:T(2,128)(2,1)}, u32[]{:S(2)}, u32[]{:S(2)}) async-start(bf16[4,2,81920]{2,1,0:T(2,128)(2,1)} %reshape.1714), calls=%async_computation.7 | async-start | bytes 2621440 | tf_op jit(solution)/shard_map/all_to_all | solution.py:149
  356.0 35.6 %all-to-all-start.3 = ((bf16[4,2,81920]{2,1,0:T(2,128)(2,1)}), bf16[4,2,81920]{2,1,0:T(2,128)(2,1)}, u32[]{:S(2)}, u32[]{:S(2)}) async-start(bf16[4,2,81920]{2,1,0:T(2,128)(2,1)} %reshape.1716), calls=%async_computation.3 | async-start | bytes 2621440 | tf_op jit(solution)/shard_map/all_to_all | solution.py:149
  360.7 1518.0 %all-gather.62.cloned.1.call-start = ((), (), s32[]{:S(2)}) async-start(), calls=%async_computation.43 | async-start | bytes 11796480 | tf_op jit(solution)/shard_map/all_gather | solution.py:305
  361.4 571.9 %copy-start.69 = (f32[2560]{0:T(1024)}, f32[2560]{0:T(1024)S(1)}, u32[]{:S(2)}) copy-start(f32[2560]{0:T(1024)S(1)} %convert_element_type.358) | copy-start | bytes 30724
  408.9 524.5 %copy-start.75 = (f32[256]{0:T(256)}, f32[256]{0:T(256)S(1)}, u32[]{:S(2)}) copy-start(f32[256]{0:T(256)S(1)} %add_rsqrt_fusion.2) | copy-start | bytes 3076
  418.4 514.9 %copy-start.81 = (f32[256]{0:T(256)}, f32[256]{0:T(256)S(1)}, u32[]{:S(2)}) copy-start(f32[256]{0:T(256)S(1)} %add_rsqrt_fusion) | copy-start | bytes 3076
  442.9 320.9 %copy-start.16 = (bf16[2,1,256,2560]{3,2,1,0:T(8,128)(2,1)S(1)}, bf16[2,1,256,2560]{3,2,1,0:T(8,128)(2,1)}, u32[]{:S(2)}) copy-start(bf16[2,1,256,2560]{3,2,1,0:T(8,128)(2,1)} %param.22) | copy-start | bytes 7864324
  787.1 20.2 copy-start.12
  828.2 21.4 copy-start.50
  828.2 105.2 %copy-start.83 = (f32[256]{0:T(256)}, f32[256]{0:T(256)S(1)}, u32[]{:S(2)}) copy-start(f32[256]{0:T(256)S(1)} %broadcast_multiply_fusion.3) | copy-start | bytes 3076
  949.6 35.1 %all-to-all-start.8 = ((bf16[1,256,4,640]{3,1,0,2:T(8,128)(2,1)}), bf16[1,256,4,640]{3,1,0,2:T(8,128)(2,1)S(1)}, u32[]{:S(2)}, u32[]{:S(2)}) async-start(bf16[1,256,4,640]{3,1,0,2:T(8,128)(2,1)} %copy.243), calls=%async_computation.8 | async-start | bytes 2621440 | tf_op jit(solution)/shard_map/all_to_all | solution.py:183
  953.8 988.5 %all-gather.42.cloned.1.call-start = ((), (), s32[]{:S(2)}) async-start(), calls=%async_computation.33 | async-start | bytes 2949120 | tf_op jit(solution)/shard_map/all_gather | solution.py:301
  1003.5 16.7 slice-start.3
  1086.8 16.7 slice-start.3
  1188.1 34.3 %all-to-all-start.12 = ((bf16[1,256,4,640]{3,1,0,2:T(8,128)(2,1)}), bf16[1,256,4,640]{3,1,0,2:T(8,128)(2,1)S(1)}, u32[]{:S(2)}, u32[]{:S(2)}) async-start(bf16[1,256,4,640]{3,1,0,2:T(8,128)(2,1)} %copy.254), calls=%async_computation.12 | async-start | bytes 2621440 | tf_op jit(solution)/shard_map/all_to_all | solution.py:183
  1222.4 12.7 all-to-all-start.10
  1226.5 719.6 %all-gather.40.cloned.1.call-start = ((), (), s32[]{:S(2)}) async-start(), calls=%async_computation.32 | async-start | bytes 2949120 | tf_op jit(solution)/shard_map/all_gather | solution.py:300
  1239.3 710.7 %all-gather.50.cloned.1.call-start = ((), (), s32[]{:S(2)}) async-start(), calls=%async_computation.37 | async-start | bytes 2949120 | tf_op jit(solution)/shard_map/all_gather | solution.py:301
  1255.0 17.2 slice-start.7
  1338.8 16.7 slice-start.7
  1431.0 522.8 %all-gather.48.cloned.1.call-start = ((), (), s32[]{:S(2)}) async-start(), calls=%async_computation.36 | async-start | bytes 2949120 | tf_op jit(solution)/shard_map/all_gather | solution.py:300
  1456.3 501.4 %all-gather.44.cloned.1.call-start = ((), (), s32[]{:S(2)}) async-start(), calls=%async_computation.34 | async-start | bytes 11796480 | tf_op jit(solution)/shard_map/all_gather | solution.py:302
  1456.8 508.0 %all-gather.52.cloned.1.call-start = ((), (), s32[]{:S(2)}) async-start(), calls=%async_computation.38 | async-start | bytes 11796480 | tf_op jit(solution)/shard_map/all_gather | solution.py:302
  1457.4 517.0 %all-gather.38.cloned.1.call-start = ((), (), s32[]{:S(2)}) async-start(), calls=%async_computation.31 | async-start | bytes 11796480 | tf_op jit(solution)/shard_map/all_gather | solution.py:299
  1521.5 462.7 %all-gather.46.cloned.1.call-start = ((), (), s32[]{:S(2)}) async-start(), calls=%async_computation.35 | async-start | bytes 11796480 | tf_op jit(solution)/shard_map/all_gather | solution.py:299
  1585.2 435.5 %all-gather.56.cloned.1.call-start = ((), (), s32[]{:S(2)}) async-start(), calls=%async_computation.40 | async-start | bytes 33030144 | tf_op jit(solution)/shard_map/all_gather | solution.py:304
  1585.8 580.0 %all-gather.54.cloned.1.call-start = ((), (), s32[]{:S(2)}) async-start(), calls=%async_computation.39 | async-start | bytes 33030144 | tf_op jit(solution)/shard_map/all_gather | solution.py:303
  1586.5 724.1 %all-gather.60.cloned.1.call-start = ((), (), s32[]{:S(2)}) async-start(), calls=%async_computation.42 | async-start | bytes 33030144 | tf_op jit(solution)/shard_map/all_gather | solution.py:304
  1587.1 868.4 %all-gather.58.cloned.1.call-start = ((), (), s32[]{:S(2)}) async-start(), calls=%async_computation.41 | async-start | bytes 33030144 | tf_op jit(solution)/shard_map/all_gather | solution.py:303
  1600.7 62.1 %copy-start.20 = (bf16[1,256,4,1,640]{1,4,2,3,0:T(8,128)(2,1)S(1)}, bf16[1,256,4,1,640]{1,4,2,3,0:T(8,128)(2,1)}, u32[]{:S(2)}) copy-start(bf16[1,256,4,1,640]{1,4,2,3,0:T(8,128)(2,1)} %copy.232) | copy-start | bytes 3932164
  1662.9 34.2 %copy-start.30 = (bf16[256,2560]{1,0:T(8,128)(2,1)S(1)}, bf16[256,2560]{1,0:T(8,128)(2,1)}, u32[]{:S(2)}) copy-start(bf16[256,2560]{1,0:T(8,128)(2,1)} %copy-done.29) | copy-start | bytes 3932164
  1690.2 35.5 %all-to-all-start.19 = ((bf16[256,8,320]{0,2,1:T(8,128)(2,1)}), bf16[256,8,320]{0,2,1:T(8,128)(2,1)}, u32[]{:S(2)}, u32[]{:S(2)}) async-start(bf16[256,8,320]{0,2,1:T(8,128)(2,1)} %bitcast.84), calls=%async_computation.19 | async-start | bytes 2621440 | tf_op jit(solution)/shard_map/all_to_all | solution.py:272
  1725.7 27.8 all-to-all-start.20
  1753.5 28.3 all-to-all-start.21
  1781.8 62.5 %all-to-all-start.23 = ((bf16[256,8,896]{2,0,1:T(8,128)(2,1)}), bf16[256,8,896]{2,0,1:T(8,128)(2,1)}, u32[]{:S(2)}, u32[]{:S(2)}) async-start(bf16[256,8,896]{2,0,1:T(8,128)(2,1)} %bitcast.920), calls=%async_computation.23 | async-start | bytes 7340032 | tf_op jit(solution)/shard_map/all_to_all | solution.py:286
  1844.2 81.3 %all-to-all-start.22 = ((bf16[256,8,896]{2,0,1:T(8,128)(2,1)}), bf16[256,8,896]{2,0,1:T(8,128)(2,1)}, u32[]{:S(2)}, u32[]{:S(2)}) async-start(bf16[256,8,896]{2,0,1:T(8,128)(2,1)} %bitcast.919), calls=%async_computation.22 | async-start | bytes 7340032 | tf_op jit(solution)/shard_map/all_to_all | solution.py:286
  1852.1 1233.1 %all-reduce.10.cloned.1.call-start = ((), (), s32[]{:S(2)}) async-start(), calls=%async_computation.45 | async-start | bytes 35717120 | tf_op jit(solution)/shard_map/psum | solution.py:362
  1854.0 99.8 %copy-start.53 = (bf16[40,8,8,256]{3,1,2,0:T(8,128)(2,1)}, bf16[40,8,8,256]{3,1,2,0:T(8,128)(2,1)S(1)}, u32[]{:S(2)}) copy-start(bf16[40,8,8,256]{3,1,2,0:T(8,128)(2,1)S(1)} %copy.319) | copy-start | bytes 3932164
  2020.7 145.0 %copy-start.52 = (bf16[40,8,8,256]{3,1,2,0:T(8,128)(2,1)S(1)}, bf16[40,8,8,256]{3,1,2,0:T(8,128)(2,1)}, u32[]{:S(2)}) copy-start(bf16[40,8,8,256]{3,1,2,0:T(8,128)(2,1)} %copy.321) | copy-start | bytes 3932164
  2042.2 268.4 %copy-start.51 = (bf16[40,8,8,256]{3,1,2,0:T(8,128)(2,1)S(1)}, bf16[40,8,8,256]{3,1,2,0:T(8,128)(2,1)}, u32[]{:S(2)}) copy-start(bf16[40,8,8,256]{3,1,2,0:T(8,128)(2,1)} %copy.322) | copy-start | bytes 3932164
  2455.5 17.3 copy-start.27
  2486.9 19.5 copy-start.13
  2551.3 37.7 %copy-start.70 = (f32[2560]{0:T(1024)S(1)}, f32[2560]{0:T(1024)}, u32[]{:S(2)}) copy-start(f32[2560]{0:T(1024)} %copy-done.69) | copy-start | bytes 30724
  2551.3 37.7 %copy-start.82 = (f32[256]{0:T(256)S(1)}, f32[256]{0:T(256)}, u32[]{:S(2)}) copy-start(f32[256]{0:T(256)} %copy-done.81) | copy-start | bytes 3076
  2551.3 37.7 %copy-start.86 = (f32[256]{0:T(256)S(1)}, f32[256]{0:T(256)}, u32[]{:S(2)}) copy-start(f32[256]{0:T(256)} %copy-done.85) | copy-start | bytes 3076
  (104 other events, 745.1 us)
Sparse Core Ops, SparseCore 0:
  9.9 35.5 all-gather.25
  47.4 32.8 all-gather.27
  82.1 74.3 all-gather.23
  158.2 74.3 all-gather.29
  234.4 175.1 all-gather.31
  411.4 175.1 all-gather.33
  588.5 175.1 all-gather.35
  765.7 63.2 all-gather.63
  830.8 63.3 all-gather.61
  1178.3 30.7 all-gather.41
  1239.4 31.0 all-gather.39
  1431.1 30.7 all-gather.49
  1463.8 30.5 all-gather.47
  1496.1 63.2 all-gather.43
  1561.1 76.5 all-gather.51
  1639.5 91.3 all-gather.37
  1732.6 101.9 all-gather.45
  1836.9 183.8 all-gather.55
  2022.6 143.0 all-gather.53
  2167.5 143.0 all-gather.59
  2312.4 143.0 all-gather.57
  2486.3 598.8 all-reduce.9
where the time goes:
time: 3140 us; the launch traced here: 3120 us
  waiting for transfers between devices  1520 us (48%)
  matrix products  698 us (22%)
  local copies, waits for them, and re-layouts  350 us (11%)
  blocking collectives  246 us (8%)
  other arithmetic  189 us (6%)
  starting transfers between devices  86.6 us (3%)
    psum x1, waiting for transfers between devices, body(): lax.psum(attn_shard.astype(jnp.bfloat16), 'sp').astype(jnp.float32)  485 us
    all_gather x2, waiting for transfers between devices, run_layer(): lax.all_gather(gate_grad, 'fsdp', axis=0, tiled=True)  251 us
    dot_general x14, matrix products, right_trans(): lax.dot_general(left, right, (((1,), (1,)), ((), ())), preferred_element_...  172 us
    dot_general x14, matrix products, trans_dot(): lax.dot_general(left, right, (((0,), (0,)), ((), ())), preferred_element_...  158 us
    all_gather x1, waiting for transfers between devices, run_layer(): lax.all_gather(w_down, 'fsdp', axis=0, tiled=True)  155 us
    all_gather x2, waiting for transfers between devices, run_layer(): lax.all_gather(up_grad, 'fsdp', axis=0, tiled=True)  148 us
    all_gather x1, waiting for transfers between devices, run_layer(): lax.all_gather(w_up, 'fsdp', axis=0, tiled=True)  144 us
    dynamic_update_slice x8, local copies, waits for them, and re-layouts, run_layer(): lax.map(attend_forward, jnp.arange(blocks, dtype=jnp.int32))  102 us
  transfers between devices with their start and end apart: 38, of which 22 were waited for; matrix products, arithmetic and copies ran while one was open for 37% of the time, Pallas kernels for 0%

commit v1 on v0

v1 whole, which is shorter than its diff:
```python
import functools, math
import jax, jax.numpy as jnp
from jax import lax
from jax.experimental import pallas as pl
from jax.experimental.pallas import tpu as pltpu
from jax.sharding import PartitionSpec as P

D = 2560
HEADS = 32
KV_HEADS = 8
HEAD_DIM = 80
GROUP = HEADS // KV_HEADS
HALVES = 2
SCALE = HEAD_DIM ** -0.5
LOG2E = 1.0 / math.log(2.0)
QW = D // HALVES
KW = KV_HEADS * HEAD_DIM // HALVES
CHUNK = 640


def nt(left, right):
    return lax.dot_general(left, right, (((1,), (1,)), ((), ())), preferred_element_type=jnp.float32)


def tn(left, right):
    return lax.dot_general(left, right, (((0,), (0,)), ((), ())), preferred_element_type=jnp.float32)


def nn(left, right):
    return jnp.dot(left, right, preferred_element_type=jnp.float32)


def head(h):
    return slice(h * HEAD_DIM, (h + 1) * HEAD_DIM)


def spin(x, cosine, sine_up, sine_down):
    half = HEAD_DIM // 2
    width = x.shape[1]
    return x * cosine + pltpu.roll(x, width - half, 1) * sine_up + pltpu.roll(x, half, 1) * sine_down


def project_kernel(n_ref, w_ref, cos_ref, up_ref, down_ref, out_ref):
    j = pl.program_id(0)
    x = nn(n_ref[...], w_ref[...])
    turned = spin(x, cos_ref[...], up_ref[...], down_ref[...])
    lane = lax.broadcasted_iota(jnp.int32, x.shape, 1)
    keep = (j < D // CHUNK) | (lane < KW)
    out_ref[...] = jnp.where(keep, turned, x).astype(jnp.bfloat16)


def project(normed, weights, tables):
    rows = normed.shape[0]
    chunks = (D + 4 * KW) // CHUNK
    table = pl.BlockSpec((rows, CHUNK), lambda j: (0, 0))
    return pl.pallas_call(
        project_kernel,
        grid=(chunks,),
        in_specs=[pl.BlockSpec((rows, D), lambda j: (0, 0)), pl.BlockSpec((D, CHUNK), lambda j: (0, j)), table, table, table],
        out_specs=pl.BlockSpec((rows, CHUNK), lambda j: (0, j)),
        out_shape=jax.ShapeDtypeStruct((rows, chunks * CHUNK), jnp.bfloat16),
        compiler_params=pltpu.CompilerParams(vmem_limit_bytes=48 << 20),
        cost_estimate=pl.CostEstimate(flops=2 * rows * D * chunks * CHUNK, bytes_accessed=2 * (rows * D + D * chunks * CHUNK + rows * chunks * CHUNK), transcendentals=0),
        name="project",
    )(normed, weights, *tables)


def forward_kernel(blocks, q_ref, *refs):
    kv_refs = refs[:blocks]
    bias_ref, ctx_ref, lse_ref = refs[blocks:]
    rows = q_ref.shape[0]
    bias = [bias_ref[s] for s in range(blocks)]
    lane = lax.broadcasted_iota(jnp.int32, (rows, 128), 1)
    lse_all = jnp.zeros((rows, 128), jnp.float32)
    for h in range(QW // HEAD_DIM):
        c = h // GROUP
        q = q_ref[:, head(h)]
        scores = [nt(q, kv_refs[s][:, head(c)]) * (SCALE * LOG2E) + bias_ref[s] for s in range(blocks)]
        top = functools.reduce(jnp.maximum, scores).max(axis=1, keepdims=True)
        probs = [jnp.exp2(x - top) for x in scores]
        total = functools.reduce(jnp.add, probs).sum(axis=1, keepdims=True)
        ctx = functools.reduce(jnp.add, [nn(p.astype(jnp.bfloat16), kv_refs[s][:, KW + c * HEAD_DIM:KW + (c + 1) * HEAD_DIM]) for s, p in enumerate(probs)])
        ctx_ref[:, head(h)] = (ctx / total).astype(jnp.bfloat16)
        lse_all = jnp.where(lane == h, top + jnp.log2(total), lse_all)
    lse_ref[...] = lse_all


def attend(qkv, kv_blocks, bias, at):
    rows = kv_blocks[0].shape[0]
    blocks = len(kv_blocks)
    kv_spec = pl.BlockSpec((rows, 2 * KW), lambda h: (0, h))
    return pl.pallas_call(
        functools.partial(forward_kernel, blocks),
        grid=(HALVES,),
        in_specs=[pl.BlockSpec((rows, QW), lambda h: (at, h))] + [kv_spec] * blocks + [pl.BlockSpec((blocks, rows, rows), lambda h: (0, 0, 0))],
        out_specs=[pl.BlockSpec((rows, QW), lambda h: (0, h)), pl.BlockSpec((rows, 128), lambda h: (0, h))],
        out_shape=[jax.ShapeDtypeStruct((rows, D), jnp.bfloat16), jax.ShapeDtypeStruct((rows, HALVES * 128), jnp.float32)],
        compiler_params=pltpu.CompilerParams(vmem_limit_bytes=48 << 20),
        cost_estimate=pl.CostEstimate(flops=4 * rows * rows * blocks * HEADS * 128, bytes_accessed=2 * rows * D * (2 + blocks // 2), transcendentals=rows * rows * blocks * HEADS),
        name="attend",
    )(qkv, *kv_blocks, bias)


def backward_kernel(blocks, q_ref, dctx_ref, ctx_ref, lse_ref, *refs):
    kv_refs = refs[:blocks]
    bias_ref, cos_ref, up_ref, down_ref, dq_ref = refs[blocks:blocks + 5]
    dkv_refs = refs[blocks + 5:2 * blocks + 5]
    dq_acc = refs[-1]
    rows = q_ref.shape[0]
    count = QW // HEAD_DIM
    owner = lax.broadcasted_iota(jnp.int32, (count, QW), 0)
    lane = lax.broadcasted_iota(jnp.int32, (count, QW), 1)
    pick = ((lane >= owner * HEAD_DIM) & (lane < owner * HEAD_DIM + HEAD_DIM)).astype(jnp.float32)
    product = dctx_ref[...].astype(jnp.float32) * ctx_ref[...].astype(jnp.float32)
    delta = lax.dot_general(pick, product, (((1,), (1,)), ((), ())), precision=lax.Precision.HIGHEST, preferred_element_type=jnp.float32)
    for c in range(KV_HEADS // HALVES):
        heads = range(c * GROUP, (c + 1) * GROUP)
        qs = [q_ref[:, head(h)] for h in heads]
        ds = [dctx_ref[:, head(h)] for h in heads]
        q_stack = jnp.concatenate(qs, axis=0)
        d_stack = jnp.concatenate(ds, axis=0)
        dq = [None] * GROUP
        for s in range(blocks):
            k = kv_refs[s][:, head(c)]
            v = kv_refs[s][:, KW + c * HEAD_DIM:KW + (c + 1) * HEAD_DIM]
            ps, dss = [], []
            for g, h in enumerate(heads):
                score = nt(k, qs[g]) * (SCALE * LOG2E) + bias_ref[s]
                p = jnp.exp2(score - lse_ref[h:h + 1, :])
                dp = nt(v, ds[g])
                d = (p * (dp - delta[h:h + 1, :])).astype(jnp.bfloat16)
                ps.append(p.astype(jnp.bfloat16))
                dss.append(d)
                term = tn(d, k)
                dq[g] = term if dq[g] is None else dq[g] + term
            dkv_refs[s][:, head(c)] = (nn(jnp.concatenate(dss, axis=1), q_stack) * SCALE).astype(jnp.bfloat16)
            dkv_refs[s][:, KW + c * HEAD_DIM:KW + (c + 1) * HEAD_DIM] = nn(jnp.concatenate(ps, axis=1), d_stack).astype(jnp.bfloat16)
        for g, h in enumerate(heads):
            dq_acc[:, head(h)] = dq[g] * SCALE
    for j in range(QW // CHUNK):
        part = slice(j * CHUNK, (j + 1) * CHUNK)
        dq_ref[:, part] = spin(dq_acc[:, part], cos_ref[...], -up_ref[...], -down_ref[...]).astype(jnp.bfloat16)


def attend_back(qkv, dctx, ctx, lse_rows, kv_blocks, bias_t, tables, at):
    rows = kv_blocks[0].shape[0]
    blocks = len(kv_blocks)
    count = QW // HEAD_DIM
    half = pl.BlockSpec((rows, QW), lambda h: (0, h))
    kv_spec = pl.BlockSpec((rows, 2 * KW), lambda h: (0, h))
    table = pl.BlockSpec((rows, CHUNK), lambda h: (at, 0))
    outs = pl.pallas_call(
        functools.partial(backward_kernel, blocks),
        grid=(HALVES,),
        in_specs=[pl.BlockSpec((rows, QW), lambda h: (at, h)), half, half, pl.BlockSpec((count, rows), lambda h: (h, 0))]
        + [kv_spec] * blocks + [pl.BlockSpec((blocks, rows, rows), lambda h: (0, 0, 0)), table, table, table],
        out_specs=[half] + [kv_spec] * blocks,
        out_shape=[jax.ShapeDtypeStruct((rows, D), jnp.bfloat16)] + [jax.ShapeDtypeStruct((rows, 4 * KW), jnp.bfloat16)] * blocks,
        scratch_shapes=[pltpu.VMEM((rows, QW), jnp.float32)],
        compiler_params=pltpu.CompilerParams(vmem_limit_bytes=48 << 20),
        cost_estimate=pl.CostEstimate(flops=10 * rows * rows * blocks * HEADS * 128, bytes_accessed=2 * rows * D * (4 + blocks), transcendentals=rows * rows * blocks * HEADS),
        name="attend_back",
    )(qkv, dctx, ctx, lse_rows, *kv_blocks, bias_t, *tables)
    return outs[0], outs[1:]


RMS_EPS = 1e-05
ROPE_BASE = 1000000.0


def finish_kernel(own_ref, other_ref, cos_ref, up_ref, down_ref, out_ref):
    x = own_ref[...].astype(jnp.float32) + other_ref[...].astype(jnp.float32)
    turned = spin(x, cos_ref[...], -up_ref[...], -down_ref[...])
    lane = lax.broadcasted_iota(jnp.int32, x.shape, 1)
    out_ref[...] = jnp.where(lane < KW, turned, x).astype(jnp.bfloat16)


def finish_keys(own, other, tables, at):
    rows = own.shape[0]
    half = pl.BlockSpec((rows, 2 * KW), lambda h: (0, h))
    table = pl.BlockSpec((rows, CHUNK), lambda h: (at, 0))
    return pl.pallas_call(
        finish_kernel,
        grid=(HALVES,),
        in_specs=[half, half, table, table, table],
        out_specs=half,
        out_shape=jax.ShapeDtypeStruct(own.shape, jnp.bfloat16),
        cost_estimate=pl.CostEstimate(flops=8 * rows * 4 * KW, bytes_accessed=6 * rows * 4 * KW, transcendentals=0),
        name="finish_keys",
    )(own, other, *tables)


def rms_scale(values):
    return lax.rsqrt(jnp.mean(values * values, axis=-1, keepdims=True) + RMS_EPS)


def norm_back(grad_normed, gain, normed_x, scale_row, grad_rest):
    scaled = grad_normed * gain
    inner = jnp.mean(scaled * normed_x, axis=-1, keepdims=True)
    return grad_rest + scale_row * (scaled - normed_x * inner)


def rope_lanes(position):
    lane = jnp.arange(CHUNK, dtype=jnp.int32) % HEAD_DIM
    half = HEAD_DIM // 2
    index = (lane % half).astype(jnp.float32)
    inverse = jnp.exp(index * (-2.0 * math.log(ROPE_BASE) / HEAD_DIM))
    angles = position.astype(jnp.float32)[:, None] * inverse[None, :]
    sine = jnp.sin(angles)
    first = (lane < half)[None, :]
    return jnp.cos(angles), jnp.where(first, -sine, 0.0), jnp.where(first, 0.0, sine)


def stream_layout(starts, places):
    begun = starts[:, None, :] <= places[None, :, None]
    doc_ids = jnp.sum(begun.astype(jnp.int32), axis=-1) - 1
    first_token = jnp.max(jnp.where(begun, starts[:, None, :], 0), axis=-1)
    return doc_ids, places[None, :] - first_token


def right_pairs(count, lowest=0):
    return [(k, k + 1) for k in range(lowest, count - 1)]


def left_pairs(count):
    return [(k + 1, k) for k in range(count - 1)]


def exchange(blocks):
    parts = lax.axis_size("fsdp")
    me = lax.axis_index("fsdp")
    own = lax.dynamic_index_in_dim(blocks, me, 0, keepdims=True)
    out = lax.dynamic_update_slice_in_dim(jnp.zeros_like(blocks), own, me, 0)
    for d in range(1, parts):
        block = lax.dynamic_index_in_dim(blocks, me ^ d, 0, keepdims=True)
        came = lax.ppermute(block, "fsdp", [(j, j ^ d) for j in range(parts)])
        out = lax.dynamic_update_slice_in_dim(out, came, me ^ d, 0)
    return out


def line_scatter(chunks):
    n = lax.axis_size("sp")
    me = lax.axis_index("sp")

    def take(j):
        return lax.dynamic_index_in_dim(chunks, jnp.clip(j, 0, n - 1), 0, keepdims=False)

    right = left = None
    for s in range(n - 1):
        to_right = take(me + (n - 1) - s)
        to_left = take(me - (n - 1) + s)
        if right is not None:
            to_right = to_right + right
            to_left = to_left + left
        right = lax.ppermute(to_right, "sp", [(k, k + 1) for k in range(s + 1)])
        left = lax.ppermute(to_left, "sp", [(n - 1 - k, n - 2 - k) for k in range(s + 1)])
    return take(me).astype(jnp.float32) + right.astype(jnp.float32) + left.astype(jnp.float32)


def line_gather(mine):
    n = lax.axis_size("sp")
    me = lax.axis_index("sp")
    rights, lefts = [mine], [mine]
    for s in range(n - 1):
        rights.append(lax.ppermute(rights[-1], "sp", [(k, k + 1) for k in range(s, n - 1)]))
        lefts.append(lax.ppermute(lefts[-1], "sp", [(n - 1 - k, n - 2 - k) for k in range(s, n - 1)]))
    rows = mine.shape[0]
    out = jnp.zeros((n * rows,) + mine.shape[1:], jnp.float32)
    out = lax.dynamic_update_slice_in_dim(out, mine.astype(jnp.float32), me * rows, 0)
    for s in range(1, n):
        came = jnp.where(me >= s, rights[s], lefts[n - s]).astype(jnp.float32)
        out = lax.dynamic_update_slice_in_dim(out, came, ((me - s + n) % n) * rows, 0)
    return out


def body(tokens, doc_starts, cotangent, gain_attn, gain_ffn, w_query, w_key, w_value, w_out, w_gate, w_up, w_down):
    micro, _, rows, _ = tokens.shape
    parts = lax.axis_size("fsdp")
    seq = lax.axis_size("sp")
    place = lax.axis_index("sp")
    count = micro * rows
    d_own = w_query.shape[0]
    hidden_own = w_down.shape[0]
    bf16 = jnp.bfloat16
    f32 = jnp.float32

    gains = jnp.pad(jnp.stack([gain_attn, gain_ffn], axis=1), ((0, 0), (0, 126)))
    w_in = jnp.concatenate(
        [w_query, w_key[:, :KW], w_value[:, :KW], w_key[:, KW:], w_value[:, KW:], gains], axis=1
    )
    w_in = lax.all_gather(w_in, "fsdp", axis=0, tiled=True)
    gain_one = w_in[:, D + 4 * KW].astype(f32)
    gain_two = w_in[:, D + 4 * KW + 1].astype(f32)
    w_out_full = lax.all_gather(w_out, "fsdp", axis=0, tiled=True)
    w_both = jnp.concatenate(
        [w_gate.reshape(d_own, parts, hidden_own), w_up.reshape(d_own, parts, hidden_own)], axis=2
    )
    w_both = exchange(jnp.moveaxis(w_both, 1, 0)).reshape(D, 2 * hidden_own)

    starts = doc_starts.reshape(micro, -1)
    offsets = (place - jnp.arange(seq, dtype=jnp.int32)) * rows
    key_places = (offsets[:, None] + jnp.arange(rows, dtype=jnp.int32)[None, :]).reshape(-1)
    docs, positions = stream_layout(starts, key_places)
    docs = docs.reshape(micro, seq, rows)
    key_places = key_places.reshape(seq, rows)
    tables = rope_lanes(positions.reshape(micro, seq, rows)[:, 0].reshape(count))
    allowed = (docs[:, :1, :, None] == docs[:, :, None, :]) & (
        key_places[None, :, None, :] <= key_places[None, :1, :, None]
    )
    bias = jnp.where(allowed, 0.0, -1e30).astype(f32)
    bias_t = jnp.where(jnp.swapaxes(allowed, 2, 3), 0.0, -1e30).astype(f32)

    inputs = tokens.reshape(count, D).astype(f32)
    scale_one = rms_scale(inputs)
    normed_x1 = inputs * scale_one
    normed = (normed_x1 * gain_one).astype(bf16)
    qkv = project(normed, w_in, tables)

    g_low = cotangent.reshape(micro, rows, D)
    state = []
    for m in range(micro):
        kv = [qkv[m * rows:(m + 1) * rows, D:]]
        for s in range(seq - 1):
            kv.append(lax.ppermute(kv[-1], "sp", right_pairs(seq, s)))
        context, lse = attend(qkv, kv, bias[m], m)
        lse_rows = jnp.swapaxes(lse.reshape(rows, HALVES, 128)[:, :, :QW // HEAD_DIM].reshape(rows, HEADS), 0, 1)
        mixed = inputs[m * rows:(m + 1) * rows] + nn(context, w_out_full)
        scale_two = rms_scale(mixed)
        normed_x2 = mixed * scale_two
        normed_ffn = (normed_x2 * gain_two).astype(bf16)
        n2_all = lax.all_gather(normed_ffn, "fsdp", axis=0, tiled=True)
        g_all = lax.all_gather(g_low[m], "fsdp", axis=0, tiled=True)
        state.append((kv, context, lse_rows, mixed, scale_two, normed_x2, n2_all, g_all))

    ffn = []
    for m in range(micro):
        n2_all, g_all = state[m][6:]
        both = nn(n2_all, w_both)
        gate, up = both[:, :hidden_own], both[:, hidden_own:]
        sigm = jax.nn.sigmoid(gate)
        hidden = (gate * sigm * up).astype(bf16)
        hidden_grad = nt(g_all, w_down)
        gate_grad = hidden_grad * up * sigm * (1.0 + gate * (1.0 - sigm))
        up_grad = hidden_grad * gate * sigm
        both_grad = jnp.concatenate([gate_grad.astype(bf16), up_grad.astype(bf16)], axis=1)
        normed_grad = lax.psum_scatter(nt(both_grad, w_both).astype(bf16), "fsdp", scatter_dimension=0, tiled=True)
        out_term = lax.psum_scatter(nn(hidden, w_down).astype(bf16), "fsdp", scatter_dimension=0, tiled=True)
        ffn.append((hidden, both_grad, normed_grad, out_term))

    down_grad = sum(tn(ffn[m][0], state[m][7]) for m in range(micro)).astype(bf16)
    wide_grad = sum(tn(state[m][6], ffn[m][1]) for m in range(micro)).astype(bf16)

    down_part = line_scatter(down_grad.reshape(seq, hidden_own // seq, D)).astype(bf16)
    down_total = line_gather(down_part)
    slab = d_own // seq
    wide_chunks = jnp.moveaxis(wide_grad.reshape(parts, seq, slab, 2 * hidden_own), 1, 0)
    wide_part = exchange(line_scatter(wide_chunks).astype(bf16))
    wide_part = jnp.moveaxis(wide_part.reshape(parts, slab, 2, hidden_own), 0, 2).reshape(slab, 2 * parts * hidden_own)
    wide_total = line_gather(wide_part)
    ff = parts * hidden_own

    outputs, mixed_grads, context_pairs, attn_grads, gain_two_term, query_grads, kv_grads = [], [], [], [], 0.0, [], []
    for m in range(micro):
        kv, context, lse_rows, mixed, scale_two, normed_x2, _, _ = state[m]
        _, _, normed_grad, out_term = ffn[m]
        outputs.append((mixed + out_term.astype(f32)).astype(bf16))
        normed_grad = normed_grad.astype(f32)
        gain_two_term = gain_two_term + jnp.sum(normed_grad * normed_x2, axis=0)
        mixed_grad = norm_back(normed_grad, gain_two, normed_x2, scale_two, g_low[m].astype(f32))
        attn_grad = mixed_grad.astype(bf16)
        context_grad = nt(attn_grad, w_out_full).astype(bf16)
        query_grad, kv_parts = attend_back(qkv, context_grad, context, lse_rows, kv, bias_t[m], tables, m)
        running = kv_parts[seq - 1]
        for s in range(seq - 1):
            came = lax.ppermute(running, "sp", [(seq - 1 - k, seq - 2 - k) for k in range(s + 1)])
            if s < seq - 2:
                running = (kv_parts[seq - 2 - s].astype(f32) + came.astype(f32)).astype(bf16)
        kv_grad = finish_keys(kv_parts[0], came, tables, m)
        mixed_grads.append(mixed_grad)
        attn_grads.append(attn_grad)
        query_grads.append(query_grad)
        kv_grads.append(kv_grad)

    rows_of = lambda pieces: jnp.concatenate(pieces, axis=0)
    out_grad = tn(rows_of([state[m][1] for m in range(micro)]), rows_of(attn_grads)).astype(bf16)
    query_grad, kv_grad = rows_of(query_grads), rows_of(kv_grads)
    in_grad = jnp.concatenate([query_grad, kv_grad], axis=1)
    normed_grad = nt(in_grad, w_in[:, :D + 4 * KW])
    gain_one_term = jnp.sum(normed_grad * normed_x1, axis=0)
    input_grad = norm_back(normed_grad, gain_one, normed_x1, scale_one, rows_of(mixed_grads)).astype(bf16)

    gain_terms = jnp.pad(jnp.stack([gain_one_term, gain_two_term], axis=1).astype(bf16), ((0, 0), (0, 126)))
    in_total = jnp.concatenate([tn(normed, in_grad).astype(bf16), gain_terms], axis=1)
    in_shard = lax.psum_scatter(in_total, "fsdp", scatter_dimension=0, tiled=True)
    out_shard = lax.psum_scatter(out_grad, "fsdp", scatter_dimension=0, tiled=True)
    out_total = line_gather(line_scatter(out_shard.reshape(seq, slab, D)).astype(bf16))
    in_total = line_gather(line_scatter(in_shard.reshape(seq, slab, in_shard.shape[1])).astype(bf16))

    keys_at = D
    first_key = in_total[:, keys_at:keys_at + KW]
    first_value = in_total[:, keys_at + KW:keys_at + 2 * KW]
    second_key = in_total[:, keys_at + 2 * KW:keys_at + 3 * KW]
    second_value = in_total[:, keys_at + 3 * KW:keys_at + 4 * KW]
    return (
        rows_of(outputs).reshape(tokens.shape),
        input_grad.reshape(tokens.shape),
        in_total[:, keys_at + 4 * KW],
        in_total[:, keys_at + 4 * KW + 1],
        in_total[:, :D],
        jnp.concatenate([first_key, second_key], axis=1),
        jnp.concatenate([first_value, second_value], axis=1),
        out_total,
        wide_total[:, :ff],
        wide_total[:, ff:],
        down_total,
    )


def solution(mesh):
    split = P("fsdp", None)
    stream = P(None, "fsdp", "sp", None)
    return jax.shard_map(
        body,
        mesh=mesh,
        in_specs=(stream, P(None, "fsdp", None), stream, P("fsdp"), P("fsdp")) + (split,) * 7,
        out_specs=(stream, stream, P("fsdp"), P("fsdp")) + (split,) * 7,
        check_vma=False,
    )
```

time: 3140 us -> 1990 us (0.63)
  waiting for transfers between devices: 1520 us -> 908 us
  matrix products: 698 us -> 349 us
  blocking collectives: 246 us -> 0 us
  local copies, waits for them, and re-layouts: 350 us -> 141 us
  Pallas kernels: 0 us -> 190 us
  starting transfers between devices: 86.6 us -> 231 us
  other arithmetic: 189 us -> 125 us
    all_gather x21 -> x6, waiting for transfers between devices: 772 us -> 230 us  [the longest x1 99.3 us: body(): w_in = lax.all_gather(w_in, 'fsdp', axis=0, tiled=True)]
    ppermute x0 -> x74, waiting for transfers between devices: none -> 505 us  [the longest x12 189 us: line_gather(): lax.ppermute(lefts[-1], 'sp', [(n - 1 - k, n - 2 - k) for k in range(s, n...]
    psum x1 -> x0, waiting for transfers between devices: 485 us -> none  [body(): lax.psum(attn_shard.astype(jnp.bfloat16), 'sp').astype(jnp.float32)]
    dot_general x70 -> x19, matrix products: 698 us -> 349 us  [the longest x7 131 us: nt(): lax.dot_general(left, right, (((1,), (1,)), ((), ())), preferred_element_...]
    all_to_all x16 -> x0, waiting for transfers between devices: 252 us -> none  [the longest x2 96.3 us: run_layer(): lax.all_to_all(hidden.reshape(count, width_parts, hidden_slice), 'fsdp',...]
    ppermute x0 -> x74, starting transfers between devices: none -> 231 us  [the longest x12 117 us: line_scatter(): right = lax.ppermute(to_right, 'sp', [(k, k + 1) for k in range(s + 1)])]
    all_to_all x8 -> x0, blocking collectives: 192 us -> none  [the longest x2 66.7 us: run_layer(): lax.all_to_all(query_grad.reshape(micro, length, 1, -1), 'sp', split_axis...]
    pallas_call x0 -> x7, Pallas kernels: none -> 190 us  [the longest x2 105 us: attend_back(): pl.pallas_call(functools.partial(backward_kernel, blocks), grid=(HALVES,)...]
  transfers between devices with their start and end apart: 38 -> 86, of which waited for: 22 -> 37; matrix products, arithmetic and copies ran while one was open for 37% -> 24% of each run, Pallas kernels for 0% -> 10%
where the time goes in v1:
time: 1990 us; the launch traced here: 1960 us
  waiting for transfers between devices  908 us (46%)
  matrix products  349 us (18%)
  starting transfers between devices  231 us (12%)
  Pallas kernels  190 us (10%)
  local copies, waits for them, and re-layouts  141 us (7%)
  other arithmetic  125 us (6%)
    ppermute x12, waiting for transfers between devices, line_gather(): lax.ppermute(lefts[-1], 'sp', [(n - 1 - k, n - 2 - k) for k in range(s, n...  189 us
    ppermute x14, waiting for transfers between devices, exchange(): came = lax.ppermute(block, 'fsdp', [(j, j ^ d) for j in range(parts)])  150 us
    reduce_scatter x2, waiting for transfers between devices, body(): lax.psum_scatter(nn(hidden, w_down).astype(bf16), 'fsdp', scatter_dimensi...  145 us
    dot_general x7, matrix products, nt(): lax.dot_general(left, right, (((1,), (1,)), ((), ())), preferred_element_...  131 us
    ppermute x12, starting transfers between devices, line_scatter(): right = lax.ppermute(to_right, 'sp', [(k, k + 1) for k in range(s + 1)])  117 us
    dot_general x6, matrix products, tn(): lax.dot_general(left, right, (((0,), (0,)), ((), ())), preferred_element_...  112 us
    dot_general x6, matrix products, nn(): return jnp.dot(left, right, preferred_element_type=jnp.float32)  107 us
    pallas_call x2, Pallas kernels, attend_back(): pl.pallas_call(functools.partial(backward_kernel, blocks), grid=(HALVES,)...  105 us
  transfers between devices with their start and end apart: 86, of which 37 were waited for; matrix products, arithmetic and copies ran while one was open for 24% of the time, Pallas kernels for 10%

profile of v1, /device:TPU:1, one launch (start us, length us, event | category | flops | bytes accessed | tf_op | source)
XLA Modules:
  0.0 1960.8 jit_solution(4233141233186993411)
XLA Ops:
  21.6 99.3 %all-gather.9.cloned.1.call-done.w_ref = bf16[2560,3968]{1,0:T(8,128)(2,1)} async-done(((bf16[320,3968]{1,0:T(8,128)(2,1)}), bf16[2560,3968]{1,0:T(8,128)(2,1)}) %all-gather.9.cloned.1.call-update) | async-done | bytes 20316176 | tf_op jit(solution)/shard_map/all_gather | solution.py:291
  126.9 19.2 project.1.q_ref
  151.5 13.8 collective-permute-done.refs_1_
  173.4 35.5 %attend.2 = (bf16[256,2560]{1,0:T(8,128)(2,1)S(1)}, f32[256,256]{1,0:T(8,128)S(1)}) custom-call(bf16[512,3840]{1,0:T(8,128)(2,1)} %project.1.q_ref, bf16[256,1280]{1,0:T(8,128)(2,1)S(1)} %get-tuple-element.144.refs_0_, bf16[256,1280]{1,0:T(8,128)(2,1)S(1)} %collective-permute-done.refs_1_, bf16[256,1280]{1,0:T(8,128)(2,1)S(1)} %collective-permute-done.1.refs_2_, ...), custom_call_target="tpu_custom_call" | custom-call | flops 4294967296 | bytes 5242880 | tf_op jit(solution)/shard_map/attend/pallas_call | solution.py:92
  210.1 9.5 multiply_reduce_fusion.4
  241.1 20.2 %constant_dynamic-slice_fusion.7 = (bf16[320,1,1792]{2,1,0:T(2,128)(2,1)S(1)}, bf16[320,1,1792]{2,1,0:T(2,128)(2,1)}, bf16[320,1,1792]{2,1,0:T(2,128)(2,1)}, bf1...) fusion(bf16[320,8,1792]{2,1,0:T(8,128)(2,1)S(1)} %constant_dyna, ...), kind=kLoop, calls=%fused_computation.178 | loop fusion | bytes 18350112 | tf_op jit(solution)/shard_map/dynamic-slice.7
  279.7 31.8 %collective-permute-done.4 = bf16[1,320,1792]{2,1,0:T(8,128)(2,1)S(1)} collective-permute-done((bf16[1,320,1792]{2,1,0:T(8,128)(2,1)}, bf16[1,320,1792]{2,1,0:T(8,128)(2,1)S(1)}, u32[]{:S(2)}, u32[]{:S(2)}) %collective-permute-start.4) | collective-permute-done | bytes 1146912 | tf_op jit(solution)/shard_map/ppermute | solution.py:236
  315.0 38.9 %collective-permute-done.5 = bf16[1,320,1792]{2,1,0:T(8,128)(2,1)S(1)} collective-permute-done((bf16[1,320,1792]{2,1,0:T(8,128)(2,1)}, bf16[1,320,1792]{2,1,0:T(8,128)(2,1)S(1)}, u32[]{:S(2)}, u32[]{:S(2)}) %collective-permute-start.5) | collective-permute-done | bytes 1146912 | tf_op jit(solution)/shard_map/ppermute | solution.py:236
  357.1 35.7 %collective-permute-done.8 = bf16[1,320,1792]{2,1,0:T(8,128)(2,1)S(1)} collective-permute-done((bf16[1,320,1792]{2,1,0:T(8,128)(2,1)S(1)}, bf16[1,320,1792]{2,1,0:T(8,128)(2,1)S(1)}, u32[]{:S(2)}, u32[]{:S(2)}) %collective-permute-start.8) | collective-permute-done | bytes 1146912 | tf_op jit(solution)/shard_map/ppermute | solution.py:236
  394.0 23.5 %collective-permute-done.9 = bf16[1,320,1792]{2,1,0:T(8,128)(2,1)S(1)} collective-permute-done((bf16[1,320,1792]{2,1,0:T(8,128)(2,1)S(1)}, bf16[1,320,1792]{2,1,0:T(8,128)(2,1)S(1)}, u32[]{:S(2)}, u32[]{:S(2)}) %collective-permute-start.9) | collective-permute-done | bytes 1146912 | tf_op jit(solution)/shard_map/ppermute | solution.py:236
  418.5 26.1 %fusion.80 = f32[2048,1792]{0,1:T(8,128)} fusion(bf16[2048,2560]{1,0:T(8,128)(2,1)} %all-gather.13.cloned.1.call-done, bf16[2560,1792]{1,0:T(8,128)(2,1)} %bitcast.6), kind=kOutput, calls=%fused_computation.239 | convolution fusion | flops 18790481920 | bytes 34340864 | tf_op jit(solution)/shard_map/dot_general | solution.py:30
  444.7 20.6 %all-gather.17.cloned.1.call-done = bf16[1,1,2048,2560]{3,2,1,0:T(8,128)(2,1)} async-done(((bf16[1,1,256,2560]{3,2,1,0:T(8,128)(2,1)}), bf16[1,1,2048,2560]{3,2,1,0:T(8,128)(2,1)}) %all-gather.17.cloned.1.call-update) | async-done | bytes 10485776 | tf_op jit(solution)/shard_map/all_gather | solution.py:332
  465.3 21.7 %multiply_convert_fusion.3 = (bf16[2048,896]{0,1:T(8,128)(2,1)S(1)}, bf16[2048,896]{0,1:T(8,128)(2,1)}, bf16[2048,896]{0,1:T(8,128)(2,1)}) fusion(f32[2048,1792]{0,1:T(8,128)} %fusion.80, bf16[896,2560]{1,0:T(8,128)(2,1)} %param.23, bf16[1,1,2048,2560]{3,2,1,0:T(8,128)(2,1)} %all-gather.17.cloned.1.call-done), kind=kOutput, calls=%fused_computation.26 | convolution fusion | flops 9424601088 | bytes 40763392 | tf_op jit(solution)/shard_map/dot_general | solution.py:22
  488.9 25.4 %convolution_convert_fusion.3 = bf16[2048,2560]{1,0:T(8,128)(2,1)} fusion(bf16[2560,1792]{1,0:T(8,128)(2,1)} %bitcast.6, bf16[2048,896]{0,1:T(8,128)(2,1)} %get-tuple-element.117, bf16[2048,896]{0,1:T(8,128)(2,1)S(1)} %get-tuple-element.116), kind=kOutput, calls=%fused_computation.9 | convolution fusion | flops 18810404864 | bytes 27000832 | tf_op jit(solution)/shard_map/dot_general | solution.py:22
  518.5 13.8 collective-permute-done.10.refs_1_
  533.7 23.2 %attend.3 = (bf16[256,2560]{1,0:T(8,128)(2,1)S(1)}, f32[256,256]{1,0:T(8,128)S(1)}) custom-call(bf16[512,3840]{1,0:T(8,128)(2,1)} %project.1.q_ref, bf16[256,1280]{1,0:T(8,128)(2,1)S(1)} %copy-done.3, bf16[256,1280]{1,0:T(8,128)(2,1)S(1)} %collective-permute-done.10.refs_1_, bf16[256,1280]{1,0:T(8,128)(2,1)S(1)} %collective-permute-done.11.refs_2_, ...), custom_call_target="tpu_custom_call" | custom-call | flops 4294967296 | bytes 5242880 | tf_op jit(solution)/shard_map/attend/pallas_call | solution.py:92
  557.0 11.3 multiply_reduce_fusion.3
  568.4 27.2 %reduce-scatter.11.cloned.1.call-done = bf16[256,2560]{1,0:T(8,128)(2,1)} async-done(((bf16[2048,2560]{1,0:T(8,128)(2,1)}), bf16[256,2560]{1,0:T(8,128)(2,1)}) %reduce-scatter.11.cloned.1.call-update) | async-done | bytes 1310736 | tf_op jit(solution)/shard_map/reduce_scatter | solution.py:346
  602.0 70.7 %all-gather.15.cloned.1.call-done = bf16[2048,2560]{1,0:T(8,128)(2,1)} async-done(((bf16[256,2560]{1,0:T(8,128)(2,1)}), bf16[2048,2560]{1,0:T(8,128)(2,1)}) %all-gather.15.cloned.1.call-update) | async-done | bytes 10485776 | tf_op jit(solution)/shard_map/all_gather | solution.py:331
  672.7 26.1 %fusion.81 = f32[2048,1792]{0,1:T(8,128)} fusion(bf16[2048,2560]{1,0:T(8,128)(2,1)} %all-gather.15.cloned.1.call-done, bf16[2560,1792]{1,0:T(8,128)(2,1)} %bitcast.6), kind=kOutput, calls=%fused_computation.240 | convolution fusion | flops 18790481920 | bytes 34340864 | tf_op jit(solution)/shard_map/dot_general | solution.py:30
  698.9 39.0 %all-gather.19.cloned.1.call-done = bf16[1,1,2048,2560]{3,2,1,0:T(8,128)(2,1)} async-done(((bf16[1,1,256,2560]{3,2,1,0:T(8,128)(2,1)}), bf16[1,1,2048,2560]{3,2,1,0:T(8,128)(2,1)}) %all-gather.19.cloned.1.call-update) | async-done | bytes 10485776 | tf_op jit(solution)/shard_map/all_gather | solution.py:332
  737.9 21.3 %multiply_convert_fusion.1 = (bf16[2048,896]{0,1:T(8,128)(2,1)S(1)}, bf16[2048,896]{0,1:T(8,128)(2,1)}, bf16[2048,896]{0,1:T(8,128)(2,1)}) fusion(f32[2048,1792]{0,1:T(8,128)} %fusion.81, bf16[896,2560]{1,0:T(8,128)(2,1)} %param.23, bf16[1,1,2048,2560]{3,2,1,0:T(8,128)(2,1)} %all-gather.19.cloned.1.call-done), kind=kOutput, calls=%fused_computation.24 | convolution fusion | flops 9424601088 | bytes 40763392 | tf_op jit(solution)/shard_map/dot_general | solution.py:22
  761.1 25.5 %convolution_convert_fusion.2 = bf16[2048,2560]{1,0:T(8,128)(2,1)} fusion(bf16[2560,1792]{1,0:T(8,128)(2,1)} %bitcast.6, bf16[2048,896]{0,1:T(8,128)(2,1)} %get-tuple-element.119, bf16[2048,896]{0,1:T(8,128)(2,1)S(1)} %get-tuple-element.118), kind=kOutput, calls=%fused_computation.8 | convolution fusion | flops 18810404864 | bytes 27000832 | tf_op jit(solution)/shard_map/dot_general | solution.py:22
  786.7 16.9 convolution_convert_fusion.5
  803.6 16.8 convolution_convert_fusion.4
  823.8 26.4 %fusion.15 = f32[2560,1792]{1,0:T(8,128)} fusion(bf16[2048,2560]{1,0:T(8,128)(2,1)} %all-gather.13.cloned.1.call-done, bf16[2048,896]{0,1:T(8,128)(2,1)} %get-tuple-element.117, bf16[2048,896]{0,1:T(8,128)(2,1)} %copy-done.63), kind=kOutput, calls=%fused_computation.38 | convolution fusion | flops 18805161984 | bytes 36175872 | tf_op jit(solution)/shard_map/dot_general | solution.py:26
  850.2 27.0 %add_convert_fusion = bf16[2560,1792]{1,0:T(8,128)(2,1)} fusion(f32[2560,1792]{1,0:T(8,128)} %fusion.15, bf16[2048,2560]{1,0:T(8,128)(2,1)} %all-gather.15.cloned.1.call-done, bf16[2048,896]{0,1:T(8,128)(2,1)} %get-tuple-element.119, bf16[2048,896]{0,1:T(8,128)(2,1)} %copy-done.64), kind=kOutput, calls=%fused_computation.6 | convolution fusion | flops 18814337024 | bytes 45350912 | tf_op jit(solution)/shard_map/dot_general | solution.py:26
  892.9 60.1 %reduce-scatter.7.cloned.1.call-done = bf16[256,2560]{1,0:T(8,128)(2,1)} async-done(((bf16[2048,2560]{1,0:T(8,128)(2,1)}), bf16[256,2560]{1,0:T(8,128)(2,1)}) %reduce-scatter.7.cloned.1.call-update) | async-done | bytes 1310736 | tf_op jit(solution)/shard_map/reduce_scatter | solution.py:347
  953.0 84.9 %reduce-scatter.9.cloned.1.call-done = bf16[256,2560]{1,0:T(8,128)(2,1)} async-done(((bf16[2048,2560]{1,0:T(8,128)(2,1)}), bf16[256,2560]{1,0:T(8,128)(2,1)}) %reduce-scatter.9.cloned.1.call-update) | async-done | bytes 1310736 | tf_op jit(solution)/shard_map/reduce_scatter | solution.py:347
  1038.0 8.9 fusion.70
  1048.3 10.1 convolution_convert_fusion.1
  1058.5 9.8 convolution_convert_fusion.7.dctx_ref
  1068.3 52.1 %attend_back.2 = (bf16[256,2560]{1,0:T(8,128)(2,1)}, bf16[256,1280]{1,0:T(8,128)(2,1)S(1)}, bf16[256,1280]{1,0:T(8,128)(2,1)S(1)}, bf16[256,1280]{1,0:T(8,128)(2,1)S(1)}, bf16[256,1280]{1,0:T(8,128)(2,1)S(1)}) custom-call(bf16[512,3840]{1,0:T(8,128)(2,1)} %project.1.q_ref, bf16[256,2560]{1,0:T(8,128)(2,1)} %convolution_convert_fusion.7.dctx_ref, ...), custom_call_target="tpu_custom_call" | custom-call | flops 10737418240 | bytes 10485760 | tf_op jit(solution)/shard_map/attend_back/pallas_call | solution.py:152
  1122.2 9.5 convolution_convert_fusion.6.dctx_ref
  1131.6 52.7 %attend_back.3 = (bf16[256,2560]{1,0:T(8,128)(2,1)}, bf16[256,1280]{1,0:T(8,128)(2,1)S(1)}, bf16[256,1280]{1,0:T(8,128)(2,1)S(1)}, bf16[256,1280]{1,0:T(8,128)(2,1)S(1)}, bf16[256,1280]{1,0:T(8,128)(2,1)S(1)}) custom-call(bf16[512,3840]{1,0:T(8,128)(2,1)} %project.1.q_ref, bf16[256,2560]{1,0:T(8,128)(2,1)} %convolution_convert_fusion.6.dctx_ref, ...), custom_call_target="tpu_custom_call" | custom-call | flops 10737418240 | bytes 10485760 | tf_op jit(solution)/shard_map/attend_back/pallas_call | solution.py:152
  1185.1 15.6 fusion.4
  1202.7 15.9 add_convert_fusion.1
  1225.6 18.5 collective-permute-start.44
  1254.3 17.3 multiply_reduce_fusion
  1272.1 16.9 convolution_convert_fusion
  1289.0 16.6 fusion.1
  1308.4 13.8 collective-permute-start.62
  1322.2 8.1 bitcast_add_fusion.3
  1334.1 11.5 collective-permute-done.62
  1361.2 14.1 collective-permute-done.63
  1379.8 15.5 collective-permute-start.64
  1399.1 25.4 %collective-permute-done.45 = bf16[8,80,1792]{2,1,0:T(8,128)(2,1)} collective-permute-done((bf16[8,80,1792]{2,1,0:T(8,128)(2,1)}, bf16[8,80,1792]{2,1,0:T(8,128)(2,1)}, u32[]{:S(2)}, u32[]{:S(2)}) %collective-permute-start.45) | collective-permute-done | bytes 2293792 | tf_op jit(solution)/shard_map/ppermute | solution.py:255
  1424.4 10.7 collective-permute-done.48
  1449.0 36.0 %collective-permute-done.67 = bf16[224,2560]{1,0:T(8,128)(2,1)} collective-permute-done((bf16[224,2560]{1,0:T(8,128)(2,1)}, bf16[224,2560]{1,0:T(8,128)(2,1)}, u32[]{:S(2)}, u32[]{:S(2)}) %collective-permute-start.67) | collective-permute-done | bytes 1146912 | tf_op jit(solution)/shard_map/ppermute | solution.py:256
  1495.3 26.1 %collective-permute-start.68 = (bf16[224,2560]{1,0:T(8,128)(2,1)}, bf16[224,2560]{1,0:T(8,128)(2,1)}, u32[]{:S(2)}, u32[]{:S(2)}) collective-permute-start(bf16[224,2560]{1,0:T(8,128)(2,1)} %get-tuple-element.107), channel_id=1, source_target_pairs={{0,1},{1,2},{2,3},{4,5},{5,6},{6,7},{8,9},{9,10},{10,11},{12,13},{... | collective-permute-start | bytes 3440648 | tf_op jit(solution)/shard_map/ppermute | solution.py:265
  1537.9 14.6 collective-permute-done.53
  1569.3 73.1 %collective-permute-done.70 = bf16[224,2560]{1,0:T(8,128)(2,1)} collective-permute-done((bf16[224,2560]{1,0:T(8,128)(2,1)}, bf16[224,2560]{1,0:T(8,128)(2,1)}, u32[]{:S(2)}, u32[]{:S(2)}) %collective-permute-start.70) | collective-permute-done | bytes 1146912 | tf_op jit(solution)/shard_map/ppermute | solution.py:266
  1651.0 19.0 collective-permute-done.71
  1678.9 18.3 collective-permute-done.56
  1699.2 19.8 %collective-permute-done.58 = bf16[80,14336]{1,0:T(8,128)(2,1)S(1)} collective-permute-done((bf16[80,14336]{1,0:T(8,128)(2,1)}, bf16[80,14336]{1,0:T(8,128)(2,1)S(1)}, u32[]{:S(2)}, u32[]{:S(2)}) %collective-permute-start.58) | collective-permute-done | bytes 2293792 | tf_op jit(solution)/shard_map/ppermute | solution.py:266
  1720.3 8.4 broadcast_in_dim.87
  1736.7 35.7 %collective-permute-done.59 = bf16[80,14336]{1,0:T(8,128)(2,1)S(1)} collective-permute-done((bf16[80,14336]{1,0:T(8,128)(2,1)S(1)}, bf16[80,14336]{1,0:T(8,128)(2,1)S(1)}, u32[]{:S(2)}, u32[]{:S(2)}) %collective-permute-start.59) | collective-permute-done | bytes 2293792 | tf_op jit(solution)/shard_map/ppermute | solution.py:266
  1802.1 32.4 %collective-permute-start.19 = (bf16[80,3968]{1,0:T(8,128)(2,1)S(1)}, bf16[80,3968]{1,0:T(8,128)(2,1)S(1)}, u32[]{:S(2)}, u32[]{:S(2)}) collective-permute-start(bf16[80,3968]{1,0:T(8,128)(2,1)S(1)} %get-tuple-element.154), channel_id=1, source_target_pairs={{0,1},{4,5},{8,9},{12,13},{16,17},{20,21},{24,25},{28,29}} | collective-permute-start | bytes 1904648 | tf_op jit(solution)/shard_map/ppermute | solution.py:255
  1858.0 13.6 fusion.74
  1873.7 7.5 collective-permute-start.21
  1889.3 7.5 collective-permute-done.24
  1907.8 11.3 collective-permute-done.26
  1921.2 11.6 collective-permute-done.27
  1936.0 11.6 collective-permute-done.28
  (415 shorter events, 343.7 us)
Async XLA Ops:
  7.2 113.7 %all-gather.9.cloned.1.call-start = ((), (), s32[]{:S(2)}) async-start(), calls=%async_computation.6 | async-start | bytes 22855680 | tf_op jit(solution)/shard_map/all_gather | solution.py:291
  13.4 196.7 %all-gather.11.cloned.1.call-start = ((), (), s32[]{:S(2)}) async-start(), calls=%async_computation.7 | async-start | bytes 14745600 | tf_op jit(solution)/shard_map/all_gather | solution.py:294
  14.1 404.4 %all-gather.13.cloned.1.call-start = ((), (), s32[]{:S(2)}) async-start(), calls=%async_computation.8 | async-start | bytes 11796480 | tf_op jit(solution)/shard_map/all_gather | solution.py:331
  148.5 16.9 collective-permute-start
  222.4 242.9 %all-gather.17.cloned.1.call-start = ((), (), s32[]{:S(2)}) async-start(), calls=%async_computation.16 | async-start | bytes 11796480 | tf_op jit(solution)/shard_map/all_gather | solution.py:332
  225.9 369.7 %reduce-scatter.11.cloned.1.call-start = ((), (), s32[]{:S(2)}) async-start(), calls=%async_computation.12 | async-start | bytes 11796480 | tf_op jit(solution)/shard_map/reduce_scatter | solution.py:346
  265.6 45.9 %collective-permute-start.4 = (bf16[1,320,1792]{2,1,0:T(8,128)(2,1)}, bf16[1,320,1792]{2,1,0:T(8,128)(2,1)S(1)}, u32[]{:S(2)}, u32[]{:S(2)}) collective-permute-start(bf16[1,320,1792]{2,1,0:T(8,128)(2,1)} %bitcast.199), channel_id=1, source_target_pairs={{0,8},{4,12},{8,0},{12,4},{16,24},{20,28},{24,16},{28,20},{1,9},{5... | collective-permute-start | bytes 3440648 | tf_op jit(solution)/shard_map/ppermute | solution.py:236
  267.9 86.0 %collective-permute-start.5 = (bf16[1,320,1792]{2,1,0:T(8,128)(2,1)}, bf16[1,320,1792]{2,1,0:T(8,128)(2,1)S(1)}, u32[]{:S(2)}, u32[]{:S(2)}) collective-permute-start(bf16[1,320,1792]{2,1,0:T(8,128)(2,1)} %bitcast.198), channel_id=1, source_target_pairs={{0,12},{4,8},{8,4},{12,0},{16,28},{20,24},{24,20},{28,16},{1,13},{... | collective-permute-start | bytes 3440648 | tf_op jit(solution)/shard_map/ppermute | solution.py:236
  268.9 86.1 %collective-permute-start.6 = (bf16[1,320,1792]{2,1,0:T(8,128)(2,1)S(1)}, bf16[1,320,1792]{2,1,0:T(8,128)(2,1)S(1)}, u32[]{:S(2)}, u32[]{:S(2)}) collective-permute-start(bf16[1,320,1792]{2,1,0:T(8,128)(2,1)S(1)} %bitcast.236), channel_id=1, source_target_pairs={{0,16},{4,20},{8,24},{12,28},{16,0},{20,4},{24,8},{28,12},{1,17},{... | collective-permute-start | bytes 3440648 | tf_op jit(solution)/shard_map/ppermute | solution.py:236
  269.5 86.5 %collective-permute-start.7 = (bf16[1,320,1792]{2,1,0:T(8,128)(2,1)S(1)}, bf16[1,320,1792]{2,1,0:T(8,128)(2,1)S(1)}, u32[]{:S(2)}, u32[]{:S(2)}) collective-permute-start(bf16[1,320,1792]{2,1,0:T(8,128)(2,1)S(1)} %bitcast.235), channel_id=1, source_target_pairs={{0,20},{4,16},{8,28},{12,24},{16,4},{20,0},{24,12},{28,8},{1,21},{... | collective-permute-start | bytes 3440648 | tf_op jit(solution)/shard_map/ppermute | solution.py:236
  277.2 115.6 %collective-permute-start.8 = (bf16[1,320,1792]{2,1,0:T(8,128)(2,1)S(1)}, bf16[1,320,1792]{2,1,0:T(8,128)(2,1)S(1)}, u32[]{:S(2)}, u32[]{:S(2)}) collective-permute-start(bf16[1,320,1792]{2,1,0:T(8,128)(2,1)S(1)} %bitcast.237), channel_id=1, source_target_pairs={{0,24},{4,28},{8,16},{12,20},{16,8},{20,12},{24,0},{28,4},{1,25},{... | collective-permute-start | bytes 3440648 | tf_op jit(solution)/shard_map/ppermute | solution.py:236
  311.5 106.0 %collective-permute-start.9 = (bf16[1,320,1792]{2,1,0:T(8,128)(2,1)S(1)}, bf16[1,320,1792]{2,1,0:T(8,128)(2,1)S(1)}, u32[]{:S(2)}, u32[]{:S(2)}) collective-permute-start(bf16[1,320,1792]{2,1,0:T(8,128)(2,1)S(1)} %bitcast.234), channel_id=1, source_target_pairs={{0,28},{4,24},{8,20},{12,16},{16,12},{20,8},{24,4},{28,0},{1,29},{... | collective-permute-start | bytes 3440648 | tf_op jit(solution)/shard_map/ppermute | solution.py:236
  514.3 158.5 %all-gather.15.cloned.1.call-start = ((), (), s32[]{:S(2)}) async-start(), calls=%async_computation.10 | async-start | bytes 11796480 | tf_op jit(solution)/shard_map/all_gather | solution.py:331
  515.3 17.0 collective-permute-start.10
  601.2 136.7 %all-gather.19.cloned.1.call-start = ((), (), s32[]{:S(2)}) async-start(), calls=%async_computation.17 | async-start | bytes 11796480 | tf_op jit(solution)/shard_map/all_gather | solution.py:332
  602.0 287.7 %reduce-scatter.13.cloned.1.call-start = ((), (), s32[]{:S(2)}) async-start(), calls=%async_computation.13 | async-start | bytes 11796480 | tf_op jit(solution)/shard_map/reduce_scatter | solution.py:346
  786.7 166.4 %reduce-scatter.7.cloned.1.call-start = ((), (), s32[]{:S(2)}) async-start(), calls=%async_computation.9 | async-start | bytes 11796480 | tf_op jit(solution)/shard_map/reduce_scatter | solution.py:347
  803.6 234.4 %reduce-scatter.9.cloned.1.call-start = ((), (), s32[]{:S(2)}) async-start(), calls=%async_computation.11 | async-start | bytes 11796480 | tf_op jit(solution)/shard_map/reduce_scatter | solution.py:347
  820.4 954.7 %reduce-scatter.17.cloned.1.call-start = ((), (), s32[]{:S(2)}) async-start(), calls=%async_computation.15 | async-start | bytes 14745600 | tf_op jit(solution)/shard_map/reduce_scatter | solution.py:395
  882.8 338.8 %collective-permute-start.43 = (bf16[8,80,1792]{2,1,0:T(8,128)(2,1)}, bf16[8,80,1792]{2,1,0:T(8,128)(2,1)}, u32[]{:S(2)}, u32[]{:S(2)}) collective-permute-start(bf16[8,80,1792]{2,1,0:T(8,128)(2,1)} %get-tuple-element.126), channel_id=1, source_target_pairs={{0,1},{4,5},{8,9},{12,13},{16,17},{20,21},{24,25},{28,29}} | collective-permute-start | bytes 6881288 | tf_op jit(solution)/shard_map/ppermute | solution.py:255
  887.7 434.5 %collective-permute-start.46 = (bf16[8,80,1792]{2,1,0:T(8,128)(2,1)}, bf16[8,80,1792]{2,1,0:T(8,128)(2,1)}, u32[]{:S(2)}, u32[]{:S(2)}) collective-permute-start(bf16[8,80,1792]{2,1,0:T(8,128)(2,1)} %get-tuple-element.127), channel_id=1, source_target_pairs={{3,2},{7,6},{11,10},{15,14},{19,18},{23,22},{27,26},{31,30}} | collective-permute-start | bytes 6881288 | tf_op jit(solution)/shard_map/ppermute | solution.py:256
  1058.4 742.2 %reduce-scatter.15.cloned.1.call-start = ((), (), s32[]{:S(2)}) async-start(), calls=%async_computation.14 | async-start | bytes 22855680 | tf_op jit(solution)/shard_map/reduce_scatter | solution.py:394
  1121.3 79.3 %collective-permute-start.13 = (bf16[256,1280]{1,0:T(8,128)(2,1)S(1)}, bf16[256,1280]{1,0:T(8,128)(2,1)S(1)}, u32[]{:S(2)}, u32[]{:S(2)}) collective-permute-start(bf16[256,1280]{1,0:T(8,128)(2,1)S(1)} %get-tuple-element.34), channel_id=1, source_target_pairs={{3,2},{7,6},{11,10},{15,14},{19,18},{23,22},{27,26},{31,30}} | collective-permute-start | bytes 1966088 | tf_op jit(solution)/shard_map/ppermute | solution.py:375
  1184.4 17.3 collective-permute-start.16
  1200.8 17.8 collective-permute-start.14
  1201.8 18.3 collective-permute-start.17
  1218.8 25.2 %collective-permute-start.15 = (bf16[256,1280]{1,0:T(8,128)(2,1)S(1)}, bf16[256,1280]{1,0:T(8,128)(2,1)S(1)}, u32[]{:S(2)}, u32[]{:S(2)}) collective-permute-start(bf16[256,1280]{1,0:T(8,128)(2,1)S(1)} %add_convert_fusion.6), channel_id=1, source_target_pairs={{3,2},{2,1},{1,0},{7,6},{6,5},{5,4},{11,10},{10,9},{9,8},{15,14},{... | collective-permute-start | bytes 1966088 | tf_op jit(solution)/shard_map/ppermute | solution.py:375
  1220.3 30.7 %collective-permute-start.18 = (bf16[256,1280]{1,0:T(8,128)(2,1)S(1)}, bf16[256,1280]{1,0:T(8,128)(2,1)}, u32[]{:S(2)}, u32[]{:S(2)}) collective-permute-start(bf16[256,1280]{1,0:T(8,128)(2,1)S(1)} %add_convert_fusion.4), channel_id=1, source_target_pairs={{3,2},{2,1},{1,0},{7,6},{6,5},{5,4},{11,10},{10,9},{9,8},{15,14},{... | collective-permute-start | bytes 1966088 | tf_op jit(solution)/shard_map/ppermute | solution.py:375
  1225.6 96.6 %collective-permute-start.44 = (bf16[8,80,1792]{2,1,0:T(8,128)(2,1)}, bf16[8,80,1792]{2,1,0:T(8,128)(2,1)}, u32[]{:S(2)}, u32[]{:S(2)}) collective-permute-start(bf16[8,80,1792]{2,1,0:T(8,128)(2,1)} %bitcast_add_fusion.2), channel_id=1, source_target_pairs={{0,1},{1,2},{4,5},{5,6},{8,9},{9,10},{12,13},{13,14},{16,17},{17,1... | collective-permute-start | bytes 6881288 | tf_op jit(solution)/shard_map/ppermute | solution.py:255
  1308.4 37.2 %collective-permute-start.62 = (bf16[224,2560]{1,0:T(8,128)(2,1)S(1)}, bf16[224,2560]{1,0:T(8,128)(2,1)S(1)}, u32[]{:S(2)}, u32[]{:S(2)}) collective-permute-start(bf16[224,2560]{1,0:T(8,128)(2,1)S(1)} %get-tuple-element.142), channel_id=1, source_target_pairs={{0,1},{4,5},{8,9},{12,13},{16,17},{20,21},{24,25},{28,29}} | collective-permute-start | bytes 3440648 | tf_op jit(solution)/shard_map/ppermute | solution.py:255
  1330.3 25.6 %collective-permute-start.47 = (bf16[8,80,1792]{2,1,0:T(8,128)(2,1)}, bf16[8,80,1792]{2,1,0:T(8,128)(2,1)}, u32[]{:S(2)}, u32[]{:S(2)}) collective-permute-start(bf16[8,80,1792]{2,1,0:T(8,128)(2,1)} %get-tuple-element.125), channel_id=1, source_target_pairs={{3,2},{2,1},{7,6},{6,5},{11,10},{10,9},{15,14},{14,13},{19,18},{18... | collective-permute-start | bytes 6881288 | tf_op jit(solution)/shard_map/ppermute | solution.py:256
  1332.4 28.8 %collective-permute-start.65 = (bf16[224,2560]{1,0:T(8,128)(2,1)}, bf16[224,2560]{1,0:T(8,128)(2,1)}, u32[]{:S(2)}, u32[]{:S(2)}) collective-permute-start(bf16[224,2560]{1,0:T(8,128)(2,1)} %get-tuple-element.143), channel_id=1, source_target_pairs={{3,2},{7,6},{11,10},{15,14},{19,18},{23,22},{27,26},{31,30}} | collective-permute-start | bytes 3440648 | tf_op jit(solution)/shard_map/ppermute | solution.py:256
  1348.0 27.2 %collective-permute-start.63 = (bf16[224,2560]{1,0:T(8,128)(2,1)}, bf16[224,2560]{1,0:T(8,128)(2,1)}, u32[]{:S(2)}, u32[]{:S(2)}) collective-permute-start(bf16[224,2560]{1,0:T(8,128)(2,1)} %bitcast_add_fusion.6), channel_id=1, source_target_pairs={{0,1},{1,2},{4,5},{5,6},{8,9},{9,10},{12,13},{13,14},{16,17},{17,1... | collective-permute-start | bytes 3440648 | tf_op jit(solution)/shard_map/ppermute | solution.py:255
  1353.3 71.2 %collective-permute-start.45 = (bf16[8,80,1792]{2,1,0:T(8,128)(2,1)}, bf16[8,80,1792]{2,1,0:T(8,128)(2,1)}, u32[]{:S(2)}, u32[]{:S(2)}) collective-permute-start(bf16[8,80,1792]{2,1,0:T(8,128)(2,1)} %get-tuple-element.124), channel_id=1, source_target_pairs={{0,1},{1,2},{2,3},{4,5},{5,6},{6,7},{8,9},{9,10},{10,11},{12,13},{... | collective-permute-start | bytes 6881288 | tf_op jit(solution)/shard_map/ppermute | solution.py:255
  1359.9 75.2 %collective-permute-start.48 = (bf16[8,80,1792]{2,1,0:T(8,128)(2,1)}, bf16[8,80,1792]{2,1,0:T(8,128)(2,1)}, u32[]{:S(2)}, u32[]{:S(2)}) collective-permute-start(bf16[8,80,1792]{2,1,0:T(8,128)(2,1)} %bitcast_add_fusion.1), channel_id=1, source_target_pairs={{3,2},{2,1},{1,0},{7,6},{6,5},{5,4},{11,10},{10,9},{9,8},{15,14},{... | collective-permute-start | bytes 6881288 | tf_op jit(solution)/shard_map/ppermute | solution.py:256
  1379.8 69.2 %collective-permute-start.64 = (bf16[224,2560]{1,0:T(8,128)(2,1)}, bf16[224,2560]{1,0:T(8,128)(2,1)}, u32[]{:S(2)}, u32[]{:S(2)}) collective-permute-start(bf16[224,2560]{1,0:T(8,128)(2,1)} %get-tuple-element.140), channel_id=1, source_target_pairs={{0,1},{1,2},{2,3},{4,5},{5,6},{6,7},{8,9},{9,10},{10,11},{12,13},{... | collective-permute-start | bytes 3440648 | tf_op jit(solution)/shard_map/ppermute | solution.py:255
  1397.8 87.2 %collective-permute-start.67 = (bf16[224,2560]{1,0:T(8,128)(2,1)}, bf16[224,2560]{1,0:T(8,128)(2,1)}, u32[]{:S(2)}, u32[]{:S(2)}) collective-permute-start(bf16[224,2560]{1,0:T(8,128)(2,1)} %bitcast_add_fusion.5), channel_id=1, source_target_pairs={{3,2},{2,1},{1,0},{7,6},{6,5},{5,4},{11,10},{10,9},{9,8},{15,14},{... | collective-permute-start | bytes 3440648 | tf_op jit(solution)/shard_map/ppermute | solution.py:256
  1441.5 84.3 %collective-permute-start.49 = (bf16[1,80,1792]{2,1,0:T(8,128)(2,1)S(1)}, bf16[1,80,1792]{2,1,0:T(8,128)(2,1)S(1)}, u32[]{:S(2)}, u32[]{:S(2)}) collective-permute-start(bf16[1,80,1792]{2,1,0:T(8,128)(2,1)S(1)} %get-tuple-element.162), channel_id=1, source_target_pairs={{0,4},{4,0},{8,12},{12,8},{16,20},{20,16},{24,28},{28,24},{1,5},{5... | collective-permute-start | bytes 860168 | tf_op jit(solution)/shard_map/ppermute | solution.py:236
  1444.7 81.9 %collective-permute-start.50 = (bf16[1,80,1792]{2,1,0:T(8,128)(2,1)S(1)}, bf16[1,80,1792]{2,1,0:T(8,128)(2,1)S(1)}, u32[]{:S(2)}, u32[]{:S(2)}) collective-permute-start(bf16[1,80,1792]{2,1,0:T(8,128)(2,1)S(1)} %get-tuple-element.161), channel_id=1, source_target_pairs={{0,8},{4,12},{8,0},{12,4},{16,24},{20,28},{24,16},{28,20},{1,9},{5... | collective-permute-start | bytes 860168 | tf_op jit(solution)/shard_map/ppermute | solution.py:236
  1494.0 72.3 %collective-permute-start.69 = (bf16[224,2560]{1,0:T(8,128)(2,1)}, bf16[224,2560]{1,0:T(8,128)(2,1)}, u32[]{:S(2)}, u32[]{:S(2)}) collective-permute-start(bf16[224,2560]{1,0:T(8,128)(2,1)} %get-tuple-element.107), channel_id=1, source_target_pairs={{3,2},{2,1},{1,0},{7,6},{6,5},{5,4},{11,10},{10,9},{9,8},{15,14},{... | collective-permute-start | bytes 3440648 | tf_op jit(solution)/shard_map/ppermute | solution.py:266
  1495.3 72.3 %collective-permute-start.68 = (bf16[224,2560]{1,0:T(8,128)(2,1)}, bf16[224,2560]{1,0:T(8,128)(2,1)}, u32[]{:S(2)}, u32[]{:S(2)}) collective-permute-start(bf16[224,2560]{1,0:T(8,128)(2,1)} %get-tuple-element.107), channel_id=1, source_target_pairs={{0,1},{1,2},{2,3},{4,5},{5,6},{6,7},{8,9},{9,10},{10,11},{12,13},{... | collective-permute-start | bytes 3440648 | tf_op jit(solution)/shard_map/ppermute | solution.py:265
  1526.5 25.9 %collective-permute-start.53 = (bf16[1,80,1792]{2,1,0:T(8,128)(2,1)S(1)}, bf16[1,80,1792]{2,1,0:T(8,128)(2,1)S(1)}, u32[]{:S(2)}, u32[]{:S(2)}) collective-permute-start(bf16[1,80,1792]{2,1,0:T(8,128)(2,1)S(1)} %get-tuple-element.158), channel_id=1, source_target_pairs={{0,20},{4,16},{8,28},{12,24},{16,4},{20,0},{24,12},{28,8},{1,21},{... | collective-permute-start | bytes 860168 | tf_op jit(solution)/shard_map/ppermute | solution.py:236
  1533.4 19.8 %collective-permute-start.54 = (bf16[1,80,1792]{2,1,0:T(8,128)(2,1)S(1)}, bf16[1,80,1792]{2,1,0:T(8,128)(2,1)S(1)}, u32[]{:S(2)}, u32[]{:S(2)}) collective-permute-start(bf16[1,80,1792]{2,1,0:T(8,128)(2,1)S(1)} %get-tuple-element.157), channel_id=1, source_target_pairs={{0,24},{4,28},{8,16},{12,20},{16,8},{20,12},{24,0},{28,4},{1,25},{... | collective-permute-start | bytes 860168 | tf_op jit(solution)/shard_map/ppermute | solution.py:236
  1534.7 19.2 collective-permute-start.55
  1565.0 84.7 %collective-permute-start.57 = (bf16[80,14336]{1,0:T(8,128)(2,1)}, bf16[80,14336]{1,0:T(8,128)(2,1)}, u32[]{:S(2)}, u32[]{:S(2)}) collective-permute-start(bf16[80,14336]{1,0:T(8,128)(2,1)} %bitcast.89), channel_id=1, source_target_pairs={{3,2},{2,1},{1,0},{7,6},{6,5},{5,4},{11,10},{10,9},{9,8},{15,14},{... | collective-permute-start | bytes 6881288 | tf_op jit(solution)/shard_map/ppermute | solution.py:266
  1566.3 76.2 %collective-permute-start.70 = (bf16[224,2560]{1,0:T(8,128)(2,1)}, bf16[224,2560]{1,0:T(8,128)(2,1)}, u32[]{:S(2)}, u32[]{:S(2)}) collective-permute-start(bf16[224,2560]{1,0:T(8,128)(2,1)} %collective-permute-done.69), channel_id=1, source_target_pairs={{2,1},{1,0},{6,5},{5,4},{10,9},{9,8},{14,13},{13,12},{18,17},{17,1... | collective-permute-start | bytes 3440648 | tf_op jit(solution)/shard_map/ppermute | solution.py:266
  1567.6 76.2 %collective-permute-start.72 = (bf16[224,2560]{1,0:T(8,128)(2,1)}, bf16[224,2560]{1,0:T(8,128)(2,1)}, u32[]{:S(2)}, u32[]{:S(2)}) collective-permute-start(bf16[224,2560]{1,0:T(8,128)(2,1)} %collective-permute-done.68), channel_id=1, source_target_pairs={{1,2},{2,3},{5,6},{6,7},{9,10},{10,11},{13,14},{14,15},{17,18},{18... | collective-permute-start | bytes 3440648 | tf_op jit(solution)/shard_map/ppermute | solution.py:265
  1642.5 27.5 %collective-permute-start.71 = (bf16[224,2560]{1,0:T(8,128)(2,1)}, bf16[224,2560]{1,0:T(8,128)(2,1)}, u32[]{:S(2)}, u32[]{:S(2)}) collective-permute-start(bf16[224,2560]{1,0:T(8,128)(2,1)} %collective-permute-done.70), channel_id=1, source_target_pairs={{1,0},{5,4},{9,8},{13,12},{17,16},{21,20},{25,24},{29,28}} | collective-permute-start | bytes 3440648 | tf_op jit(solution)/shard_map/ppermute | solution.py:266
  1643.8 32.1 %collective-permute-start.73 = (bf16[224,2560]{1,0:T(8,128)(2,1)}, bf16[224,2560]{1,0:T(8,128)(2,1)S(1)}, u32[]{:S(2)}, u32[]{:S(2)}) collective-permute-start(bf16[224,2560]{1,0:T(8,128)(2,1)} %collective-permute-done.72), channel_id=1, source_target_pairs={{2,3},{6,7},{10,11},{14,15},{18,19},{22,23},{26,27},{30,31}} | collective-permute-start | bytes 3440648 | tf_op jit(solution)/shard_map/ppermute | solution.py:265
  1644.6 52.6 %collective-permute-start.56 = (bf16[80,14336]{1,0:T(8,128)(2,1)}, bf16[80,14336]{1,0:T(8,128)(2,1)S(1)}, u32[]{:S(2)}, u32[]{:S(2)}) collective-permute-start(bf16[80,14336]{1,0:T(8,128)(2,1)} %bitcast.89), channel_id=1, source_target_pairs={{0,1},{1,2},{2,3},{4,5},{5,6},{6,7},{8,9},{9,10},{10,11},{12,13},{... | collective-permute-start | bytes 6881288 | tf_op jit(solution)/shard_map/ppermute | solution.py:265
  1649.7 69.4 %collective-permute-start.58 = (bf16[80,14336]{1,0:T(8,128)(2,1)}, bf16[80,14336]{1,0:T(8,128)(2,1)S(1)}, u32[]{:S(2)}, u32[]{:S(2)}) collective-permute-start(bf16[80,14336]{1,0:T(8,128)(2,1)} %collective-permute-done.57), channel_id=1, source_target_pairs={{2,1},{1,0},{6,5},{5,4},{10,9},{9,8},{14,13},{13,12},{18,17},{17,1... | collective-permute-start | bytes 6881288 | tf_op jit(solution)/shard_map/ppermute | solution.py:266
  1697.2 35.8 %collective-permute-start.60 = (bf16[80,14336]{1,0:T(8,128)(2,1)S(1)}, bf16[80,14336]{1,0:T(8,128)(2,1)}, u32[]{:S(2)}, u32[]{:S(2)}) collective-permute-start(bf16[80,14336]{1,0:T(8,128)(2,1)S(1)} %collective-permute-done.56), channel_id=1, source_target_pairs={{1,2},{2,3},{5,6},{6,7},{9,10},{10,11},{13,14},{14,15},{17,18},{18... | collective-permute-start | bytes 6881288 | tf_op jit(solution)/shard_map/ppermute | solution.py:265
  1719.0 53.4 %collective-permute-start.59 = (bf16[80,14336]{1,0:T(8,128)(2,1)S(1)}, bf16[80,14336]{1,0:T(8,128)(2,1)S(1)}, u32[]{:S(2)}, u32[]{:S(2)}) collective-permute-start(bf16[80,14336]{1,0:T(8,128)(2,1)S(1)} %collective-permute-done.58), channel_id=1, source_target_pairs={{1,0},{5,4},{9,8},{13,12},{17,16},{21,20},{25,24},{29,28}} | collective-permute-start | bytes 6881288 | tf_op jit(solution)/shard_map/ppermute | solution.py:266
  1733.0 56.0 %collective-permute-start.61 = (bf16[80,14336]{1,0:T(8,128)(2,1)}, bf16[80,14336]{1,0:T(8,128)(2,1)}, u32[]{:S(2)}, u32[]{:S(2)}) collective-permute-start(bf16[80,14336]{1,0:T(8,128)(2,1)} %collective-permute-done.60), channel_id=1, source_target_pairs={{2,3},{6,7},{10,11},{14,15},{18,19},{22,23},{26,27},{30,31}} | collective-permute-start | bytes 6881288 | tf_op jit(solution)/shard_map/ppermute | solution.py:265
  1794.6 39.9 %collective-permute-start.35 = (bf16[80,2560]{1,0:T(8,128)(2,1)}, bf16[80,2560]{1,0:T(8,128)(2,1)S(1)}, u32[]{:S(2)}, u32[]{:S(2)}) collective-permute-start(bf16[80,2560]{1,0:T(8,128)(2,1)} %get-tuple-element.169), channel_id=1, source_target_pairs={{3,2},{2,1},{7,6},{6,5},{11,10},{10,9},{15,14},{14,13},{19,18},{18... | collective-permute-start | bytes 1228808 | tf_op jit(solution)/shard_map/ppermute | solution.py:256
  1795.3 53.0 %collective-permute-start.33 = (bf16[80,2560]{1,0:T(8,128)(2,1)}, bf16[80,2560]{1,0:T(8,128)(2,1)S(1)}, u32[]{:S(2)}, u32[]{:S(2)}) collective-permute-start(bf16[80,2560]{1,0:T(8,128)(2,1)} %get-tuple-element.168), channel_id=1, source_target_pairs={{0,1},{1,2},{2,3},{4,5},{5,6},{6,7},{8,9},{9,10},{10,11},{12,13},{... | collective-permute-start | bytes 1228808 | tf_op jit(solution)/shard_map/ppermute | solution.py:255
  1802.1 41.9 %collective-permute-start.19 = (bf16[80,3968]{1,0:T(8,128)(2,1)S(1)}, bf16[80,3968]{1,0:T(8,128)(2,1)S(1)}, u32[]{:S(2)}, u32[]{:S(2)}) collective-permute-start(bf16[80,3968]{1,0:T(8,128)(2,1)S(1)} %get-tuple-element.154), channel_id=1, source_target_pairs={{0,1},{4,5},{8,9},{12,13},{16,17},{20,21},{24,25},{28,29}} | collective-permute-start | bytes 1904648 | tf_op jit(solution)/shard_map/ppermute | solution.py:255
  1836.9 19.1 collective-permute-start.22
  1849.9 21.7 %collective-permute-start.38 = (bf16[80,2560]{1,0:T(8,128)(2,1)S(1)}, bf16[80,2560]{1,0:T(8,128)(2,1)}, u32[]{:S(2)}, u32[]{:S(2)}) collective-permute-start(bf16[80,2560]{1,0:T(8,128)(2,1)S(1)} %get-tuple-element.109), channel_id=1, source_target_pairs={{3,2},{2,1},{1,0},{7,6},{6,5},{5,4},{11,10},{10,9},{9,8},{15,14},{... | collective-permute-start | bytes 1228808 | tf_op jit(solution)/shard_map/ppermute | solution.py:266
  1851.2 21.7 %collective-permute-start.37 = (bf16[80,2560]{1,0:T(8,128)(2,1)S(1)}, bf16[80,2560]{1,0:T(8,128)(2,1)}, u32[]{:S(2)}, u32[]{:S(2)}) collective-permute-start(bf16[80,2560]{1,0:T(8,128)(2,1)S(1)} %get-tuple-element.109), channel_id=1, source_target_pairs={{0,1},{1,2},{2,3},{4,5},{5,6},{6,7},{8,9},{9,10},{10,11},{12,13},{... | collective-permute-start | bytes 1228808 | tf_op jit(solution)/shard_map/ppermute | solution.py:265
  1857.2 24.0 %collective-permute-start.23 = (bf16[80,3968]{1,0:T(8,128)(2,1)S(1)}, bf16[80,3968]{1,0:T(8,128)(2,1)S(1)}, u32[]{:S(2)}, u32[]{:S(2)}) collective-permute-start(bf16[80,3968]{1,0:T(8,128)(2,1)S(1)} %get-tuple-element.153), channel_id=1, source_target_pairs={{3,2},{2,1},{7,6},{6,5},{11,10},{10,9},{15,14},{14,13},{19,18},{18... | collective-permute-start | bytes 1904648 | tf_op jit(solution)/shard_map/ppermute | solution.py:256
  1887.0 18.4 collective-permute-start.40
  1888.6 45.5 %collective-permute-start.42 = (bf16[80,2560]{1,0:T(8,128)(2,1)S(1)}, bf16[80,2560]{1,0:T(8,128)(2,1)S(1)}, u32[]{:S(2)}, u32[]{:S(2)}) collective-permute-start(bf16[80,2560]{1,0:T(8,128)(2,1)S(1)} %collective-permute-done.41), channel_id=1, source_target_pairs={{2,3},{6,7},{10,11},{14,15},{18,19},{22,23},{26,27},{30,31}} | collective-permute-start | bytes 1228808 | tf_op jit(solution)/shard_map/ppermute | solution.py:265
  1897.4 21.6 %collective-permute-start.26 = (bf16[80,3968]{1,0:T(8,128)(2,1)S(1)}, bf16[80,3968]{1,0:T(8,128)(2,1)S(1)}, u32[]{:S(2)}, u32[]{:S(2)}) collective-permute-start(bf16[80,3968]{1,0:T(8,128)(2,1)S(1)} %get-tuple-element.111), channel_id=1, source_target_pairs={{3,2},{2,1},{1,0},{7,6},{6,5},{5,4},{11,10},{10,9},{9,8},{15,14},{... | collective-permute-start | bytes 1904648 | tf_op jit(solution)/shard_map/ppermute | solution.py:266
  (89 other events, 1749.2 us)
Sparse Core Ops, SparseCore 0:
  13.5 107.3 all-gather.8
  122.8 74.3 all-gather.10
  222.5 125.9 all-gather.12
  350.2 114.9 all-gather.16
  514.4 81.1 reduce-scatter.10
  601.4 71.3 all-gather.14
  674.6 63.2 all-gather.18
  786.8 81.1 reduce-scatter.12
  871.4 81.5 reduce-scatter.6
  956.4 81.5 reduce-scatter.8
  1058.5 95.1 reduce-scatter.16
  1305.7 143.2 reduce-scatter.14

commit v2 on v1

v2 whole, which is shorter than its diff:
```python
import functools, math
import jax, jax.numpy as jnp
from jax import lax
from jax.experimental import pallas as pl
from jax.experimental.pallas import tpu as pltpu
from jax.sharding import PartitionSpec as P

D = 2560
HEADS = 32
KV_HEADS = 8
HEAD_DIM = 80
GROUP = HEADS // KV_HEADS
HALVES = 2
SCALE = HEAD_DIM ** -0.5
LOG2E = 1.0 / math.log(2.0)
QW = D // HALVES
KW = KV_HEADS * HEAD_DIM // HALVES
CHUNK = 640
SPEED = 1 << 28


def work(micros):
    return pl.CostEstimate(flops=micros * SPEED, bytes_accessed=1 << 16, transcendentals=0)


def nt(left, right):
    return lax.dot_general(left, right, (((1,), (1,)), ((), ())), preferred_element_type=jnp.float32)


def tn(left, right):
    return lax.dot_general(left, right, (((0,), (0,)), ((), ())), preferred_element_type=jnp.float32)


def nn(left, right):
    return jnp.dot(left, right, preferred_element_type=jnp.float32)


def head(h):
    return slice(h * HEAD_DIM, (h + 1) * HEAD_DIM)


def spin(x, cosine, sine_up, sine_down):
    half = HEAD_DIM // 2
    width = x.shape[1]
    return x * cosine + pltpu.roll(x, width - half, 1) * sine_up + pltpu.roll(x, half, 1) * sine_down


def project_kernel(n_ref, w_ref, cos_ref, up_ref, down_ref, out_ref):
    j = pl.program_id(0)
    x = nn(n_ref[...], w_ref[...])
    turned = spin(x, cos_ref[...], up_ref[...], down_ref[...])
    lane = lax.broadcasted_iota(jnp.int32, x.shape, 1)
    keep = (j < D // CHUNK) | (lane < KW)
    out_ref[...] = jnp.where(keep, turned, x).astype(jnp.bfloat16)


def project(normed, weights, tables):
    rows = normed.shape[0]
    chunks = (D + 4 * KW) // CHUNK
    table = pl.BlockSpec((rows, CHUNK), lambda j: (0, 0))
    return pl.pallas_call(
        project_kernel,
        grid=(chunks,),
        in_specs=[pl.BlockSpec((rows, D), lambda j: (0, 0)), pl.BlockSpec((D, CHUNK), lambda j: (0, j)), table, table, table],
        out_specs=pl.BlockSpec((rows, CHUNK), lambda j: (0, j)),
        out_shape=jax.ShapeDtypeStruct((rows, chunks * CHUNK), jnp.bfloat16),
        compiler_params=pltpu.CompilerParams(vmem_limit_bytes=48 << 20),
        cost_estimate=work(19),
        name="project",
    )(normed, weights, *tables)


def forward_kernel(blocks, q_ref, *refs):
    kv_refs = refs[:blocks]
    bias_ref, ctx_ref, lse_ref = refs[blocks:]
    rows = q_ref.shape[0]
    bias = [bias_ref[s] for s in range(blocks)]
    lane = lax.broadcasted_iota(jnp.int32, (rows, 128), 1)
    lse_all = jnp.zeros((rows, 128), jnp.float32)
    for h in range(QW // HEAD_DIM):
        c = h // GROUP
        q = q_ref[:, head(h)]
        scores = [nt(q, kv_refs[s][:, head(c)]) * (SCALE * LOG2E) + bias_ref[s] for s in range(blocks)]
        top = functools.reduce(jnp.maximum, scores).max(axis=1, keepdims=True)
        probs = [jnp.exp2(x - top) for x in scores]
        total = functools.reduce(jnp.add, probs).sum(axis=1, keepdims=True)
        ctx = functools.reduce(jnp.add, [nn(p.astype(jnp.bfloat16), kv_refs[s][:, KW + c * HEAD_DIM:KW + (c + 1) * HEAD_DIM]) for s, p in enumerate(probs)])
        ctx_ref[:, head(h)] = (ctx / total).astype(jnp.bfloat16)
        lse_all = jnp.where(lane == h, top + jnp.log2(total), lse_all)
    lse_ref[...] = lse_all


def attend(qkv, kv_blocks, bias, at):
    rows = kv_blocks[0].shape[0]
    blocks = len(kv_blocks)
    kv_spec = pl.BlockSpec((rows, 2 * KW), lambda h: (0, h))
    return pl.pallas_call(
        functools.partial(forward_kernel, blocks),
        grid=(HALVES,),
        in_specs=[pl.BlockSpec((rows, QW), lambda h: (at, h))] + [kv_spec] * blocks + [pl.BlockSpec((blocks, rows, rows), lambda h: (0, 0, 0))],
        out_specs=[pl.BlockSpec((rows, QW), lambda h: (0, h)), pl.BlockSpec((rows, 128), lambda h: (0, h))],
        out_shape=[jax.ShapeDtypeStruct((rows, D), jnp.bfloat16), jax.ShapeDtypeStruct((rows, HALVES * 128), jnp.float32)],
        compiler_params=pltpu.CompilerParams(vmem_limit_bytes=48 << 20),
        cost_estimate=work(23),
        name="attend",
    )(qkv, *kv_blocks, bias)


def backward_kernel(blocks, skipped, q_ref, dctx_ref, ctx_ref, lse_ref, *refs):
    kv_refs = refs[:blocks]
    bias_ref, cos_ref, up_ref, down_ref = refs[blocks:blocks + 4]
    dq_ref = refs[blocks + 4 + skipped]
    dkv_refs = refs[blocks + 5 + skipped:2 * blocks + 5 + skipped]
    dq_acc = refs[-1]
    rows = q_ref.shape[0]
    count = QW // HEAD_DIM
    owner = lax.broadcasted_iota(jnp.int32, (count, QW), 0)
    lane = lax.broadcasted_iota(jnp.int32, (count, QW), 1)
    pick = ((lane >= owner * HEAD_DIM) & (lane < owner * HEAD_DIM + HEAD_DIM)).astype(jnp.float32)
    product = dctx_ref[...].astype(jnp.float32) * ctx_ref[...].astype(jnp.float32)
    delta = lax.dot_general(pick, product, (((1,), (1,)), ((), ())), precision=lax.Precision.HIGHEST, preferred_element_type=jnp.float32)
    for c in range(KV_HEADS // HALVES):
        heads = range(c * GROUP, (c + 1) * GROUP)
        qs = [q_ref[:, head(h)] for h in heads]
        ds = [dctx_ref[:, head(h)] for h in heads]
        q_stack = jnp.concatenate(qs, axis=0)
        d_stack = jnp.concatenate(ds, axis=0)
        dq = [None] * GROUP
        for s in range(blocks):
            k = kv_refs[s][:, head(c)]
            v = kv_refs[s][:, KW + c * HEAD_DIM:KW + (c + 1) * HEAD_DIM]
            ps, dss = [], []
            for g, h in enumerate(heads):
                score = nt(k, qs[g]) * (SCALE * LOG2E) + bias_ref[s]
                p = jnp.exp2(score - lse_ref[h:h + 1, :])
                dp = nt(v, ds[g])
                d = (p * (dp - delta[h:h + 1, :])).astype(jnp.bfloat16)
                ps.append(p.astype(jnp.bfloat16))
                dss.append(d)
                term = tn(d, k)
                dq[g] = term if dq[g] is None else dq[g] + term
            dkv_refs[s][:, head(c)] = (nn(jnp.concatenate(dss, axis=1), q_stack) * SCALE).astype(jnp.bfloat16)
            dkv_refs[s][:, KW + c * HEAD_DIM:KW + (c + 1) * HEAD_DIM] = nn(jnp.concatenate(ps, axis=1), d_stack).astype(jnp.bfloat16)
        for g, h in enumerate(heads):
            dq_acc[:, head(h)] = dq[g] * SCALE
    for j in range(QW // CHUNK):
        part = slice(j * CHUNK, (j + 1) * CHUNK)
        dq_ref[:, part] = spin(dq_acc[:, part], cos_ref[...], -up_ref[...], -down_ref[...]).astype(jnp.bfloat16)


def attend_back(qkv, dctx, ctx, lse_rows, kv_blocks, bias_t, tables, at, half, before=None):
    rows = kv_blocks[0].shape[0]
    blocks = len(kv_blocks)
    count = QW // HEAD_DIM
    lanes = pl.BlockSpec((rows, QW), lambda h: (0, half))
    kv_spec = pl.BlockSpec((rows, 2 * KW), lambda h: (0, half))
    table = pl.BlockSpec((rows, CHUNK), lambda h: (at, 0))
    before = [] if before is None else list(before)
    inputs = 4 + blocks + 4
    outs = pl.pallas_call(
        functools.partial(backward_kernel, blocks, len(before)),
        grid=(1,),
        in_specs=[pl.BlockSpec((rows, QW), lambda h: (at, half)), lanes, lanes, pl.BlockSpec((count, rows), lambda h: (half, 0))]
        + [kv_spec] * blocks + [pl.BlockSpec((blocks, rows, rows), lambda h: (0, 0, 0)), table, table, table]
        + [pl.BlockSpec(memory_space=pl.ANY)] * len(before),
        out_specs=[lanes] + [kv_spec] * blocks,
        out_shape=[jax.ShapeDtypeStruct((rows, D), jnp.bfloat16)] + [jax.ShapeDtypeStruct((rows, 4 * KW), jnp.bfloat16)] * blocks,
        scratch_shapes=[pltpu.VMEM((rows, QW), jnp.float32)],
        input_output_aliases={inputs + k: k for k in range(len(before))},
        compiler_params=pltpu.CompilerParams(vmem_limit_bytes=48 << 20),
        cost_estimate=work(100),
        name="attend_back",
    )(qkv, dctx, ctx, lse_rows, *kv_blocks, bias_t, *tables, *before)
    return outs


RMS_EPS = 1e-05
ROPE_BASE = 1000000.0


def finish_kernel(own_ref, other_ref, cos_ref, up_ref, down_ref, out_ref):
    x = own_ref[...].astype(jnp.float32) + other_ref[...].astype(jnp.float32)
    turned = spin(x, cos_ref[...], -up_ref[...], -down_ref[...])
    lane = lax.broadcasted_iota(jnp.int32, x.shape, 1)
    out_ref[...] = jnp.where(lane < KW, turned, x).astype(jnp.bfloat16)


def finish_keys(own, other, tables, at):
    rows = own.shape[0]
    half = pl.BlockSpec((rows, 2 * KW), lambda h: (0, h))
    table = pl.BlockSpec((rows, CHUNK), lambda h: (at, 0))
    return pl.pallas_call(
        finish_kernel,
        grid=(HALVES,),
        in_specs=[half, half, table, table, table],
        out_specs=half,
        out_shape=jax.ShapeDtypeStruct(own.shape, jnp.bfloat16),
        cost_estimate=work(2),
        name="finish_keys",
    )(own, other, *tables)


def rms_scale(values):
    return lax.rsqrt(jnp.mean(values * values, axis=-1, keepdims=True) + RMS_EPS)


def norm_back(grad_normed, gain, normed_x, scale_row, grad_rest):
    scaled = grad_normed * gain
    inner = jnp.mean(scaled * normed_x, axis=-1, keepdims=True)
    return grad_rest + scale_row * (scaled - normed_x * inner)


def rope_lanes(position):
    lane = jnp.arange(CHUNK, dtype=jnp.int32) % HEAD_DIM
    half = HEAD_DIM // 2
    index = (lane % half).astype(jnp.float32)
    inverse = jnp.exp(index * (-2.0 * math.log(ROPE_BASE) / HEAD_DIM))
    angles = position.astype(jnp.float32)[:, None] * inverse[None, :]
    sine = jnp.sin(angles)
    first = (lane < half)[None, :]
    return jnp.cos(angles), jnp.where(first, -sine, 0.0), jnp.where(first, 0.0, sine)


def stream_layout(starts, places):
    begun = starts[:, None, :] <= places[None, :, None]
    doc_ids = jnp.sum(begun.astype(jnp.int32), axis=-1) - 1
    first_token = jnp.max(jnp.where(begun, starts[:, None, :], 0), axis=-1)
    return doc_ids, places[None, :] - first_token


def right_pairs(count, lowest=0):
    return [(k, k + 1) for k in range(lowest, count - 1)]


def left_pairs(count):
    return [(k + 1, k) for k in range(count - 1)]


def tie(x, *before):
    return lax.optimization_barrier((x,) + before)[0]


class Order:
    def __init__(self):
        self.last = ()

    def at(self, x, *more):
        return tie(x, *self.last, *more)

    def did(self, y):
        self.last = (y,)
        return y


def partner(x):
    return lax.ppermute(x, "fsdp", [(j, j ^ 1) for j in range(lax.axis_size("fsdp"))])


def same_core():
    parts = lax.axis_size("fsdp")
    return [list(range(c, parts, 2)) for c in range(2)]


def gather_chips(x):
    return lax.all_gather(x, "fsdp", axis=0, tiled=True, axis_index_groups=same_core())


def scatter_chips(x):
    return lax.psum_scatter(x, "fsdp", scatter_dimension=0, tiled=True, axis_index_groups=same_core())


def exchange(blocks):
    parts = lax.axis_size("fsdp")
    me = lax.axis_index("fsdp")
    chips, core = parts // 2, me % 2
    shape = blocks.shape[1:]
    blocks = blocks.reshape((chips, 2) + shape)
    mine = lax.dynamic_index_in_dim(blocks, core, 1, keepdims=False)
    came = partner(lax.dynamic_index_in_dim(blocks, 1 - core, 1, keepdims=False))
    return jnp.where(core == 0, jnp.stack([mine, came], axis=1), jnp.stack([came, mine], axis=1))


def exchange_chips(pair):
    parts = lax.axis_size("fsdp")
    chips, chip = parts // 2, lax.axis_index("fsdp") // 2
    own = lax.dynamic_index_in_dim(pair, chip, 0, keepdims=True)
    pieces = [own]
    for d in range(1, chips):
        block = lax.dynamic_index_in_dim(pair, chip ^ d, 0, keepdims=True)
        pieces.append(lax.ppermute(block, "fsdp", [(j, j ^ (2 * d)) for j in range(parts)]))
    return pieces


def exchanged(pieces):
    parts = lax.axis_size("fsdp")
    chip = lax.axis_index("fsdp") // 2
    out = jnp.zeros((parts // 2,) + pieces[0].shape[1:], pieces[0].dtype)
    for d, piece in enumerate(pieces):
        out = lax.dynamic_update_slice_in_dim(out, piece, chip ^ d, 0)
    return out


def columns_kernel(blocks, place_ref, gate_ref, up_ref, out_ref):
    j = pl.program_id(0)

    @pl.when(place_ref[blocks + j] == 0)
    def _():
        out_ref[...] = gate_ref[...]

    @pl.when(place_ref[blocks + j] == 1)
    def _():
        out_ref[...] = up_ref[...]


def columns_for(w_gate, w_up, picks, width):
    rows = w_gate.shape[0]
    blocks = len(picks)
    if width % 128:
        both = jnp.stack([w_gate.reshape(rows, -1, width), w_up.reshape(rows, -1, width)])
        return jnp.concatenate([both[which, :, at] for at, which in picks], axis=1)
    place = jnp.stack([jnp.asarray(x, jnp.int32) for x in [p[0] for p in picks] + [p[1] for p in picks]])
    source = lambda own: pl.BlockSpec(
        (rows, width), lambda j, place: (0, jnp.where(place[blocks + j] == own, place[j], place[0]))
    )
    return pl.pallas_call(
        functools.partial(columns_kernel, blocks),
        grid_spec=pltpu.PrefetchScalarGridSpec(
            num_scalar_prefetch=1,
            grid=(blocks,),
            in_specs=[source(0), source(1)],
            out_specs=pl.BlockSpec((rows, width), lambda j, place: (0, j)),
        ),
        out_shape=jax.ShapeDtypeStruct((rows, blocks * width), w_gate.dtype),
        cost_estimate=work(blocks),
        name="columns_for",
    )(place, w_gate, w_up)


def weave_kernel(count, chips, width, place_ref, *refs):
    out_ref = refs[-1]
    j = pl.program_id(0)
    half = 2 * width
    for d in range(chips):
        for c in range(2):
            mine, other = refs[2 * (c * chips + d):2 * (c * chips + d) + 2]
            for odd in range(2):
                @pl.when((j == 2 * d + c) & (place_ref[count] == odd))
                def _(mine=mine, other=other, c=c, odd=odd):
                    for which, ref in ((odd, mine), (1 - odd, other)):
                        for k in range(2):
                            at = which * half + k * width
                            from_lane = (k ^ c) * width
                            out_ref[:, at:at + width] = ref[:, from_lane:from_lane + width]


def weave(mine, other, places, odd, width):
    rows = mine[0].shape[0]
    count = len(mine)
    chips = count // 2
    tile = next(t for t in (160, 64, 32, 16) if rows % t == 0)
    tiles = rows // tile
    specs, arrays = [], []
    for c in range(2):
        for d in range(chips):
            index = lambda j, t, place, k=2 * d + c: (jnp.where(j == k, t, 0), 0)
            specs += [pl.BlockSpec((tile, 2 * width), index)] * 2
            arrays += [mine[c * chips + d], other[c * chips + d]]
    return pl.pallas_call(
        functools.partial(weave_kernel, count, chips, width),
        grid_spec=pltpu.PrefetchScalarGridSpec(
            num_scalar_prefetch=1,
            grid=(count, tiles),
            in_specs=specs,
            out_specs=pl.BlockSpec((tile, 4 * width), lambda j, t, place: (place[j] * tiles + t, 0)),
        ),
        out_shape=jax.ShapeDtypeStruct((count * rows, 4 * width), mine[0].dtype),
        compiler_params=pltpu.CompilerParams(vmem_limit_bytes=56 << 20),
        cost_estimate=work(21),
        name="weave",
    )(jnp.stack([jnp.asarray(x, jnp.int32) for x in places + [odd]]), *arrays)


class Reshard:
    def __init__(self, w_gate, w_up):
        parts = lax.axis_size("fsdp")
        me = lax.axis_index("fsdp")
        self.chips = parts // 2
        self.chip, self.core = me // 2, me % 2
        self.odd = lax.axis_index("sp") % 2
        self.width = w_gate.shape[1] // parts
        pair = lambda d, which: [(2 * (self.chip ^ d) + c, which) for c in (self.core, 1 - self.core)]
        self.local = columns_for(w_gate, w_up, pair(0, self.odd) + pair(0, 1 - self.odd), self.width)
        self.sent = [columns_for(w_gate, w_up, pair(d, self.odd), self.width) for d in range(1, self.chips)]

    def fetch(self):
        parts = 2 * self.chips
        half = 2 * self.width
        self.mine = [self.local[:, :half]] + [
            lax.ppermute(x, "fsdp", [(j, j ^ (2 * d)) for j in range(parts)]) for d, x in enumerate(self.sent, 1)
        ]
        pairs = [(k, k ^ 1) for k in range(lax.axis_size("sp"))]
        self.other = [self.local[:, half:]] + [lax.ppermute(x, "sp", pairs) for x in self.mine[1:]]
        return self.other[1:]

    def result(self, *before):
        mine = self.mine + [partner(x) for x in self.mine]
        other = self.other + [partner(x) for x in self.other]
        places = []
        for d in range(self.chips):
            places += [2 * (self.chip ^ d) + self.core, 2 * (self.chip ^ d) + 1 - self.core]
        return weave([tie(mine[0], *before)] + mine[1:], other, places, self.odd, self.width)


def features_kernel(count, width, core_ref, x_ref, mine_ref, other_ref):
    for c in range(2):
        @pl.when(core_ref[0] == c)
        def _(c=c):
            for q in range(count):
                at = slice(q * width, (q + 1) * width)
                mine_ref[:, at] = x_ref[:, (2 * q + c) * width:(2 * q + c + 1) * width]
                other_ref[:, at] = x_ref[:, (2 * q + 1 - c) * width:(2 * q + 2 - c) * width]


def features(x, core, width):
    rows = x.shape[0]
    count = x.shape[1] // (2 * width)
    tile = min(rows, 256)
    out = pl.BlockSpec((tile, count * width), lambda t, core: (t, 0))
    return pl.pallas_call(
        functools.partial(features_kernel, count, width),
        grid_spec=pltpu.PrefetchScalarGridSpec(
            num_scalar_prefetch=1,
            grid=(rows // tile,),
            in_specs=[pl.BlockSpec((tile, x.shape[1]), lambda t, core: (t, 0))],
            out_specs=[out, out],
        ),
        out_shape=[jax.ShapeDtypeStruct((rows, count * width), x.dtype)] * 2,
        cost_estimate=work(3),
        name="features",
    )(core.reshape(1).astype(jnp.int32), x)


def sum_tn_kernel(segments, pairs, *refs):
    lefts = [ref[...] for ref in refs[:pairs]]
    extra = refs[pairs + segments * pairs:-1]
    out_ref = refs[-1]
    width = out_ref.shape[1] // segments
    for j in range(segments):
        rights = refs[pairs + j * pairs:pairs + (j + 1) * pairs]
        part = slice(j * width, (j + 1) * width)
        total = sum(tn(a, b[...]) for a, b in zip(lefts, rights))
        for more in extra:
            total = total + more[:, part].astype(jnp.float32)
        out_ref[:, part] = total.astype(out_ref.dtype)


def sum_tn(lefts, rights, half, *extra, weight=1):
    segments, pairs = len(rights), len(lefts)
    tokens = lefts[0].shape[0]
    if segments == 1:
        width = lefts[0].shape[1] // 2
        if width % 128:
            total = sum(tn(a[:, half * width:(half + 1) * width], b) for a, b in zip(lefts, rights[0]))
            return sum((e.astype(jnp.float32) for e in extra), total).astype(jnp.bfloat16)
        shape = (width, D)
        block = (width, CHUNK)
        left = pl.BlockSpec((tokens, width), lambda i: (0, half))
        right = pl.BlockSpec((tokens, CHUNK), lambda i: (0, i))
        out = pl.BlockSpec(block, lambda i: (0, i))
    else:
        width = rights[0][0].shape[1] // 2
        if width % 128:
            cut = slice(half * width, (half + 1) * width)
            total = jnp.concatenate([sum(tn(a, b[:, cut]) for a, b in zip(lefts, r)) for r in rights], axis=1)
            return sum((e.astype(jnp.float32) for e in extra), total).astype(jnp.bfloat16)
        shape = (D, segments * width)
        left = pl.BlockSpec((tokens, CHUNK), lambda i: (0, i))
        right = pl.BlockSpec((tokens, width), lambda i: (0, half))
        out = pl.BlockSpec((CHUNK, segments * width), lambda i: (i, 0))
    return pl.pallas_call(
        functools.partial(sum_tn_kernel, segments, pairs),
        grid=(D // CHUNK,),
        in_specs=[left] * pairs + [right] * (segments * pairs) + [out] * len(extra),
        out_specs=out,
        out_shape=jax.ShapeDtypeStruct(shape, jnp.bfloat16),
        compiler_params=pltpu.CompilerParams(vmem_limit_bytes=56 << 20),
        cost_estimate=work((26 if segments == 2 else 16) * weight),
        name="sum_tn",
    )(*lefts, *[b for r in rights for b in r], *extra)


def ffn_kernel(n_ref, g_ref, wg_ref, wu_ref, wd_ref, hidden_ref, gate_grad_ref, up_grad_ref):
    gate = nn(n_ref[...], wg_ref[...])
    up = nn(n_ref[...], wu_ref[...])
    hidden_grad = nt(g_ref[...], wd_ref[...])
    sigm = 1.0 / (1.0 + jnp.exp(-gate))
    act = gate * sigm
    hidden_ref[...] = (act * up).astype(jnp.bfloat16)
    up_grad_ref[...] = (hidden_grad * act).astype(jnp.bfloat16)
    gate_grad_ref[...] = (hidden_grad * up * (sigm + act * (1.0 - sigm))).astype(jnp.bfloat16)


def feed_forward(n2, g, w_both, w_down):
    tokens, hidden = n2.shape[0], w_down.shape[0]
    tile = 256 if hidden % 256 == 0 else 128
    tiles = hidden // tile
    full = pl.BlockSpec((tokens, D), lambda j: (0, 0))
    out = pl.BlockSpec((tokens, tile), lambda j: (0, j))
    return pl.pallas_call(
        ffn_kernel,
        grid=(tiles,),
        in_specs=[full, full, pl.BlockSpec((D, tile), lambda j: (0, j)), pl.BlockSpec((D, tile), lambda j: (0, tiles + j)),
                  pl.BlockSpec((tile, D), lambda j: (j, 0))],
        out_specs=[out] * 3,
        out_shape=[jax.ShapeDtypeStruct((tokens, hidden), jnp.bfloat16)] * 3,
        compiler_params=pltpu.CompilerParams(vmem_limit_bytes=56 << 20),
        cost_estimate=work(36),
        name="feed_forward",
    )(n2, g, w_both, w_both, w_down)


def sum_nt_kernel(*refs):
    pairs = len(refs) // 2
    refs[-1][...] = sum(nt(refs[k][...], refs[pairs + k][...]) for k in range(pairs)).astype(jnp.bfloat16)


def sum_nt(lefts, right, weight=1):
    (tokens, depth), columns = lefts[0].shape, right.shape[0]
    tile, block = tokens // 2, columns // 2
    return pl.pallas_call(
        sum_nt_kernel,
        grid=(columns // block, tokens // tile),
        in_specs=[pl.BlockSpec((tile, depth), lambda j, i: (i, 0))] * len(lefts)
        + [pl.BlockSpec((block, depth), lambda j, i, k=k: (j, k)) for k in range(len(lefts))],
        out_specs=pl.BlockSpec((tile, block), lambda j, i: (i, j)),
        out_shape=jax.ShapeDtypeStruct((tokens, columns), jnp.bfloat16),
        compiler_params=pltpu.CompilerParams(vmem_limit_bytes=56 << 20),
        cost_estimate=work(26 * weight),
        name="sum_nt",
    )(*lefts, *([right] * len(lefts)))


def plain_nn_kernel(a_ref, b_ref, out_ref):
    out_ref[...] = nn(a_ref[...], b_ref[...]).astype(jnp.bfloat16)


def plain_nn(a, b, weight=1):
    (tokens, depth), columns = a.shape, b.shape[1]
    return pl.pallas_call(
        plain_nn_kernel,
        grid=(columns // CHUNK,),
        in_specs=[pl.BlockSpec((tokens, depth), lambda j: (0, 0)), pl.BlockSpec((depth, CHUNK), lambda j: (0, j))],
        out_specs=pl.BlockSpec((tokens, CHUNK), lambda j: (0, j)),
        out_shape=jax.ShapeDtypeStruct((tokens, columns), jnp.bfloat16),
        compiler_params=pltpu.CompilerParams(vmem_limit_bytes=56 << 20),
        cost_estimate=work(16 * weight),
        name="plain_nn",
    )(a, b)


class Scatter:
    def __init__(self, take):
        self.take = take
        self.hops = 0
        self.right = self.left = None

    def hop(self):
        n = lax.axis_size("sp")
        me = lax.axis_index("sp")
        s = self.hops
        to_right = self.take(jnp.clip(me + (n - 1) - s, 0, n - 1))
        to_left = self.take(jnp.clip(me - (n - 1) + s, 0, n - 1))
        if s:
            to_right = to_right + self.right
            to_left = to_left + self.left
        self.right = lax.ppermute(to_right, "sp", [(k, k + 1) for k in range(s + 1)])
        self.left = lax.ppermute(to_left, "sp", [(n - 1 - k, n - 2 - k) for k in range(s + 1)])
        self.hops += 1
        return self.right, self.left

    def result(self):
        while self.hops < lax.axis_size("sp") - 1:
            self.hop()
        total = self.take(lax.axis_index("sp")).astype(jnp.float32) + self.right.astype(jnp.float32)
        return (total + self.left.astype(jnp.float32)).astype(jnp.bfloat16)


def chunk_of(x):
    return lambda j: lax.dynamic_index_in_dim(x, j, 0, keepdims=False)


class KeySum:
    def __init__(self, parts):
        self.parts = parts
        self.running = parts[-1]
        self.hops = 0

    def hop(self, *before):
        n = lax.axis_size("sp")
        s = self.hops
        if s:
            self.running = (self.parts[n - 1 - s].astype(jnp.float32) + self.running.astype(jnp.float32)).astype(jnp.bfloat16)
        pairs = [(n - 1 - k, n - 2 - k) for k in range(s + 1)]
        self.running = lax.ppermute(tie(self.running, *before), "sp", pairs)
        self.hops += 1
        return self.running

    def result(self):
        while self.hops < lax.axis_size("sp") - 1:
            self.hop()
        return self.parts[0], self.running


class Gather:
    def __init__(self, mine):
        self.rights, self.lefts = [mine], [mine]

    def hop(self):
        n = lax.axis_size("sp")
        s = len(self.rights) - 1
        self.rights.append(lax.ppermute(self.rights[-1], "sp", [(k, k + 1) for k in range(s, n - 1)]))
        self.lefts.append(lax.ppermute(self.lefts[-1], "sp", [(n - 1 - k, n - 2 - k) for k in range(s, n - 1)]))
        return self.rights[-1], self.lefts[-1]

    def result(self):
        n = lax.axis_size("sp")
        while len(self.rights) < n:
            self.hop()
        return [(self.rights[0], None)] + [(self.rights[k], self.lefts[n - k]) for k in range(1, n)]


def place_kernel(conditions, plan, place_ref, *refs):
    sources, outs = refs[:len(conditions)], refs[len(conditions):]
    for (k, side), source in zip(conditions, sources):
        active = pl.program_id(0) == k
        if side == 1:
            active = active & (place_ref[0] >= k)
        elif side == 2:
            active = active & (place_ref[0] < k)

        @pl.when(active)
        def _(source=source):
            for out, spans in zip(outs, plan):
                at = 0
                for start, width in spans:
                    out[:, at:at + width] = source[:, start:start + width].astype(jnp.float32)
                    at += width


def assemble(slots, plan):
    n = len(slots)
    me = lax.axis_index("sp")
    rows, width = slots[0][0].shape
    if rows % 16:
        out = jnp.zeros((n * rows, width), jnp.float32)
        for k, (left, right) in enumerate(slots):
            came = left if right is None else jnp.where(me >= k, left, right)
            out = lax.dynamic_update_slice_in_dim(out, came.astype(jnp.float32), ((me - k + n) % n) * rows, 0)
        return [jnp.concatenate([out[:, a:a + w] for a, w in spans], axis=1) for spans in plan]
    tile = max(t for t in range(16, rows + 1, 16) if rows % t == 0 and (t == 16 or t * width <= 1 << 19))
    tiles = rows // tile
    sources, conditions = [], []
    for k, (left, right) in enumerate(slots):
        sources.append(left)
        conditions.append((k, 0 if right is None else 1))
        if right is not None:
            sources.append(right)
            conditions.append((k, 2))

    def spec(k, side):
        def index(s, t, place):
            active = s == k
            if side == 1:
                active = active & (place[0] >= k)
            elif side == 2:
                active = active & (place[0] < k)
            return jnp.where(active, t, 0), 0
        return pl.BlockSpec((tile, width), index)

    out_index = lambda s, t, place: (lax.rem(place[0] - s + n, n) * tiles + t, 0)
    widths = [sum(w for _, w in spans) for spans in plan]
    return pl.pallas_call(
        functools.partial(place_kernel, conditions, plan),
        grid_spec=pltpu.PrefetchScalarGridSpec(
            num_scalar_prefetch=1,
            grid=(n, tiles),
            in_specs=[spec(*c) for c in conditions],
            out_specs=[pl.BlockSpec((tile, w), out_index) for w in widths],
        ),
        out_shape=[jax.ShapeDtypeStruct((n * rows, w), jnp.float32) for w in widths],
        compiler_params=pltpu.CompilerParams(vmem_limit_bytes=48 << 20),
        cost_estimate=work(1 + (n * rows * width >> 18)),
        name="assemble",
    )(me.reshape(1).astype(jnp.int32), *sources)


def rows_of(pieces):
    return jnp.concatenate(pieces, axis=0)


def body(tokens, doc_starts, cotangent, gain_attn, gain_ffn, w_query, w_key, w_value, w_out, w_gate, w_up, w_down):
    micro, _, rows, _ = tokens.shape
    parts = lax.axis_size("fsdp")
    chips = parts // 2
    core = lax.axis_index("fsdp") % 2
    seq = lax.axis_size("sp")
    place = lax.axis_index("sp")
    count = micro * rows
    d_own = w_query.shape[0]
    hidden_own = w_down.shape[0]
    hidden_chip = 2 * hidden_own
    bf16 = jnp.bfloat16
    f32 = jnp.float32

    gains = jnp.pad(jnp.stack([gain_attn, gain_ffn], axis=1), ((0, 0), (0, 126)))
    w_in = jnp.concatenate(
        [w_query, w_key[:, :KW], w_value[:, :KW], w_key[:, KW:], w_value[:, KW:], gains], axis=1
    )
    w_in = lax.all_gather(w_in, "fsdp", axis=0, tiled=True)
    w_out_full = lax.all_gather(w_out, "fsdp", axis=0, tiled=True)
    gain_one = w_in[:, D + 4 * KW].astype(f32)
    gain_two = w_in[:, D + 4 * KW + 1].astype(f32)
    reshard = Reshard(w_gate, w_up)
    came_columns = reshard.fetch()

    starts = doc_starts.reshape(micro, -1)
    offsets = (place - jnp.arange(seq, dtype=jnp.int32)) * rows
    key_places = (offsets[:, None] + jnp.arange(rows, dtype=jnp.int32)[None, :]).reshape(-1)
    docs, positions = stream_layout(starts, key_places)
    docs = docs.reshape(micro, seq, rows)
    key_places = key_places.reshape(seq, rows)
    tables = rope_lanes(positions.reshape(micro, seq, rows)[:, 0].reshape(count))
    allowed = (docs[:, :1, :, None] == docs[:, :, None, :]) & (
        key_places[None, :, None, :] <= key_places[None, :1, :, None]
    )
    bias = jnp.where(allowed, 0.0, -1e30).astype(f32)
    bias_t = jnp.where(jnp.swapaxes(allowed, 2, 3), 0.0, -1e30).astype(f32)

    inputs = tokens.reshape(count, D).astype(f32)
    scale_one = rms_scale(inputs)
    normed_x1 = inputs * scale_one
    normed = tie((normed_x1 * gain_one).astype(bf16), *tables, bias, bias_t)
    normed = tie(normed, *came_columns)
    w_down_other = partner(w_down)
    order = Order()
    qkv = order.did(project(normed, w_in, tables))

    g_low = cotangent.reshape(micro, rows, D)
    g_all = [gather_chips(tie(g_low[0], qkv))]
    state, n2_alls = [], []
    for m in range(micro):
        kv = [qkv[m * rows:(m + 1) * rows, D:]]
        for s in range(seq - 1):
            kv.append(lax.ppermute(kv[-1], "sp", right_pairs(seq, s)))
        context, lse = attend(order.at(qkv), kv, bias[m], m)
        lse_rows = jnp.swapaxes(lse.reshape(rows, HALVES, 128)[:, :, :QW // HEAD_DIM].reshape(rows, HEADS), 0, 1)
        mixed = inputs[m * rows:(m + 1) * rows] + nn(context, w_out_full)
        scale_two = rms_scale(mixed)
        normed_x2 = mixed * scale_two
        normed_ffn = order.did((normed_x2 * gain_two).astype(bf16))
        if m == 0:
            normed_ffn = tie(normed_ffn, g_all[0])
        n2_alls.append(gather_chips(normed_ffn))
        if m:
            g_all.append(gather_chips(tie(g_low[m], normed_ffn)))
        state.append((kv, context, lse_rows, mixed, scale_two, normed_x2))
    w_both = order.did(reshard.result(*order.last))
    w_down_chip = order.did(rows_of([order.at(w_down), w_down_other]))

    hiddens, gate_grads, up_grads, normed_grads, out_terms = [], [], [], [], []

    def forward_back(m):
        hidden, gate_grad, up_grad = feed_forward(order.at(n2_alls[m]), g_all[m], w_both, w_down_chip)
        hiddens.append(hidden)
        gate_grads.append(gate_grad)
        up_grads.append(order.did(up_grad))

    def normed_part(m, *before):
        part = order.did(sum_nt([order.at(gate_grads[m], *before), up_grads[m]], w_both))
        normed_grads.append(scatter_chips(part))

    def out_part(m, *before):
        part = order.did(plain_nn(order.at(hiddens[m], *before), w_down_chip))
        out_terms.append(scatter_chips(part))

    slab = d_own // seq
    ff = parts * hidden_own
    forward_back(0)
    normed_part(0, g_all[-1])
    for m in range(1, micro):
        forward_back(m)
    wide_other = order.did(sum_tn(n2_alls, [[order.at(gate_grads[0])] + gate_grads[1:], up_grads], 1))
    wide_came = partner(wide_other)
    down_other = order.did(sum_tn([order.at(hiddens[0])] + hiddens[1:], [g_all], 1, weight=10))
    down_came = partner(down_other)
    wide_grad = order.did(sum_tn(n2_alls, [[order.at(gate_grads[0])] + gate_grads[1:], up_grads], 0, wide_came))
    wide_blocks = wide_grad.reshape(parts, seq, slab, hidden_chip)
    wide = Scatter(lambda j: lax.dynamic_index_in_dim(wide_blocks, j, 1, keepdims=False))
    hops = wide.hop()
    order.last = order.last + (normed_grads[0],)
    down_grad = order.did(sum_tn([order.at(hiddens[0])] + hiddens[1:], [g_all], 0, down_came))
    down = Scatter(chunk_of(down_grad.reshape(seq, hidden_own // seq, D)))
    normed_part(1)
    out_part(0)
    order.last = order.last + hops
    hops = wide.hop() + down.hop()
    for m in range(1, micro):
        out_part(m)
    normed_mine, normed_other = features(order.at(normed), core, d_own)
    normed_chip = rows_of([normed_mine, partner(normed_other)])
    context_mine, context_other = features(rows_of([state[m][1] for m in range(micro)]), core, d_own)
    context_chip = rows_of([context_mine, partner(context_other)])
    order.did(normed_mine)

    mixed_grads, attn_grads, query_grads, kv_sums = [], [], [], []
    gain_two_term = 0.0
    chip_rows = lambda pieces: rows_of(pieces + [partner(p) for p in pieces])
    for m in range(micro):
        kv, context, lse_rows, mixed, scale_two, normed_x2 = state[m]
        normed_grad = order.at(normed_grads[m]).astype(f32)
        gain_two_term = gain_two_term + jnp.sum(normed_grad * normed_x2, axis=0)
        mixed_grad = norm_back(normed_grad, gain_two, normed_x2, scale_two, g_low[m].astype(f32))
        attn_grad = mixed_grad.astype(bf16)
        attn_grads.append(attn_grad)
        mixed_grads.append(mixed_grad)
        context_grad = order.did(nt(attn_grad, w_out_full).astype(bf16))
        if m == micro - 1:
            out_half = order.did(tn(context_chip, chip_rows(attn_grads)).astype(bf16))
            out_shard = scatter_chips(out_half)
        if m == 1:
            order.last = order.last + hops
            pair = exchange(wide.result())
            order.last = order.last + (pair,)
            pieces = exchange_chips(pair)
            hops = down.hop()
        args = (context, lse_rows, kv, bias_t[m], tables, m)
        first = attend_back(qkv, order.at(context_grad), *args, 0)
        order.last = hops
        if m == 0:
            hops = wide.hop() + down.hop()
        elif m == 1:
            wide_part = exchanged([order.at(pieces[0], *pieces[1:])] + pieces[1:])
            wide_part = jnp.moveaxis(wide_part.reshape(parts, slab, 2, hidden_own), 0, 2).reshape(slab, 2 * ff)
            wide_gather, down_gather = Gather(wide_part), Gather(down.result())
            hops = wide_gather.hop()
            order.last = (wide_part,)
        second = attend_back(qkv, order.at(context_grad), *args, 1, first)
        query_grads.append(order.did(second[0]))
        kv_sums.append(KeySum(second[1:]))
        kv_sums[-1].hop()

    order.last = order.last + tuple(out_terms) + (out_shard,) + hops
    hops = wide_gather.hop() + down_gather.hop()
    query_half = order.did(tn(normed_chip, chip_rows(query_grads[:-1] + [order.at(query_grads[-1])])).astype(bf16))
    query_shard = scatter_chips(query_half)
    kv_hop = tuple(keys.hop() for keys in kv_sums)
    normed_grad = order.did(nt(order.at(rows_of(query_grads), *kv_hop), w_in[:, :D]))
    kv_grads = [keys.result() for keys in kv_sums]
    order.last = order.last + hops
    kv_grads = [order.did(finish_keys(own, order.at(came), tables, m)) for m, (own, came) in enumerate(kv_grads)]
    hops = wide_gather.hop() + down_gather.hop()
    kv_grad = rows_of(kv_grads)
    kv_half = order.did(tn(normed_chip, chip_rows(kv_grads)).astype(bf16))
    normed_grad = normed_grad + nt(kv_grad, w_in[:, D:D + 4 * KW])
    gain_one_term = jnp.sum(normed_grad * normed_x1, axis=0)
    input_grad = norm_back(normed_grad, gain_one, normed_x1, scale_one, rows_of(mixed_grads)).astype(bf16)

    gain_blocks = jnp.stack([gain_one_term, gain_two_term], axis=1).astype(bf16).reshape(chips, 2, d_own, 2)
    gain_lanes = jnp.concatenate(
        [lax.dynamic_index_in_dim(gain_blocks, c, 1, keepdims=False) for c in (core, 1 - core)], axis=2
    ).reshape(chips * d_own, 4)
    kv_shard = scatter_chips(tie(jnp.concatenate([kv_half, jnp.pad(gain_lanes, ((0, 0), (0, 124)))], axis=1), query_shard))
    out_total, query_total, kv_total = (
        x.astype(f32) for x in lax.psum((tie(out_shard, kv_shard), tie(query_shard, kv_shard), kv_shard), "sp")
    )
    kv_piece = lambda k: kv_total[:, k * KW:(k + 1) * KW]
    gain_lanes = kv_total[:, 4 * KW:4 * KW + 4]
    gain_total = gain_lanes[:, :2] + partner(gain_lanes)[:, 2:]
    order.last = order.last + hops
    down_slots = down_gather.result()
    wide_gather.hop()
    (down_total,) = assemble([(order.at(down_slots[0][0]), None)] + down_slots[1:], [[(0, D)]])
    gate_total, up_total = assemble(wide_gather.result(), [[(0, ff)], [(ff, ff)]])
    outputs = [(state[m][3] + order.at(out_terms[m]).astype(f32)).astype(bf16) for m in range(micro)]
    return (
        rows_of(outputs).reshape(tokens.shape),
        input_grad.reshape(tokens.shape),
        gain_total[:, 0],
        gain_total[:, 1],
        query_total,
        jnp.concatenate([kv_piece(0), kv_piece(2)], axis=1),
        jnp.concatenate([kv_piece(1), kv_piece(3)], axis=1),
        out_total,
        gate_total,
        up_total,
        down_total,
    )


def solution(mesh):
    split = P("fsdp", None)
    stream = P(None, "fsdp", "sp", None)
    return jax.shard_map(
        body,
        mesh=mesh,
        in_specs=(stream, P(None, "fsdp", None), stream, P("fsdp"), P("fsdp")) + (split,) * 7,
        out_specs=(stream, stream, P("fsdp"), P("fsdp")) + (split,) * 7,
        check_vma=False,
    )
```

time: 1990 us -> 1620 us (0.81)
  Pallas kernels: 190 us -> 497 us
  waiting for transfers between devices: 908 us -> 603 us
  matrix products: 349 us -> 87.3 us
  local copies, waits for them, and re-layouts: 141 us -> 84 us
  other arithmetic: 125 us -> 94.5 us
    pallas_call x2 -> x23, Pallas kernels: 105 us -> 424 us  [the longest x4 108 us: attend_back(): pl.pallas_call(functools.partial(backward_kernel, blocks, len(before)), g...]
    reduce_scatter x6, waiting for transfers between devices: 172 us -> 0.02 us  [scatter_chips(): lax.psum_scatter(x, 'fsdp', scatter_dimension=0, tiled=True, axis_index_g...]
    ppermute x68 -> x60, waiting for transfers between devices: 477 us -> 328 us  [the longest x6 184 us: hop(): lax.ppermute(self.lefts[-1], 'sp', [(n - 1 - k, n - 2 - k) for k in range...]
    dot_general x6 -> x2, matrix products: 107 us -> 16.5 us  [nn(): return jnp.dot(left, right, preferred_element_type=jnp.float32)]
    dot_general x7 -> x4, matrix products: 131 us -> 43.3 us  [nt(): lax.dot_general(left, right, (((1,), (1,)), ((), ())), preferred_element_...]
    dot_general x6 -> x3, matrix products: 112 us -> 27.5 us  [tn(): lax.dot_general(left, right, (((0,), (0,)), ((), ())), preferred_element_...]
    psum x0 -> x1, waiting for transfers between devices: none -> 43.4 us  [body(): lax.psum((tie(out_shard, kv_shard), tie(query_shard, kv_shard), kv_shard)...]
    unnamed x12 -> x15, waiting for transfers between devices: 1.56 us -> 41.6 us
  transfers between devices with their start and end apart: 86 -> 80, of which waited for: 37 -> 28; matrix products, arithmetic and copies ran while one was open for 24% -> 13% of each run, Pallas kernels for 10% -> 28%
where the time goes in v2:
time: 1620 us; the launch traced here: 1610 us
  waiting for transfers between devices  603 us (37%)
  Pallas kernels  497 us (31%)
  starting transfers between devices  228 us (14%)
  other arithmetic  94.5 us (6%)
  matrix products  87.3 us (5%)
  local copies, waits for them, and re-layouts  84 us (5%)
    ppermute x6, waiting for transfers between devices, hop(): lax.ppermute(self.lefts[-1], 'sp', [(n - 1 - k, n - 2 - k) for k in range...  184 us
    pallas_call x4, Pallas kernels, attend_back(): pl.pallas_call(functools.partial(backward_kernel, blocks, len(before)), g...  108 us
    ppermute x6, starting transfers between devices, hop(): lax.ppermute(to_right, 'sp', [(k, k + 1) for k in range(s + 1)])  99.7 us
    all_gather x4, waiting for transfers between devices, gather_chips(): lax.all_gather(x, 'fsdp', axis=0, tiled=True, axis_index_groups=same_core())  92.7 us
    pallas_call x4, Pallas kernels, sum_tn(): pl.pallas_call(functools.partial(sum_tn_kernel, segments, pairs), grid=(D...  90.6 us
    pallas_call x2, Pallas kernels, feed_forward(): pl.pallas_call(ffn_kernel, grid=(tiles,), in_specs=[full, full, pl.BlockS...  73.7 us
    ppermute x6, waiting for transfers between devices, hop(): lax.ppermute(to_right, 'sp', [(k, k + 1) for k in range(s + 1)])  69 us
    all_gather x1, waiting for transfers between devices, body(): w_in = lax.all_gather(w_in, 'fsdp', axis=0, tiled=True)  69 us
  transfers between devices with their start and end apart: 80, of which 28 were waited for; matrix products, arithmetic and copies ran while one was open for 13% of the time, Pallas kernels for 28%

profile of v2, /device:TPU:1, one launch (start us, length us, event | category | flops | bytes accessed | tf_op | source)
XLA Modules:
  0.0 1609.7 jit_solution(1773095596284436732)
XLA Ops:
  30.4 5.8 fusion.48
  41.5 20.4 %collective-permute-done.refs_2_ = bf16[320,1792]{1,0:T(8,128)(2,1)} collective-permute-done((bf16[320,1792]{1,0:T(8,128)(2,1)}, bf16[320,1792]{1,0:T(8,128)(2,1)}, u32[]{:S(2)}, u32[]{:S(2)}) %collective-permute-start) | collective-permute-done | bytes 1146912 | tf_op jit(solution)/shard_map/ppermute | solution.py:399
  63.1 15.5 collective-permute-done.2.refs_4_
  78.6 19.2 %collective-permute-done.4.refs_6_ = bf16[320,1792]{1,0:T(8,128)(2,1)} collective-permute-done((bf16[320,1792]{1,0:T(8,128)(2,1)}, bf16[320,1792]{1,0:T(8,128)(2,1)}, u32[]{:S(2)}, u32[]{:S(2)}) %collective-permute-start.4) | collective-permute-done | bytes 1146912 | tf_op jit(solution)/shard_map/ppermute | solution.py:399
  99.1 69.0 %all-gather.7.cloned.1.call-done.w_ref = bf16[2560,3968]{1,0:T(8,128)(2,1)} async-done(((bf16[320,3968]{1,0:T(8,128)(2,1)}), bf16[2560,3968]{1,0:T(8,128)(2,1)}) %all-gather.7.cloned.1.call-update) | async-done | bytes 20316176 | tf_op jit(solution)/shard_map/all_gather | solution.py:719
  174.3 19.3 %project.1.q_ref = bf16[512,3840]{1,0:T(8,128)(2,1)} custom-call(bf16[512,2560]{1,0:T(8,128)(2,1)} %multiply_convert_fusion.n_ref.x_ref, bf16[2560,3968]{1,0:T(8,128)(2,1)} %all-gather.7.cloned.1.call-done.w_ref, f32[512,640]{1,0:T(8,128)S(1)} %copy-done.2, f32[512,640]{1,0:T(8,128)S(1)} %get-tuple-element.270.up_ref.refs_6_, ...), custom_call_target="tpu_custom_call" | custom-call | flops 5100273664 | bytes 65536 | tf_op jit(solution)/shard_map/project/pallas_call | solution.py:61
  198.3 13.9 collective-permute-done.6.refs_1_
  213.8 4.8 convert_element_type.185
  218.9 23.0 %attend.2 = (bf16[256,2560]{1,0:T(8,128)(2,1)S(1)}, f32[256,256]{1,0:T(8,128)S(1)}) custom-call(bf16[512,3840]{1,0:T(8,128)(2,1)} %project.1.q_ref, bf16[256,1280]{1,0:T(8,128)(2,1)S(1)} %get-tuple-element.244.refs_0_, bf16[256,1280]{1,0:T(8,128)(2,1)S(1)} %collective-permute-done.6.refs_1_, bf16[256,1280]{1,0:T(8,128)(2,1)S(1)} %collective-permute-done.7.refs_2_, ...), custom_call_target="tpu_custom_call" | custom-call | flops 6174015488 | bytes 65536 | tf_op jit(solution)/shard_map/attend/pallas_call | solution.py:97
  244.4 9.1 multiply_reduce_fusion.4
  256.3 51.5 %all-gather.11.cloned.1.call-done.g_ref.refs_2_ = bf16[1024,2560]{1,0:T(8,128)(2,1)} async-done(((bf16[256,2560]{1,0:T(8,128)(2,1)}), bf16[1024,2560]{1,0:T(8,128)(2,1)}) %all-gather.11.cloned.1.call-update) | async-done | bytes 5242896 | tf_op jit(solution)/shard_map/all_gather | solution.py:265
  311.2 13.3 collective-permute-done.9.refs_1_
  326.0 23.8 %attend.3 = (bf16[256,2560]{1,0:T(8,128)(2,1)S(1)}, f32[256,256]{1,0:T(8,128)S(1)}) custom-call(bf16[512,3840]{1,0:T(8,128)(2,1)} %project.1.q_ref, bf16[256,1280]{1,0:T(8,128)(2,1)S(1)} %get-tuple-element.243.refs_0_, bf16[256,1280]{1,0:T(8,128)(2,1)S(1)} %collective-permute-done.9.refs_1_, bf16[256,1280]{1,0:T(8,128)(2,1)S(1)} %collective-permute-done.10.refs_2_, ...), custom_call_target="tpu_custom_call" | custom-call | flops 6174015488 | bytes 65536 | tf_op jit(solution)/shard_map/attend/pallas_call | solution.py:97
  350.0 7.4 multiply_reduce_fusion.3
  363.1 4.7 columns_for.7
  372.6 4.8 collective-permute-done.13.refs_9_
  384.3 21.9 %weave.1.wg_ref.wu_ref.refs_2_.refs_3_ = bf16[2560,3584]{1,0:T(8,128)(2,1)} custom-call(s32[9]{0:T(128)} %stack.118.place_ref, bf16[320,1792]{1,0:T(8,128)(2,1)} %copy-done.49, bf16[320,1792]{1,0:T(8,128)(2,1)} %copy-done.48, bf16[320,1792]{1,0:T(8,128)(2,1)} %collective-permute-done.refs_2_, bf16[320,1792]{1,0:T(8,128)(2,1)} %collective-permute-done.1.refs_3_, ...), custom_call_target="tpu_custom_call" | custom-call | flops 5637144576 | bytes 65536 | tf_op jit(solution)/shard_map/weave/pallas_call | solution.py:368
  406.2 4.7 constant_dynamic-update-slice_fusion.1
  411.0 4.7 constant_dynamic-update-slice_fusion.wd_ref.b_ref
  415.7 36.7 %feed_forward.2 = (bf16[1024,1792]{1,0:T(8,128)(2,1)}, bf16[1024,1792]{1,0:T(8,128)(2,1)}, bf16[1024,1792]{1,0:T(8,128)(2,1)}) custom-call(bf16[1024,2560]{1,0:T(8,128)(2,1)} %all-gather.13.cloned.1.call-done.n_ref.refs_0_, bf16[1024,2560]{1,0:T(8,128)(2,1)} %all-gather.11.cloned.1.call-done.g_ref.refs_2_, ...), custom_call_target="tpu_custom_call" | custom-call | flops 9663676416 | bytes 65536 | tf_op jit(solution)/shard_map/feed_forward/pallas_call | solution.py:509
  456.5 26.5 %sum_nt.2 = bf16[1024,2560]{1,0:T(8,128)(2,1)} custom-call(bf16[1024,1792]{1,0:T(8,128)(2,1)} %get-tuple-element.106.refs_0_.refs_2_, bf16[1024,1792]{1,0:T(8,128)(2,1)} %get-tuple-element.97.refs_1_.refs_4_, bf16[2560,3584]{1,0:T(8,128)(2,1)} %weave.1.wg_ref.wu_ref.refs_2_.refs_3_, bf16[2560,3584]{1,0:T(8,128)(2,1)} %weave.1.wg_ref.wu_ref.refs_2_.refs_3_), custom_call_target="tpu_custom_call" | custom-call | flops 6979321856 | bytes 65536 | tf_op jit(solution)/shard_map/sum_nt/pallas_call | solution.py:530
  483.1 37.1 %all-gather.15.cloned.1.call-done.n_ref.refs_1_ = bf16[1024,2560]{1,0:T(8,128)(2,1)} async-done(((bf16[256,2560]{1,0:T(8,128)(2,1)}), bf16[1024,2560]{1,0:T(8,128)(2,1)}) %all-gather.15.cloned.1.call-update) | async-done | bytes 5242896 | tf_op jit(solution)/shard_map/all_gather | solution.py:265
  520.2 37.0 %feed_forward.3 = (bf16[1024,1792]{1,0:T(8,128)(2,1)}, bf16[1024,1792]{1,0:T(8,128)(2,1)}, bf16[1024,1792]{1,0:T(8,128)(2,1)}) custom-call(bf16[1024,2560]{1,0:T(8,128)(2,1)} %all-gather.15.cloned.1.call-done.n_ref.refs_1_, bf16[1024,2560]{1,0:T(8,128)(2,1)} %all-gather.17.cloned.1.call-done.g_ref.refs_3_, ...), custom_call_target="tpu_custom_call" | custom-call | flops 9663676416 | bytes 65536 | tf_op jit(solution)/shard_map/feed_forward/pallas_call | solution.py:509
  557.2 27.9 %sum_tn.4 = bf16[2560,1792]{1,0:T(8,128)(2,1)} custom-call(bf16[1024,2560]{1,0:T(8,128)(2,1)} %all-gather.13.cloned.1.call-done.n_ref.refs_0_, bf16[1024,2560]{1,0:T(8,128)(2,1)} %all-gather.15.cloned.1.call-done.n_ref.refs_1_, bf16[1024,1792]{1,0:T(8,128)(2,1)} %get-tuple-element.106.refs_0_.refs_2_, bf16[1024,1792]{1,0:T(8,128)(2,1)} %get-tuple-element.108.refs_3_.refs_0_, ...), custom_call_target="tpu_custom_call" | custom-call | flops 6979321856 | bytes 65536 | tf_op jit(solution)/shard_map/sum_tn/pallas_call | solution.py:480
  585.8 16.2 %sum_tn.5 = bf16[896,2560]{1,0:T(8,128)(2,1)} custom-call(bf16[1024,1792]{1,0:T(8,128)(2,1)} %get-tuple-element.109.refs_0_.a_ref, bf16[1024,1792]{1,0:T(8,128)(2,1)} %get-tuple-element.110.refs_1_.a_ref, bf16[1024,2560]{1,0:T(8,128)(2,1)} %all-gather.11.cloned.1.call-done.g_ref.refs_2_, bf16[1024,2560]{1,0:T(8,128)(2,1)} %all-gather.17.cloned.1.call-done.g_ref.refs_3_), custom_call_target="tpu_custom_call" | custom-call | flops 42949672960 | bytes 65536 | tf_op jit(solution)/shard_map/sum_tn/pallas_call | solution.py:480
  602.0 29.5 %sum_tn.6 = bf16[2560,1792]{1,0:T(8,128)(2,1)} custom-call(bf16[1024,2560]{1,0:T(8,128)(2,1)} %all-gather.13.cloned.1.call-done.n_ref.refs_0_, bf16[1024,2560]{1,0:T(8,128)(2,1)} %all-gather.15.cloned.1.call-done.n_ref.refs_1_, bf16[1024,1792]{1,0:T(8,128)(2,1)} %get-tuple-element.106.refs_0_.refs_2_, bf16[1024,1792]{1,0:T(8,128)(2,1)} %get-tuple-element.108.refs_3_.refs_0_, ...), custom_call_target="tpu_custom_call" | custom-call | flops 6979321856 | bytes 65536 | tf_op jit(solution)/shard_map/sum_tn/pallas_call | solution.py:480
  631.5 17.0 %sum_tn.7 = bf16[896,2560]{1,0:T(8,128)(2,1)} custom-call(bf16[1024,1792]{1,0:T(8,128)(2,1)} %get-tuple-element.109.refs_0_.a_ref, bf16[1024,1792]{1,0:T(8,128)(2,1)} %get-tuple-element.110.refs_1_.a_ref, bf16[1024,2560]{1,0:T(8,128)(2,1)} %all-gather.11.cloned.1.call-done.g_ref.refs_2_, bf16[1024,2560]{1,0:T(8,128)(2,1)} %all-gather.17.cloned.1.call-done.g_ref.refs_3_, ...), custom_call_target="tpu_custom_call" | custom-call | flops 4294967296 | bytes 65536 | tf_op jit(solution)/shard_map/sum_tn/pallas_call | solution.py:480
  648.5 25.9 %sum_nt.3 = bf16[1024,2560]{1,0:T(8,128)(2,1)} custom-call(bf16[1024,1792]{1,0:T(8,128)(2,1)} %get-tuple-element.108.refs_3_.refs_0_, bf16[1024,1792]{1,0:T(8,128)(2,1)} %get-tuple-element.102.refs_5_.refs_1_, bf16[2560,3584]{1,0:T(8,128)(2,1)} %weave.1.wg_ref.wu_ref.refs_2_.refs_3_, bf16[2560,3584]{1,0:T(8,128)(2,1)} %weave.1.wg_ref.wu_ref.refs_2_.refs_3_), custom_call_target="tpu_custom_call" | custom-call | flops 6979321856 | bytes 65536 | tf_op jit(solution)/shard_map/sum_nt/pallas_call | solution.py:530
  674.5 16.0 plain_nn.2
  690.7 5.1 dynamic-slice_bitcast_fusion
  695.8 4.8 collective-permute-start.23
  718.8 29.3 %collective-permute-done.23 = bf16[8,80,1792]{2,1,0:T(8,128)(2,1)} collective-permute-done((bf16[8,80,1792]{2,1,0:T(8,128)(2,1)}, bf16[8,80,1792]{2,1,0:T(8,128)(2,1)}, u32[]{:S(2)}, u32[]{:S(2)}) %collective-permute-start.23) | collective-permute-done | bytes 2293792 | tf_op jit(solution)/shard_map/ppermute | solution.py:576
  748.1 15.9 plain_nn.3
  773.3 10.0 convolution_convert_fusion.4.dctx_ref
  783.4 5.1 bitcast_add_fusion.2
  794.0 27.0 %attend_back.4 = (bf16[256,2560]{1,0:T(8,128)(2,1)}, bf16[256,1280]{1,0:T(8,128)(2,1)S(1)}, bf16[256,1280]{1,0:T(8,128)(2,1)S(1)}, bf16[256,1280]{1,0:T(8,128)(2,1)S(1)}, bf16[256,1280]{1,0:T(8,128)(2,1)S(1)}) custom-call(bf16[512,3840]{1,0:T(8,128)(2,1)} %project.1.q_ref, bf16[256,2560]{1,0:T(8,128)(2,1)} %convolution_convert_fusion.4.dctx_ref, ...), custom_call_target="tpu_custom_call" | custom-call | flops 26843545600 | bytes 65536 | tf_op jit(solution)/shard_map/attend_back/pallas_call | solution.py:160
  824.0 15.7 collective-permute-done.26
  841.9 27.2 %attend_back.5 = (bf16[256,2560]{1,0:T(8,128)(2,1)}, bf16[256,1280]{1,0:T(8,128)(2,1)S(1)}, bf16[256,1280]{1,0:T(8,128)(2,1)S(1)}, bf16[256,1280]{1,0:T(8,128)(2,1)S(1)}, bf16[256,1280]{1,0:T(8,128)(2,1)S(1)}) custom-call(bf16[512,3840]{1,0:T(8,128)(2,1)} %project.1.q_ref, ...), custom_call_target="tpu_custom_call", output_to_operand_aliasing={{0}: (12, {}), {1}: (13, {}), {2}: (14, {}), {3}: (15, {}),... | custom-call | flops 26843545600 | bytes 65536 | tf_op jit(solution)/shard_map/attend_back/pallas_call | solution.py:160
  885.4 11.3 convolution_convert_fusion.1
  898.4 5.6 bitcast_add_fusion.1
  904.0 8.8 collective-permute-start.33
  923.0 74.3 %collective-permute-start.36 = (bf16[224,2560]{1,0:T(8,128)(2,1)}, bf16[224,2560]{1,0:T(8,128)(2,1)}, u32[]{:S(2)}, u32[]{:S(2)}) collective-permute-start(bf16[224,2560]{1,0:T(8,128)(2,1)} %get-tuple-element.240), channel_id=1, source_target_pairs={{0,1},{1,2},{4,5},{5,6},{8,9},{9,10},{12,13},{13,14},{16,17},{17,1... | collective-permute-start | bytes 3440648 | tf_op jit(solution)/shard_map/ppermute | solution.py:576
  1007.0 12.9 collective-permute-done.36
  1022.6 5.1 collective-permute-start.37
  1038.3 11.1 collective-permute-done.37
  1052.5 5.1 collective-permute-done.42
  1070.1 9.8 convolution_convert_fusion.3.dctx_ref
  1079.9 26.8 %attend_back.6 = (bf16[256,2560]{1,0:T(8,128)(2,1)}, bf16[256,1280]{1,0:T(8,128)(2,1)S(1)}, bf16[256,1280]{1,0:T(8,128)(2,1)S(1)}, bf16[256,1280]{1,0:T(8,128)(2,1)S(1)}, bf16[256,1280]{1,0:T(8,128)(2,1)S(1)}) custom-call(bf16[512,3840]{1,0:T(8,128)(2,1)} %project.1.q_ref, bf16[256,2560]{1,0:T(8,128)(2,1)} %convolution_convert_fusion.3.dctx_ref, ...), custom_call_target="tpu_custom_call" | custom-call | flops 26843545600 | bytes 65536 | tf_op jit(solution)/shard_map/attend_back/pallas_call | solution.py:160
  1106.7 27.2 %attend_back.7 = (bf16[256,2560]{1,0:T(8,128)(2,1)}, bf16[256,1280]{1,0:T(8,128)(2,1)S(1)}, bf16[256,1280]{1,0:T(8,128)(2,1)S(1)}, bf16[256,1280]{1,0:T(8,128)(2,1)S(1)}, bf16[256,1280]{1,0:T(8,128)(2,1)S(1)}) custom-call(bf16[512,3840]{1,0:T(8,128)(2,1)} %project.1.q_ref, ...), custom_call_target="tpu_custom_call", output_to_operand_aliasing={{0}: (12, {}), {1}: (13, {}), {2}: (14, {}), {3}: (15, {}),... | custom-call | flops 26843545600 | bytes 65536 | tf_op jit(solution)/shard_map/attend_back/pallas_call | solution.py:160
  1146.1 10.1 convolution_convert_fusion
  1167.1 37.0 %collective-permute-start.54 = (bf16[224,2560]{1,0:T(8,128)(2,1)S(1)}, bf16[224,2560]{1,0:T(8,128)(2,1)}, u32[]{:S(2)}, u32[]{:S(2)}) collective-permute-start(bf16[224,2560]{1,0:T(8,128)(2,1)S(1)} %fusion.47.refs_0_), channel_id=1, source_target_pairs={{0,1},{1,2},{2,3},{4,5},{5,6},{6,7},{8,9},{9,10},{10,11},{12,13},{... | collective-permute-start | bytes 3440648 | tf_op jit(solution)/shard_map/ppermute | solution.py:621
  1214.2 11.6 fusion
  1226.3 68.0 %collective-permute-done.55.refs_6_ = bf16[224,2560]{1,0:T(8,128)(2,1)S(1)} collective-permute-done((bf16[224,2560]{1,0:T(8,128)(2,1)S(1)}, bf16[224,2560]{1,0:T(8,128)(2,1)S(1)}, u32[]{:S(2)}, u32[]{:S(2)}) %collective-permute-start.55) | collective-permute-done | bytes 1146912 | tf_op jit(solution)/shard_map/ppermute | solution.py:622
  1298.6 8.9 collective-permute-start.57
  1316.4 11.9 multiply_reduce_fusion
  1328.8 6.1 convolution_convert_fusion.2
  1336.9 6.0 copy.75
  1349.4 40.2 %reduce-scatter.22.cloned.1.call-done = bf16[320,1408]{1,0:T(8,128)(2,1)} async-done(((bf16[1280,1408]{1,0:T(8,128)(2,1)}), bf16[320,1408]{1,0:T(8,128)(2,1)}) %reduce-scatter.22.cloned.1.call-update) | async-done | bytes 901136
  1391.9 89.6 %collective-permute-done.62.refs_4_ = bf16[224,2560]{1,0:T(8,128)(2,1)} collective-permute-done((bf16[224,2560]{1,0:T(8,128)(2,1)}, bf16[224,2560]{1,0:T(8,128)(2,1)}, u32[]{:S(2)}, u32[]{:S(2)}) %collective-permute-start.62) | collective-permute-done | bytes 1146912 | tf_op jit(solution)/shard_map/ppermute | solution.py:622
  1484.8 16.7 %assemble.2 = (f32[320,7168]{1,0:T(8,128)}, f32[320,7168]{1,0:T(8,128)}) custom-call(s32[1]{0:T(128)} %bitcast.59.place_ref, bf16[80,14336]{1,0:T(8,128)(2,1)S(1)} %bitcast.138, bf16[80,14336]{1,0:T(8,128)(2,1)} %collective-permute-done.46.refs_1_, bf16[80,14336]{1,0:T(8,128)(2,1)} %collective-permute-done.60.refs_2_, ...), custom_call_target="tpu_custom_call" | custom-call | flops 4831838208 | bytes 65536 | tf_op jit(solution)/shard_map/assemble/pallas_call | solution.py:682
  1501.5 6.2 fusion.18
  1507.8 26.1 %collective-permute-done.64.refs_2_ = bf16[224,2560]{1,0:T(8,128)(2,1)S(1)} collective-permute-done((bf16[224,2560]{1,0:T(8,128)(2,1)}, bf16[224,2560]{1,0:T(8,128)(2,1)S(1)}, u32[]{:S(2)}, u32[]{:S(2)}) %collective-permute-start.64) | collective-permute-done | bytes 1146912 | tf_op jit(solution)/shard_map/ppermute | solution.py:622
  1533.8 8.1 assemble.3
  1546.0 43.4 %all-reduce.5.cloned.1.call-done = (bf16[320,1408]{0,1:T(8,128)(2,1)}, bf16[320,2560]{1,0:T(8,128)(2,1)}, bf16[320,2560]{1,0:T(8,128)(2,1)}) async-done(((bf16[320,1408]{0,1:T(8,128)(2,1)}, bf16[320,2560]{1,0:T(8,128)(2,1)}, bf16[320,2560]{1,0:T(8,128)(2,1)}), (bf16[320,1408]{0,1:T(8,128)(2,1)}, bf16[320,2560]{1,0:T(8,128)(2,1)}, bf16[320,2560]{1,0:T(8,128)(2,1)})) %all-reduce.5.cloned.1.call-update) | async-done | bytes 4177936 | tf_op jit(solution)/shard_map/psum | solution.py:874
  (442 shorter events, 259.3 us)
Async XLA Ops:
  7.2 160.9 %all-gather.7.cloned.1.call-start = ((), (), s32[]{:S(2)}) async-start(), calls=%async_computation.7 | async-start | bytes 22855680 | tf_op jit(solution)/shard_map/all_gather | solution.py:719
  13.4 231.0 %all-gather.9.cloned.1.call-start = ((), (), s32[]{:S(2)}) async-start(), calls=%async_computation.8 | async-start | bytes 14745600 | tf_op jit(solution)/shard_map/all_gather | solution.py:720
  14.1 293.7 %all-gather.11.cloned.1.call-start = ((), (), s32[]{:S(2)}) async-start(), calls=%async_computation.9 | async-start | bytes 6553600 | tf_op jit(solution)/shard_map/all_gather | solution.py:265
  17.8 44.2 %collective-permute-start = (bf16[320,1792]{1,0:T(8,128)(2,1)}, bf16[320,1792]{1,0:T(8,128)(2,1)}, u32[]{:S(2)}, u32[]{:S(2)}) collective-permute-start(bf16[320,1792]{1,0:T(8,128)(2,1)} %columns_for.4), channel_id=1, source_target_pairs={{0,8},{4,12},{8,0},{12,4},{16,24},{20,28},{24,16},{28,20},{1,9},{5... | collective-permute-start | bytes 3440648 | tf_op jit(solution)/shard_map/ppermute | solution.py:399
  23.5 55.2 %collective-permute-start.2 = (bf16[320,1792]{1,0:T(8,128)(2,1)}, bf16[320,1792]{1,0:T(8,128)(2,1)}, u32[]{:S(2)}, u32[]{:S(2)}) collective-permute-start(bf16[320,1792]{1,0:T(8,128)(2,1)} %columns_for.5), channel_id=1, source_target_pairs={{0,16},{4,20},{8,24},{12,28},{16,0},{20,4},{24,8},{28,12},{1,17},{... | collective-permute-start | bytes 3440648 | tf_op jit(solution)/shard_map/ppermute | solution.py:399
  28.8 69.0 %collective-permute-start.4 = (bf16[320,1792]{1,0:T(8,128)(2,1)}, bf16[320,1792]{1,0:T(8,128)(2,1)}, u32[]{:S(2)}, u32[]{:S(2)}) collective-permute-start(bf16[320,1792]{1,0:T(8,128)(2,1)} %columns_for.6), channel_id=1, source_target_pairs={{0,24},{4,28},{8,16},{12,20},{16,8},{20,12},{24,0},{28,4},{1,25},{... | collective-permute-start | bytes 3440648 | tf_op jit(solution)/shard_map/ppermute | solution.py:399
  61.9 112.3 %collective-permute-start.1 = (bf16[320,1792]{1,0:T(8,128)(2,1)}, bf16[320,1792]{1,0:T(8,128)(2,1)}, u32[]{:S(2)}, u32[]{:S(2)}) collective-permute-start(bf16[320,1792]{1,0:T(8,128)(2,1)} %collective-permute-done.refs_2_), channel_id=1, source_target_pairs={{0,1},{1,0},{2,3},{3,2},{4,5},{5,4},{6,7},{7,6},{8,9},{9,8},{10,11... | collective-permute-start | bytes 3440648 | tf_op jit(solution)/shard_map/ppermute | solution.py:402
  78.6 95.6 %collective-permute-start.3 = (bf16[320,1792]{1,0:T(8,128)(2,1)}, bf16[320,1792]{1,0:T(8,128)(2,1)}, u32[]{:S(2)}, u32[]{:S(2)}) collective-permute-start(bf16[320,1792]{1,0:T(8,128)(2,1)} %collective-permute-done.2.refs_4_), channel_id=1, source_target_pairs={{0,1},{1,0},{2,3},{3,2},{4,5},{5,4},{6,7},{7,6},{8,9},{9,8},{10,11... | collective-permute-start | bytes 3440648 | tf_op jit(solution)/shard_map/ppermute | solution.py:402
  97.8 76.4 %collective-permute-start.5 = (bf16[320,1792]{1,0:T(8,128)(2,1)}, bf16[320,1792]{1,0:T(8,128)(2,1)}, u32[]{:S(2)}, u32[]{:S(2)}) collective-permute-start(bf16[320,1792]{1,0:T(8,128)(2,1)} %collective-permute-done.4.refs_6_), channel_id=1, source_target_pairs={{0,1},{1,0},{2,3},{3,2},{4,5},{5,4},{6,7},{7,6},{8,9},{9,8},{10,11... | collective-permute-start | bytes 3440648 | tf_op jit(solution)/shard_map/ppermute | solution.py:402
  193.6 222.1 %all-gather.13.cloned.1.call-start = ((), (), s32[]{:S(2)}) async-start(), calls=%async_computation.10 | async-start | bytes 6553600 | tf_op jit(solution)/shard_map/all_gather | solution.py:265
  195.0 17.2 %collective-permute-start.6 = (bf16[256,1280]{1,0:T(8,128)(2,1)S(1)}, bf16[256,1280]{1,0:T(8,128)(2,1)S(1)}, u32[]{:S(2)}, u32[]{:S(2)}) collective-permute-start(bf16[256,1280]{1,0:T(8,128)(2,1)S(1)} %get-tuple-element.244.refs_0_), channel_id=1, source_target_pairs={{0,1},{1,2},{2,3},{4,5},{5,6},{6,7},{8,9},{9,10},{10,11},{12,13},{... | collective-permute-start | bytes 1966088 | tf_op jit(solution)/shard_map/ppermute | solution.py:754
  307.9 148.6 %all-gather.17.cloned.1.call-start = ((), (), s32[]{:S(2)}) async-start(), calls=%async_computation.12 | async-start | bytes 6553600 | tf_op jit(solution)/shard_map/all_gather | solution.py:265
  307.9 16.6 %collective-permute-start.9 = (bf16[256,1280]{1,0:T(8,128)(2,1)S(1)}, bf16[256,1280]{1,0:T(8,128)(2,1)S(1)}, u32[]{:S(2)}, u32[]{:S(2)}) collective-permute-start(bf16[256,1280]{1,0:T(8,128)(2,1)S(1)} %get-tuple-element.243.refs_0_), channel_id=1, source_target_pairs={{0,1},{1,2},{2,3},{4,5},{5,6},{6,7},{8,9},{9,10},{10,11},{12,13},{... | collective-permute-start | bytes 1966088 | tf_op jit(solution)/shard_map/ppermute | solution.py:754
  360.2 160.0 %all-gather.15.cloned.1.call-start = ((), (), s32[]{:S(2)}) async-start(), calls=%async_computation.11 | async-start | bytes 6553600 | tf_op jit(solution)/shard_map/all_gather | solution.py:265
  360.8 270.7 %reduce-scatter.10.cloned.1.call-start = ((), (), s32[]{:S(2)}) async-start(), calls=%async_computation.13 | async-start | bytes 6553600 | tf_op jit(solution)/shard_map/reduce_scatter | solution.py:269
  360.9 50.1 %collective-permute-start.20 = (bf16[896,2560]{1,0:T(8,128)(2,1)}, bf16[896,2560]{1,0:T(8,128)(2,1)}, u32[]{:S(2)}, u32[]{:S(2)}) collective-permute-start(bf16[896,2560]{1,0:T(8,128)(2,1)} %param.23), channel_id=1, source_target_pairs={{0,4},{4,0},{8,12},{12,8},{16,20},{20,16},{24,28},{28,24},{1,5},{5... | collective-permute-start | bytes 13762568 | tf_op jit(solution)/shard_map/ppermute | solution.py:256
  370.2 8.2 collective-permute-start.14
  370.3 9.4 collective-permute-start.16
  483.0 388.6 %reduce-scatter.14.cloned.1.call-start = ((), (), s32[]{:S(2)}) async-start(), calls=%async_computation.15 | async-start | bytes 6553600 | tf_op jit(solution)/shard_map/reduce_scatter | solution.py:269
  585.1 16.9 %collective-permute-start.21 = (bf16[2560,1792]{1,0:T(8,128)(2,1)}, bf16[2560,1792]{1,0:T(8,128)(2,1)}, u32[]{:S(2)}, u32[]{:S(2)}) collective-permute-start(bf16[2560,1792]{1,0:T(8,128)(2,1)} %sum_tn.4), channel_id=1, source_target_pairs={{0,4},{4,0},{8,12},{12,8},{16,20},{20,16},{24,28},{28,24},{1,5},{5... | collective-permute-start | bytes 27525128 | tf_op jit(solution)/shard_map/ppermute | solution.py:256
  602.0 29.5 %collective-permute-start.22 = (bf16[896,2560]{1,0:T(8,128)(2,1)}, bf16[896,2560]{1,0:T(8,128)(2,1)}, u32[]{:S(2)}, u32[]{:S(2)}) collective-permute-start(bf16[896,2560]{1,0:T(8,128)(2,1)} %sum_tn.5), channel_id=1, source_target_pairs={{0,4},{4,0},{8,12},{12,8},{16,20},{20,16},{24,28},{28,24},{1,5},{5... | collective-permute-start | bytes 13762568 | tf_op jit(solution)/shard_map/ppermute | solution.py:256
  674.4 462.8 %reduce-scatter.12.cloned.1.call-start = ((), (), s32[]{:S(2)}) async-start(), calls=%async_computation.14 | async-start | bytes 6553600 | tf_op jit(solution)/shard_map/reduce_scatter | solution.py:269
  690.4 446.8 %reduce-scatter.16.cloned.1.call-start = ((), (), s32[]{:S(2)}) async-start(), calls=%async_computation.16 | async-start | bytes 6553600 | tf_op jit(solution)/shard_map/reduce_scatter | solution.py:269
  695.8 52.4 %collective-permute-start.23 = (bf16[8,80,1792]{2,1,0:T(8,128)(2,1)}, bf16[8,80,1792]{2,1,0:T(8,128)(2,1)}, u32[]{:S(2)}, u32[]{:S(2)}) collective-permute-start(bf16[8,80,1792]{2,1,0:T(8,128)(2,1)} %get-tuple-element.238), channel_id=1, source_target_pairs={{0,1},{4,5},{8,9},{12,13},{16,17},{20,21},{24,25},{28,29}} | collective-permute-start | bytes 6881288 | tf_op jit(solution)/shard_map/ppermute | solution.py:576
  700.5 47.6 %collective-permute-start.24 = (bf16[8,80,1792]{2,1,0:T(8,128)(2,1)}, bf16[8,80,1792]{2,1,0:T(8,128)(2,1)}, u32[]{:S(2)}, u32[]{:S(2)}) collective-permute-start(bf16[8,80,1792]{2,1,0:T(8,128)(2,1)} %get-tuple-element.237), channel_id=1, source_target_pairs={{3,2},{7,6},{11,10},{15,14},{19,18},{23,22},{27,26},{31,30}} | collective-permute-start | bytes 6881288 | tf_op jit(solution)/shard_map/ppermute | solution.py:577
  710.8 171.7 %collective-permute-start.43 = (bf16[512,1280]{1,0:T(8,128)(2,1)}, bf16[512,1280]{1,0:T(8,128)(2,1)}, u32[]{:S(2)}, u32[]{:S(2)}) collective-permute-start(bf16[512,1280]{1,0:T(8,128)(2,1)} %get-tuple-element.133), channel_id=1, source_target_pairs={{0,4},{4,0},{8,12},{12,8},{16,20},{20,16},{24,28},{28,24},{1,5},{5... | collective-permute-start | bytes 3932168 | tf_op jit(solution)/shard_map/ppermute | solution.py:256
  714.8 106.2 %collective-permute-start.29 = (bf16[224,2560]{1,0:T(8,128)(2,1)}, bf16[224,2560]{1,0:T(8,128)(2,1)}, u32[]{:S(2)}, u32[]{:S(2)}) collective-permute-start(bf16[224,2560]{1,0:T(8,128)(2,1)} %get-tuple-element.241), channel_id=1, source_target_pairs={{3,2},{7,6},{11,10},{15,14},{19,18},{23,22},{27,26},{31,30}} | collective-permute-start | bytes 3440648 | tf_op jit(solution)/shard_map/ppermute | solution.py:577
  716.5 107.5 %collective-permute-start.28 = (bf16[224,2560]{1,0:T(8,128)(2,1)}, bf16[224,2560]{1,0:T(8,128)(2,1)}, u32[]{:S(2)}, u32[]{:S(2)}) collective-permute-start(bf16[224,2560]{1,0:T(8,128)(2,1)} %get-tuple-element.242), channel_id=1, source_target_pairs={{0,1},{4,5},{8,9},{12,13},{16,17},{20,21},{24,25},{28,29}} | collective-permute-start | bytes 3440648 | tf_op jit(solution)/shard_map/ppermute | solution.py:576
  773.2 364.0 %reduce-scatter.18.cloned.1.call-start = ((), (), s32[]{:S(2)}) async-start(), calls=%async_computation.17 | async-start | bytes 8192000 | tf_op jit(solution)/shard_map/reduce_scatter | solution.py:269
  788.5 51.2 %collective-permute-start.26 = (bf16[8,80,1792]{2,1,0:T(8,128)(2,1)}, bf16[8,80,1792]{2,1,0:T(8,128)(2,1)S(1)}, u32[]{:S(2)}, u32[]{:S(2)}) collective-permute-start(bf16[8,80,1792]{2,1,0:T(8,128)(2,1)} %get-tuple-element.236), channel_id=1, source_target_pairs={{0,1},{1,2},{4,5},{5,6},{8,9},{9,10},{12,13},{13,14},{16,17},{17,1... | collective-permute-start | bytes 6881288 | tf_op jit(solution)/shard_map/ppermute | solution.py:576
  793.0 46.7 %collective-permute-start.27 = (bf16[8,80,1792]{2,1,0:T(8,128)(2,1)}, bf16[8,80,1792]{2,1,0:T(8,128)(2,1)S(1)}, u32[]{:S(2)}, u32[]{:S(2)}) collective-permute-start(bf16[8,80,1792]{2,1,0:T(8,128)(2,1)} %get-tuple-element.235), channel_id=1, source_target_pairs={{3,2},{2,1},{7,6},{6,5},{11,10},{10,9},{15,14},{14,13},{19,18},{18... | collective-permute-start | bytes 6881288 | tf_op jit(solution)/shard_map/ppermute | solution.py:577
  821.1 61.5 %collective-permute-start.44 = (bf16[256,2560]{1,0:T(8,128)(2,1)}, bf16[256,2560]{1,0:T(8,128)(2,1)}, u32[]{:S(2)}, u32[]{:S(2)}) collective-permute-start(bf16[256,2560]{1,0:T(8,128)(2,1)} %get-tuple-element.231), channel_id=1, source_target_pairs={{0,4},{4,0},{8,12},{12,8},{16,20},{20,16},{24,28},{28,24},{1,5},{5... | collective-permute-start | bytes 3932168 | tf_op jit(solution)/shard_map/ppermute | solution.py:256
  896.7 440.1 %reduce-scatter.20.cloned.1.call-start = ((), (), s32[]{:S(2)}) async-start(), calls=%async_computation.18 | async-start | bytes 8192000 | tf_op jit(solution)/shard_map/reduce_scatter | solution.py:269
  904.0 93.3 %collective-permute-start.33 = (bf16[8,80,1792]{2,1,0:T(8,128)(2,1)}, bf16[8,80,1792]{2,1,0:T(8,128)(2,1)S(1)}, u32[]{:S(2)}, u32[]{:S(2)}) collective-permute-start(bf16[8,80,1792]{2,1,0:T(8,128)(2,1)} %get-tuple-element.233), channel_id=1, source_target_pairs={{0,1},{1,2},{2,3},{4,5},{5,6},{6,7},{8,9},{9,10},{10,11},{12,13},{... | collective-permute-start | bytes 6881288 | tf_op jit(solution)/shard_map/ppermute | solution.py:576
  912.7 85.9 %collective-permute-start.34 = (bf16[8,80,1792]{2,1,0:T(8,128)(2,1)}, bf16[8,80,1792]{2,1,0:T(8,128)(2,1)}, u32[]{:S(2)}, u32[]{:S(2)}) collective-permute-start(bf16[8,80,1792]{2,1,0:T(8,128)(2,1)} %get-tuple-element.234), channel_id=1, source_target_pairs={{3,2},{2,1},{1,0},{7,6},{6,5},{5,4},{11,10},{10,9},{9,8},{15,14},{... | collective-permute-start | bytes 6881288 | tf_op jit(solution)/shard_map/ppermute | solution.py:577
  923.0 96.9 %collective-permute-start.36 = (bf16[224,2560]{1,0:T(8,128)(2,1)}, bf16[224,2560]{1,0:T(8,128)(2,1)}, u32[]{:S(2)}, u32[]{:S(2)}) collective-permute-start(bf16[224,2560]{1,0:T(8,128)(2,1)} %get-tuple-element.240), channel_id=1, source_target_pairs={{0,1},{1,2},{4,5},{5,6},{8,9},{9,10},{12,13},{13,14},{16,17},{17,1... | collective-permute-start | bytes 3440648 | tf_op jit(solution)/shard_map/ppermute | solution.py:576
  1004.0 23.7 %collective-permute-start.35 = (bf16[4,80,1792]{2,1,0:T(8,128)(2,1)}, bf16[4,80,1792]{2,1,0:T(8,128)(2,1)S(1)}, u32[]{:S(2)}, u32[]{:S(2)}) collective-permute-start(bf16[4,80,1792]{2,1,0:T(8,128)(2,1)} %get-tuple-element.252), channel_id=1, source_target_pairs={{0,4},{4,0},{8,12},{12,8},{16,20},{20,16},{24,28},{28,24},{1,5},{5... | collective-permute-start | bytes 3440648 | tf_op jit(solution)/shard_map/ppermute | solution.py:256
  1005.5 29.5 %collective-permute-start.39 = (bf16[224,2560]{1,0:T(8,128)(2,1)}, bf16[224,2560]{1,0:T(8,128)(2,1)}, u32[]{:S(2)}, u32[]{:S(2)}) collective-permute-start(bf16[224,2560]{1,0:T(8,128)(2,1)} %get-tuple-element.239), channel_id=1, source_target_pairs={{3,2},{2,1},{1,0},{7,6},{6,5},{5,4},{11,10},{10,9},{9,8},{15,14},{... | collective-permute-start | bytes 3440648 | tf_op jit(solution)/shard_map/ppermute | solution.py:577
  1022.6 26.8 %collective-permute-start.37 = (bf16[224,2560]{1,0:T(8,128)(2,1)}, bf16[224,2560]{1,0:T(8,128)(2,1)}, u32[]{:S(2)}, u32[]{:S(2)}) collective-permute-start(bf16[224,2560]{1,0:T(8,128)(2,1)} %bitcast_add_fusion.7), channel_id=1, source_target_pairs={{0,1},{1,2},{2,3},{4,5},{5,6},{6,7},{8,9},{9,10},{10,11},{12,13},{... | collective-permute-start | bytes 3440648 | tf_op jit(solution)/shard_map/ppermute | solution.py:576
  1032.2 20.3 %collective-permute-start.40 = (bf16[1,2,80,1792]{3,2,1,0:T(8,128)(2,1)}, bf16[1,2,80,1792]{3,2,1,0:T(8,128)(2,1)S(1)}, u32[]{:S(2)}, u32[]{:S(2)}) collective-permute-start(bf16[1,2,80,1792]{3,2,1,0:T(8,128)(2,1)} %get-tuple-element.249), channel_id=1, source_target_pairs={{0,8},{4,12},{8,0},{12,4},{16,24},{20,28},{24,16},{28,20},{1,9},{5... | collective-permute-start | bytes 1720328 | tf_op jit(solution)/shard_map/ppermute | solution.py:290
  1033.3 19.2 %collective-permute-start.41 = (bf16[1,2,80,1792]{3,2,1,0:T(8,128)(2,1)}, bf16[1,2,80,1792]{3,2,1,0:T(8,128)(2,1)S(1)}, u32[]{:S(2)}, u32[]{:S(2)}) collective-permute-start(bf16[1,2,80,1792]{3,2,1,0:T(8,128)(2,1)} %get-tuple-element.248), channel_id=1, source_target_pairs={{0,16},{4,20},{8,24},{12,28},{16,0},{20,4},{24,8},{28,12},{1,17},{... | collective-permute-start | bytes 1720328 | tf_op jit(solution)/shard_map/ppermute | solution.py:290
  1034.2 23.5 %collective-permute-start.42 = (bf16[1,2,80,1792]{3,2,1,0:T(8,128)(2,1)}, bf16[1,2,80,1792]{3,2,1,0:T(8,128)(2,1)S(1)}, u32[]{:S(2)}, u32[]{:S(2)}) collective-permute-start(bf16[1,2,80,1792]{3,2,1,0:T(8,128)(2,1)} %get-tuple-element.247), channel_id=1, source_target_pairs={{0,24},{4,28},{8,16},{12,20},{16,8},{20,12},{24,0},{28,4},{1,25},{... | collective-permute-start | bytes 1720328 | tf_op jit(solution)/shard_map/ppermute | solution.py:290
  1035.0 108.1 %collective-permute-start.25 = (bf16[512,1280]{1,0:T(8,128)(2,1)}, bf16[512,1280]{1,0:T(8,128)(2,1)}, u32[]{:S(2)}, u32[]{:S(2)}) collective-permute-start(bf16[512,1280]{1,0:T(8,128)(2,1)} %get-tuple-element.113), channel_id=1, source_target_pairs={{0,4},{4,0},{8,12},{12,8},{16,20},{20,16},{24,28},{28,24},{1,5},{5... | collective-permute-start | bytes 3932168 | tf_op jit(solution)/shard_map/ppermute | solution.py:256
  1049.4 95.1 %collective-permute-start.48 = (bf16[256,2560]{1,0:T(8,128)(2,1)}, bf16[256,2560]{1,0:T(8,128)(2,1)}, u32[]{:S(2)}, u32[]{:S(2)}) collective-permute-start(bf16[256,2560]{1,0:T(8,128)(2,1)} %get-tuple-element.127), channel_id=1, source_target_pairs={{0,4},{4,0},{8,12},{12,8},{16,20},{20,16},{24,28},{28,24},{1,5},{5... | collective-permute-start | bytes 3932168 | tf_op jit(solution)/shard_map/ppermute | solution.py:256
  1065.5 70.9 %collective-permute-start.46 = (bf16[80,14336]{1,0:T(8,128)(2,1)S(1)}, bf16[80,14336]{1,0:T(8,128)(2,1)}, u32[]{:S(2)}, u32[]{:S(2)}) collective-permute-start(bf16[80,14336]{1,0:T(8,128)(2,1)S(1)} %bitcast.136), channel_id=1, source_target_pairs={{0,1},{1,2},{2,3},{4,5},{5,6},{6,7},{8,9},{9,10},{10,11},{12,13},{... | collective-permute-start | bytes 6881288 | tf_op jit(solution)/shard_map/ppermute | solution.py:621
  1068.7 68.6 %collective-permute-start.47 = (bf16[80,14336]{1,0:T(8,128)(2,1)S(1)}, bf16[80,14336]{1,0:T(8,128)(2,1)}, u32[]{:S(2)}, u32[]{:S(2)}) collective-permute-start(bf16[80,14336]{1,0:T(8,128)(2,1)S(1)} %bitcast.137), channel_id=1, source_target_pairs={{3,2},{2,1},{1,0},{7,6},{6,5},{5,4},{11,10},{10,9},{9,8},{15,14},{... | collective-permute-start | bytes 6881288 | tf_op jit(solution)/shard_map/ppermute | solution.py:622
  1156.2 233.4 %reduce-scatter.22.cloned.1.call-start = ((), (), s32[]{:S(2)}) async-start(), calls=%async_computation.19 | async-start | bytes 4505600
  1160.8 52.1 %collective-permute-start.32 = (bf16[256,1280]{1,0:T(8,128)(2,1)}, bf16[256,1280]{1,0:T(8,128)(2,1)}, u32[]{:S(2)}, u32[]{:S(2)}) collective-permute-start(bf16[256,1280]{1,0:T(8,128)(2,1)} %add_convert_fusion.4), channel_id=1, source_target_pairs={{3,2},{2,1},{1,0},{7,6},{6,5},{5,4},{11,10},{10,9},{9,8},{15,14},{... | collective-permute-start | bytes 1966088 | tf_op jit(solution)/shard_map/ppermute | solution.py:604
  1163.1 46.4 %collective-permute-start.51 = (bf16[256,1280]{1,0:T(8,128)(2,1)}, bf16[256,1280]{1,0:T(8,128)(2,1)}, u32[]{:S(2)}, u32[]{:S(2)}) collective-permute-start(bf16[256,1280]{1,0:T(8,128)(2,1)} %add_convert_fusion.3), channel_id=1, source_target_pairs={{3,2},{2,1},{7,6},{6,5},{11,10},{10,9},{15,14},{14,13},{19,18},{18... | collective-permute-start | bytes 1966088 | tf_op jit(solution)/shard_map/ppermute | solution.py:604
  1167.1 59.2 %collective-permute-start.54 = (bf16[224,2560]{1,0:T(8,128)(2,1)S(1)}, bf16[224,2560]{1,0:T(8,128)(2,1)}, u32[]{:S(2)}, u32[]{:S(2)}) collective-permute-start(bf16[224,2560]{1,0:T(8,128)(2,1)S(1)} %fusion.47.refs_0_), channel_id=1, source_target_pairs={{0,1},{1,2},{2,3},{4,5},{5,6},{6,7},{8,9},{9,10},{10,11},{12,13},{... | collective-permute-start | bytes 3440648 | tf_op jit(solution)/shard_map/ppermute | solution.py:621
  1204.1 91.2 %collective-permute-start.52 = (bf16[80,14336]{1,0:T(8,128)(2,1)}, bf16[80,14336]{1,0:T(8,128)(2,1)}, u32[]{:S(2)}, u32[]{:S(2)}) collective-permute-start(bf16[80,14336]{1,0:T(8,128)(2,1)} %collective-permute-done.46.refs_1_), channel_id=1, source_target_pairs={{1,2},{2,3},{5,6},{6,7},{9,10},{10,11},{13,14},{14,15},{17,18},{18... | collective-permute-start | bytes 6881288 | tf_op jit(solution)/shard_map/ppermute | solution.py:621
  1206.2 89.2 %collective-permute-start.53 = (bf16[80,14336]{1,0:T(8,128)(2,1)}, bf16[80,14336]{1,0:T(8,128)(2,1)}, u32[]{:S(2)}, u32[]{:S(2)}) collective-permute-start(bf16[80,14336]{1,0:T(8,128)(2,1)} %collective-permute-done.47.refs_6_), channel_id=1, source_target_pairs={{2,1},{1,0},{6,5},{5,4},{10,9},{9,8},{14,13},{13,12},{18,17},{17,1... | collective-permute-start | bytes 6881288 | tf_op jit(solution)/shard_map/ppermute | solution.py:622
  1209.5 84.8 %collective-permute-start.55 = (bf16[224,2560]{1,0:T(8,128)(2,1)S(1)}, bf16[224,2560]{1,0:T(8,128)(2,1)S(1)}, u32[]{:S(2)}, u32[]{:S(2)}) collective-permute-start(bf16[224,2560]{1,0:T(8,128)(2,1)S(1)} %fusion.47.refs_0_), channel_id=1, source_target_pairs={{3,2},{2,1},{1,0},{7,6},{6,5},{5,4},{11,10},{10,9},{9,8},{15,14},{... | collective-permute-start | bytes 3440648 | tf_op jit(solution)/shard_map/ppermute | solution.py:622
  1212.9 95.5 %collective-permute-start.56 = (bf16[256,1280]{1,0:T(8,128)(2,1)}, bf16[256,1280]{1,0:T(8,128)(2,1)}, u32[]{:S(2)}, u32[]{:S(2)}) collective-permute-start(bf16[256,1280]{1,0:T(8,128)(2,1)} %add_convert_fusion.2), channel_id=1, source_target_pairs={{3,2},{2,1},{1,0},{7,6},{6,5},{5,4},{11,10},{10,9},{9,8},{15,14},{... | collective-permute-start | bytes 1966088 | tf_op jit(solution)/shard_map/ppermute | solution.py:604
  1298.6 30.1 %collective-permute-start.57 = (bf16[256,1280]{1,0:T(8,128)(2,1)}, bf16[256,1280]{1,0:T(8,128)(2,1)}, u32[]{:S(2)}, u32[]{:S(2)}) collective-permute-start(bf16[256,1280]{1,0:T(8,128)(2,1)} %finish_keys.2), channel_id=1, source_target_pairs={{0,4},{4,0},{8,12},{12,8},{16,20},{20,16},{24,28},{28,24},{1,5},{5... | collective-permute-start | bytes 1966088 | tf_op jit(solution)/shard_map/ppermute | solution.py:256
  1311.7 17.0 %collective-permute-start.58 = (bf16[256,1280]{1,0:T(8,128)(2,1)}, bf16[256,1280]{1,0:T(8,128)(2,1)}, u32[]{:S(2)}, u32[]{:S(2)}) collective-permute-start(bf16[256,1280]{1,0:T(8,128)(2,1)} %finish_keys.3), channel_id=1, source_target_pairs={{0,4},{4,0},{8,12},{12,8},{16,20},{20,16},{24,28},{28,24},{1,5},{5... | collective-permute-start | bytes 1966088 | tf_op jit(solution)/shard_map/ppermute | solution.py:256
  1342.9 246.5 %all-reduce.5.cloned.1.call-start = ((), (), s32[]{:S(2)}) async-start(), calls=%async_computation.20 | async-start | bytes 8716288 | tf_op jit(solution)/shard_map/psum | solution.py:874
  1343.0 141.7 %collective-permute-start.59 = (bf16[80,14336]{1,0:T(8,128)(2,1)}, bf16[80,14336]{1,0:T(8,128)(2,1)}, u32[]{:S(2)}, u32[]{:S(2)}) collective-permute-start(bf16[80,14336]{1,0:T(8,128)(2,1)} %collective-permute-done.52.refs_3_), channel_id=1, source_target_pairs={{2,3},{6,7},{10,11},{14,15},{18,19},{22,23},{26,27},{30,31}} | collective-permute-start | bytes 6881288 | tf_op jit(solution)/shard_map/ppermute | solution.py:621
  1345.1 139.7 %collective-permute-start.60 = (bf16[80,14336]{1,0:T(8,128)(2,1)}, bf16[80,14336]{1,0:T(8,128)(2,1)}, u32[]{:S(2)}, u32[]{:S(2)}) collective-permute-start(bf16[80,14336]{1,0:T(8,128)(2,1)} %collective-permute-done.53.refs_4_), channel_id=1, source_target_pairs={{1,0},{5,4},{9,8},{13,12},{17,16},{21,20},{25,24},{29,28}} | collective-permute-start | bytes 6881288 | tf_op jit(solution)/shard_map/ppermute | solution.py:622
  1346.4 135.1 %collective-permute-start.62 = (bf16[224,2560]{1,0:T(8,128)(2,1)}, bf16[224,2560]{1,0:T(8,128)(2,1)}, u32[]{:S(2)}, u32[]{:S(2)}) collective-permute-start(bf16[224,2560]{1,0:T(8,128)(2,1)} %copy-done.62), channel_id=1, source_target_pairs={{2,1},{1,0},{6,5},{5,4},{10,9},{9,8},{14,13},{13,12},{18,17},{17,1... | collective-permute-start | bytes 3440648 | tf_op jit(solution)/shard_map/ppermute | solution.py:622
  1347.7 135.1 %collective-permute-start.61 = (bf16[224,2560]{1,0:T(8,128)(2,1)}, bf16[224,2560]{1,0:T(8,128)(2,1)}, u32[]{:S(2)}, u32[]{:S(2)}) collective-permute-start(bf16[224,2560]{1,0:T(8,128)(2,1)} %collective-permute-done.54.refs_1_), channel_id=1, source_target_pairs={{1,2},{2,3},{5,6},{6,7},{9,10},{10,11},{13,14},{14,15},{17,18},{18... | collective-permute-start | bytes 3440648 | tf_op jit(solution)/shard_map/ppermute | solution.py:621
  1481.5 52.4 %collective-permute-start.64 = (bf16[224,2560]{1,0:T(8,128)(2,1)}, bf16[224,2560]{1,0:T(8,128)(2,1)S(1)}, u32[]{:S(2)}, u32[]{:S(2)}) collective-permute-start(bf16[224,2560]{1,0:T(8,128)(2,1)} %collective-permute-done.62.refs_4_), channel_id=1, source_target_pairs={{1,0},{5,4},{9,8},{13,12},{17,16},{21,20},{25,24},{29,28}} | collective-permute-start | bytes 3440648 | tf_op jit(solution)/shard_map/ppermute | solution.py:622
  1482.8 51.1 %collective-permute-start.65 = (bf16[224,2560]{1,0:T(8,128)(2,1)}, bf16[224,2560]{1,0:T(8,128)(2,1)}, u32[]{:S(2)}, u32[]{:S(2)}) collective-permute-start(bf16[224,2560]{1,0:T(8,128)(2,1)} %collective-permute-done.61.refs_3_), channel_id=1, source_target_pairs={{2,3},{6,7},{10,11},{14,15},{18,19},{22,23},{26,27},{30,31}} | collective-permute-start | bytes 3440648 | tf_op jit(solution)/shard_map/ppermute | solution.py:621
  1591.1 10.3 collective-permute-start.63
  (107 other events, 1561.7 us)
Sparse Core Ops, SparseCore 0:
  13.5 154.5 all-gather.6
  170.0 74.3 all-gather.8
  246.8 60.9 all-gather.10
  309.5 61.4 all-gather.12
  373.3 83.1 all-gather.16
  458.8 61.4 all-gather.14
  523.8 61.4 reduce-scatter.9
  674.5 61.2 reduce-scatter.13
  738.8 61.4 reduce-scatter.11
  803.7 61.4 reduce-scatter.15
  896.9 75.7 reduce-scatter.17
  1156.3 71.1 reduce-scatter.19
  1343.1 46.4 reduce-scatter.21
  1392.0 197.3 all-reduce.4

commit v3 on v2

--- a/solution.py
+++ b/solution.py
@@ -265,8 +265,18 @@
     return lax.all_gather(x, "fsdp", axis=0, tiled=True, axis_index_groups=same_core())
 
 
-def scatter_chips(x):
-    return lax.psum_scatter(x, "fsdp", scatter_dimension=0, tiled=True, axis_index_groups=same_core())
+def scatter_chips(x, *before):
+    parts = lax.axis_size("fsdp")
+    chips, chip = parts // 2, lax.axis_index("fsdp") // 2
+    blocks = x.reshape((chips, x.shape[0] // chips) + x.shape[1:])
+    take = lambda q: lax.dynamic_index_in_dim(blocks, q, 0, keepdims=False)
+    came = [lax.ppermute(take(chip ^ d), "fsdp", [(j, j ^ (2 * d)) for j in range(parts)]) for d in range(1, chips)]
+    return take(chip), came
+
+
+def added(pieces):
+    own, came = pieces
+    return sum((c.astype(jnp.float32) for c in came), own.astype(jnp.float32))
 
 
 def exchange(blocks):
@@ -444,17 +454,27 @@
     lefts = [ref[...] for ref in refs[:pairs]]
     extra = refs[pairs + segments * pairs:-1]
     out_ref = refs[-1]
-    width = out_ref.shape[1] // segments
+    width = out_ref.shape[-1] // segments
     for j in range(segments):
         rights = refs[pairs + j * pairs:pairs + (j + 1) * pairs]
         part = slice(j * width, (j + 1) * width)
         total = sum(tn(a, b[...]) for a, b in zip(lefts, rights))
-        for more in extra:
-            total = total + more[:, part].astype(jnp.float32)
-        out_ref[:, part] = total.astype(out_ref.dtype)
-
-
-def sum_tn(lefts, rights, half, *extra, weight=1):
+        if len(out_ref.shape) == 2:
+            for more in extra:
+                total = total + more[:, part].astype(jnp.float32)
+            out_ref[:, part] = total.astype(out_ref.dtype)
+        else:
+            slabs, blocks, rows, _ = out_ref.shape
+            for s in range(slabs):
+                for k in range(blocks):
+                    at = (k * slabs + s) * rows
+                    piece = total[at:at + rows]
+                    for more in extra:
+                        piece = piece + more[s, k, :, part].astype(jnp.float32)
+                    out_ref[s, k, :, part] = piece.astype(out_ref.dtype)
+
+
+def sum_tn(lefts, rights, half, *extra, weight=1, slabs=1, rows=1):
     segments, pairs = len(rights), len(lefts)
     tokens = lefts[0].shape[0]
     if segments == 1:
@@ -472,11 +492,13 @@
         if width % 128:
             cut = slice(half * width, (half + 1) * width)
             total = jnp.concatenate([sum(tn(a, b[:, cut]) for a, b in zip(lefts, r)) for r in rights], axis=1)
+            total = jnp.moveaxis(total.reshape(-1, slabs, rows, segments * width), 1, 0)
             return sum((e.astype(jnp.float32) for e in extra), total).astype(jnp.bfloat16)
-        shape = (D, segments * width)
+        blocks = CHUNK // (slabs * rows)
+        shape = (slabs, D // (slabs * rows), rows, segments * width)
         left = pl.BlockSpec((tokens, CHUNK), lambda i: (0, i))
         right = pl.BlockSpec((tokens, width), lambda i: (0, half))
-        out = pl.BlockSpec((CHUNK, segments * width), lambda i: (i, 0))
+        out = pl.BlockSpec((slabs, blocks, rows, segments * width), lambda i: (0, i, 0, 0))
     return pl.pallas_call(
         functools.partial(sum_tn_kernel, segments, pairs),
         grid=(D // CHUNK,),
@@ -558,37 +580,6 @@
     )(a, b)
 
 
-class Scatter:
-    def __init__(self, take):
-        self.take = take
-        self.hops = 0
-        self.right = self.left = None
-
-    def hop(self):
-        n = lax.axis_size("sp")
-        me = lax.axis_index("sp")
-        s = self.hops
-        to_right = self.take(jnp.clip(me + (n - 1) - s, 0, n - 1))
-        to_left = self.take(jnp.clip(me - (n - 1) + s, 0, n - 1))
-        if s:
-            to_right = to_right + self.right
-            to_left = to_left + self.left
-        self.right = lax.ppermute(to_right, "sp", [(k, k + 1) for k in range(s + 1)])
-        self.left = lax.ppermute(to_left, "sp", [(n - 1 - k, n - 2 - k) for k in range(s + 1)])
-        self.hops += 1
-        return self.right, self.left
-
-    def result(self):
-        while self.hops < lax.axis_size("sp") - 1:
-            self.hop()
-        total = self.take(lax.axis_index("sp")).astype(jnp.float32) + self.right.astype(jnp.float32)
-        return (total + self.left.astype(jnp.float32)).astype(jnp.bfloat16)
-
-
-def chunk_of(x):
-    return lambda j: lax.dynamic_index_in_dim(x, j, 0, keepdims=False)
-
-
 class KeySum:
     def __init__(self, parts):
         self.parts = parts
@@ -609,89 +600,6 @@
         while self.hops < lax.axis_size("sp") - 1:
             self.hop()
         return self.parts[0], self.running
-
-
-class Gather:
-    def __init__(self, mine):
-        self.rights, self.lefts = [mine], [mine]
-
-    def hop(self):
-        n = lax.axis_size("sp")
-        s = len(self.rights) - 1
-        self.rights.append(lax.ppermute(self.rights[-1], "sp", [(k, k + 1) for k in range(s, n - 1)]))
-        self.lefts.append(lax.ppermute(self.lefts[-1], "sp", [(n - 1 - k, n - 2 - k) for k in range(s, n - 1)]))
-        return self.rights[-1], self.lefts[-1]
-
-    def result(self):
-        n = lax.axis_size("sp")
-        while len(self.rights) < n:
-            self.hop()
-        return [(self.rights[0], None)] + [(self.rights[k], self.lefts[n - k]) for k in range(1, n)]
-
-
-def place_kernel(conditions, plan, place_ref, *refs):
-    sources, outs = refs[:len(conditions)], refs[len(conditions):]
-    for (k, side), source in zip(conditions, sources):
-        active = pl.program_id(0) == k
-        if side == 1:
-            active = active & (place_ref[0] >= k)
-        elif side == 2:
-            active = active & (place_ref[0] < k)
-
-        @pl.when(active)
-        def _(source=source):
-            for out, spans in zip(outs, plan):
-                at = 0
-                for start, width in spans:
-                    out[:, at:at + width] = source[:, start:start + width].astype(jnp.float32)
-                    at += width
-
-
-def assemble(slots, plan):
-    n = len(slots)
-    me = lax.axis_index("sp")
-    rows, width = slots[0][0].shape
-    if rows % 16:
-        out = jnp.zeros((n * rows, width), jnp.float32)
-        for k, (left, right) in enumerate(slots):
-            came = left if right is None else jnp.where(me >= k, left, right)
-            out = lax.dynamic_update_slice_in_dim(out, came.astype(jnp.float32), ((me - k + n) % n) * rows, 0)
-        return [jnp.concatenate([out[:, a:a + w] for a, w in spans], axis=1) for spans in plan]
-    tile = max(t for t in range(16, rows + 1, 16) if rows % t == 0 and (t == 16 or t * width <= 1 << 19))
-    tiles = rows // tile
-    sources, conditions = [], []
-    for k, (left, right) in enumerate(slots):
-        sources.append(left)
-        conditions.append((k, 0 if right is None else 1))
-        if right is not None:
-            sources.append(right)
-            conditions.append((k, 2))
-
-    def spec(k, side):
-        def index(s, t, place):
-            active = s == k
-            if side == 1:
-                active = active & (place[0] >= k)
-            elif side == 2:
-                active = active & (place[0] < k)
-            return jnp.where(active, t, 0), 0
-        return pl.BlockSpec((tile, width), index)
-
-    out_index = lambda s, t, place: (lax.rem(place[0] - s + n, n) * tiles + t, 0)
-    widths = [sum(w for _, w in spans) for spans in plan]
-    return pl.pallas_call(
-        functools.partial(place_kernel, conditions, plan),
-        grid_spec=pltpu.PrefetchScalarGridSpec(
-            num_scalar_prefetch=1,
-            grid=(n, tiles),
-            in_specs=[spec(*c) for c in conditions],
-            out_specs=[pl.BlockSpec((tile, w), out_index) for w in widths],
-        ),
-        out_shape=[jax.ShapeDtypeStruct((n * rows, w), jnp.float32) for w in widths],
-        compiler_params=pltpu.CompilerParams(vmem_limit_bytes=48 << 20),
-        cost_estimate=work(1 + (n * rows * width >> 18)),
-        name="assemble",
-    )(me.reshape(1).astype(jnp.int32), *sources)
 
 
 def rows_of(pieces):
@@ -789,22 +697,17 @@
     normed_part(0, g_all[-1])
     for m in range(1, micro):
         forward_back(m)
-    wide_other = order.did(sum_tn(n2_alls, [[order.at(gate_grads[0])] + gate_grads[1:], up_grads], 1))
+    wide = dict(slabs=seq, rows=slab)
+    wide_other = order.did(sum_tn(n2_alls, [[order.at(gate_grads[0])] + gate_grads[1:], up_grads], 1, **wide))
     wide_came = partner(wide_other)
-    down_other = order.did(sum_tn([order.at(hiddens[0])] + hiddens[1:], [g_all], 1, weight=10))
+    down_other = order.did(sum_tn([order.at(hiddens[0])] + hiddens[1:], [g_all], 1))
     down_came = partner(down_other)
-    wide_grad = order.did(sum_tn(n2_alls, [[order.at(gate_grads[0])] + gate_grads[1:], up_grads], 0, wide_came))
-    wide_blocks = wide_grad.reshape(parts, seq, slab, hidden_chip)
-    wide = Scatter(lambda j: lax.dynamic_index_in_dim(wide_blocks, j, 1, keepdims=False))
-    hops = wide.hop()
-    order.last = order.last + (normed_grads[0],)
+    wide_grad = order.did(sum_tn(n2_alls, [[order.at(gate_grads[0])] + gate_grads[1:], up_grads], 0, wide_came, **wide))
+    wide_mine = lax.psum_scatter(wide_grad, "sp", scatter_dimension=0, tiled=False)
     down_grad = order.did(sum_tn([order.at(hiddens[0])] + hiddens[1:], [g_all], 0, down_came))
-    down = Scatter(chunk_of(down_grad.reshape(seq, hidden_own // seq, D)))
+    down_total = lax.psum(down_grad, "sp")
     normed_part(1)
-    out_part(0)
-    order.last = order.last + hops
-    hops = wide.hop() + down.hop()
-    for m in range(1, micro):
+    for m in range(micro):
         out_part(m)
     normed_mine, normed_other = features(order.at(normed), core, d_own)
     normed_chip = rows_of([normed_mine, partner(normed_other)])
@@ -817,7 +720,10 @@
     chip_rows = lambda pieces: rows_of(pieces + [partner(p) for p in pieces])
     for m in range(micro):
         kv, context, lse_rows, mixed, scale_two, normed_x2 = state[m]
-        normed_grad = order.at(normed_grads[m]).astype(f32)
+        if m == micro - 1:
+            order.last = order.last + (wide_mine,)
+            pieces = exchange_chips(exchange(wide_mine))
+        normed_grad = added((order.at(normed_grads[m][0]), normed_grads[m][1]))
         gain_two_term = gain_two_term + jnp.sum(normed_grad * normed_x2, axis=0)
         mixed_grad = norm_back(normed_grad, gain_two, normed_x2, scale_two, g_low[m].astype(f32))
         attn_grad = mixed_grad.astype(bf16)
@@ -826,39 +732,27 @@
         context_grad = order.did(nt(attn_grad, w_out_full).astype(bf16))
         if m == micro - 1:
             out_half = order.did(tn(context_chip, chip_rows(attn_grads)).astype(bf16))
-            out_shard = scatter_chips(out_half)
-        if m == 1:
-            order.last = order.last + hops
-            pair = exchange(wide.result())
-            order.last = order.last + (pair,)
-            pieces = exchange_chips(pair)
-            hops = down.hop()
+            out_shard = added(scatter_chips(out_half)).astype(bf16)
         args = (context, lse_rows, kv, bias_t[m], tables, m)
         first = attend_back(qkv, order.at(context_grad), *args, 0)
-        order.last = hops
-        if m == 0:
-            hops = wide.hop() + down.hop()
-        elif m == 1:
-            wide_part = exchanged([order.at(pieces[0], *pieces[1:])] + pieces[1:])
-            wide_part = jnp.moveaxis(wide_part.reshape(parts, slab, 2, hidden_own), 0, 2).reshape(slab, 2 * ff)
-            wide_gather, down_gather = Gather(wide_part), Gather(down.result())
-            hops = wide_gather.hop()
-            order.last = (wide_part,)
+        order.last = ()
+        if m == micro - 1:
+            order.last = tuple(pieces)
         second = attend_back(qkv, order.at(context_grad), *args, 1, first)
         query_grads.append(order.did(second[0]))
         kv_sums.append(KeySum(second[1:]))
         kv_sums[-1].hop()
 
-    order.last = order.last + tuple(out_terms) + (out_shard,) + hops
-    hops = wide_gather.hop() + down_gather.hop()
+    order.last = order.last + (out_shard, down_total)
+    wide_part = exchanged([order.at(pieces[0], *pieces[1:])] + pieces[1:])
+    wide_part = order.did(jnp.moveaxis(wide_part.reshape(parts, slab, 2, hidden_own), 0, 2).reshape(slab, 2 * ff))
+    wide_total = lax.all_gather(wide_part, "sp", axis=0, tiled=True)
     query_half = order.did(tn(normed_chip, chip_rows(query_grads[:-1] + [order.at(query_grads[-1])])).astype(bf16))
-    query_shard = scatter_chips(query_half)
+    query_shard = added(scatter_chips(query_half)).astype(bf16)
     kv_hop = tuple(keys.hop() for keys in kv_sums)
     normed_grad = order.did(nt(order.at(rows_of(query_grads), *kv_hop), w_in[:, :D]))
     kv_grads = [keys.result() for keys in kv_sums]
-    order.last = order.last + hops
     kv_grads = [order.did(finish_keys(own, order.at(came), tables, m)) for m, (own, came) in enumerate(kv_grads)]
-    hops = wide_gather.hop() + down_gather.hop()
     kv_grad = rows_of(kv_grads)
     kv_half = order.did(tn(normed_chip, chip_rows(kv_grads)).astype(bf16))
     normed_grad = normed_grad + nt(kv_grad, w_in[:, D:D + 4 * KW])
@@ -869,19 +763,13 @@
     gain_lanes = jnp.concatenate(
         [lax.dynamic_index_in_dim(gain_blocks, c, 1, keepdims=False) for c in (core, 1 - core)], axis=2
     ).reshape(chips * d_own, 4)
-    kv_shard = scatter_chips(tie(jnp.concatenate([kv_half, jnp.pad(gain_lanes, ((0, 0), (0, 124)))], axis=1), query_shard))
-    out_total, query_total, kv_total = (
-        x.astype(f32) for x in lax.psum((tie(out_shard, kv_shard), tie(query_shard, kv_shard), kv_shard), "sp")
-    )
+    kv_shard = added(scatter_chips(jnp.concatenate([kv_half, jnp.pad(gain_lanes, ((0, 0), (0, 124)))], axis=1))).astype(bf16)
+    out_total, query_total, kv_total = lax.psum((tie(out_shard, down_total), query_shard, kv_shard), "sp")
+    query_total, kv_total = query_total.astype(f32), kv_total.astype(f32)
     kv_piece = lambda k: kv_total[:, k * KW:(k + 1) * KW]
     gain_lanes = kv_total[:, 4 * KW:4 * KW + 4]
     gain_total = gain_lanes[:, :2] + partner(gain_lanes)[:, 2:]
-    order.last = order.last + hops
-    down_slots = down_gather.result()
-    wide_gather.hop()
-    (down_total,) = assemble([(order.at(down_slots[0][0]), None)] + down_slots[1:], [[(0, D)]])
-    gate_total, up_total = assemble(wide_gather.result(), [[(0, ff)], [(ff, ff)]])
-    outputs = [(state[m][3] + order.at(out_terms[m]).astype(f32)).astype(bf16) for m in range(micro)]
+    outputs = [(state[m][3] + added((order.at(out_terms[m][0]), out_terms[m][1]))).astype(bf16) for m in range(micro)]
     return (
         rows_of(outputs).reshape(tokens.shape),
         input_grad.reshape(tokens.shape),
@@ -890,10 +778,10 @@
         query_total,
         jnp.concatenate([kv_piece(0), kv_piece(2)], axis=1),
         jnp.concatenate([kv_piece(1), kv_piece(3)], axis=1),
-        out_total,
-        gate_total,
-        up_total,
-        down_total,
+        out_total.astype(f32),
+        wide_total[:, :ff].astype(f32),
+        wide_total[:, ff:].astype(f32),
+        down_total.astype(f32),
     )
 
 

time: 1620 us -> 1550 us (0.957)
  starting transfers between devices: 228 us -> 55.8 us
  waiting for transfers between devices: 603 us -> 720 us
  Pallas kernels: 497 us -> 472 us
    all_gather x0 -> x1, waiting for transfers between devices: none -> 152 us  [body(): wide_total = lax.all_gather(wide_part, 'sp', axis=0, tiled=True)]
    ppermute x24 -> x21, starting transfers between devices: 165 us -> 18.1 us  [scatter_chips(): lax.ppermute(take(chip ^ d), 'fsdp', [(j, j ^ 2 * d) for j in range(parts)])]
    ppermute x24 -> x21, waiting for transfers between devices: 253 us -> 165 us  [scatter_chips(): lax.ppermute(take(chip ^ d), 'fsdp', [(j, j ^ 2 * d) for j in range(parts)])]
    ppermute x6, waiting for transfers between devices: 0.95 us -> 54.6 us  [hop(): self.running = lax.ppermute(tie(self.running, *before), 'sp', pairs)]
    unnamed x15 -> x10, waiting for transfers between devices: 41.6 us -> 1.61 us
    psum x1 -> x2, waiting for transfers between devices: 43.4 us -> 71 us  [the longest x1 50.9 us: body(): lax.psum((tie(out_shard, down_total), query_shard, kv_shard), 'sp')]
    ppermute x21, starting transfers between devices: 37.6 us -> 11.8 us  [partner(): lax.ppermute(x, 'fsdp', [(j, j ^ 1) for j in range(lax.axis_size('fsdp'))])]
    pallas_call x2 -> x0, Pallas kernels: 24.8 us -> none  [assemble(): pl.pallas_call(functools.partial(place_kernel, conditions, plan), grid_sp...]
  transfers between devices with their start and end apart: 80 -> 73, of which waited for: 28 -> 31; matrix products, arithmetic and copies ran while one was open for 13% -> 15% of each run, Pallas kernels for 28% -> 25%
where the time goes in v3:
time: 1550 us; the launch traced here: 1540 us
  waiting for transfers between devices  720 us (46%)
  Pallas kernels  472 us (30%)
  local copies, waits for them, and re-layouts  97.1 us (6%)
  other arithmetic  94.1 us (6%)
  matrix products  84.7 us (5%)
  starting transfers between devices  55.8 us (4%)
  between operations  15.9 us (1%)
    ppermute x21, waiting for transfers between devices, scatter_chips(): lax.ppermute(take(chip ^ d), 'fsdp', [(j, j ^ 2 * d) for j in range(parts)])  165 us
    all_gather x1, waiting for transfers between devices, body(): wide_total = lax.all_gather(wide_part, 'sp', axis=0, tiled=True)  152 us
    pallas_call x4, Pallas kernels, attend_back(): pl.pallas_call(functools.partial(backward_kernel, blocks, len(before)), g...  108 us
    all_gather x4, waiting for transfers between devices, gather_chips(): lax.all_gather(x, 'fsdp', axis=0, tiled=True, axis_index_groups=same_core())  92.8 us
    pallas_call x4, Pallas kernels, sum_tn(): pl.pallas_call(functools.partial(sum_tn_kernel, segments, pairs), grid=(D...  90.2 us
    pallas_call x2, Pallas kernels, feed_forward(): pl.pallas_call(ffn_kernel, grid=(tiles,), in_specs=[full, full, pl.BlockS...  73.4 us
    all_gather x1, waiting for transfers between devices, body(): w_in = lax.all_gather(w_in, 'fsdp', axis=0, tiled=True)  69 us
    ppermute x3, waiting for transfers between devices, fetch(): lax.ppermute(x, 'fsdp', [(j, j ^ 2 * d) for j in range(parts)])  55.1 us
  transfers between devices with their start and end apart: 73, of which 31 were waited for; matrix products, arithmetic and copies ran while one was open for 15% of the time, Pallas kernels for 25%

profile of v3, /device:TPU:1, one launch (start us, length us, event | category | flops | bytes accessed | tf_op | source)
XLA Modules:
  0.0 1540.1 jit_solution(13177600697248579869)
XLA Ops:
  30.4 5.8 fusion.38
  41.5 20.4 %collective-permute-done.refs_2_ = bf16[320,1792]{1,0:T(8,128)(2,1)} collective-permute-done((bf16[320,1792]{1,0:T(8,128)(2,1)}, bf16[320,1792]{1,0:T(8,128)(2,1)}, u32[]{:S(2)}, u32[]{:S(2)}) %collective-permute-start) | collective-permute-done | bytes 1146912 | tf_op jit(solution)/shard_map/ppermute | solution.py:409
  63.1 15.5 %collective-permute-done.2.refs_4_ = bf16[320,1792]{1,0:T(8,128)(2,1)} collective-permute-done((bf16[320,1792]{1,0:T(8,128)(2,1)}, bf16[320,1792]{1,0:T(8,128)(2,1)}, u32[]{:S(2)}, u32[]{:S(2)}) %collective-permute-start.2) | collective-permute-done | bytes 1146912 | tf_op jit(solution)/shard_map/ppermute | solution.py:409
  78.6 19.2 %collective-permute-done.4.refs_6_ = bf16[320,1792]{1,0:T(8,128)(2,1)} collective-permute-done((bf16[320,1792]{1,0:T(8,128)(2,1)}, bf16[320,1792]{1,0:T(8,128)(2,1)}, u32[]{:S(2)}, u32[]{:S(2)}) %collective-permute-start.4) | collective-permute-done | bytes 1146912 | tf_op jit(solution)/shard_map/ppermute | solution.py:409
  99.1 69.0 %all-gather.8.cloned.1.call-done.w_ref = bf16[2560,3968]{1,0:T(8,128)(2,1)} async-done(((bf16[320,3968]{1,0:T(8,128)(2,1)}), bf16[2560,3968]{1,0:T(8,128)(2,1)}) %all-gather.8.cloned.1.call-update) | async-done | bytes 20316176 | tf_op jit(solution)/shard_map/all_gather | solution.py:627
  174.3 19.3 %project.1.q_ref = bf16[512,3840]{1,0:T(8,128)(2,1)} custom-call(bf16[512,2560]{1,0:T(8,128)(2,1)} %multiply_convert_fusion.n_ref.x_ref, bf16[2560,3968]{1,0:T(8,128)(2,1)} %all-gather.8.cloned.1.call-done.w_ref, f32[512,640]{1,0:T(8,128)S(1)} %copy-done.2, f32[512,640]{1,0:T(8,128)S(1)} %get-tuple-element.275.up_ref.refs_6_, ...), custom_call_target="tpu_custom_call" | custom-call | flops 5100273664 | bytes 65536 | tf_op jit(solution)/shard_map/project/pallas_call | solution.py:61
  198.5 13.9 collective-permute-done.6.refs_1_
  217.3 23.5 %attend.2 = (bf16[256,2560]{1,0:T(8,128)(2,1)S(1)}, f32[256,256]{1,0:T(8,128)S(1)}) custom-call(bf16[512,3840]{1,0:T(8,128)(2,1)} %project.1.q_ref, bf16[256,1280]{1,0:T(8,128)(2,1)S(1)} %get-tuple-element.246.refs_0_, bf16[256,1280]{1,0:T(8,128)(2,1)S(1)} %collective-permute-done.6.refs_1_, bf16[256,1280]{1,0:T(8,128)(2,1)S(1)} %collective-permute-done.7.refs_2_, ...), custom_call_target="tpu_custom_call" | custom-call | flops 6174015488 | bytes 65536 | tf_op jit(solution)/shard_map/attend/pallas_call | solution.py:97
  244.4 9.1 multiply_reduce_fusion.8
  256.3 51.5 %all-gather.12.cloned.1.call-done.g_ref.refs_2_ = bf16[1024,2560]{1,0:T(8,128)(2,1)} async-done(((bf16[256,2560]{1,0:T(8,128)(2,1)}), bf16[1024,2560]{1,0:T(8,128)(2,1)}) %all-gather.12.cloned.1.call-update) | async-done | bytes 5242896 | tf_op jit(solution)/shard_map/all_gather | solution.py:265
  311.1 13.3 collective-permute-done.9.refs_1_
  325.9 23.4 %attend.3 = (bf16[256,2560]{1,0:T(8,128)(2,1)S(1)}, f32[256,256]{1,0:T(8,128)S(1)}) custom-call(bf16[512,3840]{1,0:T(8,128)(2,1)} %project.1.q_ref, bf16[256,1280]{1,0:T(8,128)(2,1)S(1)} %get-tuple-element.245.refs_0_, bf16[256,1280]{1,0:T(8,128)(2,1)S(1)} %collective-permute-done.9.refs_1_, bf16[256,1280]{1,0:T(8,128)(2,1)S(1)} %collective-permute-done.10.refs_2_, ...), custom_call_target="tpu_custom_call" | custom-call | flops 6174015488 | bytes 65536 | tf_op jit(solution)/shard_map/attend/pallas_call | solution.py:97
  349.3 9.6 multiply_reduce_fusion.7
  364.6 4.7 columns_for.7
  374.1 4.8 collective-permute-done.13.refs_9_
  385.8 21.9 %weave.1.wg_ref.wu_ref.refs_2_.refs_3_ = bf16[2560,3584]{1,0:T(8,128)(2,1)} custom-call(s32[9]{0:T(128)} %stack.118.place_ref, bf16[320,1792]{1,0:T(8,128)(2,1)} %copy-done.49, bf16[320,1792]{1,0:T(8,128)(2,1)} %copy-done.48, bf16[320,1792]{1,0:T(8,128)(2,1)} %collective-permute-done.refs_2_, bf16[320,1792]{1,0:T(8,128)(2,1)} %collective-permute-done.1.refs_3_, ...), custom_call_target="tpu_custom_call" | custom-call | flops 5637144576 | bytes 65536 | tf_op jit(solution)/shard_map/weave/pallas_call | solution.py:378
  407.7 4.7 constant_dynamic-update-slice_fusion.1
  412.5 4.7 constant_dynamic-update-slice_fusion.wd_ref.b_ref
  417.2 36.7 %feed_forward.2 = (bf16[1024,1792]{1,0:T(8,128)(2,1)}, bf16[1024,1792]{1,0:T(8,128)(2,1)}, bf16[1024,1792]{1,0:T(8,128)(2,1)}) custom-call(bf16[1024,2560]{1,0:T(8,128)(2,1)} %all-gather.14.cloned.1.call-done.n_ref.refs_0_, bf16[1024,2560]{1,0:T(8,128)(2,1)} %all-gather.12.cloned.1.call-done.g_ref.refs_2_, ...), custom_call_target="tpu_custom_call" | custom-call | flops 9663676416 | bytes 65536 | tf_op jit(solution)/shard_map/feed_forward/pallas_call | solution.py:531
  458.0 26.5 %sum_nt.2 = bf16[1024,2560]{1,0:T(8,128)(2,1)} custom-call(bf16[1024,1792]{1,0:T(8,128)(2,1)} %get-tuple-element.100.refs_0_.refs_2_, bf16[1024,1792]{1,0:T(8,128)(2,1)} %get-tuple-element.91.refs_1_.refs_4_, bf16[2560,3584]{1,0:T(8,128)(2,1)} %weave.1.wg_ref.wu_ref.refs_2_.refs_3_, bf16[2560,3584]{1,0:T(8,128)(2,1)} %weave.1.wg_ref.wu_ref.refs_2_.refs_3_), custom_call_target="tpu_custom_call" | custom-call | flops 6979321856 | bytes 65536 | tf_op jit(solution)/shard_map/sum_nt/pallas_call | solution.py:552
  484.6 37.2 %all-gather.16.cloned.1.call-done.n_ref.refs_1_ = bf16[1024,2560]{1,0:T(8,128)(2,1)} async-done(((bf16[256,2560]{1,0:T(8,128)(2,1)}), bf16[1024,2560]{1,0:T(8,128)(2,1)}) %all-gather.16.cloned.1.call-update) | async-done | bytes 5242896 | tf_op jit(solution)/shard_map/all_gather | solution.py:265
  521.8 36.7 %feed_forward.3 = (bf16[1024,1792]{1,0:T(8,128)(2,1)}, bf16[1024,1792]{1,0:T(8,128)(2,1)}, bf16[1024,1792]{1,0:T(8,128)(2,1)}) custom-call(bf16[1024,2560]{1,0:T(8,128)(2,1)} %all-gather.16.cloned.1.call-done.n_ref.refs_1_, bf16[1024,2560]{1,0:T(8,128)(2,1)} %all-gather.18.cloned.1.call-done.g_ref.refs_3_, ...), custom_call_target="tpu_custom_call" | custom-call | flops 9663676416 | bytes 65536 | tf_op jit(solution)/shard_map/feed_forward/pallas_call | solution.py:531
  558.5 28.1 %sum_tn.4 = bf16[4,8,80,1792]{3,2,1,0:T(8,128)(2,1)} custom-call(bf16[1024,2560]{1,0:T(8,128)(2,1)} %all-gather.14.cloned.1.call-done.n_ref.refs_0_, bf16[1024,2560]{1,0:T(8,128)(2,1)} %all-gather.16.cloned.1.call-done.n_ref.refs_1_, bf16[1024,1792]{1,0:T(8,128)(2,1)} %get-tuple-element.100.refs_0_.refs_2_, ...), custom_call_target="tpu_custom_call" | custom-call | flops 6979321856 | bytes 65536 | tf_op jit(solution)/shard_map/sum_tn/pallas_call | solution.py:502
  587.2 16.1 %sum_tn.5 = bf16[896,2560]{1,0:T(8,128)(2,1)} custom-call(bf16[1024,1792]{1,0:T(8,128)(2,1)} %get-tuple-element.103.refs_0_.a_ref, bf16[1024,1792]{1,0:T(8,128)(2,1)} %get-tuple-element.104.refs_1_.a_ref, bf16[1024,2560]{1,0:T(8,128)(2,1)} %all-gather.12.cloned.1.call-done.g_ref.refs_2_, bf16[1024,2560]{1,0:T(8,128)(2,1)} %all-gather.18.cloned.1.call-done.g_ref.refs_3_), custom_call_target="tpu_custom_call" | custom-call | flops 4294967296 | bytes 65536 | tf_op jit(solution)/shard_map/sum_tn/pallas_call | solution.py:502
  603.3 28.7 %sum_tn.6 = bf16[4,8,80,1792]{3,2,1,0:T(8,128)(2,1)} custom-call(bf16[1024,2560]{1,0:T(8,128)(2,1)} %all-gather.14.cloned.1.call-done.n_ref.refs_0_, bf16[1024,2560]{1,0:T(8,128)(2,1)} %all-gather.16.cloned.1.call-done.n_ref.refs_1_, bf16[1024,1792]{1,0:T(8,128)(2,1)} %get-tuple-element.100.refs_0_.refs_2_, ...), custom_call_target="tpu_custom_call" | custom-call | flops 6979321856 | bytes 65536 | tf_op jit(solution)/shard_map/sum_tn/pallas_call | solution.py:502
  642.5 17.3 %sum_tn.7 = bf16[896,2560]{1,0:T(8,128)(2,1)} custom-call(bf16[1024,1792]{1,0:T(8,128)(2,1)} %get-tuple-element.103.refs_0_.a_ref, bf16[1024,1792]{1,0:T(8,128)(2,1)} %get-tuple-element.104.refs_1_.a_ref, bf16[1024,2560]{1,0:T(8,128)(2,1)} %all-gather.12.cloned.1.call-done.g_ref.refs_2_, bf16[1024,2560]{1,0:T(8,128)(2,1)} %all-gather.18.cloned.1.call-done.g_ref.refs_3_, ...), custom_call_target="tpu_custom_call" | custom-call | flops 4294967296 | bytes 65536 | tf_op jit(solution)/shard_map/sum_tn/pallas_call | solution.py:502
  659.8 25.9 %sum_nt.3 = bf16[1024,2560]{1,0:T(8,128)(2,1)} custom-call(bf16[1024,1792]{1,0:T(8,128)(2,1)} %get-tuple-element.102.refs_3_.refs_0_, bf16[1024,1792]{1,0:T(8,128)(2,1)} %get-tuple-element.96.refs_5_.refs_1_, bf16[2560,3584]{1,0:T(8,128)(2,1)} %weave.1.wg_ref.wu_ref.refs_2_.refs_3_, bf16[2560,3584]{1,0:T(8,128)(2,1)} %weave.1.wg_ref.wu_ref.refs_2_.refs_3_), custom_call_target="tpu_custom_call" | custom-call | flops 6979321856 | bytes 65536 | tf_op jit(solution)/shard_map/sum_nt/pallas_call | solution.py:552
  685.6 16.0 %plain_nn.2 = bf16[1024,2560]{1,0:T(8,128)(2,1)} custom-call(bf16[1024,1792]{1,0:T(8,128)(2,1)} %get-tuple-element.103.refs_0_.a_ref, bf16[1792,2560]{1,0:T(8,128)(2,1)} %constant_dynamic-update-slice_fusion.wd_ref.b_ref), custom_call_target="tpu_custom_call" | custom-call | flops 4294967296 | bytes 65536 | tf_op jit(solution)/shard_map/plain_nn/pallas_call | solution.py:571
  701.6 16.2 %plain_nn.3 = bf16[1024,2560]{1,0:T(8,128)(2,1)} custom-call(bf16[1024,1792]{1,0:T(8,128)(2,1)} %get-tuple-element.104.refs_1_.a_ref, bf16[1792,2560]{1,0:T(8,128)(2,1)} %constant_dynamic-update-slice_fusion.wd_ref.b_ref), custom_call_target="tpu_custom_call" | custom-call | flops 4294967296 | bytes 65536 | tf_op jit(solution)/shard_map/plain_nn/pallas_call | solution.py:571
  721.2 4.8 multiply_reduce_fusion.4
  726.0 5.7 fusion.70
  731.7 9.9 convolution_convert_fusion.4.dctx_ref
  746.5 27.3 %attend_back.4 = (bf16[256,2560]{1,0:T(8,128)(2,1)}, bf16[256,1280]{1,0:T(8,128)(2,1)S(1)}, bf16[256,1280]{1,0:T(8,128)(2,1)S(1)}, bf16[256,1280]{1,0:T(8,128)(2,1)S(1)}, bf16[256,1280]{1,0:T(8,128)(2,1)}) custom-call(bf16[512,3840]{1,0:T(8,128)(2,1)} %project.1.q_ref, bf16[256,2560]{1,0:T(8,128)(2,1)} %convolution_convert_fusion.4.dctx_ref, ...), custom_call_target="tpu_custom_call" | custom-call | flops 26843545600 | bytes 65536 | tf_op jit(solution)/shard_map/attend_back/pallas_call | solution.py:160
  773.8 27.0 %attend_back.5 = (bf16[256,2560]{1,0:T(8,128)(2,1)}, bf16[256,1280]{1,0:T(8,128)(2,1)S(1)}, bf16[256,1280]{1,0:T(8,128)(2,1)S(1)}, bf16[256,1280]{1,0:T(8,128)(2,1)S(1)}, bf16[256,1280]{1,0:T(8,128)(2,1)}) custom-call(bf16[512,3840]{1,0:T(8,128)(2,1)} %project.1.q_ref, ...), custom_call_target="tpu_custom_call", output_to_operand_aliasing={{0}: (12, {}), {1}: (13, {}), {2}: (14, {}), {3}: (15, {}),... | custom-call | flops 26843545600 | bytes 65536 | tf_op jit(solution)/shard_map/attend_back/pallas_call | solution.py:160
  819.0 5.2 fusion.69
  825.3 9.7 convolution_convert_fusion.3.dctx_ref
  835.0 9.0 convolution_convert_fusion.1
  857.3 26.8 %attend_back.6 = (bf16[256,2560]{1,0:T(8,128)(2,1)}, bf16[256,1280]{1,0:T(8,128)(2,1)S(1)}, bf16[256,1280]{1,0:T(8,128)(2,1)S(1)}, bf16[256,1280]{1,0:T(8,128)(2,1)S(1)}, bf16[256,1280]{1,0:T(8,128)(2,1)S(1)}) custom-call(bf16[512,3840]{1,0:T(8,128)(2,1)} %project.1.q_ref, bf16[256,2560]{1,0:T(8,128)(2,1)} %convolution_convert_fusion.3.dctx_ref, ...), custom_call_target="tpu_custom_call" | custom-call | flops 26843545600 | bytes 65536 | tf_op jit(solution)/shard_map/attend_back/pallas_call | solution.py:160
  888.4 33.5 %collective-permute-done.42 = bf16[320,2560]{1,0:T(8,128)(2,1)} collective-permute-done((bf16[320,2560]{1,0:T(8,128)(2,1)}, bf16[320,2560]{1,0:T(8,128)(2,1)}, u32[]{:S(2)}, u32[]{:S(2)}) %collective-permute-start.42) | collective-permute-done | bytes 1638432 | tf_op jit(solution)/shard_map/ppermute | solution.py:273
  923.0 5.0 fusion.27
  928.0 4.9 collective-permute-done.34
  933.0 13.5 collective-permute-done.36
  947.3 27.2 %attend_back.7 = (bf16[256,2560]{1,0:T(8,128)(2,1)}, bf16[256,1280]{1,0:T(8,128)(2,1)S(1)}, bf16[256,1280]{1,0:T(8,128)(2,1)S(1)}, bf16[256,1280]{1,0:T(8,128)(2,1)S(1)}, bf16[256,1280]{1,0:T(8,128)(2,1)S(1)}) custom-call(bf16[512,3840]{1,0:T(8,128)(2,1)} %project.1.q_ref, ...), custom_call_target="tpu_custom_call", output_to_operand_aliasing={{0}: (12, {}), {1}: (13, {}), {2}: (14, {}), {3}: (15, {}),... | custom-call | flops 26843545600 | bytes 65536 | tf_op jit(solution)/shard_map/attend_back/pallas_call | solution.py:160
  975.4 20.1 %all-reduce.6.cloned.1.call-done = bf16[896,2560]{1,0:T(8,128)(2,1)} async-done(((bf16[896,2560]{1,0:T(8,128)(2,1)}), bf16[896,2560]{1,0:T(8,128)(2,1)}) %all-reduce.6.cloned.1.call-update) | async-done | bytes 4587536 | tf_op jit(solution)/shard_map/psum | solution.py:708
  1000.4 5.5 reshape.284
  1018.6 8.9 convolution_convert_fusion
  1035.9 11.8 fusion
  1047.6 11.5 collective-permute-done.29.other_ref
  1063.0 43.0 %collective-permute-done.47.other_ref = bf16[256,1280]{1,0:T(8,128)(2,1)S(1)} collective-permute-done((bf16[256,1280]{1,0:T(8,128)(2,1)S(1)}, bf16[256,1280]{1,0:T(8,128)(2,1)S(1)}, u32[]{:S(2)}, u32[]{:S(2)}) %collective-permute-start.47) | collective-permute-done | bytes 655392 | tf_op jit(solution)/shard_map/ppermute | solution.py:595
  1112.2 10.9 multiply_reduce_fusion
  1123.5 5.9 convolution_convert_fusion.2
  1131.5 6.0 copy.67
  1142.2 4.9 fusion.24
  1147.1 14.1 collective-permute-done.56
  1161.1 19.4 %collective-permute-done.58 = bf16[320,1408]{1,0:T(8,128)(2,1)S(1)} collective-permute-done((bf16[320,1408]{1,0:T(8,128)(2,1)S(1)}, bf16[320,1408]{1,0:T(8,128)(2,1)S(1)}, u32[]{:S(2)}, u32[]{:S(2)}) %collective-permute-start.58) | collective-permute-done | bytes 901152 | tf_op jit(solution)/shard_map/ppermute | solution.py:273
  1183.8 4.7 dynamic-slice_bitcast_fusion.21
  1194.7 4.9 convert_element_type.330
  1199.6 18.6 %collective-permute-done.50 = bf16[256,2560]{1,0:T(8,128)(2,1)S(1)} collective-permute-done((bf16[256,2560]{1,0:T(8,128)(2,1)}, bf16[256,2560]{1,0:T(8,128)(2,1)S(1)}, u32[]{:S(2)}, u32[]{:S(2)}) %collective-permute-start.50) | collective-permute-done | bytes 1310752 | tf_op jit(solution)/shard_map/ppermute | solution.py:273
  1223.6 23.5 %collective-permute-done.52 = bf16[256,2560]{1,0:T(8,128)(2,1)S(1)} collective-permute-done((bf16[256,2560]{1,0:T(8,128)(2,1)}, bf16[256,2560]{1,0:T(8,128)(2,1)S(1)}, u32[]{:S(2)}, u32[]{:S(2)}) %collective-permute-start.52) | collective-permute-done | bytes 1310752 | tf_op jit(solution)/shard_map/ppermute | solution.py:273
  1247.9 26.6 %collective-permute-done.53 = bf16[256,2560]{1,0:T(8,128)(2,1)S(1)} collective-permute-done((bf16[256,2560]{1,0:T(8,128)(2,1)}, bf16[256,2560]{1,0:T(8,128)(2,1)S(1)}, u32[]{:S(2)}, u32[]{:S(2)}) %collective-permute-start.53) | collective-permute-done | bytes 1310752 | tf_op jit(solution)/shard_map/ppermute | solution.py:273
  1275.0 28.3 %collective-permute-done.55 = bf16[256,2560]{1,0:T(8,128)(2,1)S(1)} collective-permute-done((bf16[256,2560]{1,0:T(8,128)(2,1)}, bf16[256,2560]{1,0:T(8,128)(2,1)S(1)}, u32[]{:S(2)}, u32[]{:S(2)}) %collective-permute-start.55) | collective-permute-done | bytes 1310752 | tf_op jit(solution)/shard_map/ppermute | solution.py:273
  1305.8 50.9 %all-reduce.8.cloned.1.call-done = (bf16[320,1408]{1,0:T(8,128)(2,1)}, bf16[320,2560]{1,0:T(8,128)(2,1)}, bf16[320,2560]{1,0:T(8,128)(2,1)}) async-done(((bf16[320,1408]{1,0:T(8,128)(2,1)}, bf16[320,2560]{1,0:T(8,128)(2,1)}, bf16[320,2560]{1,0:T(8,128)(2,1)}), (bf16[320,1408]{1,0:T(8,128)(2,1)}, bf16[320,2560]{1,0:T(8,128)(2,1)}, bf16[320,2560]{1,0:T(8,128)(2,1)})) %all-reduce.8.cloned.1.call-update) | async-done | bytes 4177936 | tf_op jit(solution)/shard_map/psum | solution.py:767
  1367.9 152.0 %all-gather.20.cloned.1.call-done = bf16[320,14336]{1,0:T(8,128)(2,1)} async-done(((bf16[80,14336]{1,0:T(8,128)(2,1)}), bf16[320,14336]{1,0:T(8,128)(2,1)}) %all-gather.20.cloned.1.call-update) | async-done | bytes 9175056 | tf_op jit(solution)/shard_map/all_gather | solution.py:749
  1519.9 12.9 slice_convert_fusion
  (410 shorter events, 210.4 us)
Async XLA Ops:
  7.2 160.9 %all-gather.8.cloned.1.call-start = ((), (), s32[]{:S(2)}) async-start(), calls=%async_computation.1 | async-start | bytes 22855680 | tf_op jit(solution)/shard_map/all_gather | solution.py:627
  13.4 231.0 %all-gather.10.cloned.1.call-start = ((), (), s32[]{:S(2)}) async-start(), calls=%async_computation.2 | async-start | bytes 14745600 | tf_op jit(solution)/shard_map/all_gather | solution.py:628
  14.1 293.7 %all-gather.12.cloned.1.call-start = ((), (), s32[]{:S(2)}) async-start(), calls=%async_computation.3 | async-start | bytes 6553600 | tf_op jit(solution)/shard_map/all_gather | solution.py:265
  17.8 44.2 %collective-permute-start = (bf16[320,1792]{1,0:T(8,128)(2,1)}, bf16[320,1792]{1,0:T(8,128)(2,1)}, u32[]{:S(2)}, u32[]{:S(2)}) collective-permute-start(bf16[320,1792]{1,0:T(8,128)(2,1)} %columns_for.4), channel_id=1, source_target_pairs={{0,8},{4,12},{8,0},{12,4},{16,24},{20,28},{24,16},{28,20},{1,9},{5... | collective-permute-start | bytes 3440648 | tf_op jit(solution)/shard_map/ppermute | solution.py:409
  23.5 55.2 %collective-permute-start.2 = (bf16[320,1792]{1,0:T(8,128)(2,1)}, bf16[320,1792]{1,0:T(8,128)(2,1)}, u32[]{:S(2)}, u32[]{:S(2)}) collective-permute-start(bf16[320,1792]{1,0:T(8,128)(2,1)} %columns_for.5), channel_id=1, source_target_pairs={{0,16},{4,20},{8,24},{12,28},{16,0},{20,4},{24,8},{28,12},{1,17},{... | collective-permute-start | bytes 3440648 | tf_op jit(solution)/shard_map/ppermute | solution.py:409
  28.8 69.0 %collective-permute-start.4 = (bf16[320,1792]{1,0:T(8,128)(2,1)}, bf16[320,1792]{1,0:T(8,128)(2,1)}, u32[]{:S(2)}, u32[]{:S(2)}) collective-permute-start(bf16[320,1792]{1,0:T(8,128)(2,1)} %columns_for.6), channel_id=1, source_target_pairs={{0,24},{4,28},{8,16},{12,20},{16,8},{20,12},{24,0},{28,4},{1,25},{... | collective-permute-start | bytes 3440648 | tf_op jit(solution)/shard_map/ppermute | solution.py:409
  61.9 112.3 %collective-permute-start.1 = (bf16[320,1792]{1,0:T(8,128)(2,1)}, bf16[320,1792]{1,0:T(8,128)(2,1)}, u32[]{:S(2)}, u32[]{:S(2)}) collective-permute-start(bf16[320,1792]{1,0:T(8,128)(2,1)} %collective-permute-done.refs_2_), channel_id=1, source_target_pairs={{0,1},{1,0},{2,3},{3,2},{4,5},{5,4},{6,7},{7,6},{8,9},{9,8},{10,11... | collective-permute-start | bytes 3440648 | tf_op jit(solution)/shard_map/ppermute | solution.py:412
  78.6 95.6 %collective-permute-start.3 = (bf16[320,1792]{1,0:T(8,128)(2,1)}, bf16[320,1792]{1,0:T(8,128)(2,1)}, u32[]{:S(2)}, u32[]{:S(2)}) collective-permute-start(bf16[320,1792]{1,0:T(8,128)(2,1)} %collective-permute-done.2.refs_4_), channel_id=1, source_target_pairs={{0,1},{1,0},{2,3},{3,2},{4,5},{5,4},{6,7},{7,6},{8,9},{9,8},{10,11... | collective-permute-start | bytes 3440648 | tf_op jit(solution)/shard_map/ppermute | solution.py:412
  97.8 76.4 %collective-permute-start.5 = (bf16[320,1792]{1,0:T(8,128)(2,1)}, bf16[320,1792]{1,0:T(8,128)(2,1)}, u32[]{:S(2)}, u32[]{:S(2)}) collective-permute-start(bf16[320,1792]{1,0:T(8,128)(2,1)} %collective-permute-done.4.refs_6_), channel_id=1, source_target_pairs={{0,1},{1,0},{2,3},{3,2},{4,5},{5,4},{6,7},{7,6},{8,9},{9,8},{10,11... | collective-permute-start | bytes 3440648 | tf_op jit(solution)/shard_map/ppermute | solution.py:412
  193.6 223.6 %all-gather.14.cloned.1.call-start = ((), (), s32[]{:S(2)}) async-start(), calls=%async_computation.4 | async-start | bytes 6553600 | tf_op jit(solution)/shard_map/all_gather | solution.py:265
  195.2 17.2 %collective-permute-start.6 = (bf16[256,1280]{1,0:T(8,128)(2,1)S(1)}, bf16[256,1280]{1,0:T(8,128)(2,1)S(1)}, u32[]{:S(2)}, u32[]{:S(2)}) collective-permute-start(bf16[256,1280]{1,0:T(8,128)(2,1)S(1)} %get-tuple-element.246.refs_0_), channel_id=1, source_target_pairs={{0,1},{1,2},{2,3},{4,5},{5,6},{6,7},{8,9},{9,10},{10,11},{12,13},{... | collective-permute-start | bytes 1966088 | tf_op jit(solution)/shard_map/ppermute | solution.py:662
  307.9 150.2 %all-gather.18.cloned.1.call-start = ((), (), s32[]{:S(2)}) async-start(), calls=%async_computation.6 | async-start | bytes 6553600 | tf_op jit(solution)/shard_map/all_gather | solution.py:265
  307.9 16.5 %collective-permute-start.9 = (bf16[256,1280]{1,0:T(8,128)(2,1)S(1)}, bf16[256,1280]{1,0:T(8,128)(2,1)S(1)}, u32[]{:S(2)}, u32[]{:S(2)}) collective-permute-start(bf16[256,1280]{1,0:T(8,128)(2,1)S(1)} %get-tuple-element.245.refs_0_), channel_id=1, source_target_pairs={{0,1},{1,2},{2,3},{4,5},{5,6},{6,7},{8,9},{9,10},{10,11},{12,13},{... | collective-permute-start | bytes 1966088 | tf_op jit(solution)/shard_map/ppermute | solution.py:662
  361.8 160.0 %all-gather.16.cloned.1.call-start = ((), (), s32[]{:S(2)}) async-start(), calls=%async_computation.5 | async-start | bytes 6553600 | tf_op jit(solution)/shard_map/all_gather | solution.py:265
  362.4 488.6 %reduce-scatter.2.cloned.1.call-start = ((), (), s32[]{:S(2)}) async-start(), calls=%async_computation.7 | async-start | bytes 11468800 | tf_op jit(solution)/shard_map/reduce_scatter | solution.py:706
  362.4 50.1 %collective-permute-start.20 = (bf16[896,2560]{1,0:T(8,128)(2,1)}, bf16[896,2560]{1,0:T(8,128)(2,1)}, u32[]{:S(2)}, u32[]{:S(2)}) collective-permute-start(bf16[896,2560]{1,0:T(8,128)(2,1)} %param.23), channel_id=1, source_target_pairs={{0,4},{4,0},{8,12},{12,8},{16,20},{20,16},{24,28},{28,24},{1,5},{5... | collective-permute-start | bytes 13762568 | tf_op jit(solution)/shard_map/ppermute | solution.py:256
  371.2 7.7 collective-permute-start.13
  371.7 8.2 collective-permute-start.14
  371.8 9.4 collective-permute-start.16
  374.0 8.2 collective-permute-start.18
  586.5 16.8 %collective-permute-start.21 = (bf16[4,8,80,1792]{3,2,1,0:T(8,128)(2,1)}, bf16[4,8,80,1792]{3,2,1,0:T(8,128)(2,1)}, u32[]{:S(2)}, u32[]{:S(2)}) collective-permute-start(bf16[4,8,80,1792]{3,2,1,0:T(8,128)(2,1)} %sum_tn.4), channel_id=1, source_target_pairs={{0,4},{4,0},{8,12},{12,8},{16,20},{20,16},{24,28},{28,24},{1,5},{5... | collective-permute-start | bytes 27525128 | tf_op jit(solution)/shard_map/ppermute | solution.py:256
  632.0 363.4 %all-reduce.6.cloned.1.call-start = ((), (), s32[]{:S(2)}) async-start(), calls=%async_computation.8 | async-start | bytes 9175040 | tf_op jit(solution)/shard_map/psum | solution.py:708
  632.1 10.4 collective-permute-start.22
  639.8 81.3 %collective-permute-start.24 = (bf16[256,2560]{1,0:T(8,128)(2,1)}, bf16[256,2560]{1,0:T(8,128)(2,1)}, u32[]{:S(2)}, u32[]{:S(2)}) collective-permute-start(bf16[256,2560]{1,0:T(8,128)(2,1)} %get-tuple-element.236), channel_id=1, source_target_pairs={{0,8},{4,12},{8,0},{12,4},{16,24},{20,28},{24,16},{28,20},{1,9},{5... | collective-permute-start | bytes 3932168 | tf_op jit(solution)/shard_map/ppermute | solution.py:273
  641.0 80.1 %collective-permute-start.25 = (bf16[256,2560]{1,0:T(8,128)(2,1)}, bf16[256,2560]{1,0:T(8,128)(2,1)}, u32[]{:S(2)}, u32[]{:S(2)}) collective-permute-start(bf16[256,2560]{1,0:T(8,128)(2,1)} %get-tuple-element.235), channel_id=1, source_target_pairs={{0,16},{4,20},{8,24},{12,28},{16,0},{20,4},{24,8},{28,12},{1,17},{... | collective-permute-start | bytes 3932168 | tf_op jit(solution)/shard_map/ppermute | solution.py:273
  641.6 79.6 %collective-permute-start.26 = (bf16[256,2560]{1,0:T(8,128)(2,1)}, bf16[256,2560]{1,0:T(8,128)(2,1)}, u32[]{:S(2)}, u32[]{:S(2)}) collective-permute-start(bf16[256,2560]{1,0:T(8,128)(2,1)} %get-tuple-element.234), channel_id=1, source_target_pairs={{0,24},{4,28},{8,16},{12,20},{16,8},{20,12},{24,0},{28,4},{1,25},{... | collective-permute-start | bytes 3932168 | tf_op jit(solution)/shard_map/ppermute | solution.py:273
  743.8 70.1 %collective-permute-start.30 = (bf16[256,2560]{1,0:T(8,128)(2,1)}, bf16[256,2560]{1,0:T(8,128)(2,1)}, u32[]{:S(2)}, u32[]{:S(2)}) collective-permute-start(bf16[256,2560]{1,0:T(8,128)(2,1)} %get-tuple-element.240), channel_id=1, source_target_pairs={{0,8},{4,12},{8,0},{12,4},{16,24},{20,28},{24,16},{28,20},{1,9},{5... | collective-permute-start | bytes 3932168 | tf_op jit(solution)/shard_map/ppermute | solution.py:273
  745.0 69.5 %collective-permute-start.31 = (bf16[256,2560]{1,0:T(8,128)(2,1)}, bf16[256,2560]{1,0:T(8,128)(2,1)}, u32[]{:S(2)}, u32[]{:S(2)}) collective-permute-start(bf16[256,2560]{1,0:T(8,128)(2,1)} %get-tuple-element.239), channel_id=1, source_target_pairs={{0,16},{4,20},{8,24},{12,28},{16,0},{20,4},{24,8},{28,12},{1,17},{... | collective-permute-start | bytes 3932168 | tf_op jit(solution)/shard_map/ppermute | solution.py:273
  745.6 70.0 %collective-permute-start.32 = (bf16[256,2560]{1,0:T(8,128)(2,1)}, bf16[256,2560]{1,0:T(8,128)(2,1)}, u32[]{:S(2)}, u32[]{:S(2)}) collective-permute-start(bf16[256,2560]{1,0:T(8,128)(2,1)} %get-tuple-element.238), channel_id=1, source_target_pairs={{0,24},{4,28},{8,16},{12,20},{16,8},{20,12},{24,0},{28,4},{1,25},{... | collective-permute-start | bytes 3932168 | tf_op jit(solution)/shard_map/ppermute | solution.py:273
  803.4 10.3 collective-permute-start.27
  809.0 25.9 %collective-permute-start.37 = (bf16[512,1280]{1,0:T(8,128)(2,1)}, bf16[512,1280]{1,0:T(8,128)(2,1)}, u32[]{:S(2)}, u32[]{:S(2)}) collective-permute-start(bf16[512,1280]{1,0:T(8,128)(2,1)} %get-tuple-element.125), channel_id=1, source_target_pairs={{0,4},{4,0},{8,12},{12,8},{16,20},{20,16},{24,28},{28,24},{1,5},{5... | collective-permute-start | bytes 3932168 | tf_op jit(solution)/shard_map/ppermute | solution.py:256
  811.0 545.7 %all-reduce.8.cloned.1.call-start = ((), (), s32[]{:S(2)}) async-start(), calls=%async_computation.10 | async-start | bytes 8355840 | tf_op jit(solution)/shard_map/psum | solution.py:767
  813.7 21.2 %collective-permute-start.38 = (bf16[256,2560]{1,0:T(8,128)(2,1)}, bf16[256,2560]{1,0:T(8,128)(2,1)S(1)}, u32[]{:S(2)}, u32[]{:S(2)}) collective-permute-start(bf16[256,2560]{1,0:T(8,128)(2,1)} %get-tuple-element.219), channel_id=1, source_target_pairs={{0,4},{4,0},{8,12},{12,8},{16,20},{20,16},{24,28},{28,24},{1,5},{5... | collective-permute-start | bytes 3932168 | tf_op jit(solution)/shard_map/ppermute | solution.py:256
  813.9 204.7 %collective-permute-start.43 = (bf16[256,2560]{1,0:T(8,128)(2,1)}, bf16[256,2560]{1,0:T(8,128)(2,1)}, u32[]{:S(2)}, u32[]{:S(2)}) collective-permute-start(bf16[256,2560]{1,0:T(8,128)(2,1)} %get-tuple-element.120), channel_id=1, source_target_pairs={{0,4},{4,0},{8,12},{12,8},{16,20},{20,16},{24,28},{28,24},{1,5},{5... | collective-permute-start | bytes 3932168 | tf_op jit(solution)/shard_map/ppermute | solution.py:256
  814.5 9.8 collective-permute-start.28
  824.2 10.8 collective-permute-start.39
  848.3 37.2 %collective-permute-start.40 = (bf16[320,2560]{1,0:T(8,128)(2,1)}, bf16[320,2560]{1,0:T(8,128)(2,1)}, u32[]{:S(2)}, u32[]{:S(2)}) collective-permute-start(bf16[320,2560]{1,0:T(8,128)(2,1)} %get-tuple-element.226), channel_id=1, source_target_pairs={{0,8},{4,12},{8,0},{12,4},{16,24},{20,28},{24,16},{28,20},{1,9},{5... | collective-permute-start | bytes 4915208 | tf_op jit(solution)/shard_map/ppermute | solution.py:273
  849.7 37.3 %collective-permute-start.41 = (bf16[320,2560]{1,0:T(8,128)(2,1)}, bf16[320,2560]{1,0:T(8,128)(2,1)}, u32[]{:S(2)}, u32[]{:S(2)}) collective-permute-start(bf16[320,2560]{1,0:T(8,128)(2,1)} %get-tuple-element.228), channel_id=1, source_target_pairs={{0,16},{4,20},{8,24},{12,28},{16,0},{20,4},{24,8},{28,12},{1,17},{... | collective-permute-start | bytes 4915208 | tf_op jit(solution)/shard_map/ppermute | solution.py:273
  850.4 71.5 %collective-permute-start.42 = (bf16[320,2560]{1,0:T(8,128)(2,1)}, bf16[320,2560]{1,0:T(8,128)(2,1)}, u32[]{:S(2)}, u32[]{:S(2)}) collective-permute-start(bf16[320,2560]{1,0:T(8,128)(2,1)} %get-tuple-element.227), channel_id=1, source_target_pairs={{0,24},{4,28},{8,16},{12,20},{16,8},{20,12},{24,0},{28,4},{1,25},{... | collective-permute-start | bytes 4915208 | tf_op jit(solution)/shard_map/ppermute | solution.py:273
  852.7 31.5 %collective-permute-start.33 = (bf16[4,80,1792]{2,1,0:T(8,128)(2,1)S(1)}, bf16[4,80,1792]{2,1,0:T(8,128)(2,1)S(1)}, u32[]{:S(2)}, u32[]{:S(2)}) collective-permute-start(bf16[4,80,1792]{2,1,0:T(8,128)(2,1)S(1)} %get-tuple-element.257), channel_id=1, source_target_pairs={{0,4},{4,0},{8,12},{12,8},{16,20},{20,16},{24,28},{28,24},{1,5},{5... | collective-permute-start | bytes 3440648 | tf_op jit(solution)/shard_map/ppermute | solution.py:256
  884.2 129.4 %collective-permute-start.23 = (bf16[512,1280]{1,0:T(8,128)(2,1)}, bf16[512,1280]{1,0:T(8,128)(2,1)}, u32[]{:S(2)}, u32[]{:S(2)}) collective-permute-start(bf16[512,1280]{1,0:T(8,128)(2,1)} %get-tuple-element.107), channel_id=1, source_target_pairs={{0,4},{4,0},{8,12},{12,8},{16,20},{20,16},{24,28},{28,24},{1,5},{5... | collective-permute-start | bytes 3932168 | tf_op jit(solution)/shard_map/ppermute | solution.py:256
  885.5 47.4 %collective-permute-start.34 = (bf16[1,2,80,1792]{3,2,1,0:T(8,128)(2,1)S(1)}, bf16[1,2,80,1792]{3,2,1,0:T(8,128)(2,1)S(1)}, u32[]{:S(2)}, u32[]{:S(2)}) collective-permute-start(bf16[1,2,80,1792]{3,2,1,0:T(8,128)(2,1)S(1)} %get-tuple-element.254), channel_id=1, source_target_pairs={{0,8},{4,12},{8,0},{12,4},{16,24},{20,28},{24,16},{28,20},{1,9},{5... | collective-permute-start | bytes 1720328 | tf_op jit(solution)/shard_map/ppermute | solution.py:300
  887.0 46.0 %collective-permute-start.35 = (bf16[1,2,80,1792]{3,2,1,0:T(8,128)(2,1)S(1)}, bf16[1,2,80,1792]{3,2,1,0:T(8,128)(2,1)S(1)}, u32[]{:S(2)}, u32[]{:S(2)}) collective-permute-start(bf16[1,2,80,1792]{3,2,1,0:T(8,128)(2,1)S(1)} %get-tuple-element.253), channel_id=1, source_target_pairs={{0,16},{4,20},{8,24},{12,28},{16,0},{20,4},{24,8},{28,12},{1,17},{... | collective-permute-start | bytes 1720328 | tf_op jit(solution)/shard_map/ppermute | solution.py:300
  921.9 24.6 %collective-permute-start.36 = (bf16[1,2,80,1792]{3,2,1,0:T(8,128)(2,1)S(1)}, bf16[1,2,80,1792]{3,2,1,0:T(8,128)(2,1)S(1)}, u32[]{:S(2)}, u32[]{:S(2)}) collective-permute-start(bf16[1,2,80,1792]{3,2,1,0:T(8,128)(2,1)S(1)} %get-tuple-element.252), channel_id=1, source_target_pairs={{0,24},{4,28},{8,16},{12,20},{16,8},{20,12},{24,0},{28,4},{1,25},{... | collective-permute-start | bytes 1720328 | tf_op jit(solution)/shard_map/ppermute | solution.py:300
  1010.8 7.8 collective-permute-start.44
  1011.6 47.6 %collective-permute-start.29 = (bf16[256,1280]{1,0:T(8,128)(2,1)}, bf16[256,1280]{1,0:T(8,128)(2,1)}, u32[]{:S(2)}, u32[]{:S(2)}) collective-permute-start(bf16[256,1280]{1,0:T(8,128)(2,1)} %add_convert_fusion.4), channel_id=1, source_target_pairs={{3,2},{2,1},{1,0},{7,6},{6,5},{5,4},{11,10},{10,9},{9,8},{15,14},{... | collective-permute-start | bytes 1966088 | tf_op jit(solution)/shard_map/ppermute | solution.py:595
  1017.9 16.5 %collective-permute-start.46 = (bf16[256,1280]{1,0:T(8,128)(2,1)S(1)}, bf16[256,1280]{1,0:T(8,128)(2,1)S(1)}, u32[]{:S(2)}, u32[]{:S(2)}) collective-permute-start(bf16[256,1280]{1,0:T(8,128)(2,1)S(1)} %add_convert_fusion.3), channel_id=1, source_target_pairs={{3,2},{2,1},{7,6},{6,5},{11,10},{10,9},{15,14},{14,13},{19,18},{18... | collective-permute-start | bytes 1966088 | tf_op jit(solution)/shard_map/ppermute | solution.py:595
  1031.8 109.2 %collective-permute-start.60 = (bf16[320,2560]{1,0:T(8,128)(2,1)}, bf16[320,2560]{1,0:T(8,128)(2,1)}, u32[]{:S(2)}, u32[]{:S(2)}) collective-permute-start(bf16[320,2560]{1,0:T(8,128)(2,1)} %get-tuple-element.223), channel_id=1, source_target_pairs={{0,8},{4,12},{8,0},{12,4},{16,24},{20,28},{24,16},{28,20},{1,9},{5... | collective-permute-start | bytes 4915208 | tf_op jit(solution)/shard_map/ppermute | solution.py:273
  1033.0 109.2 %collective-permute-start.61 = (bf16[320,2560]{1,0:T(8,128)(2,1)}, bf16[320,2560]{1,0:T(8,128)(2,1)}, u32[]{:S(2)}, u32[]{:S(2)}) collective-permute-start(bf16[320,2560]{1,0:T(8,128)(2,1)} %get-tuple-element.225), channel_id=1, source_target_pairs={{0,16},{4,20},{8,24},{12,28},{16,0},{20,4},{24,8},{28,12},{1,17},{... | collective-permute-start | bytes 4915208 | tf_op jit(solution)/shard_map/ppermute | solution.py:273
  1034.2 108.0 %collective-permute-start.62 = (bf16[320,2560]{1,0:T(8,128)(2,1)}, bf16[320,2560]{1,0:T(8,128)(2,1)}, u32[]{:S(2)}, u32[]{:S(2)}) collective-permute-start(bf16[320,2560]{1,0:T(8,128)(2,1)} %get-tuple-element.224), channel_id=1, source_target_pairs={{0,24},{4,28},{8,16},{12,20},{16,8},{20,12},{24,0},{28,4},{1,25},{... | collective-permute-start | bytes 4915208 | tf_op jit(solution)/shard_map/ppermute | solution.py:273
  1034.6 71.5 %collective-permute-start.47 = (bf16[256,1280]{1,0:T(8,128)(2,1)S(1)}, bf16[256,1280]{1,0:T(8,128)(2,1)S(1)}, u32[]{:S(2)}, u32[]{:S(2)}) collective-permute-start(bf16[256,1280]{1,0:T(8,128)(2,1)S(1)} %add_convert_fusion.2), channel_id=1, source_target_pairs={{3,2},{2,1},{1,0},{7,6},{6,5},{5,4},{11,10},{10,9},{9,8},{15,14},{... | collective-permute-start | bytes 1966088 | tf_op jit(solution)/shard_map/ppermute | solution.py:595
  1062.5 61.1 %collective-permute-start.48 = (bf16[256,1280]{1,0:T(8,128)(2,1)}, bf16[256,1280]{1,0:T(8,128)(2,1)}, u32[]{:S(2)}, u32[]{:S(2)}) collective-permute-start(bf16[256,1280]{1,0:T(8,128)(2,1)} %finish_keys.2), channel_id=1, source_target_pairs={{0,4},{4,0},{8,12},{12,8},{16,20},{20,16},{24,28},{28,24},{1,5},{5... | collective-permute-start | bytes 1966088 | tf_op jit(solution)/shard_map/ppermute | solution.py:256
  1110.4 13.1 collective-permute-start.49
  1139.5 21.7 %collective-permute-start.56 = (bf16[320,1408]{1,0:T(8,128)(2,1)S(1)}, bf16[320,1408]{1,0:T(8,128)(2,1)S(1)}, u32[]{:S(2)}, u32[]{:S(2)}) collective-permute-start(bf16[320,1408]{1,0:T(8,128)(2,1)S(1)} %get-tuple-element.247), channel_id=1, source_target_pairs={{0,8},{4,12},{8,0},{12,4},{16,24},{20,28},{24,16},{28,20},{1,9},{5... | collective-permute-start | bytes 2703368 | tf_op jit(solution)/shard_map/ppermute | solution.py:273
  1139.8 21.3 %collective-permute-start.57 = (bf16[320,1408]{1,0:T(8,128)(2,1)S(1)}, bf16[320,1408]{1,0:T(8,128)(2,1)S(1)}, u32[]{:S(2)}, u32[]{:S(2)}) collective-permute-start(bf16[320,1408]{1,0:T(8,128)(2,1)S(1)} %get-tuple-element.249), channel_id=1, source_target_pairs={{0,16},{4,20},{8,24},{12,28},{16,0},{20,4},{24,8},{28,12},{1,17},{... | collective-permute-start | bytes 2703368 | tf_op jit(solution)/shard_map/ppermute | solution.py:273
  1141.0 39.6 %collective-permute-start.58 = (bf16[320,1408]{1,0:T(8,128)(2,1)S(1)}, bf16[320,1408]{1,0:T(8,128)(2,1)S(1)}, u32[]{:S(2)}, u32[]{:S(2)}) collective-permute-start(bf16[320,1408]{1,0:T(8,128)(2,1)S(1)} %get-tuple-element.248), channel_id=1, source_target_pairs={{0,24},{4,28},{8,16},{12,20},{16,8},{20,12},{24,0},{28,4},{1,25},{... | collective-permute-start | bytes 2703368 | tf_op jit(solution)/shard_map/ppermute | solution.py:273
  1183.2 336.7 %all-gather.20.cloned.1.call-start = ((), (), s32[]{:S(2)}) async-start(), calls=%async_computation.9 | async-start | bytes 11468800 | tf_op jit(solution)/shard_map/all_gather | solution.py:749
  1188.6 29.6 %collective-permute-start.50 = (bf16[256,2560]{1,0:T(8,128)(2,1)}, bf16[256,2560]{1,0:T(8,128)(2,1)S(1)}, u32[]{:S(2)}, u32[]{:S(2)}) collective-permute-start(bf16[256,2560]{1,0:T(8,128)(2,1)} %get-tuple-element.232), channel_id=1, source_target_pairs={{0,8},{4,12},{8,0},{12,4},{16,24},{20,28},{24,16},{28,20},{1,9},{5... | collective-permute-start | bytes 3932168 | tf_op jit(solution)/shard_map/ppermute | solution.py:273
  1189.6 34.0 %collective-permute-start.51 = (bf16[256,2560]{1,0:T(8,128)(2,1)}, bf16[256,2560]{1,0:T(8,128)(2,1)S(1)}, u32[]{:S(2)}, u32[]{:S(2)}) collective-permute-start(bf16[256,2560]{1,0:T(8,128)(2,1)} %get-tuple-element.231), channel_id=1, source_target_pairs={{0,16},{4,20},{8,24},{12,28},{16,0},{20,4},{24,8},{28,12},{1,17},{... | collective-permute-start | bytes 3932168 | tf_op jit(solution)/shard_map/ppermute | solution.py:273
  1189.9 57.1 %collective-permute-start.52 = (bf16[256,2560]{1,0:T(8,128)(2,1)}, bf16[256,2560]{1,0:T(8,128)(2,1)S(1)}, u32[]{:S(2)}, u32[]{:S(2)}) collective-permute-start(bf16[256,2560]{1,0:T(8,128)(2,1)} %get-tuple-element.230), channel_id=1, source_target_pairs={{0,24},{4,28},{8,16},{12,20},{16,8},{20,12},{24,0},{28,4},{1,25},{... | collective-permute-start | bytes 3932168 | tf_op jit(solution)/shard_map/ppermute | solution.py:273
  1193.3 81.1 %collective-permute-start.53 = (bf16[256,2560]{1,0:T(8,128)(2,1)}, bf16[256,2560]{1,0:T(8,128)(2,1)S(1)}, u32[]{:S(2)}, u32[]{:S(2)}) collective-permute-start(bf16[256,2560]{1,0:T(8,128)(2,1)} %get-tuple-element.244), channel_id=1, source_target_pairs={{0,8},{4,12},{8,0},{12,4},{16,24},{20,28},{24,16},{28,20},{1,9},{5... | collective-permute-start | bytes 3932168 | tf_op jit(solution)/shard_map/ppermute | solution.py:273
  1194.4 80.6 %collective-permute-start.54 = (bf16[256,2560]{1,0:T(8,128)(2,1)}, bf16[256,2560]{1,0:T(8,128)(2,1)S(1)}, u32[]{:S(2)}, u32[]{:S(2)}) collective-permute-start(bf16[256,2560]{1,0:T(8,128)(2,1)} %get-tuple-element.243), channel_id=1, source_target_pairs={{0,16},{4,20},{8,24},{12,28},{16,0},{20,4},{24,8},{28,12},{1,17},{... | collective-permute-start | bytes 3932168 | tf_op jit(solution)/shard_map/ppermute | solution.py:273
  1218.2 85.1 %collective-permute-start.55 = (bf16[256,2560]{1,0:T(8,128)(2,1)}, bf16[256,2560]{1,0:T(8,128)(2,1)S(1)}, u32[]{:S(2)}, u32[]{:S(2)}) collective-permute-start(bf16[256,2560]{1,0:T(8,128)(2,1)} %get-tuple-element.242), channel_id=1, source_target_pairs={{0,24},{4,28},{8,16},{12,20},{16,8},{20,12},{24,0},{28,4},{1,25},{... | collective-permute-start | bytes 3932168 | tf_op jit(solution)/shard_map/ppermute | solution.py:273
  1357.6 9.3 collective-permute-start.59
  (93 other events, 1146.0 us)
Sparse Core Ops, SparseCore 0:
  13.5 154.5 all-gather.7
  170.0 74.3 all-gather.9
  246.8 60.9 all-gather.11
  309.5 61.4 all-gather.13
  373.3 84.7 all-gather.17
  460.3 61.4 all-gather.15
  632.2 156.1 reduce-scatter.1
  811.1 184.2 all-reduce.5
  1183.3 173.3 all-reduce.7
  1358.2 161.6 all-gather.19

commit v4 on v3

--- a/solution.py
+++ b/solution.py
@@ -764,7 +764,9 @@
         [lax.dynamic_index_in_dim(gain_blocks, c, 1, keepdims=False) for c in (core, 1 - core)], axis=2
     ).reshape(chips * d_own, 4)
     kv_shard = added(scatter_chips(jnp.concatenate([kv_half, jnp.pad(gain_lanes, ((0, 0), (0, 124)))], axis=1))).astype(bf16)
-    out_total, query_total, kv_total = lax.psum((tie(out_shard, down_total), query_shard, kv_shard), "sp")
+    out_total, query_total, kv_total = lax.psum(
+        (tie(out_shard, down_total), tie(query_shard, wide_total), tie(kv_shard, wide_total)), "sp"
+    )
     query_total, kv_total = query_total.astype(f32), kv_total.astype(f32)
     kv_piece = lambda k: kv_total[:, k * KW:(k + 1) * KW]
     gain_lanes = kv_total[:, 4 * KW:4 * KW + 4]

time: 1550 us -> 1470 us (0.948)
  waiting for transfers between devices: 720 us -> 579 us
  starting transfers between devices: 55.8 us -> 103 us
    all_gather x1, waiting for transfers between devices: 152 us -> 0.01 us  [body(): wide_total = lax.all_gather(wide_part, 'sp', axis=0, tiled=True)]
    ppermute x6, waiting for transfers between devices: 54.6 us -> 123 us  [hop(): self.running = lax.ppermute(tie(self.running, *before), 'sp', pairs)]
    ppermute x3, starting transfers between devices: 4.02 us -> 37 us  [exchange_chips(): lax.ppermute(block, 'fsdp', [(j, j ^ 2 * d) for j in range(parts)])]
    psum x1, waiting for transfers between devices: 20.1 us -> 0.15 us  [body(): down_total = lax.psum(down_grad, 'sp')]
    ppermute x21, waiting for transfers between devices: 165 us -> 147 us  [scatter_chips(): lax.ppermute(take(chip ^ d), 'fsdp', [(j, j ^ 2 * d) for j in range(parts)])]
    psum x1, waiting for transfers between devices: 50.9 us -> 34.6 us  [body(): lax.psum((tie(out_shard, down_total), tie(query_shard, wide_total), tie(k...]
  transfers between devices with their start and end apart: 73 -> 73, of which waited for: 31 -> 30; matrix products, arithmetic and copies ran while one was open for 15% -> 18% of each run, Pallas kernels for 25% -> 26%
where the time goes in v4:
time: 1470 us
  waiting for transfers between devices  579 us (39%)
  Pallas kernels  472 us (32%)
  other arithmetic  108 us (7%)
  starting transfers between devices  103 us (7%)
  local copies, waits for them, and re-layouts  101 us (7%)
  matrix products  86.3 us (6%)
  between operations  15.6 us (1%)
    ppermute x21, waiting for transfers between devices, scatter_chips(): lax.ppermute(take(chip ^ d), 'fsdp', [(j, j ^ 2 * d) for j in range(parts)])  147 us
    ppermute x6, waiting for transfers between devices, hop(): self.running = lax.ppermute(tie(self.running, *before), 'sp', pairs)  123 us
    pallas_call x4, Pallas kernels, attend_back(): pl.pallas_call(functools.partial(backward_kernel, blocks, len(before)), g...  108 us
    all_gather x4, waiting for transfers between devices, gather_chips(): lax.all_gather(x, 'fsdp', axis=0, tiled=True, axis_index_groups=same_core())  92.8 us
    pallas_call x4, Pallas kernels, sum_tn(): pl.pallas_call(functools.partial(sum_tn_kernel, segments, pairs), grid=(D...  89.9 us
    pallas_call x2, Pallas kernels, feed_forward(): pl.pallas_call(ffn_kernel, grid=(tiles,), in_specs=[full, full, pl.BlockS...  73.6 us
    all_gather x1, waiting for transfers between devices, body(): w_in = lax.all_gather(w_in, 'fsdp', axis=0, tiled=True)  69 us
    ppermute x3, waiting for transfers between devices, fetch(): lax.ppermute(x, 'fsdp', [(j, j ^ 2 * d) for j in range(parts)])  55.1 us
  transfers between devices with their start and end apart: 73, of which 30 were waited for; matrix products, arithmetic and copies ran while one was open for 18% of the time, Pallas kernels for 26%

profile of v4, /device:TPU:1, one launch (start us, length us, event | category | flops | bytes accessed | tf_op | source)
XLA Modules:
  0.0 1465.3 jit_solution(423205386938577289)
XLA Ops:
  30.4 5.8 fusion.38
  41.5 20.4 %collective-permute-done.refs_2_ = bf16[320,1792]{1,0:T(8,128)(2,1)} collective-permute-done((bf16[320,1792]{1,0:T(8,128)(2,1)}, bf16[320,1792]{1,0:T(8,128)(2,1)}, u32[]{:S(2)}, u32[]{:S(2)}) %collective-permute-start) | collective-permute-done | bytes 1146912 | tf_op jit(solution)/shard_map/ppermute | solution.py:409
  63.1 15.5 %collective-permute-done.2.refs_4_ = bf16[320,1792]{1,0:T(8,128)(2,1)} collective-permute-done((bf16[320,1792]{1,0:T(8,128)(2,1)}, bf16[320,1792]{1,0:T(8,128)(2,1)}, u32[]{:S(2)}, u32[]{:S(2)}) %collective-permute-start.2) | collective-permute-done | bytes 1146912 | tf_op jit(solution)/shard_map/ppermute | solution.py:409
  78.6 19.2 %collective-permute-done.4.refs_6_ = bf16[320,1792]{1,0:T(8,128)(2,1)} collective-permute-done((bf16[320,1792]{1,0:T(8,128)(2,1)}, bf16[320,1792]{1,0:T(8,128)(2,1)}, u32[]{:S(2)}, u32[]{:S(2)}) %collective-permute-start.4) | collective-permute-done | bytes 1146912 | tf_op jit(solution)/shard_map/ppermute | solution.py:409
  99.1 69.0 %all-gather.8.cloned.1.call-done.w_ref = bf16[2560,3968]{1,0:T(8,128)(2,1)} async-done(((bf16[320,3968]{1,0:T(8,128)(2,1)}), bf16[2560,3968]{1,0:T(8,128)(2,1)}) %all-gather.8.cloned.1.call-update) | async-done | bytes 20316176 | tf_op jit(solution)/shard_map/all_gather | solution.py:627
  174.2 19.3 %project.1.q_ref = bf16[512,3840]{1,0:T(8,128)(2,1)} custom-call(bf16[512,2560]{1,0:T(8,128)(2,1)} %multiply_convert_fusion.n_ref.x_ref, bf16[2560,3968]{1,0:T(8,128)(2,1)} %all-gather.8.cloned.1.call-done.w_ref, f32[512,640]{1,0:T(8,128)S(1)} %copy-done.2, f32[512,640]{1,0:T(8,128)S(1)} %get-tuple-element.279.up_ref.refs_6_, ...), custom_call_target="tpu_custom_call" | custom-call | flops 5100273664 | bytes 65536 | tf_op jit(solution)/shard_map/project/pallas_call | solution.py:61
  198.4 13.8 collective-permute-done.6.refs_1_
  218.1 23.0 %attend.2 = (bf16[256,2560]{1,0:T(8,128)(2,1)S(1)}, f32[256,256]{1,0:T(8,128)S(1)}) custom-call(bf16[512,3840]{1,0:T(8,128)(2,1)} %project.1.q_ref, bf16[256,1280]{1,0:T(8,128)(2,1)S(1)} %get-tuple-element.250.refs_0_, bf16[256,1280]{1,0:T(8,128)(2,1)S(1)} %collective-permute-done.6.refs_1_, bf16[256,1280]{1,0:T(8,128)(2,1)S(1)} %collective-permute-done.7.refs_2_, ...), custom_call_target="tpu_custom_call" | custom-call | flops 6174015488 | bytes 65536 | tf_op jit(solution)/shard_map/attend/pallas_call | solution.py:97
  244.4 9.1 multiply_reduce_fusion.8
  256.3 51.5 %all-gather.12.cloned.1.call-done.g_ref.refs_2_ = bf16[1024,2560]{1,0:T(8,128)(2,1)} async-done(((bf16[256,2560]{1,0:T(8,128)(2,1)}), bf16[1024,2560]{1,0:T(8,128)(2,1)}) %all-gather.12.cloned.1.call-update) | async-done | bytes 5242896 | tf_op jit(solution)/shard_map/all_gather | solution.py:265
  311.1 13.3 collective-permute-done.9.refs_1_
  327.3 23.4 %attend.3 = (bf16[256,2560]{1,0:T(8,128)(2,1)S(1)}, f32[256,256]{1,0:T(8,128)S(1)}) custom-call(bf16[512,3840]{1,0:T(8,128)(2,1)} %project.1.q_ref, bf16[256,1280]{1,0:T(8,128)(2,1)S(1)} %get-tuple-element.249.refs_0_, bf16[256,1280]{1,0:T(8,128)(2,1)S(1)} %collective-permute-done.9.refs_1_, bf16[256,1280]{1,0:T(8,128)(2,1)S(1)} %collective-permute-done.10.refs_2_, ...), custom_call_target="tpu_custom_call" | custom-call | flops 6174015488 | bytes 65536 | tf_op jit(solution)/shard_map/attend/pallas_call | solution.py:97
  350.8 10.7 multiply_reduce_fusion.7
  368.1 4.7 columns_for.7
  389.3 21.9 %weave.1.wg_ref.wu_ref.refs_2_.refs_3_ = bf16[2560,3584]{1,0:T(8,128)(2,1)} custom-call(s32[9]{0:T(128)} %stack.118.place_ref, bf16[320,1792]{1,0:T(8,128)(2,1)} %copy-done.44, bf16[320,1792]{1,0:T(8,128)(2,1)} %copy-done.43, bf16[320,1792]{1,0:T(8,128)(2,1)} %collective-permute-done.refs_2_, bf16[320,1792]{1,0:T(8,128)(2,1)} %collective-permute-done.1.refs_3_, ...), custom_call_target="tpu_custom_call" | custom-call | flops 5637144576 | bytes 65536 | tf_op jit(solution)/shard_map/weave/pallas_call | solution.py:378
  411.2 4.7 constant_dynamic-update-slice_fusion.1
  415.9 4.7 constant_dynamic-update-slice_fusion.wd_ref.b_ref
  420.6 36.7 %feed_forward.2 = (bf16[1024,1792]{1,0:T(8,128)(2,1)}, bf16[1024,1792]{1,0:T(8,128)(2,1)}, bf16[1024,1792]{1,0:T(8,128)(2,1)}) custom-call(bf16[1024,2560]{1,0:T(8,128)(2,1)} %all-gather.14.cloned.1.call-done.n_ref.refs_0_, bf16[1024,2560]{1,0:T(8,128)(2,1)} %all-gather.12.cloned.1.call-done.g_ref.refs_2_, ...), custom_call_target="tpu_custom_call" | custom-call | flops 9663676416 | bytes 65536 | tf_op jit(solution)/shard_map/feed_forward/pallas_call | solution.py:531
  457.4 4.1 all-gather.18.cloned.1.call-done.g_ref.refs_3_
  461.5 26.5 %sum_nt.2 = bf16[1024,2560]{1,0:T(8,128)(2,1)} custom-call(bf16[1024,1792]{1,0:T(8,128)(2,1)} %get-tuple-element.102.refs_0_.refs_2_, bf16[1024,1792]{1,0:T(8,128)(2,1)} %get-tuple-element.93.refs_1_.refs_4_, bf16[2560,3584]{1,0:T(8,128)(2,1)} %weave.1.wg_ref.wu_ref.refs_2_.refs_3_, bf16[2560,3584]{1,0:T(8,128)(2,1)} %weave.1.wg_ref.wu_ref.refs_2_.refs_3_), custom_call_target="tpu_custom_call" | custom-call | flops 6979321856 | bytes 65536 | tf_op jit(solution)/shard_map/sum_nt/pallas_call | solution.py:552
  488.0 37.2 %all-gather.16.cloned.1.call-done.n_ref.refs_1_ = bf16[1024,2560]{1,0:T(8,128)(2,1)} async-done(((bf16[256,2560]{1,0:T(8,128)(2,1)}), bf16[1024,2560]{1,0:T(8,128)(2,1)}) %all-gather.16.cloned.1.call-update) | async-done | bytes 5242896 | tf_op jit(solution)/shard_map/all_gather | solution.py:265
  525.2 36.8 %feed_forward.3 = (bf16[1024,1792]{1,0:T(8,128)(2,1)}, bf16[1024,1792]{1,0:T(8,128)(2,1)}, bf16[1024,1792]{1,0:T(8,128)(2,1)}) custom-call(bf16[1024,2560]{1,0:T(8,128)(2,1)} %all-gather.16.cloned.1.call-done.n_ref.refs_1_, bf16[1024,2560]{1,0:T(8,128)(2,1)} %all-gather.18.cloned.1.call-done.g_ref.refs_3_, ...), custom_call_target="tpu_custom_call" | custom-call | flops 9663676416 | bytes 65536 | tf_op jit(solution)/shard_map/feed_forward/pallas_call | solution.py:531
  562.0 28.1 %sum_tn.4 = bf16[4,8,80,1792]{3,2,1,0:T(8,128)(2,1)} custom-call(bf16[1024,2560]{1,0:T(8,128)(2,1)} %all-gather.14.cloned.1.call-done.n_ref.refs_0_, bf16[1024,2560]{1,0:T(8,128)(2,1)} %all-gather.16.cloned.1.call-done.n_ref.refs_1_, bf16[1024,1792]{1,0:T(8,128)(2,1)} %get-tuple-element.102.refs_0_.refs_2_, ...), custom_call_target="tpu_custom_call" | custom-call | flops 6979321856 | bytes 65536 | tf_op jit(solution)/shard_map/sum_tn/pallas_call | solution.py:502
  590.8 16.2 %sum_tn.5 = bf16[896,2560]{1,0:T(8,128)(2,1)} custom-call(bf16[1024,1792]{1,0:T(8,128)(2,1)} %get-tuple-element.105.refs_0_.a_ref, bf16[1024,1792]{1,0:T(8,128)(2,1)} %get-tuple-element.106.refs_1_.a_ref, bf16[1024,2560]{1,0:T(8,128)(2,1)} %all-gather.12.cloned.1.call-done.g_ref.refs_2_, bf16[1024,2560]{1,0:T(8,128)(2,1)} %all-gather.18.cloned.1.call-done.g_ref.refs_3_), custom_call_target="tpu_custom_call" | custom-call | flops 4294967296 | bytes 65536 | tf_op jit(solution)/shard_map/sum_tn/pallas_call | solution.py:502
  607.0 28.7 %sum_tn.6 = bf16[4,8,80,1792]{3,2,1,0:T(8,128)(2,1)} custom-call(bf16[1024,2560]{1,0:T(8,128)(2,1)} %all-gather.14.cloned.1.call-done.n_ref.refs_0_, bf16[1024,2560]{1,0:T(8,128)(2,1)} %all-gather.16.cloned.1.call-done.n_ref.refs_1_, bf16[1024,1792]{1,0:T(8,128)(2,1)} %get-tuple-element.102.refs_0_.refs_2_, ...), custom_call_target="tpu_custom_call" | custom-call | flops 6979321856 | bytes 65536 | tf_op jit(solution)/shard_map/sum_tn/pallas_call | solution.py:502
  646.4 4.9 dynamic-slice_bitcast_fusion.20
  654.0 17.0 %sum_tn.7 = bf16[896,2560]{1,0:T(8,128)(2,1)} custom-call(bf16[1024,1792]{1,0:T(8,128)(2,1)} %get-tuple-element.105.refs_0_.a_ref, bf16[1024,1792]{1,0:T(8,128)(2,1)} %get-tuple-element.106.refs_1_.a_ref, bf16[1024,2560]{1,0:T(8,128)(2,1)} %all-gather.12.cloned.1.call-done.g_ref.refs_2_, bf16[1024,2560]{1,0:T(8,128)(2,1)} %all-gather.18.cloned.1.call-done.g_ref.refs_3_, ...), custom_call_target="tpu_custom_call" | custom-call | flops 4294967296 | bytes 65536 | tf_op jit(solution)/shard_map/sum_tn/pallas_call | solution.py:502
  671.0 26.1 %sum_nt.3 = bf16[1024,2560]{1,0:T(8,128)(2,1)} custom-call(bf16[1024,1792]{1,0:T(8,128)(2,1)} %get-tuple-element.104.refs_3_.refs_0_, bf16[1024,1792]{1,0:T(8,128)(2,1)} %get-tuple-element.98.refs_5_.refs_1_, bf16[2560,3584]{1,0:T(8,128)(2,1)} %weave.1.wg_ref.wu_ref.refs_2_.refs_3_, bf16[2560,3584]{1,0:T(8,128)(2,1)} %weave.1.wg_ref.wu_ref.refs_2_.refs_3_), custom_call_target="tpu_custom_call" | custom-call | flops 6979321856 | bytes 65536 | tf_op jit(solution)/shard_map/sum_nt/pallas_call | solution.py:552
  697.1 15.9 %plain_nn.2 = bf16[1024,2560]{1,0:T(8,128)(2,1)} custom-call(bf16[1024,1792]{1,0:T(8,128)(2,1)} %get-tuple-element.105.refs_0_.a_ref, bf16[1792,2560]{1,0:T(8,128)(2,1)} %constant_dynamic-update-slice_fusion.wd_ref.b_ref), custom_call_target="tpu_custom_call" | custom-call | flops 4294967296 | bytes 65536 | tf_op jit(solution)/shard_map/plain_nn/pallas_call | solution.py:571
  713.0 15.9 %plain_nn.3 = bf16[1024,2560]{1,0:T(8,128)(2,1)} custom-call(bf16[1024,1792]{1,0:T(8,128)(2,1)} %get-tuple-element.106.refs_1_.a_ref, bf16[1792,2560]{1,0:T(8,128)(2,1)} %constant_dynamic-update-slice_fusion.wd_ref.b_ref), custom_call_target="tpu_custom_call" | custom-call | flops 4294967296 | bytes 65536 | tf_op jit(solution)/shard_map/plain_nn/pallas_call | solution.py:571
  732.5 4.5 multiply_reduce_fusion.4
  736.9 5.5 fusion.70
  742.4 10.0 convolution_convert_fusion.4.dctx_ref
  758.3 27.4 %attend_back.4 = (bf16[256,2560]{1,0:T(8,128)(2,1)}, bf16[256,1280]{1,0:T(8,128)(2,1)S(1)}, bf16[256,1280]{1,0:T(8,128)(2,1)S(1)}, bf16[256,1280]{1,0:T(8,128)(2,1)S(1)}, bf16[256,1280]{1,0:T(8,128)(2,1)}) custom-call(bf16[512,3840]{1,0:T(8,128)(2,1)} %project.1.q_ref, bf16[256,2560]{1,0:T(8,128)(2,1)} %convolution_convert_fusion.4.dctx_ref, ...), custom_call_target="tpu_custom_call" | custom-call | flops 26843545600 | bytes 65536 | tf_op jit(solution)/shard_map/attend_back/pallas_call | solution.py:160
  785.7 26.9 %attend_back.5 = (bf16[256,2560]{1,0:T(8,128)(2,1)}, bf16[256,1280]{1,0:T(8,128)(2,1)S(1)}, bf16[256,1280]{1,0:T(8,128)(2,1)S(1)}, bf16[256,1280]{1,0:T(8,128)(2,1)S(1)}, bf16[256,1280]{1,0:T(8,128)(2,1)}) custom-call(bf16[512,3840]{1,0:T(8,128)(2,1)} %project.1.q_ref, ...), custom_call_target="tpu_custom_call", output_to_operand_aliasing={{0}: (12, {}), {1}: (13, {}), {2}: (14, {}), {3}: (15, {}),... | custom-call | flops 26843545600 | bytes 65536 | tf_op jit(solution)/shard_map/attend_back/pallas_call | solution.py:160
  819.3 6.5 fusion.69
  828.8 9.7 convolution_convert_fusion.3.dctx_ref
  838.5 9.5 convolution_convert_fusion.1
  860.9 26.7 %attend_back.6 = (bf16[256,2560]{1,0:T(8,128)(2,1)}, bf16[256,1280]{1,0:T(8,128)(2,1)S(1)}, bf16[256,1280]{1,0:T(8,128)(2,1)S(1)}, bf16[256,1280]{1,0:T(8,128)(2,1)S(1)}, bf16[256,1280]{1,0:T(8,128)(2,1)S(1)}) custom-call(bf16[512,3840]{1,0:T(8,128)(2,1)} %project.1.q_ref, bf16[256,2560]{1,0:T(8,128)(2,1)} %convolution_convert_fusion.3.dctx_ref, ...), custom_call_target="tpu_custom_call" | custom-call | flops 26843545600 | bytes 65536 | tf_op jit(solution)/shard_map/attend_back/pallas_call | solution.py:160
  891.0 35.6 %collective-permute-start.35 = (bf16[1,2,80,1792]{3,2,1,0:T(8,128)(2,1)S(1)}, bf16[1,2,80,1792]{3,2,1,0:T(8,128)(2,1)S(1)}, u32[]{:S(2)}, u32[]{:S(2)}) collective-permute-start(bf16[1,2,80,1792]{3,2,1,0:T(8,128)(2,1)S(1)} %get-tuple-element.257), channel_id=1, source_target_pairs={{0,16},{4,20},{8,24},{12,28},{16,0},{20,4},{24,8},{28,12},{1,17},{... | collective-permute-start | bytes 1720328 | tf_op jit(solution)/shard_map/ppermute | solution.py:300
  927.0 5.0 fusion.27
  932.0 5.4 collective-permute-done.34
  939.1 10.5 collective-permute-done.35
  951.4 27.0 %attend_back.7 = (bf16[256,2560]{1,0:T(8,128)(2,1)}, bf16[256,1280]{1,0:T(8,128)(2,1)S(1)}, bf16[256,1280]{1,0:T(8,128)(2,1)S(1)}, bf16[256,1280]{1,0:T(8,128)(2,1)S(1)}, bf16[256,1280]{1,0:T(8,128)(2,1)S(1)}) custom-call(bf16[512,3840]{1,0:T(8,128)(2,1)} %project.1.q_ref, ...), custom_call_target="tpu_custom_call", output_to_operand_aliasing={{0}: (12, {}), {1}: (13, {}), {2}: (14, {}), {3}: (15, {}),... | custom-call | flops 26843545600 | bytes 65536 | tf_op jit(solution)/shard_map/attend_back/pallas_call | solution.py:160
  985.2 5.5 reshape.284
  1000.2 5.1 dynamic-slice_bitcast_fusion.9
  1011.3 7.7 convert_element_type.330
  1021.8 9.0 convolution_convert_fusion
  1040.1 11.5 fusion
  1051.7 47.8 %collective-permute-done.29.other_ref = bf16[256,1280]{1,0:T(8,128)(2,1)S(1)} collective-permute-done((bf16[256,1280]{1,0:T(8,128)(2,1)S(1)}, bf16[256,1280]{1,0:T(8,128)(2,1)S(1)}, u32[]{:S(2)}, u32[]{:S(2)}) %collective-permute-start.29) | collective-permute-done | bytes 655392 | tf_op jit(solution)/shard_map/ppermute | solution.py:595
  1104.3 75.3 %collective-permute-done.47.other_ref = bf16[256,1280]{1,0:T(8,128)(2,1)S(1)} collective-permute-done((bf16[256,1280]{1,0:T(8,128)(2,1)S(1)}, bf16[256,1280]{1,0:T(8,128)(2,1)S(1)}, u32[]{:S(2)}, u32[]{:S(2)}) %collective-permute-start.47) | collective-permute-done | bytes 655392 | tf_op jit(solution)/shard_map/ppermute | solution.py:595
  1183.9 9.6 collective-permute-start.49
  1193.5 10.9 multiply_reduce_fusion
  1207.1 5.9 convolution_convert_fusion.2
  1215.0 6.1 copy.67
  1225.9 6.2 fusion.18
  1232.5 11.2 collective-permute-done.62
  1245.7 4.9 fusion.24
  1250.6 12.2 collective-permute-done.56
  1264.5 17.6 %collective-permute-done.58 = bf16[320,1408]{1,0:T(8,128)(2,1)S(1)} collective-permute-done((bf16[320,1408]{1,0:T(8,128)(2,1)S(1)}, bf16[320,1408]{1,0:T(8,128)(2,1)S(1)}, u32[]{:S(2)}, u32[]{:S(2)}) %collective-permute-start.58) | collective-permute-done | bytes 901152 | tf_op jit(solution)/shard_map/ppermute | solution.py:273
  1286.9 52.0 %collective-permute-done.51 = bf16[256,2560]{1,0:T(8,128)(2,1)} collective-permute-done((bf16[256,2560]{1,0:T(8,128)(2,1)}, bf16[256,2560]{1,0:T(8,128)(2,1)}, u32[]{:S(2)}, u32[]{:S(2)}) %collective-permute-start.51) | collective-permute-done | bytes 1310752 | tf_op jit(solution)/shard_map/ppermute | solution.py:273
  1342.2 52.6 %collective-permute-done.54 = bf16[256,2560]{1,0:T(8,128)(2,1)} collective-permute-done((bf16[256,2560]{1,0:T(8,128)(2,1)}, bf16[256,2560]{1,0:T(8,128)(2,1)}, u32[]{:S(2)}, u32[]{:S(2)}) %collective-permute-start.54) | collective-permute-done | bytes 1310752 | tf_op jit(solution)/shard_map/ppermute | solution.py:273
  1400.3 12.9 slice_convert_fusion
  1413.2 34.6 %all-reduce.8.cloned.1.call-done = (bf16[320,1408]{1,0:T(8,128)(2,1)}, bf16[320,2560]{1,0:T(8,128)(2,1)}, bf16[320,2560]{1,0:T(8,128)(2,1)}) async-done(((bf16[320,1408]{1,0:T(8,128)(2,1)}, bf16[320,2560]{1,0:T(8,128)(2,1)}, bf16[320,2560]{1,0:T(8,128)(2,1)}), (bf16[320,1408]{1,0:T(8,128)(2,1)}, bf16[320,2560]{1,0:T(8,128)(2,1)}, bf16[320,2560]{1,0:T(8,128)(2,1)})) %all-reduce.8.cloned.1.call-update) | async-done | bytes 4177936 | tf_op jit(solution)/shard_map/psum | solution.py:767
  (400 shorter events, 216.6 us)
Async XLA Ops:
  7.2 160.9 %all-gather.8.cloned.1.call-start = ((), (), s32[]{:S(2)}) async-start(), calls=%async_computation.1 | async-start | bytes 22855680 | tf_op jit(solution)/shard_map/all_gather | solution.py:627
  13.4 231.0 %all-gather.10.cloned.1.call-start = ((), (), s32[]{:S(2)}) async-start(), calls=%async_computation.2 | async-start | bytes 14745600 | tf_op jit(solution)/shard_map/all_gather | solution.py:628
  14.1 293.7 %all-gather.12.cloned.1.call-start = ((), (), s32[]{:S(2)}) async-start(), calls=%async_computation.3 | async-start | bytes 6553600 | tf_op jit(solution)/shard_map/all_gather | solution.py:265
  17.8 44.2 %collective-permute-start = (bf16[320,1792]{1,0:T(8,128)(2,1)}, bf16[320,1792]{1,0:T(8,128)(2,1)}, u32[]{:S(2)}, u32[]{:S(2)}) collective-permute-start(bf16[320,1792]{1,0:T(8,128)(2,1)} %columns_for.4), channel_id=1, source_target_pairs={{0,8},{4,12},{8,0},{12,4},{16,24},{20,28},{24,16},{28,20},{1,9},{5... | collective-permute-start | bytes 3440648 | tf_op jit(solution)/shard_map/ppermute | solution.py:409
  23.5 55.2 %collective-permute-start.2 = (bf16[320,1792]{1,0:T(8,128)(2,1)}, bf16[320,1792]{1,0:T(8,128)(2,1)}, u32[]{:S(2)}, u32[]{:S(2)}) collective-permute-start(bf16[320,1792]{1,0:T(8,128)(2,1)} %columns_for.5), channel_id=1, source_target_pairs={{0,16},{4,20},{8,24},{12,28},{16,0},{20,4},{24,8},{28,12},{1,17},{... | collective-permute-start | bytes 3440648 | tf_op jit(solution)/shard_map/ppermute | solution.py:409
  28.8 69.0 %collective-permute-start.4 = (bf16[320,1792]{1,0:T(8,128)(2,1)}, bf16[320,1792]{1,0:T(8,128)(2,1)}, u32[]{:S(2)}, u32[]{:S(2)}) collective-permute-start(bf16[320,1792]{1,0:T(8,128)(2,1)} %columns_for.6), channel_id=1, source_target_pairs={{0,24},{4,28},{8,16},{12,20},{16,8},{20,12},{24,0},{28,4},{1,25},{... | collective-permute-start | bytes 3440648 | tf_op jit(solution)/shard_map/ppermute | solution.py:409
  61.9 112.2 %collective-permute-start.1 = (bf16[320,1792]{1,0:T(8,128)(2,1)}, bf16[320,1792]{1,0:T(8,128)(2,1)}, u32[]{:S(2)}, u32[]{:S(2)}) collective-permute-start(bf16[320,1792]{1,0:T(8,128)(2,1)} %collective-permute-done.refs_2_), channel_id=1, source_target_pairs={{0,1},{1,0},{2,3},{3,2},{4,5},{5,4},{6,7},{7,6},{8,9},{9,8},{10,11... | collective-permute-start | bytes 3440648 | tf_op jit(solution)/shard_map/ppermute | solution.py:412
  78.6 95.5 %collective-permute-start.3 = (bf16[320,1792]{1,0:T(8,128)(2,1)}, bf16[320,1792]{1,0:T(8,128)(2,1)}, u32[]{:S(2)}, u32[]{:S(2)}) collective-permute-start(bf16[320,1792]{1,0:T(8,128)(2,1)} %collective-permute-done.2.refs_4_), channel_id=1, source_target_pairs={{0,1},{1,0},{2,3},{3,2},{4,5},{5,4},{6,7},{7,6},{8,9},{9,8},{10,11... | collective-permute-start | bytes 3440648 | tf_op jit(solution)/shard_map/ppermute | solution.py:412
  97.8 76.4 %collective-permute-start.5 = (bf16[320,1792]{1,0:T(8,128)(2,1)}, bf16[320,1792]{1,0:T(8,128)(2,1)}, u32[]{:S(2)}, u32[]{:S(2)}) collective-permute-start(bf16[320,1792]{1,0:T(8,128)(2,1)} %collective-permute-done.4.refs_6_), channel_id=1, source_target_pairs={{0,1},{1,0},{2,3},{3,2},{4,5},{5,4},{6,7},{7,6},{8,9},{9,8},{10,11... | collective-permute-start | bytes 3440648 | tf_op jit(solution)/shard_map/ppermute | solution.py:412
  193.5 227.1 %all-gather.14.cloned.1.call-start = ((), (), s32[]{:S(2)}) async-start(), calls=%async_computation.4 | async-start | bytes 6553600 | tf_op jit(solution)/shard_map/all_gather | solution.py:265
  195.1 17.1 %collective-permute-start.6 = (bf16[256,1280]{1,0:T(8,128)(2,1)S(1)}, bf16[256,1280]{1,0:T(8,128)(2,1)S(1)}, u32[]{:S(2)}, u32[]{:S(2)}) collective-permute-start(bf16[256,1280]{1,0:T(8,128)(2,1)S(1)} %get-tuple-element.250.refs_0_), channel_id=1, source_target_pairs={{0,1},{1,2},{2,3},{4,5},{5,6},{6,7},{8,9},{9,10},{10,11},{12,13},{... | collective-permute-start | bytes 1966088 | tf_op jit(solution)/shard_map/ppermute | solution.py:662
  307.9 153.6 %all-gather.18.cloned.1.call-start = ((), (), s32[]{:S(2)}) async-start(), calls=%async_computation.6 | async-start | bytes 6553600 | tf_op jit(solution)/shard_map/all_gather | solution.py:265
  307.9 16.5 %collective-permute-start.9 = (bf16[256,1280]{1,0:T(8,128)(2,1)S(1)}, bf16[256,1280]{1,0:T(8,128)(2,1)S(1)}, u32[]{:S(2)}, u32[]{:S(2)}) collective-permute-start(bf16[256,1280]{1,0:T(8,128)(2,1)S(1)} %get-tuple-element.249.refs_0_), channel_id=1, source_target_pairs={{0,1},{1,2},{2,3},{4,5},{5,6},{6,7},{8,9},{9,10},{10,11},{12,13},{... | collective-permute-start | bytes 1966088 | tf_op jit(solution)/shard_map/ppermute | solution.py:662
  365.2 160.0 %all-gather.16.cloned.1.call-start = ((), (), s32[]{:S(2)}) async-start(), calls=%async_computation.5 | async-start | bytes 6553600 | tf_op jit(solution)/shard_map/all_gather | solution.py:265
  365.8 489.1 %reduce-scatter.2.cloned.1.call-start = ((), (), s32[]{:S(2)}) async-start(), calls=%async_computation.7 | async-start | bytes 11468800 | tf_op jit(solution)/shard_map/reduce_scatter | solution.py:706
  365.8 50.1 %collective-permute-start.20 = (bf16[896,2560]{1,0:T(8,128)(2,1)}, bf16[896,2560]{1,0:T(8,128)(2,1)}, u32[]{:S(2)}, u32[]{:S(2)}) collective-permute-start(bf16[896,2560]{1,0:T(8,128)(2,1)} %param.23), channel_id=1, source_target_pairs={{0,4},{4,0},{8,12},{12,8},{16,20},{20,16},{24,28},{28,24},{1,5},{5... | collective-permute-start | bytes 13762568 | tf_op jit(solution)/shard_map/ppermute | solution.py:256
  376.1 8.1 collective-permute-start.16
  377.4 8.5 collective-permute-start.18
  381.7 5.9 collective-permute-start.17
  590.1 16.9 %collective-permute-start.21 = (bf16[4,8,80,1792]{3,2,1,0:T(8,128)(2,1)}, bf16[4,8,80,1792]{3,2,1,0:T(8,128)(2,1)}, u32[]{:S(2)}, u32[]{:S(2)}) collective-permute-start(bf16[4,8,80,1792]{3,2,1,0:T(8,128)(2,1)} %sum_tn.4), channel_id=1, source_target_pairs={{0,4},{4,0},{8,12},{12,8},{16,20},{20,16},{24,28},{28,24},{1,5},{5... | collective-permute-start | bytes 27525128 | tf_op jit(solution)/shard_map/ppermute | solution.py:256
  635.7 344.6 %all-reduce.6.cloned.1.call-start = ((), (), s32[]{:S(2)}) async-start(), calls=%async_computation.8 | async-start | bytes 9175040 | tf_op jit(solution)/shard_map/psum | solution.py:708
  635.7 18.3 %collective-permute-start.22 = (bf16[896,2560]{1,0:T(8,128)(2,1)}, bf16[896,2560]{1,0:T(8,128)(2,1)}, u32[]{:S(2)}, u32[]{:S(2)}) collective-permute-start(bf16[896,2560]{1,0:T(8,128)(2,1)} %sum_tn.5), channel_id=1, source_target_pairs={{0,4},{4,0},{8,12},{12,8},{16,20},{20,16},{24,28},{28,24},{1,5},{5... | collective-permute-start | bytes 13762568 | tf_op jit(solution)/shard_map/ppermute | solution.py:256
  645.8 192.7 %collective-permute-start.37 = (bf16[512,1280]{1,0:T(8,128)(2,1)}, bf16[512,1280]{1,0:T(8,128)(2,1)}, u32[]{:S(2)}, u32[]{:S(2)}) collective-permute-start(bf16[512,1280]{1,0:T(8,128)(2,1)} %get-tuple-element.127), channel_id=1, source_target_pairs={{0,4},{4,0},{8,12},{12,8},{16,20},{20,16},{24,28},{28,24},{1,5},{5... | collective-permute-start | bytes 3932168 | tf_op jit(solution)/shard_map/ppermute | solution.py:256
  651.3 81.1 %collective-permute-start.24 = (bf16[256,2560]{1,0:T(8,128)(2,1)}, bf16[256,2560]{1,0:T(8,128)(2,1)}, u32[]{:S(2)}, u32[]{:S(2)}) collective-permute-start(bf16[256,2560]{1,0:T(8,128)(2,1)} %get-tuple-element.240), channel_id=1, source_target_pairs={{0,8},{4,12},{8,0},{12,4},{16,24},{20,28},{24,16},{28,20},{1,9},{5... | collective-permute-start | bytes 3932168 | tf_op jit(solution)/shard_map/ppermute | solution.py:273
  652.5 79.9 %collective-permute-start.25 = (bf16[256,2560]{1,0:T(8,128)(2,1)}, bf16[256,2560]{1,0:T(8,128)(2,1)}, u32[]{:S(2)}, u32[]{:S(2)}) collective-permute-start(bf16[256,2560]{1,0:T(8,128)(2,1)} %get-tuple-element.239), channel_id=1, source_target_pairs={{0,16},{4,20},{8,24},{12,28},{16,0},{20,4},{24,8},{28,12},{1,17},{... | collective-permute-start | bytes 3932168 | tf_op jit(solution)/shard_map/ppermute | solution.py:273
  653.1 79.3 %collective-permute-start.26 = (bf16[256,2560]{1,0:T(8,128)(2,1)}, bf16[256,2560]{1,0:T(8,128)(2,1)}, u32[]{:S(2)}, u32[]{:S(2)}) collective-permute-start(bf16[256,2560]{1,0:T(8,128)(2,1)} %get-tuple-element.238), channel_id=1, source_target_pairs={{0,24},{4,28},{8,16},{12,20},{16,8},{20,12},{24,0},{28,4},{1,25},{... | collective-permute-start | bytes 3932168 | tf_op jit(solution)/shard_map/ppermute | solution.py:273
  752.4 86.1 %collective-permute-start.38 = (bf16[256,2560]{1,0:T(8,128)(2,1)}, bf16[256,2560]{1,0:T(8,128)(2,1)}, u32[]{:S(2)}, u32[]{:S(2)}) collective-permute-start(bf16[256,2560]{1,0:T(8,128)(2,1)} %get-tuple-element.223), channel_id=1, source_target_pairs={{0,4},{4,0},{8,12},{12,8},{16,20},{20,16},{24,28},{28,24},{1,5},{5... | collective-permute-start | bytes 3932168 | tf_op jit(solution)/shard_map/ppermute | solution.py:256
  755.6 58.1 %collective-permute-start.30 = (bf16[256,2560]{1,0:T(8,128)(2,1)}, bf16[256,2560]{1,0:T(8,128)(2,1)}, u32[]{:S(2)}, u32[]{:S(2)}) collective-permute-start(bf16[256,2560]{1,0:T(8,128)(2,1)} %get-tuple-element.244), channel_id=1, source_target_pairs={{0,8},{4,12},{8,0},{12,4},{16,24},{20,28},{24,16},{28,20},{1,9},{5... | collective-permute-start | bytes 3932168 | tf_op jit(solution)/shard_map/ppermute | solution.py:273
  756.6 58.1 %collective-permute-start.31 = (bf16[256,2560]{1,0:T(8,128)(2,1)}, bf16[256,2560]{1,0:T(8,128)(2,1)}, u32[]{:S(2)}, u32[]{:S(2)}) collective-permute-start(bf16[256,2560]{1,0:T(8,128)(2,1)} %get-tuple-element.243), channel_id=1, source_target_pairs={{0,16},{4,20},{8,24},{12,28},{16,0},{20,4},{24,8},{28,12},{1,17},{... | collective-permute-start | bytes 3932168 | tf_op jit(solution)/shard_map/ppermute | solution.py:273
  757.3 57.9 %collective-permute-start.32 = (bf16[256,2560]{1,0:T(8,128)(2,1)}, bf16[256,2560]{1,0:T(8,128)(2,1)}, u32[]{:S(2)}, u32[]{:S(2)}) collective-permute-start(bf16[256,2560]{1,0:T(8,128)(2,1)} %get-tuple-element.242), channel_id=1, source_target_pairs={{0,24},{4,28},{8,16},{12,20},{16,8},{20,12},{24,0},{28,4},{1,25},{... | collective-permute-start | bytes 3932168 | tf_op jit(solution)/shard_map/ppermute | solution.py:273
  813.4 473.5 %all-gather.20.cloned.1.call-start = ((), (), s32[]{:S(2)}) async-start(), calls=%async_computation.9 | async-start | bytes 11468800 | tf_op jit(solution)/shard_map/all_gather | solution.py:749
  813.7 208.0 %collective-permute-start.43 = (bf16[256,2560]{1,0:T(8,128)(2,1)}, bf16[256,2560]{1,0:T(8,128)(2,1)}, u32[]{:S(2)}, u32[]{:S(2)}) collective-permute-start(bf16[256,2560]{1,0:T(8,128)(2,1)} %get-tuple-element.122), channel_id=1, source_target_pairs={{0,4},{4,0},{8,12},{12,8},{16,20},{20,16},{24,28},{28,24},{1,5},{5... | collective-permute-start | bytes 3932168 | tf_op jit(solution)/shard_map/ppermute | solution.py:256
  825.8 12.7 collective-permute-start.39
  852.3 37.7 %collective-permute-start.40 = (bf16[320,2560]{1,0:T(8,128)(2,1)}, bf16[320,2560]{1,0:T(8,128)(2,1)}, u32[]{:S(2)}, u32[]{:S(2)}) collective-permute-start(bf16[320,2560]{1,0:T(8,128)(2,1)} %get-tuple-element.230), channel_id=1, source_target_pairs={{0,8},{4,12},{8,0},{12,4},{16,24},{20,28},{24,16},{28,20},{1,9},{5... | collective-permute-start | bytes 4915208 | tf_op jit(solution)/shard_map/ppermute | solution.py:273
  853.3 37.7 %collective-permute-start.41 = (bf16[320,2560]{1,0:T(8,128)(2,1)}, bf16[320,2560]{1,0:T(8,128)(2,1)}, u32[]{:S(2)}, u32[]{:S(2)}) collective-permute-start(bf16[320,2560]{1,0:T(8,128)(2,1)} %get-tuple-element.232), channel_id=1, source_target_pairs={{0,16},{4,20},{8,24},{12,28},{16,0},{20,4},{24,8},{28,12},{1,17},{... | collective-permute-start | bytes 4915208 | tf_op jit(solution)/shard_map/ppermute | solution.py:273
  854.4 72.2 %collective-permute-start.42 = (bf16[320,2560]{1,0:T(8,128)(2,1)}, bf16[320,2560]{1,0:T(8,128)(2,1)}, u32[]{:S(2)}, u32[]{:S(2)}) collective-permute-start(bf16[320,2560]{1,0:T(8,128)(2,1)} %get-tuple-element.231), channel_id=1, source_target_pairs={{0,24},{4,28},{8,16},{12,20},{16,8},{20,12},{24,0},{28,4},{1,25},{... | collective-permute-start | bytes 4915208 | tf_op jit(solution)/shard_map/ppermute | solution.py:273
  856.7 30.9 %collective-permute-start.33 = (bf16[4,80,1792]{2,1,0:T(8,128)(2,1)S(1)}, bf16[4,80,1792]{2,1,0:T(8,128)(2,1)S(1)}, u32[]{:S(2)}, u32[]{:S(2)}) collective-permute-start(bf16[4,80,1792]{2,1,0:T(8,128)(2,1)S(1)} %get-tuple-element.261), channel_id=1, source_target_pairs={{0,4},{4,0},{8,12},{12,8},{16,20},{20,16},{24,28},{28,24},{1,5},{5... | collective-permute-start | bytes 3440648 | tf_op jit(solution)/shard_map/ppermute | solution.py:256
  887.6 120.4 %collective-permute-start.23 = (bf16[512,1280]{1,0:T(8,128)(2,1)}, bf16[512,1280]{1,0:T(8,128)(2,1)}, u32[]{:S(2)}, u32[]{:S(2)}) collective-permute-start(bf16[512,1280]{1,0:T(8,128)(2,1)} %get-tuple-element.109), channel_id=1, source_target_pairs={{0,4},{4,0},{8,12},{12,8},{16,20},{20,16},{24,28},{28,24},{1,5},{5... | collective-permute-start | bytes 3932168 | tf_op jit(solution)/shard_map/ppermute | solution.py:256
  890.0 47.4 %collective-permute-start.34 = (bf16[1,2,80,1792]{3,2,1,0:T(8,128)(2,1)S(1)}, bf16[1,2,80,1792]{3,2,1,0:T(8,128)(2,1)S(1)}, u32[]{:S(2)}, u32[]{:S(2)}) collective-permute-start(bf16[1,2,80,1792]{3,2,1,0:T(8,128)(2,1)S(1)} %get-tuple-element.258), channel_id=1, source_target_pairs={{0,8},{4,12},{8,0},{12,4},{16,24},{20,28},{24,16},{28,20},{1,9},{5... | collective-permute-start | bytes 1720328 | tf_op jit(solution)/shard_map/ppermute | solution.py:300
  891.0 58.6 %collective-permute-start.35 = (bf16[1,2,80,1792]{3,2,1,0:T(8,128)(2,1)S(1)}, bf16[1,2,80,1792]{3,2,1,0:T(8,128)(2,1)S(1)}, u32[]{:S(2)}, u32[]{:S(2)}) collective-permute-start(bf16[1,2,80,1792]{3,2,1,0:T(8,128)(2,1)S(1)} %get-tuple-element.257), channel_id=1, source_target_pairs={{0,16},{4,20},{8,24},{12,28},{16,0},{20,4},{24,8},{28,12},{1,17},{... | collective-permute-start | bytes 1720328 | tf_op jit(solution)/shard_map/ppermute | solution.py:300
  926.6 24.0 %collective-permute-start.36 = (bf16[1,2,80,1792]{3,2,1,0:T(8,128)(2,1)S(1)}, bf16[1,2,80,1792]{3,2,1,0:T(8,128)(2,1)S(1)}, u32[]{:S(2)}, u32[]{:S(2)}) collective-permute-start(bf16[1,2,80,1792]{3,2,1,0:T(8,128)(2,1)S(1)} %get-tuple-element.256), channel_id=1, source_target_pairs={{0,24},{4,28},{8,16},{12,20},{16,8},{20,12},{24,0},{28,4},{1,25},{... | collective-permute-start | bytes 1720328 | tf_op jit(solution)/shard_map/ppermute | solution.py:300
  937.4 58.1 %collective-permute-start.27 = (bf16[256,1280]{1,0:T(8,128)(2,1)}, bf16[256,1280]{1,0:T(8,128)(2,1)}, u32[]{:S(2)}, u32[]{:S(2)}) collective-permute-start(bf16[256,1280]{1,0:T(8,128)(2,1)} %get-tuple-element.121), channel_id=1, source_target_pairs={{3,2},{7,6},{11,10},{15,14},{19,18},{23,22},{27,26},{31,30}} | collective-permute-start | bytes 1966088 | tf_op jit(solution)/shard_map/ppermute | solution.py:595
  995.5 452.3 %all-reduce.8.cloned.1.call-start = ((), (), s32[]{:S(2)}) async-start(), calls=%async_computation.10 | async-start | bytes 8355840 | tf_op jit(solution)/shard_map/psum | solution.py:767
  996.9 8.4 collective-permute-start.28
  999.0 224.6 %collective-permute-start.50 = (bf16[256,2560]{1,0:T(8,128)(2,1)}, bf16[256,2560]{1,0:T(8,128)(2,1)}, u32[]{:S(2)}, u32[]{:S(2)}) collective-permute-start(bf16[256,2560]{1,0:T(8,128)(2,1)} %get-tuple-element.236), channel_id=1, source_target_pairs={{0,8},{4,12},{8,0},{12,4},{16,24},{20,28},{24,16},{28,20},{1,9},{5... | collective-permute-start | bytes 3932168 | tf_op jit(solution)/shard_map/ppermute | solution.py:273
  1005.5 16.2 %collective-permute-start.44 = (bf16[256,2560]{1,0:T(8,128)(2,1)}, bf16[256,2560]{1,0:T(8,128)(2,1)}, u32[]{:S(2)}, u32[]{:S(2)}) collective-permute-start(bf16[256,2560]{1,0:T(8,128)(2,1)} %get-tuple-element.136), channel_id=1, source_target_pairs={{0,4},{4,0},{8,12},{12,8},{16,20},{20,16},{24,28},{28,24},{1,5},{5... | collective-permute-start | bytes 3932168 | tf_op jit(solution)/shard_map/ppermute | solution.py:256
  1006.8 92.7 %collective-permute-start.29 = (bf16[256,1280]{1,0:T(8,128)(2,1)S(1)}, bf16[256,1280]{1,0:T(8,128)(2,1)S(1)}, u32[]{:S(2)}, u32[]{:S(2)}) collective-permute-start(bf16[256,1280]{1,0:T(8,128)(2,1)S(1)} %add_convert_fusion.4), channel_id=1, source_target_pairs={{3,2},{2,1},{1,0},{7,6},{6,5},{5,4},{11,10},{10,9},{9,8},{15,14},{... | collective-permute-start | bytes 1966088 | tf_op jit(solution)/shard_map/ppermute | solution.py:595
  1008.1 12.8 collective-permute-start.45
  1021.0 17.4 %collective-permute-start.46 = (bf16[256,1280]{1,0:T(8,128)(2,1)S(1)}, bf16[256,1280]{1,0:T(8,128)(2,1)S(1)}, u32[]{:S(2)}, u32[]{:S(2)}) collective-permute-start(bf16[256,1280]{1,0:T(8,128)(2,1)S(1)} %add_convert_fusion.3), channel_id=1, source_target_pairs={{3,2},{2,1},{7,6},{6,5},{11,10},{10,9},{15,14},{14,13},{19,18},{18... | collective-permute-start | bytes 1966088 | tf_op jit(solution)/shard_map/ppermute | solution.py:595
  1035.1 188.8 %collective-permute-start.60 = (bf16[320,2560]{1,0:T(8,128)(2,1)}, bf16[320,2560]{1,0:T(8,128)(2,1)}, u32[]{:S(2)}, u32[]{:S(2)}) collective-permute-start(bf16[320,2560]{1,0:T(8,128)(2,1)} %get-tuple-element.227), channel_id=1, source_target_pairs={{0,8},{4,12},{8,0},{12,4},{16,24},{20,28},{24,16},{28,20},{1,9},{5... | collective-permute-start | bytes 4915208 | tf_op jit(solution)/shard_map/ppermute | solution.py:273
  1036.9 195.3 %collective-permute-start.61 = (bf16[320,2560]{1,0:T(8,128)(2,1)}, bf16[320,2560]{1,0:T(8,128)(2,1)}, u32[]{:S(2)}, u32[]{:S(2)}) collective-permute-start(bf16[320,2560]{1,0:T(8,128)(2,1)} %get-tuple-element.229), channel_id=1, source_target_pairs={{0,16},{4,20},{8,24},{12,28},{16,0},{20,4},{24,8},{28,12},{1,17},{... | collective-permute-start | bytes 4915208 | tf_op jit(solution)/shard_map/ppermute | solution.py:273
  1038.6 141.0 %collective-permute-start.47 = (bf16[256,1280]{1,0:T(8,128)(2,1)S(1)}, bf16[256,1280]{1,0:T(8,128)(2,1)S(1)}, u32[]{:S(2)}, u32[]{:S(2)}) collective-permute-start(bf16[256,1280]{1,0:T(8,128)(2,1)S(1)} %add_convert_fusion.2), channel_id=1, source_target_pairs={{3,2},{2,1},{1,0},{7,6},{6,5},{5,4},{11,10},{10,9},{9,8},{15,14},{... | collective-permute-start | bytes 1966088 | tf_op jit(solution)/shard_map/ppermute | solution.py:595
  1103.6 101.3 %collective-permute-start.48 = (bf16[256,1280]{1,0:T(8,128)(2,1)}, bf16[256,1280]{1,0:T(8,128)(2,1)}, u32[]{:S(2)}, u32[]{:S(2)}) collective-permute-start(bf16[256,1280]{1,0:T(8,128)(2,1)} %finish_keys.2), channel_id=1, source_target_pairs={{0,4},{4,0},{8,12},{12,8},{16,20},{20,16},{24,28},{28,24},{1,5},{5... | collective-permute-start | bytes 1966088 | tf_op jit(solution)/shard_map/ppermute | solution.py:256
  1183.9 23.2 %collective-permute-start.49 = (bf16[256,1280]{1,0:T(8,128)(2,1)}, bf16[256,1280]{1,0:T(8,128)(2,1)}, u32[]{:S(2)}, u32[]{:S(2)}) collective-permute-start(bf16[256,1280]{1,0:T(8,128)(2,1)} %finish_keys.3), channel_id=1, source_target_pairs={{0,4},{4,0},{8,12},{12,8},{16,20},{20,16},{24,28},{28,24},{1,5},{5... | collective-permute-start | bytes 1966088 | tf_op jit(solution)/shard_map/ppermute | solution.py:256
  1204.9 38.7 %collective-permute-start.62 = (bf16[320,2560]{1,0:T(8,128)(2,1)}, bf16[320,2560]{1,0:T(8,128)(2,1)}, u32[]{:S(2)}, u32[]{:S(2)}) collective-permute-start(bf16[320,2560]{1,0:T(8,128)(2,1)} %get-tuple-element.228), channel_id=1, source_target_pairs={{0,24},{4,28},{8,16},{12,20},{16,8},{20,12},{24,0},{28,4},{1,25},{... | collective-permute-start | bytes 4915208 | tf_op jit(solution)/shard_map/ppermute | solution.py:273
  1223.2 39.6 %collective-permute-start.56 = (bf16[320,1408]{1,0:T(8,128)(2,1)S(1)}, bf16[320,1408]{1,0:T(8,128)(2,1)S(1)}, u32[]{:S(2)}, u32[]{:S(2)}) collective-permute-start(bf16[320,1408]{1,0:T(8,128)(2,1)S(1)} %get-tuple-element.251), channel_id=1, source_target_pairs={{0,8},{4,12},{8,0},{12,4},{16,24},{20,28},{24,16},{28,20},{1,9},{5... | collective-permute-start | bytes 2703368 | tf_op jit(solution)/shard_map/ppermute | solution.py:273
  1223.5 40.5 %collective-permute-start.57 = (bf16[320,1408]{1,0:T(8,128)(2,1)S(1)}, bf16[320,1408]{1,0:T(8,128)(2,1)S(1)}, u32[]{:S(2)}, u32[]{:S(2)}) collective-permute-start(bf16[320,1408]{1,0:T(8,128)(2,1)S(1)} %get-tuple-element.253), channel_id=1, source_target_pairs={{0,16},{4,20},{8,24},{12,28},{16,0},{20,4},{24,8},{28,12},{1,17},{... | collective-permute-start | bytes 2703368 | tf_op jit(solution)/shard_map/ppermute | solution.py:273
  1223.8 58.4 %collective-permute-start.58 = (bf16[320,1408]{1,0:T(8,128)(2,1)S(1)}, bf16[320,1408]{1,0:T(8,128)(2,1)S(1)}, u32[]{:S(2)}, u32[]{:S(2)}) collective-permute-start(bf16[320,1408]{1,0:T(8,128)(2,1)S(1)} %get-tuple-element.252), channel_id=1, source_target_pairs={{0,24},{4,28},{8,16},{12,20},{16,8},{20,12},{24,0},{28,4},{1,25},{... | collective-permute-start | bytes 2703368 | tf_op jit(solution)/shard_map/ppermute | solution.py:273
  1232.2 106.7 %collective-permute-start.51 = (bf16[256,2560]{1,0:T(8,128)(2,1)}, bf16[256,2560]{1,0:T(8,128)(2,1)}, u32[]{:S(2)}, u32[]{:S(2)}) collective-permute-start(bf16[256,2560]{1,0:T(8,128)(2,1)} %get-tuple-element.235), channel_id=1, source_target_pairs={{0,16},{4,20},{8,24},{12,28},{16,0},{20,4},{24,8},{28,12},{1,17},{... | collective-permute-start | bytes 3932168 | tf_op jit(solution)/shard_map/ppermute | solution.py:273
  1243.6 95.3 %collective-permute-start.52 = (bf16[256,2560]{1,0:T(8,128)(2,1)}, bf16[256,2560]{1,0:T(8,128)(2,1)}, u32[]{:S(2)}, u32[]{:S(2)}) collective-permute-start(bf16[256,2560]{1,0:T(8,128)(2,1)} %get-tuple-element.234), channel_id=1, source_target_pairs={{0,24},{4,28},{8,16},{12,20},{16,8},{20,12},{24,0},{28,4},{1,25},{... | collective-permute-start | bytes 3932168 | tf_op jit(solution)/shard_map/ppermute | solution.py:273
  1262.8 79.4 %collective-permute-start.53 = (bf16[256,2560]{1,0:T(8,128)(2,1)}, bf16[256,2560]{1,0:T(8,128)(2,1)}, u32[]{:S(2)}, u32[]{:S(2)}) collective-permute-start(bf16[256,2560]{1,0:T(8,128)(2,1)} %get-tuple-element.248), channel_id=1, source_target_pairs={{0,8},{4,12},{8,0},{12,4},{16,24},{20,28},{24,16},{28,20},{1,9},{5... | collective-permute-start | bytes 3932168 | tf_op jit(solution)/shard_map/ppermute | solution.py:273
  1264.0 130.8 %collective-permute-start.54 = (bf16[256,2560]{1,0:T(8,128)(2,1)}, bf16[256,2560]{1,0:T(8,128)(2,1)}, u32[]{:S(2)}, u32[]{:S(2)}) collective-permute-start(bf16[256,2560]{1,0:T(8,128)(2,1)} %get-tuple-element.247), channel_id=1, source_target_pairs={{0,16},{4,20},{8,24},{12,28},{16,0},{20,4},{24,8},{28,12},{1,17},{... | collective-permute-start | bytes 3932168 | tf_op jit(solution)/shard_map/ppermute | solution.py:273
  1282.2 112.7 %collective-permute-start.55 = (bf16[256,2560]{1,0:T(8,128)(2,1)}, bf16[256,2560]{1,0:T(8,128)(2,1)}, u32[]{:S(2)}, u32[]{:S(2)}) collective-permute-start(bf16[256,2560]{1,0:T(8,128)(2,1)} %get-tuple-element.246), channel_id=1, source_target_pairs={{0,24},{4,28},{8,16},{12,20},{16,8},{20,12},{24,0},{28,4},{1,25},{... | collective-permute-start | bytes 3932168 | tf_op jit(solution)/shard_map/ppermute | solution.py:273
  1449.5 7.8 collective-permute-start.59
  (89 other events, 1666.0 us)
Sparse Core Ops, SparseCore 0:
  13.5 154.5 all-gather.7
  170.0 74.3 all-gather.9
  246.8 60.9 all-gather.11
  309.5 61.4 all-gather.13
  373.3 88.1 all-gather.17
  463.7 61.4 all-gather.15
  635.8 156.1 reduce-scatter.1
  813.6 166.6 all-reduce.5
  995.6 212.4 all-gather.19
  1287.0 160.7 all-reduce.7

commit v5 on v4

--- a/solution.py
+++ b/solution.py
@@ -746,13 +746,13 @@
     order.last = order.last + (out_shard, down_total)
     wide_part = exchanged([order.at(pieces[0], *pieces[1:])] + pieces[1:])
     wide_part = order.did(jnp.moveaxis(wide_part.reshape(parts, slab, 2, hidden_own), 0, 2).reshape(slab, 2 * ff))
-    wide_total = lax.all_gather(wide_part, "sp", axis=0, tiled=True)
     query_half = order.did(tn(normed_chip, chip_rows(query_grads[:-1] + [order.at(query_grads[-1])])).astype(bf16))
     query_shard = added(scatter_chips(query_half)).astype(bf16)
     kv_hop = tuple(keys.hop() for keys in kv_sums)
     normed_grad = order.did(nt(order.at(rows_of(query_grads), *kv_hop), w_in[:, :D]))
     kv_grads = [keys.result() for keys in kv_sums]
     kv_grads = [order.did(finish_keys(own, order.at(came), tables, m)) for m, (own, came) in enumerate(kv_grads)]
+    wide_total = lax.all_gather(order.at(wide_part), "sp", axis=0, tiled=True)
     kv_grad = rows_of(kv_grads)
     kv_half = order.did(tn(normed_chip, chip_rows(kv_grads)).astype(bf16))
     normed_grad = normed_grad + nt(kv_grad, w_in[:, D:D + 4 * KW])

time: 1470 us -> 1440 us (0.980)
  starting transfers between devices: 103 us -> 58.4 us
  waiting for transfers between devices: 579 us -> 594 us
    ppermute x6, waiting for transfers between devices: 123 us -> 31.9 us  [hop(): self.running = lax.ppermute(tie(self.running, *before), 'sp', pairs)]
    ppermute x21, waiting for transfers between devices: 147 us -> 183 us  [scatter_chips(): lax.ppermute(take(chip ^ d), 'fsdp', [(j, j ^ 2 * d) for j in range(parts)])]
    ppermute x3, starting transfers between devices: 37 us -> 2.48 us  [exchange_chips(): lax.ppermute(block, 'fsdp', [(j, j ^ 2 * d) for j in range(parts)])]
    psum x1, waiting for transfers between devices: 0.15 us -> 31.2 us  [body(): down_total = lax.psum(down_grad, 'sp')]
    psum x1, waiting for transfers between devices: 34.6 us -> 56.3 us  [body(): lax.psum((tie(out_shard, down_total), tie(query_shard, wide_total), tie(k...]
    all_gather x1, waiting for transfers between devices: 0.01 us -> 18.5 us  [body(): wide_total = lax.all_gather(order.at(wide_part), 'sp', axis=0, tiled=True)]
    unnamed x167 -> x173, local copies, waits for them, and re-layouts: 29.7 us -> 29.8 us
  transfers between devices with their start and end apart: 73 -> 73, of which waited for: 30 -> 30; matrix products, arithmetic and copies ran while one was open for 18% -> 19% of each run, Pallas kernels for 26% -> 26%
where the time goes in v5:
time: 1440 us; the launch traced here: 1430 us
  waiting for transfers between devices  594 us (41%)
  Pallas kernels  471 us (33%)
  local copies, waits for them, and re-layouts  105 us (7%)
  other arithmetic  104 us (7%)
  matrix products  86.1 us (6%)
  starting transfers between devices  58.4 us (4%)
  between operations  15.5 us (1%)
    ppermute x21, waiting for transfers between devices, scatter_chips(): lax.ppermute(take(chip ^ d), 'fsdp', [(j, j ^ 2 * d) for j in range(parts)])  183 us
    pallas_call x4, Pallas kernels, attend_back(): pl.pallas_call(functools.partial(backward_kernel, blocks, len(before)), g...  108 us
    all_gather x4, waiting for transfers between devices, gather_chips(): lax.all_gather(x, 'fsdp', axis=0, tiled=True, axis_index_groups=same_core())  92.8 us
    pallas_call x4, Pallas kernels, sum_tn(): pl.pallas_call(functools.partial(sum_tn_kernel, segments, pairs), grid=(D...  90 us
    pallas_call x2, Pallas kernels, feed_forward(): pl.pallas_call(ffn_kernel, grid=(tiles,), in_specs=[full, full, pl.BlockS...  73.4 us
    all_gather x1, waiting for transfers between devices, body(): w_in = lax.all_gather(w_in, 'fsdp', axis=0, tiled=True)  69 us
    psum x1, waiting for transfers between devices, body(): lax.psum((tie(out_shard, down_total), tie(query_shard, wide_total), tie(k...  56.3 us
    ppermute x3, waiting for transfers between devices, fetch(): lax.ppermute(x, 'fsdp', [(j, j ^ 2 * d) for j in range(parts)])  55.1 us
  transfers between devices with their start and end apart: 73, of which 30 were waited for; matrix products, arithmetic and copies ran while one was open for 19% of the time, Pallas kernels for 26%

profile of v5, /device:TPU:1, one launch (start us, length us, event | category | flops | bytes accessed | tf_op | source)
XLA Modules:
  0.0 1434.3 jit_solution(1610990861602712148)
XLA Ops:
  30.4 5.8 fusion.38
  41.5 20.4 %collective-permute-done.refs_2_ = bf16[320,1792]{1,0:T(8,128)(2,1)} collective-permute-done((bf16[320,1792]{1,0:T(8,128)(2,1)}, bf16[320,1792]{1,0:T(8,128)(2,1)}, u32[]{:S(2)}, u32[]{:S(2)}) %collective-permute-start) | collective-permute-done | bytes 1146912 | tf_op jit(solution)/shard_map/ppermute | solution.py:409
  63.1 15.5 %collective-permute-done.2.refs_4_ = bf16[320,1792]{1,0:T(8,128)(2,1)} collective-permute-done((bf16[320,1792]{1,0:T(8,128)(2,1)}, bf16[320,1792]{1,0:T(8,128)(2,1)}, u32[]{:S(2)}, u32[]{:S(2)}) %collective-permute-start.2) | collective-permute-done | bytes 1146912 | tf_op jit(solution)/shard_map/ppermute | solution.py:409
  78.6 19.2 %collective-permute-done.4.refs_6_ = bf16[320,1792]{1,0:T(8,128)(2,1)} collective-permute-done((bf16[320,1792]{1,0:T(8,128)(2,1)}, bf16[320,1792]{1,0:T(8,128)(2,1)}, u32[]{:S(2)}, u32[]{:S(2)}) %collective-permute-start.4) | collective-permute-done | bytes 1146912 | tf_op jit(solution)/shard_map/ppermute | solution.py:409
  99.1 69.0 %all-gather.8.cloned.1.call-done.w_ref = bf16[2560,3968]{1,0:T(8,128)(2,1)} async-done(((bf16[320,3968]{1,0:T(8,128)(2,1)}), bf16[2560,3968]{1,0:T(8,128)(2,1)}) %all-gather.8.cloned.1.call-update) | async-done | bytes 20316176 | tf_op jit(solution)/shard_map/all_gather | solution.py:627
  174.2 19.2 %project.1.q_ref = bf16[512,3840]{1,0:T(8,128)(2,1)} custom-call(bf16[512,2560]{1,0:T(8,128)(2,1)} %multiply_convert_fusion.n_ref.x_ref, bf16[2560,3968]{1,0:T(8,128)(2,1)} %all-gather.8.cloned.1.call-done.w_ref, f32[512,640]{1,0:T(8,128)S(1)} %copy-done.2, f32[512,640]{1,0:T(8,128)S(1)} %get-tuple-element.281.up_ref.refs_6_, ...), custom_call_target="tpu_custom_call" | custom-call | flops 5100273664 | bytes 65536 | tf_op jit(solution)/shard_map/project/pallas_call | solution.py:61
  198.4 13.8 collective-permute-done.6.refs_1_
  218.0 23.4 %attend.2 = (bf16[256,2560]{1,0:T(8,128)(2,1)S(1)}, f32[256,256]{1,0:T(8,128)S(1)}) custom-call(bf16[512,3840]{1,0:T(8,128)(2,1)} %project.1.q_ref, bf16[256,1280]{1,0:T(8,128)(2,1)S(1)} %get-tuple-element.252.refs_0_, bf16[256,1280]{1,0:T(8,128)(2,1)S(1)} %collective-permute-done.6.refs_1_, bf16[256,1280]{1,0:T(8,128)(2,1)S(1)} %collective-permute-done.7.refs_2_, ...), custom_call_target="tpu_custom_call" | custom-call | flops 6174015488 | bytes 65536 | tf_op jit(solution)/shard_map/attend/pallas_call | solution.py:97
  244.4 9.1 multiply_reduce_fusion.8
  256.3 51.5 %all-gather.12.cloned.1.call-done.g_ref.refs_2_ = bf16[1024,2560]{1,0:T(8,128)(2,1)} async-done(((bf16[256,2560]{1,0:T(8,128)(2,1)}), bf16[1024,2560]{1,0:T(8,128)(2,1)}) %all-gather.12.cloned.1.call-update) | async-done | bytes 5242896 | tf_op jit(solution)/shard_map/all_gather | solution.py:265
  311.1 13.3 collective-permute-done.9.refs_1_
  327.3 23.2 %attend.3 = (bf16[256,2560]{1,0:T(8,128)(2,1)S(1)}, f32[256,256]{1,0:T(8,128)S(1)}) custom-call(bf16[512,3840]{1,0:T(8,128)(2,1)} %project.1.q_ref, bf16[256,1280]{1,0:T(8,128)(2,1)S(1)} %get-tuple-element.251.refs_0_, bf16[256,1280]{1,0:T(8,128)(2,1)S(1)} %collective-permute-done.9.refs_1_, bf16[256,1280]{1,0:T(8,128)(2,1)S(1)} %collective-permute-done.10.refs_2_, ...), custom_call_target="tpu_custom_call" | custom-call | flops 6174015488 | bytes 65536 | tf_op jit(solution)/shard_map/attend/pallas_call | solution.py:97
  350.6 9.7 multiply_reduce_fusion.7
  366.0 4.7 columns_for.7
  387.2 21.9 %weave.1.wg_ref.wu_ref.refs_2_.refs_3_ = bf16[2560,3584]{1,0:T(8,128)(2,1)} custom-call(s32[9]{0:T(128)} %stack.118.place_ref, bf16[320,1792]{1,0:T(8,128)(2,1)} %copy-done.47, bf16[320,1792]{1,0:T(8,128)(2,1)} %copy-done.46, bf16[320,1792]{1,0:T(8,128)(2,1)} %collective-permute-done.refs_2_, bf16[320,1792]{1,0:T(8,128)(2,1)} %collective-permute-done.1.refs_3_, ...), custom_call_target="tpu_custom_call" | custom-call | flops 5637144576 | bytes 65536 | tf_op jit(solution)/shard_map/weave/pallas_call | solution.py:378
  409.1 4.7 constant_dynamic-update-slice_fusion.1
  413.8 4.7 constant_dynamic-update-slice_fusion.wd_ref.b_ref
  418.6 36.7 %feed_forward.2 = (bf16[1024,1792]{1,0:T(8,128)(2,1)}, bf16[1024,1792]{1,0:T(8,128)(2,1)}, bf16[1024,1792]{1,0:T(8,128)(2,1)}) custom-call(bf16[1024,2560]{1,0:T(8,128)(2,1)} %all-gather.14.cloned.1.call-done.n_ref.refs_0_, bf16[1024,2560]{1,0:T(8,128)(2,1)} %all-gather.12.cloned.1.call-done.g_ref.refs_2_, ...), custom_call_target="tpu_custom_call" | custom-call | flops 9663676416 | bytes 65536 | tf_op jit(solution)/shard_map/feed_forward/pallas_call | solution.py:531
  459.3 26.5 %sum_nt.2 = bf16[1024,2560]{1,0:T(8,128)(2,1)} custom-call(bf16[1024,1792]{1,0:T(8,128)(2,1)} %get-tuple-element.103.refs_0_.refs_2_, bf16[1024,1792]{1,0:T(8,128)(2,1)} %get-tuple-element.94.refs_1_.refs_4_, bf16[2560,3584]{1,0:T(8,128)(2,1)} %weave.1.wg_ref.wu_ref.refs_2_.refs_3_, bf16[2560,3584]{1,0:T(8,128)(2,1)} %weave.1.wg_ref.wu_ref.refs_2_.refs_3_), custom_call_target="tpu_custom_call" | custom-call | flops 6979321856 | bytes 65536 | tf_op jit(solution)/shard_map/sum_nt/pallas_call | solution.py:552
  485.9 37.2 %all-gather.16.cloned.1.call-done.n_ref.refs_1_ = bf16[1024,2560]{1,0:T(8,128)(2,1)} async-done(((bf16[256,2560]{1,0:T(8,128)(2,1)}), bf16[1024,2560]{1,0:T(8,128)(2,1)}) %all-gather.16.cloned.1.call-update) | async-done | bytes 5242896 | tf_op jit(solution)/shard_map/all_gather | solution.py:265
  523.1 36.7 %feed_forward.3 = (bf16[1024,1792]{1,0:T(8,128)(2,1)}, bf16[1024,1792]{1,0:T(8,128)(2,1)}, bf16[1024,1792]{1,0:T(8,128)(2,1)}) custom-call(bf16[1024,2560]{1,0:T(8,128)(2,1)} %all-gather.16.cloned.1.call-done.n_ref.refs_1_, bf16[1024,2560]{1,0:T(8,128)(2,1)} %all-gather.18.cloned.1.call-done.g_ref.refs_3_, ...), custom_call_target="tpu_custom_call" | custom-call | flops 9663676416 | bytes 65536 | tf_op jit(solution)/shard_map/feed_forward/pallas_call | solution.py:531
  559.8 28.3 %sum_tn.4 = bf16[4,8,80,1792]{3,2,1,0:T(8,128)(2,1)} custom-call(bf16[1024,2560]{1,0:T(8,128)(2,1)} %all-gather.14.cloned.1.call-done.n_ref.refs_0_, bf16[1024,2560]{1,0:T(8,128)(2,1)} %all-gather.16.cloned.1.call-done.n_ref.refs_1_, bf16[1024,1792]{1,0:T(8,128)(2,1)} %get-tuple-element.103.refs_0_.refs_2_, ...), custom_call_target="tpu_custom_call" | custom-call | flops 6979321856 | bytes 65536 | tf_op jit(solution)/shard_map/sum_tn/pallas_call | solution.py:502
  588.7 16.1 %sum_tn.5 = bf16[896,2560]{1,0:T(8,128)(2,1)} custom-call(bf16[1024,1792]{1,0:T(8,128)(2,1)} %get-tuple-element.106.refs_0_.a_ref, bf16[1024,1792]{1,0:T(8,128)(2,1)} %get-tuple-element.107.refs_1_.a_ref, bf16[1024,2560]{1,0:T(8,128)(2,1)} %all-gather.12.cloned.1.call-done.g_ref.refs_2_, bf16[1024,2560]{1,0:T(8,128)(2,1)} %all-gather.18.cloned.1.call-done.g_ref.refs_3_), custom_call_target="tpu_custom_call" | custom-call | flops 4294967296 | bytes 65536 | tf_op jit(solution)/shard_map/sum_tn/pallas_call | solution.py:502
  604.8 28.7 %sum_tn.6 = bf16[4,8,80,1792]{3,2,1,0:T(8,128)(2,1)} custom-call(bf16[1024,2560]{1,0:T(8,128)(2,1)} %all-gather.14.cloned.1.call-done.n_ref.refs_0_, bf16[1024,2560]{1,0:T(8,128)(2,1)} %all-gather.16.cloned.1.call-done.n_ref.refs_1_, bf16[1024,1792]{1,0:T(8,128)(2,1)} %get-tuple-element.103.refs_0_.refs_2_, ...), custom_call_target="tpu_custom_call" | custom-call | flops 6979321856 | bytes 65536 | tf_op jit(solution)/shard_map/sum_tn/pallas_call | solution.py:502
  644.1 4.9 dynamic-slice_bitcast_fusion.20
  651.7 16.9 %sum_tn.7 = bf16[896,2560]{1,0:T(8,128)(2,1)} custom-call(bf16[1024,1792]{1,0:T(8,128)(2,1)} %get-tuple-element.106.refs_0_.a_ref, bf16[1024,1792]{1,0:T(8,128)(2,1)} %get-tuple-element.107.refs_1_.a_ref, bf16[1024,2560]{1,0:T(8,128)(2,1)} %all-gather.12.cloned.1.call-done.g_ref.refs_2_, bf16[1024,2560]{1,0:T(8,128)(2,1)} %all-gather.18.cloned.1.call-done.g_ref.refs_3_, ...), custom_call_target="tpu_custom_call" | custom-call | flops 4294967296 | bytes 65536 | tf_op jit(solution)/shard_map/sum_tn/pallas_call | solution.py:502
  668.6 26.0 %sum_nt.3 = bf16[1024,2560]{1,0:T(8,128)(2,1)} custom-call(bf16[1024,1792]{1,0:T(8,128)(2,1)} %get-tuple-element.105.refs_3_.refs_0_, bf16[1024,1792]{1,0:T(8,128)(2,1)} %get-tuple-element.99.refs_5_.refs_1_, bf16[2560,3584]{1,0:T(8,128)(2,1)} %weave.1.wg_ref.wu_ref.refs_2_.refs_3_, bf16[2560,3584]{1,0:T(8,128)(2,1)} %weave.1.wg_ref.wu_ref.refs_2_.refs_3_), custom_call_target="tpu_custom_call" | custom-call | flops 6979321856 | bytes 65536 | tf_op jit(solution)/shard_map/sum_nt/pallas_call | solution.py:552
  694.6 16.1 %plain_nn.2 = bf16[1024,2560]{1,0:T(8,128)(2,1)} custom-call(bf16[1024,1792]{1,0:T(8,128)(2,1)} %get-tuple-element.106.refs_0_.a_ref, bf16[1792,2560]{1,0:T(8,128)(2,1)} %constant_dynamic-update-slice_fusion.wd_ref.b_ref), custom_call_target="tpu_custom_call" | custom-call | flops 4294967296 | bytes 65536 | tf_op jit(solution)/shard_map/plain_nn/pallas_call | solution.py:571
  710.7 15.9 %plain_nn.3 = bf16[1024,2560]{1,0:T(8,128)(2,1)} custom-call(bf16[1024,1792]{1,0:T(8,128)(2,1)} %get-tuple-element.107.refs_1_.a_ref, bf16[1792,2560]{1,0:T(8,128)(2,1)} %constant_dynamic-update-slice_fusion.wd_ref.b_ref), custom_call_target="tpu_custom_call" | custom-call | flops 4294967296 | bytes 65536 | tf_op jit(solution)/shard_map/plain_nn/pallas_call | solution.py:571
  734.6 5.5 fusion.70
  740.1 9.9 convolution_convert_fusion.4.dctx_ref
  756.4 27.3 %attend_back.4 = (bf16[256,2560]{1,0:T(8,128)(2,1)}, bf16[256,1280]{1,0:T(8,128)(2,1)S(1)}, bf16[256,1280]{1,0:T(8,128)(2,1)S(1)}, bf16[256,1280]{1,0:T(8,128)(2,1)S(1)}, bf16[256,1280]{1,0:T(8,128)(2,1)S(1)}) custom-call(bf16[512,3840]{1,0:T(8,128)(2,1)} %project.1.q_ref, bf16[256,2560]{1,0:T(8,128)(2,1)} %convolution_convert_fusion.4.dctx_ref, ...), custom_call_target="tpu_custom_call" | custom-call | flops 26843545600 | bytes 65536 | tf_op jit(solution)/shard_map/attend_back/pallas_call | solution.py:160
  783.7 26.9 %attend_back.5 = (bf16[256,2560]{1,0:T(8,128)(2,1)}, bf16[256,1280]{1,0:T(8,128)(2,1)S(1)}, bf16[256,1280]{1,0:T(8,128)(2,1)S(1)}, bf16[256,1280]{1,0:T(8,128)(2,1)S(1)}, bf16[256,1280]{1,0:T(8,128)(2,1)S(1)}) custom-call(bf16[512,3840]{1,0:T(8,128)(2,1)} %project.1.q_ref, ...), custom_call_target="tpu_custom_call", output_to_operand_aliasing={{0}: (12, {}), {1}: (13, {}), {2}: (14, {}), {3}: (15, {}),... | custom-call | flops 26843545600 | bytes 65536 | tf_op jit(solution)/shard_map/attend_back/pallas_call | solution.py:160
  820.9 5.1 fusion.69
  827.0 9.5 convolution_convert_fusion.3.dctx_ref
  836.6 9.2 convolution_convert_fusion.1
  859.3 26.8 %attend_back.6 = (bf16[256,2560]{1,0:T(8,128)(2,1)}, bf16[256,1280]{1,0:T(8,128)(2,1)S(1)}, bf16[256,1280]{1,0:T(8,128)(2,1)S(1)}, bf16[256,1280]{1,0:T(8,128)(2,1)S(1)}, bf16[256,1280]{1,0:T(8,128)(2,1)S(1)}) custom-call(bf16[512,3840]{1,0:T(8,128)(2,1)} %project.1.q_ref, bf16[256,2560]{1,0:T(8,128)(2,1)} %convolution_convert_fusion.3.dctx_ref, ...), custom_call_target="tpu_custom_call" | custom-call | flops 26843545600 | bytes 65536 | tf_op jit(solution)/shard_map/attend_back/pallas_call | solution.py:160
  888.7 34.2 %collective-permute-done.42 = bf16[320,2560]{1,0:T(8,128)(2,1)} collective-permute-done((bf16[320,2560]{1,0:T(8,128)(2,1)}, bf16[320,2560]{1,0:T(8,128)(2,1)}, u32[]{:S(2)}, u32[]{:S(2)}) %collective-permute-start.42) | collective-permute-done | bytes 1638432 | tf_op jit(solution)/shard_map/ppermute | solution.py:273
  924.2 4.9 fusion.27
  929.0 5.6 collective-permute-done.34
  936.6 11.0 collective-permute-done.36
  948.4 26.8 %attend_back.7 = (bf16[256,2560]{1,0:T(8,128)(2,1)}, bf16[256,1280]{1,0:T(8,128)(2,1)S(1)}, bf16[256,1280]{1,0:T(8,128)(2,1)S(1)}, bf16[256,1280]{1,0:T(8,128)(2,1)S(1)}, bf16[256,1280]{1,0:T(8,128)(2,1)S(1)}) custom-call(bf16[512,3840]{1,0:T(8,128)(2,1)} %project.1.q_ref, ...), custom_call_target="tpu_custom_call", output_to_operand_aliasing={{0}: (12, {}), {1}: (13, {}), {2}: (14, {}), {3}: (15, {}),... | custom-call | flops 26843545600 | bytes 65536 | tf_op jit(solution)/shard_map/attend_back/pallas_call | solution.py:160
  976.0 31.2 %all-reduce.6.cloned.1.call-done = bf16[896,2560]{1,0:T(8,128)(2,1)} async-done(((bf16[896,2560]{1,0:T(8,128)(2,1)}), bf16[896,2560]{1,0:T(8,128)(2,1)}) %all-reduce.6.cloned.1.call-update) | async-done | bytes 4587536 | tf_op jit(solution)/shard_map/psum | solution.py:708
  1012.1 5.5 reshape.284
  1031.1 10.1 convolution_convert_fusion
  1042.7 11.6 fusion
  1058.3 31.9 %collective-permute-done.47.other_ref = bf16[256,1280]{1,0:T(8,128)(2,1)S(1)} collective-permute-done((bf16[256,1280]{1,0:T(8,128)(2,1)S(1)}, bf16[256,1280]{1,0:T(8,128)(2,1)S(1)}, u32[]{:S(2)}, u32[]{:S(2)}) %collective-permute-start.47) | collective-permute-done | bytes 655392 | tf_op jit(solution)/shard_map/ppermute | solution.py:595
  1094.9 5.1 dynamic-slice_bitcast_fusion.21
  1103.6 8.1 convert_element_type.330
  1114.0 5.0 dynamic-slice_bitcast_fusion.2
  1121.1 10.9 multiply_reduce_fusion
  1133.7 6.1 convolution_convert_fusion.2
  1141.8 6.2 copy.67
  1151.6 11.9 collective-permute-done.60
  1165.7 6.0 fusion.18
  1172.0 27.7 %collective-permute-done.62 = bf16[320,2560]{1,0:T(8,128)(2,1)} collective-permute-done((bf16[320,2560]{1,0:T(8,128)(2,1)}, bf16[320,2560]{1,0:T(8,128)(2,1)}, u32[]{:S(2)}, u32[]{:S(2)}) %collective-permute-start.62) | collective-permute-done | bytes 1638432 | tf_op jit(solution)/shard_map/ppermute | solution.py:273
  1200.8 4.9 fusion.24
  1205.7 12.3 collective-permute-done.56
  1220.4 17.9 %collective-permute-done.58 = bf16[320,1408]{1,0:T(8,128)(2,1)S(1)} collective-permute-done((bf16[320,1408]{1,0:T(8,128)(2,1)S(1)}, bf16[320,1408]{1,0:T(8,128)(2,1)S(1)}, u32[]{:S(2)}, u32[]{:S(2)}) %collective-permute-start.58) | collective-permute-done | bytes 901152 | tf_op jit(solution)/shard_map/ppermute | solution.py:273
  1242.1 18.5 %all-gather.20.cloned.1.call-done = bf16[320,14336]{1,0:T(8,128)(2,1)} async-done(((bf16[80,14336]{1,0:T(8,128)(2,1)}), bf16[320,14336]{1,0:T(8,128)(2,1)}) %all-gather.20.cloned.1.call-update) | async-done | bytes 9175056 | tf_op jit(solution)/shard_map/all_gather | solution.py:755
  1260.6 25.9 %collective-permute-done.51 = bf16[256,2560]{1,0:T(8,128)(2,1)} collective-permute-done((bf16[256,2560]{1,0:T(8,128)(2,1)}, bf16[256,2560]{1,0:T(8,128)(2,1)}, u32[]{:S(2)}, u32[]{:S(2)}) %collective-permute-start.51) | collective-permute-done | bytes 1310752 | tf_op jit(solution)/shard_map/ppermute | solution.py:273
  1293.6 49.2 %collective-permute-done.54 = bf16[256,2560]{1,0:T(8,128)(2,1)} collective-permute-done((bf16[256,2560]{1,0:T(8,128)(2,1)}, bf16[256,2560]{1,0:T(8,128)(2,1)}, u32[]{:S(2)}, u32[]{:S(2)}) %collective-permute-start.54) | collective-permute-done | bytes 1310752 | tf_op jit(solution)/shard_map/ppermute | solution.py:273
  1347.6 13.0 slice_convert_fusion
  1360.6 56.3 %all-reduce.8.cloned.1.call-done = (bf16[320,1408]{1,0:T(8,128)(2,1)}, bf16[320,2560]{1,0:T(8,128)(2,1)}, bf16[320,2560]{1,0:T(8,128)(2,1)}) async-done(((bf16[320,1408]{1,0:T(8,128)(2,1)}, bf16[320,2560]{1,0:T(8,128)(2,1)}, bf16[320,2560]{1,0:T(8,128)(2,1)}), (bf16[320,1408]{1,0:T(8,128)(2,1)}, bf16[320,2560]{1,0:T(8,128)(2,1)}, bf16[320,2560]{1,0:T(8,128)(2,1)})) %all-reduce.8.cloned.1.call-update) | async-done | bytes 4177936 | tf_op jit(solution)/shard_map/psum | solution.py:767
  (406 shorter events, 221.6 us)
Async XLA Ops:
  7.2 160.9 %all-gather.8.cloned.1.call-start = ((), (), s32[]{:S(2)}) async-start(), calls=%async_computation.1 | async-start | bytes 22855680 | tf_op jit(solution)/shard_map/all_gather | solution.py:627
  13.4 231.0 %all-gather.10.cloned.1.call-start = ((), (), s32[]{:S(2)}) async-start(), calls=%async_computation.2 | async-start | bytes 14745600 | tf_op jit(solution)/shard_map/all_gather | solution.py:628
  14.1 293.7 %all-gather.12.cloned.1.call-start = ((), (), s32[]{:S(2)}) async-start(), calls=%async_computation.3 | async-start | bytes 6553600 | tf_op jit(solution)/shard_map/all_gather | solution.py:265
  17.8 44.2 %collective-permute-start = (bf16[320,1792]{1,0:T(8,128)(2,1)}, bf16[320,1792]{1,0:T(8,128)(2,1)}, u32[]{:S(2)}, u32[]{:S(2)}) collective-permute-start(bf16[320,1792]{1,0:T(8,128)(2,1)} %columns_for.4), channel_id=1, source_target_pairs={{0,8},{4,12},{8,0},{12,4},{16,24},{20,28},{24,16},{28,20},{1,9},{5... | collective-permute-start | bytes 3440648 | tf_op jit(solution)/shard_map/ppermute | solution.py:409
  23.5 55.2 %collective-permute-start.2 = (bf16[320,1792]{1,0:T(8,128)(2,1)}, bf16[320,1792]{1,0:T(8,128)(2,1)}, u32[]{:S(2)}, u32[]{:S(2)}) collective-permute-start(bf16[320,1792]{1,0:T(8,128)(2,1)} %columns_for.5), channel_id=1, source_target_pairs={{0,16},{4,20},{8,24},{12,28},{16,0},{20,4},{24,8},{28,12},{1,17},{... | collective-permute-start | bytes 3440648 | tf_op jit(solution)/shard_map/ppermute | solution.py:409
  28.8 69.0 %collective-permute-start.4 = (bf16[320,1792]{1,0:T(8,128)(2,1)}, bf16[320,1792]{1,0:T(8,128)(2,1)}, u32[]{:S(2)}, u32[]{:S(2)}) collective-permute-start(bf16[320,1792]{1,0:T(8,128)(2,1)} %columns_for.6), channel_id=1, source_target_pairs={{0,24},{4,28},{8,16},{12,20},{16,8},{20,12},{24,0},{28,4},{1,25},{... | collective-permute-start | bytes 3440648 | tf_op jit(solution)/shard_map/ppermute | solution.py:409
  61.9 112.2 %collective-permute-start.1 = (bf16[320,1792]{1,0:T(8,128)(2,1)}, bf16[320,1792]{1,0:T(8,128)(2,1)}, u32[]{:S(2)}, u32[]{:S(2)}) collective-permute-start(bf16[320,1792]{1,0:T(8,128)(2,1)} %collective-permute-done.refs_2_), channel_id=1, source_target_pairs={{0,1},{1,0},{2,3},{3,2},{4,5},{5,4},{6,7},{7,6},{8,9},{9,8},{10,11... | collective-permute-start | bytes 3440648 | tf_op jit(solution)/shard_map/ppermute | solution.py:412
  78.6 95.5 %collective-permute-start.3 = (bf16[320,1792]{1,0:T(8,128)(2,1)}, bf16[320,1792]{1,0:T(8,128)(2,1)}, u32[]{:S(2)}, u32[]{:S(2)}) collective-permute-start(bf16[320,1792]{1,0:T(8,128)(2,1)} %collective-permute-done.2.refs_4_), channel_id=1, source_target_pairs={{0,1},{1,0},{2,3},{3,2},{4,5},{5,4},{6,7},{7,6},{8,9},{9,8},{10,11... | collective-permute-start | bytes 3440648 | tf_op jit(solution)/shard_map/ppermute | solution.py:412
  97.8 76.3 %collective-permute-start.5 = (bf16[320,1792]{1,0:T(8,128)(2,1)}, bf16[320,1792]{1,0:T(8,128)(2,1)}, u32[]{:S(2)}, u32[]{:S(2)}) collective-permute-start(bf16[320,1792]{1,0:T(8,128)(2,1)} %collective-permute-done.4.refs_6_), channel_id=1, source_target_pairs={{0,1},{1,0},{2,3},{3,2},{4,5},{5,4},{6,7},{7,6},{8,9},{9,8},{10,11... | collective-permute-start | bytes 3440648 | tf_op jit(solution)/shard_map/ppermute | solution.py:412
  193.5 225.1 %all-gather.14.cloned.1.call-start = ((), (), s32[]{:S(2)}) async-start(), calls=%async_computation.4 | async-start | bytes 6553600 | tf_op jit(solution)/shard_map/all_gather | solution.py:265
  195.1 17.1 %collective-permute-start.6 = (bf16[256,1280]{1,0:T(8,128)(2,1)S(1)}, bf16[256,1280]{1,0:T(8,128)(2,1)S(1)}, u32[]{:S(2)}, u32[]{:S(2)}) collective-permute-start(bf16[256,1280]{1,0:T(8,128)(2,1)S(1)} %get-tuple-element.252.refs_0_), channel_id=1, source_target_pairs={{0,1},{1,2},{2,3},{4,5},{5,6},{6,7},{8,9},{9,10},{10,11},{12,13},{... | collective-permute-start | bytes 1966088 | tf_op jit(solution)/shard_map/ppermute | solution.py:662
  307.9 151.5 %all-gather.18.cloned.1.call-start = ((), (), s32[]{:S(2)}) async-start(), calls=%async_computation.6 | async-start | bytes 6553600 | tf_op jit(solution)/shard_map/all_gather | solution.py:265
  307.9 16.5 %collective-permute-start.9 = (bf16[256,1280]{1,0:T(8,128)(2,1)S(1)}, bf16[256,1280]{1,0:T(8,128)(2,1)S(1)}, u32[]{:S(2)}, u32[]{:S(2)}) collective-permute-start(bf16[256,1280]{1,0:T(8,128)(2,1)S(1)} %get-tuple-element.251.refs_0_), channel_id=1, source_target_pairs={{0,1},{1,2},{2,3},{4,5},{5,6},{6,7},{8,9},{9,10},{10,11},{12,13},{... | collective-permute-start | bytes 1966088 | tf_op jit(solution)/shard_map/ppermute | solution.py:662
  363.1 160.0 %all-gather.16.cloned.1.call-start = ((), (), s32[]{:S(2)}) async-start(), calls=%async_computation.5 | async-start | bytes 6553600 | tf_op jit(solution)/shard_map/all_gather | solution.py:265
  363.7 489.1 %reduce-scatter.2.cloned.1.call-start = ((), (), s32[]{:S(2)}) async-start(), calls=%async_computation.7 | async-start | bytes 11468800 | tf_op jit(solution)/shard_map/reduce_scatter | solution.py:706
  363.7 50.1 %collective-permute-start.20 = (bf16[896,2560]{1,0:T(8,128)(2,1)}, bf16[896,2560]{1,0:T(8,128)(2,1)}, u32[]{:S(2)}, u32[]{:S(2)}) collective-permute-start(bf16[896,2560]{1,0:T(8,128)(2,1)} %param.23), channel_id=1, source_target_pairs={{0,4},{4,0},{8,12},{12,8},{16,20},{20,16},{24,28},{28,24},{1,5},{5... | collective-permute-start | bytes 13762568 | tf_op jit(solution)/shard_map/ppermute | solution.py:256
  373.5 5.3 collective-permute-start.14
  374.0 8.1 collective-permute-start.16
  375.4 8.6 collective-permute-start.18
  379.7 5.9 collective-permute-start.17
  588.0 16.8 %collective-permute-start.21 = (bf16[4,8,80,1792]{3,2,1,0:T(8,128)(2,1)}, bf16[4,8,80,1792]{3,2,1,0:T(8,128)(2,1)}, u32[]{:S(2)}, u32[]{:S(2)}) collective-permute-start(bf16[4,8,80,1792]{3,2,1,0:T(8,128)(2,1)} %sum_tn.4), channel_id=1, source_target_pairs={{0,4},{4,0},{8,12},{12,8},{16,20},{20,16},{24,28},{28,24},{1,5},{5... | collective-permute-start | bytes 27525128 | tf_op jit(solution)/shard_map/ppermute | solution.py:256
  633.5 373.6 %all-reduce.6.cloned.1.call-start = ((), (), s32[]{:S(2)}) async-start(), calls=%async_computation.8 | async-start | bytes 9175040 | tf_op jit(solution)/shard_map/psum | solution.py:708
  633.6 18.1 %collective-permute-start.22 = (bf16[896,2560]{1,0:T(8,128)(2,1)}, bf16[896,2560]{1,0:T(8,128)(2,1)}, u32[]{:S(2)}, u32[]{:S(2)}) collective-permute-start(bf16[896,2560]{1,0:T(8,128)(2,1)} %sum_tn.5), channel_id=1, source_target_pairs={{0,4},{4,0},{8,12},{12,8},{16,20},{20,16},{24,28},{28,24},{1,5},{5... | collective-permute-start | bytes 13762568 | tf_op jit(solution)/shard_map/ppermute | solution.py:256
  643.5 193.1 %collective-permute-start.37 = (bf16[512,1280]{1,0:T(8,128)(2,1)}, bf16[512,1280]{1,0:T(8,128)(2,1)}, u32[]{:S(2)}, u32[]{:S(2)}) collective-permute-start(bf16[512,1280]{1,0:T(8,128)(2,1)} %get-tuple-element.128), channel_id=1, source_target_pairs={{0,4},{4,0},{8,12},{12,8},{16,20},{20,16},{24,28},{28,24},{1,5},{5... | collective-permute-start | bytes 3932168 | tf_op jit(solution)/shard_map/ppermute | solution.py:256
  649.0 81.1 %collective-permute-start.24 = (bf16[256,2560]{1,0:T(8,128)(2,1)}, bf16[256,2560]{1,0:T(8,128)(2,1)}, u32[]{:S(2)}, u32[]{:S(2)}) collective-permute-start(bf16[256,2560]{1,0:T(8,128)(2,1)} %get-tuple-element.242), channel_id=1, source_target_pairs={{0,8},{4,12},{8,0},{12,4},{16,24},{20,28},{24,16},{28,20},{1,9},{5... | collective-permute-start | bytes 3932168 | tf_op jit(solution)/shard_map/ppermute | solution.py:273
  650.2 79.9 %collective-permute-start.25 = (bf16[256,2560]{1,0:T(8,128)(2,1)}, bf16[256,2560]{1,0:T(8,128)(2,1)}, u32[]{:S(2)}, u32[]{:S(2)}) collective-permute-start(bf16[256,2560]{1,0:T(8,128)(2,1)} %get-tuple-element.241), channel_id=1, source_target_pairs={{0,16},{4,20},{8,24},{12,28},{16,0},{20,4},{24,8},{28,12},{1,17},{... | collective-permute-start | bytes 3932168 | tf_op jit(solution)/shard_map/ppermute | solution.py:273
  650.9 79.2 %collective-permute-start.26 = (bf16[256,2560]{1,0:T(8,128)(2,1)}, bf16[256,2560]{1,0:T(8,128)(2,1)}, u32[]{:S(2)}, u32[]{:S(2)}) collective-permute-start(bf16[256,2560]{1,0:T(8,128)(2,1)} %get-tuple-element.240), channel_id=1, source_target_pairs={{0,24},{4,28},{8,16},{12,20},{16,8},{20,12},{24,0},{28,4},{1,25},{... | collective-permute-start | bytes 3932168 | tf_op jit(solution)/shard_map/ppermute | solution.py:273
  750.0 86.6 %collective-permute-start.38 = (bf16[256,2560]{1,0:T(8,128)(2,1)}, bf16[256,2560]{1,0:T(8,128)(2,1)}, u32[]{:S(2)}, u32[]{:S(2)}) collective-permute-start(bf16[256,2560]{1,0:T(8,128)(2,1)} %get-tuple-element.225), channel_id=1, source_target_pairs={{0,4},{4,0},{8,12},{12,8},{16,20},{20,16},{24,28},{28,24},{1,5},{5... | collective-permute-start | bytes 3932168 | tf_op jit(solution)/shard_map/ppermute | solution.py:256
  753.7 60.4 %collective-permute-start.30 = (bf16[256,2560]{1,0:T(8,128)(2,1)}, bf16[256,2560]{1,0:T(8,128)(2,1)}, u32[]{:S(2)}, u32[]{:S(2)}) collective-permute-start(bf16[256,2560]{1,0:T(8,128)(2,1)} %get-tuple-element.246), channel_id=1, source_target_pairs={{0,8},{4,12},{8,0},{12,4},{16,24},{20,28},{24,16},{28,20},{1,9},{5... | collective-permute-start | bytes 3932168 | tf_op jit(solution)/shard_map/ppermute | solution.py:273
  754.8 60.2 %collective-permute-start.31 = (bf16[256,2560]{1,0:T(8,128)(2,1)}, bf16[256,2560]{1,0:T(8,128)(2,1)}, u32[]{:S(2)}, u32[]{:S(2)}) collective-permute-start(bf16[256,2560]{1,0:T(8,128)(2,1)} %get-tuple-element.245), channel_id=1, source_target_pairs={{0,16},{4,20},{8,24},{12,28},{16,0},{20,4},{24,8},{28,12},{1,17},{... | collective-permute-start | bytes 3932168 | tf_op jit(solution)/shard_map/ppermute | solution.py:273
  755.6 60.7 %collective-permute-start.32 = (bf16[256,2560]{1,0:T(8,128)(2,1)}, bf16[256,2560]{1,0:T(8,128)(2,1)}, u32[]{:S(2)}, u32[]{:S(2)}) collective-permute-start(bf16[256,2560]{1,0:T(8,128)(2,1)} %get-tuple-element.244), channel_id=1, source_target_pairs={{0,24},{4,28},{8,16},{12,20},{16,8},{20,12},{24,0},{28,4},{1,25},{... | collective-permute-start | bytes 3932168 | tf_op jit(solution)/shard_map/ppermute | solution.py:273
  811.4 449.2 %all-gather.20.cloned.1.call-start = ((), (), s32[]{:S(2)}) async-start(), calls=%async_computation.9 | async-start | bytes 11468800 | tf_op jit(solution)/shard_map/all_gather | solution.py:755
  814.1 216.4 %collective-permute-start.43 = (bf16[256,2560]{1,0:T(8,128)(2,1)}, bf16[256,2560]{1,0:T(8,128)(2,1)}, u32[]{:S(2)}, u32[]{:S(2)}) collective-permute-start(bf16[256,2560]{1,0:T(8,128)(2,1)} %get-tuple-element.123), channel_id=1, source_target_pairs={{0,4},{4,0},{8,12},{12,8},{16,20},{20,16},{24,28},{28,24},{1,5},{5... | collective-permute-start | bytes 3932168 | tf_op jit(solution)/shard_map/ppermute | solution.py:256
  815.1 10.9 collective-permute-start.27
  826.0 10.6 collective-permute-start.39
  850.1 37.3 %collective-permute-start.40 = (bf16[320,2560]{1,0:T(8,128)(2,1)}, bf16[320,2560]{1,0:T(8,128)(2,1)}, u32[]{:S(2)}, u32[]{:S(2)}) collective-permute-start(bf16[320,2560]{1,0:T(8,128)(2,1)} %get-tuple-element.232), channel_id=1, source_target_pairs={{0,8},{4,12},{8,0},{12,4},{16,24},{20,28},{24,16},{28,20},{1,9},{5... | collective-permute-start | bytes 4915208 | tf_op jit(solution)/shard_map/ppermute | solution.py:273
  851.0 37.3 %collective-permute-start.41 = (bf16[320,2560]{1,0:T(8,128)(2,1)}, bf16[320,2560]{1,0:T(8,128)(2,1)}, u32[]{:S(2)}, u32[]{:S(2)}) collective-permute-start(bf16[320,2560]{1,0:T(8,128)(2,1)} %get-tuple-element.234), channel_id=1, source_target_pairs={{0,16},{4,20},{8,24},{12,28},{16,0},{20,4},{24,8},{28,12},{1,17},{... | collective-permute-start | bytes 4915208 | tf_op jit(solution)/shard_map/ppermute | solution.py:273
  851.5 71.5 %collective-permute-start.42 = (bf16[320,2560]{1,0:T(8,128)(2,1)}, bf16[320,2560]{1,0:T(8,128)(2,1)}, u32[]{:S(2)}, u32[]{:S(2)}) collective-permute-start(bf16[320,2560]{1,0:T(8,128)(2,1)} %get-tuple-element.233), channel_id=1, source_target_pairs={{0,24},{4,28},{8,16},{12,20},{16,8},{20,12},{24,0},{28,4},{1,25},{... | collective-permute-start | bytes 4915208 | tf_op jit(solution)/shard_map/ppermute | solution.py:273
  854.5 31.6 %collective-permute-start.33 = (bf16[4,80,1792]{2,1,0:T(8,128)(2,1)S(1)}, bf16[4,80,1792]{2,1,0:T(8,128)(2,1)S(1)}, u32[]{:S(2)}, u32[]{:S(2)}) collective-permute-start(bf16[4,80,1792]{2,1,0:T(8,128)(2,1)S(1)} %get-tuple-element.263), channel_id=1, source_target_pairs={{0,4},{4,0},{8,12},{12,8},{16,20},{20,16},{24,28},{28,24},{1,5},{5... | collective-permute-start | bytes 3440648 | tf_op jit(solution)/shard_map/ppermute | solution.py:256
  886.1 140.7 %collective-permute-start.23 = (bf16[512,1280]{1,0:T(8,128)(2,1)}, bf16[512,1280]{1,0:T(8,128)(2,1)}, u32[]{:S(2)}, u32[]{:S(2)}) collective-permute-start(bf16[512,1280]{1,0:T(8,128)(2,1)} %get-tuple-element.110), channel_id=1, source_target_pairs={{0,4},{4,0},{8,12},{12,8},{16,20},{20,16},{24,28},{28,24},{1,5},{5... | collective-permute-start | bytes 3932168 | tf_op jit(solution)/shard_map/ppermute | solution.py:256
  887.4 47.2 %collective-permute-start.34 = (bf16[1,2,80,1792]{3,2,1,0:T(8,128)(2,1)S(1)}, bf16[1,2,80,1792]{3,2,1,0:T(8,128)(2,1)S(1)}, u32[]{:S(2)}, u32[]{:S(2)}) collective-permute-start(bf16[1,2,80,1792]{3,2,1,0:T(8,128)(2,1)S(1)} %get-tuple-element.260), channel_id=1, source_target_pairs={{0,8},{4,12},{8,0},{12,4},{16,24},{20,28},{24,16},{28,20},{1,9},{5... | collective-permute-start | bytes 1720328 | tf_op jit(solution)/shard_map/ppermute | solution.py:300
  888.3 48.2 %collective-permute-start.35 = (bf16[1,2,80,1792]{3,2,1,0:T(8,128)(2,1)S(1)}, bf16[1,2,80,1792]{3,2,1,0:T(8,128)(2,1)S(1)}, u32[]{:S(2)}, u32[]{:S(2)}) collective-permute-start(bf16[1,2,80,1792]{3,2,1,0:T(8,128)(2,1)S(1)} %get-tuple-element.259), channel_id=1, source_target_pairs={{0,16},{4,20},{8,24},{12,28},{16,0},{20,4},{24,8},{28,12},{1,17},{... | collective-permute-start | bytes 1720328 | tf_op jit(solution)/shard_map/ppermute | solution.py:300
  923.0 24.6 %collective-permute-start.36 = (bf16[1,2,80,1792]{3,2,1,0:T(8,128)(2,1)S(1)}, bf16[1,2,80,1792]{3,2,1,0:T(8,128)(2,1)S(1)}, u32[]{:S(2)}, u32[]{:S(2)}) collective-permute-start(bf16[1,2,80,1792]{3,2,1,0:T(8,128)(2,1)S(1)} %get-tuple-element.258), channel_id=1, source_target_pairs={{0,24},{4,28},{8,16},{12,20},{16,8},{20,12},{24,0},{28,4},{1,25},{... | collective-permute-start | bytes 1720328 | tf_op jit(solution)/shard_map/ppermute | solution.py:300
  934.6 88.6 %collective-permute-start.28 = (bf16[256,1280]{1,0:T(8,128)(2,1)}, bf16[256,1280]{1,0:T(8,128)(2,1)}, u32[]{:S(2)}, u32[]{:S(2)}) collective-permute-start(bf16[256,1280]{1,0:T(8,128)(2,1)} %add_convert_fusion.5), channel_id=1, source_target_pairs={{3,2},{2,1},{7,6},{6,5},{11,10},{10,9},{15,14},{14,13},{19,18},{18... | collective-permute-start | bytes 1966088 | tf_op jit(solution)/shard_map/ppermute | solution.py:595
  1022.5 8.0 collective-permute-start.44
  1024.5 29.7 %collective-permute-start.29 = (bf16[256,1280]{1,0:T(8,128)(2,1)S(1)}, bf16[256,1280]{1,0:T(8,128)(2,1)S(1)}, u32[]{:S(2)}, u32[]{:S(2)}) collective-permute-start(bf16[256,1280]{1,0:T(8,128)(2,1)S(1)} %add_convert_fusion.4), channel_id=1, source_target_pairs={{3,2},{2,1},{1,0},{7,6},{6,5},{5,4},{11,10},{10,9},{9,8},{15,14},{... | collective-permute-start | bytes 1966088 | tf_op jit(solution)/shard_map/ppermute | solution.py:595
  1029.7 11.5 collective-permute-start.46
  1041.4 48.9 %collective-permute-start.47 = (bf16[256,1280]{1,0:T(8,128)(2,1)S(1)}, bf16[256,1280]{1,0:T(8,128)(2,1)S(1)}, u32[]{:S(2)}, u32[]{:S(2)}) collective-permute-start(bf16[256,1280]{1,0:T(8,128)(2,1)S(1)} %add_convert_fusion.2), channel_id=1, source_target_pairs={{3,2},{2,1},{1,0},{7,6},{6,5},{5,4},{11,10},{10,9},{9,8},{15,14},{... | collective-permute-start | bytes 1966088 | tf_op jit(solution)/shard_map/ppermute | solution.py:595
  1094.4 322.5 %all-reduce.8.cloned.1.call-start = ((), (), s32[]{:S(2)}) async-start(), calls=%async_computation.10 | async-start | bytes 8355840 | tf_op jit(solution)/shard_map/psum | solution.py:767
  1099.9 50.5 %collective-permute-start.50 = (bf16[256,2560]{1,0:T(8,128)(2,1)}, bf16[256,2560]{1,0:T(8,128)(2,1)}, u32[]{:S(2)}, u32[]{:S(2)}) collective-permute-start(bf16[256,2560]{1,0:T(8,128)(2,1)} %get-tuple-element.238), channel_id=1, source_target_pairs={{0,8},{4,12},{8,0},{12,4},{16,24},{20,28},{24,16},{28,20},{1,9},{5... | collective-permute-start | bytes 3932168 | tf_op jit(solution)/shard_map/ppermute | solution.py:273
  1111.7 20.7 %collective-permute-start.48 = (bf16[256,1280]{1,0:T(8,128)(2,1)S(1)}, bf16[256,1280]{1,0:T(8,128)(2,1)}, u32[]{:S(2)}, u32[]{:S(2)}) collective-permute-start(bf16[256,1280]{1,0:T(8,128)(2,1)S(1)} %copy-done.59), channel_id=1, source_target_pairs={{0,4},{4,0},{8,12},{12,8},{16,20},{20,16},{24,28},{28,24},{1,5},{5... | collective-permute-start | bytes 1966088 | tf_op jit(solution)/shard_map/ppermute | solution.py:256
  1119.0 44.6 %collective-permute-start.60 = (bf16[320,2560]{1,0:T(8,128)(2,1)}, bf16[320,2560]{1,0:T(8,128)(2,1)}, u32[]{:S(2)}, u32[]{:S(2)}) collective-permute-start(bf16[320,2560]{1,0:T(8,128)(2,1)} %get-tuple-element.229), channel_id=1, source_target_pairs={{0,8},{4,12},{8,0},{12,4},{16,24},{20,28},{24,16},{28,20},{1,9},{5... | collective-permute-start | bytes 4915208 | tf_op jit(solution)/shard_map/ppermute | solution.py:273
  1119.3 52.4 %collective-permute-start.61 = (bf16[320,2560]{1,0:T(8,128)(2,1)}, bf16[320,2560]{1,0:T(8,128)(2,1)}, u32[]{:S(2)}, u32[]{:S(2)}) collective-permute-start(bf16[320,2560]{1,0:T(8,128)(2,1)} %get-tuple-element.231), channel_id=1, source_target_pairs={{0,16},{4,20},{8,24},{12,28},{16,0},{20,4},{24,8},{28,12},{1,17},{... | collective-permute-start | bytes 4915208 | tf_op jit(solution)/shard_map/ppermute | solution.py:273
  1120.5 13.2 collective-permute-start.49
  1132.4 67.2 %collective-permute-start.62 = (bf16[320,2560]{1,0:T(8,128)(2,1)}, bf16[320,2560]{1,0:T(8,128)(2,1)}, u32[]{:S(2)}, u32[]{:S(2)}) collective-permute-start(bf16[320,2560]{1,0:T(8,128)(2,1)} %get-tuple-element.230), channel_id=1, source_target_pairs={{0,24},{4,28},{8,16},{12,20},{16,8},{20,12},{24,0},{28,4},{1,25},{... | collective-permute-start | bytes 4915208 | tf_op jit(solution)/shard_map/ppermute | solution.py:273
  1150.1 67.9 %collective-permute-start.56 = (bf16[320,1408]{1,0:T(8,128)(2,1)S(1)}, bf16[320,1408]{1,0:T(8,128)(2,1)S(1)}, u32[]{:S(2)}, u32[]{:S(2)}) collective-permute-start(bf16[320,1408]{1,0:T(8,128)(2,1)S(1)} %get-tuple-element.253), channel_id=1, source_target_pairs={{0,8},{4,12},{8,0},{12,4},{16,24},{20,28},{24,16},{28,20},{1,9},{5... | collective-permute-start | bytes 2703368 | tf_op jit(solution)/shard_map/ppermute | solution.py:273
  1150.5 68.8 %collective-permute-start.57 = (bf16[320,1408]{1,0:T(8,128)(2,1)S(1)}, bf16[320,1408]{1,0:T(8,128)(2,1)S(1)}, u32[]{:S(2)}, u32[]{:S(2)}) collective-permute-start(bf16[320,1408]{1,0:T(8,128)(2,1)S(1)} %get-tuple-element.255), channel_id=1, source_target_pairs={{0,16},{4,20},{8,24},{12,28},{16,0},{20,4},{24,8},{28,12},{1,17},{... | collective-permute-start | bytes 2703368 | tf_op jit(solution)/shard_map/ppermute | solution.py:273
  1163.6 74.7 %collective-permute-start.58 = (bf16[320,1408]{1,0:T(8,128)(2,1)S(1)}, bf16[320,1408]{1,0:T(8,128)(2,1)S(1)}, u32[]{:S(2)}, u32[]{:S(2)}) collective-permute-start(bf16[320,1408]{1,0:T(8,128)(2,1)S(1)} %get-tuple-element.254), channel_id=1, source_target_pairs={{0,24},{4,28},{8,16},{12,20},{16,8},{20,12},{24,0},{28,4},{1,25},{... | collective-permute-start | bytes 2703368 | tf_op jit(solution)/shard_map/ppermute | solution.py:273
  1171.7 114.9 %collective-permute-start.51 = (bf16[256,2560]{1,0:T(8,128)(2,1)}, bf16[256,2560]{1,0:T(8,128)(2,1)}, u32[]{:S(2)}, u32[]{:S(2)}) collective-permute-start(bf16[256,2560]{1,0:T(8,128)(2,1)} %get-tuple-element.237), channel_id=1, source_target_pairs={{0,16},{4,20},{8,24},{12,28},{16,0},{20,4},{24,8},{28,12},{1,17},{... | collective-permute-start | bytes 3932168 | tf_op jit(solution)/shard_map/ppermute | solution.py:273
  1199.6 86.9 %collective-permute-start.52 = (bf16[256,2560]{1,0:T(8,128)(2,1)}, bf16[256,2560]{1,0:T(8,128)(2,1)}, u32[]{:S(2)}, u32[]{:S(2)}) collective-permute-start(bf16[256,2560]{1,0:T(8,128)(2,1)} %get-tuple-element.236), channel_id=1, source_target_pairs={{0,24},{4,28},{8,16},{12,20},{16,8},{20,12},{24,0},{28,4},{1,25},{... | collective-permute-start | bytes 3932168 | tf_op jit(solution)/shard_map/ppermute | solution.py:273
  1218.0 75.5 %collective-permute-start.53 = (bf16[256,2560]{1,0:T(8,128)(2,1)}, bf16[256,2560]{1,0:T(8,128)(2,1)}, u32[]{:S(2)}, u32[]{:S(2)}) collective-permute-start(bf16[256,2560]{1,0:T(8,128)(2,1)} %get-tuple-element.250), channel_id=1, source_target_pairs={{0,8},{4,12},{8,0},{12,4},{16,24},{20,28},{24,16},{28,20},{1,9},{5... | collective-permute-start | bytes 3932168 | tf_op jit(solution)/shard_map/ppermute | solution.py:273
  1219.2 123.5 %collective-permute-start.54 = (bf16[256,2560]{1,0:T(8,128)(2,1)}, bf16[256,2560]{1,0:T(8,128)(2,1)}, u32[]{:S(2)}, u32[]{:S(2)}) collective-permute-start(bf16[256,2560]{1,0:T(8,128)(2,1)} %get-tuple-element.249), channel_id=1, source_target_pairs={{0,16},{4,20},{8,24},{12,28},{16,0},{20,4},{24,8},{28,12},{1,17},{... | collective-permute-start | bytes 3932168 | tf_op jit(solution)/shard_map/ppermute | solution.py:273
  1238.3 104.5 %collective-permute-start.55 = (bf16[256,2560]{1,0:T(8,128)(2,1)}, bf16[256,2560]{1,0:T(8,128)(2,1)}, u32[]{:S(2)}, u32[]{:S(2)}) collective-permute-start(bf16[256,2560]{1,0:T(8,128)(2,1)} %get-tuple-element.248), channel_id=1, source_target_pairs={{0,24},{4,28},{8,16},{12,20},{16,8},{20,12},{24,0},{28,4},{1,25},{... | collective-permute-start | bytes 3932168 | tf_op jit(solution)/shard_map/ppermute | solution.py:273
  1418.5 7.8 collective-permute-start.59
  (92 other events, 1794.9 us)
Sparse Core Ops, SparseCore 0:
  13.5 154.5 all-gather.7
  170.0 74.3 all-gather.9
  246.8 60.9 all-gather.11
  309.5 61.4 all-gather.13
  373.3 86.0 all-gather.17
  461.6 61.4 all-gather.15
  633.7 156.1 reduce-scatter.1
  811.5 195.6 all-reduce.5
  1094.5 166.0 all-gather.19
  1263.6 153.2 all-reduce.7

commit v6 on v5

--- a/solution.py
+++ b/solution.py
@@ -743,7 +743,7 @@
         kv_sums.append(KeySum(second[1:]))
         kv_sums[-1].hop()
 
-    order.last = order.last + (out_shard, down_total)
+    order.last = order.last + (out_shard,)
     wide_part = exchanged([order.at(pieces[0], *pieces[1:])] + pieces[1:])
     wide_part = order.did(jnp.moveaxis(wide_part.reshape(parts, slab, 2, hidden_own), 0, 2).reshape(slab, 2 * ff))
     query_half = order.did(tn(normed_chip, chip_rows(query_grads[:-1] + [order.at(query_grads[-1])])).astype(bf16))
@@ -783,7 +783,7 @@
         out_total.astype(f32),
         wide_total[:, :ff].astype(f32),
         wide_total[:, ff:].astype(f32),
-        down_total.astype(f32),
+        order.at(down_total).astype(f32),
     )
 
 

time: 1440 us -> 1430 us (level)
    psum x1, waiting for transfers between devices: 31.2 us -> 0.01 us  [body(): down_total = lax.psum(down_grad, 'sp')]
    ppermute x6, waiting for transfers between devices: 31.9 us -> 54.9 us  [hop(): self.running = lax.ppermute(tie(self.running, *before), 'sp', pairs)]
    unnamed x173 -> x163, local copies, waits for them, and re-layouts: 29.8 us -> 28.2 us
  transfers between devices with their start and end apart: 73 -> 73, of which waited for: 30 -> 30; matrix products, arithmetic and copies ran while one was open for 19% -> 18% of each run, Pallas kernels for 26% -> 27%
where the time goes in v6:
time: 1430 us; the launch traced here: 1420 us
  waiting for transfers between devices  591 us (41%)
  Pallas kernels  471 us (33%)
  local copies, waits for them, and re-layouts  103 us (7%)
  other arithmetic  101 us (7%)
  matrix products  86 us (6%)
  starting transfers between devices  57.2 us (4%)
  between operations  15.5 us (1%)
    ppermute x21, waiting for transfers between devices, scatter_chips(): lax.ppermute(take(chip ^ d), 'fsdp', [(j, j ^ 2 * d) for j in range(parts)])  181 us
    pallas_call x4, Pallas kernels, attend_back(): pl.pallas_call(functools.partial(backward_kernel, blocks, len(before)), g...  108 us
    all_gather x4, waiting for transfers between devices, gather_chips(): lax.all_gather(x, 'fsdp', axis=0, tiled=True, axis_index_groups=same_core())  92.8 us
    pallas_call x4, Pallas kernels, sum_tn(): pl.pallas_call(functools.partial(sum_tn_kernel, segments, pairs), grid=(D...  90.1 us
    pallas_call x2, Pallas kernels, feed_forward(): pl.pallas_call(ffn_kernel, grid=(tiles,), in_specs=[full, full, pl.BlockS...  73.6 us
    all_gather x1, waiting for transfers between devices, body(): w_in = lax.all_gather(w_in, 'fsdp', axis=0, tiled=True)  69 us
    psum x1, waiting for transfers between devices, body(): lax.psum((tie(out_shard, down_total), tie(query_shard, wide_total), tie(k...  63 us
    ppermute x3, waiting for transfers between devices, fetch(): lax.ppermute(x, 'fsdp', [(j, j ^ 2 * d) for j in range(parts)])  55.1 us
  transfers between devices with their start and end apart: 73, of which 30 were waited for; matrix products, arithmetic and copies ran while one was open for 18% of the time, Pallas kernels for 27%

profile of v6, /device:TPU:1, one launch (start us, length us, event | category | flops | bytes accessed | tf_op | source)
XLA Modules:
  0.0 1424.7 jit_solution(6055960359621681166)
XLA Ops:
  30.4 5.8 fusion.38
  41.5 20.4 %collective-permute-done.refs_2_ = bf16[320,1792]{1,0:T(8,128)(2,1)} collective-permute-done((bf16[320,1792]{1,0:T(8,128)(2,1)}, bf16[320,1792]{1,0:T(8,128)(2,1)}, u32[]{:S(2)}, u32[]{:S(2)}) %collective-permute-start) | collective-permute-done | bytes 1146912 | tf_op jit(solution)/shard_map/ppermute | solution.py:409
  63.1 15.5 %collective-permute-done.2.refs_4_ = bf16[320,1792]{1,0:T(8,128)(2,1)} collective-permute-done((bf16[320,1792]{1,0:T(8,128)(2,1)}, bf16[320,1792]{1,0:T(8,128)(2,1)}, u32[]{:S(2)}, u32[]{:S(2)}) %collective-permute-start.2) | collective-permute-done | bytes 1146912 | tf_op jit(solution)/shard_map/ppermute | solution.py:409
  78.6 19.2 %collective-permute-done.4.refs_6_ = bf16[320,1792]{1,0:T(8,128)(2,1)} collective-permute-done((bf16[320,1792]{1,0:T(8,128)(2,1)}, bf16[320,1792]{1,0:T(8,128)(2,1)}, u32[]{:S(2)}, u32[]{:S(2)}) %collective-permute-start.4) | collective-permute-done | bytes 1146912 | tf_op jit(solution)/shard_map/ppermute | solution.py:409
  99.1 69.0 %all-gather.8.cloned.1.call-done.w_ref = bf16[2560,3968]{1,0:T(8,128)(2,1)} async-done(((bf16[320,3968]{1,0:T(8,128)(2,1)}), bf16[2560,3968]{1,0:T(8,128)(2,1)}) %all-gather.8.cloned.1.call-update) | async-done | bytes 20316176 | tf_op jit(solution)/shard_map/all_gather | solution.py:627
  174.2 19.3 %project.1.q_ref = bf16[512,3840]{1,0:T(8,128)(2,1)} custom-call(bf16[512,2560]{1,0:T(8,128)(2,1)} %multiply_convert_fusion.n_ref.x_ref, bf16[2560,3968]{1,0:T(8,128)(2,1)} %all-gather.8.cloned.1.call-done.w_ref, f32[512,640]{1,0:T(8,128)S(1)} %copy-done.2, f32[512,640]{1,0:T(8,128)S(1)} %get-tuple-element.283.up_ref.refs_6_, ...), custom_call_target="tpu_custom_call" | custom-call | flops 5100273664 | bytes 65536 | tf_op jit(solution)/shard_map/project/pallas_call | solution.py:61
  198.4 13.8 collective-permute-done.6.refs_1_
  218.1 23.4 %attend.2 = (bf16[256,2560]{1,0:T(8,128)(2,1)S(1)}, f32[256,256]{1,0:T(8,128)S(1)}) custom-call(bf16[512,3840]{1,0:T(8,128)(2,1)} %project.1.q_ref, bf16[256,1280]{1,0:T(8,128)(2,1)S(1)} %get-tuple-element.254.refs_0_, bf16[256,1280]{1,0:T(8,128)(2,1)S(1)} %collective-permute-done.6.refs_1_, bf16[256,1280]{1,0:T(8,128)(2,1)S(1)} %collective-permute-done.7.refs_2_, ...), custom_call_target="tpu_custom_call" | custom-call | flops 6174015488 | bytes 65536 | tf_op jit(solution)/shard_map/attend/pallas_call | solution.py:97
  244.4 9.1 multiply_reduce_fusion.8
  256.3 51.5 %all-gather.12.cloned.1.call-done.g_ref.refs_2_ = bf16[1024,2560]{1,0:T(8,128)(2,1)} async-done(((bf16[256,2560]{1,0:T(8,128)(2,1)}), bf16[1024,2560]{1,0:T(8,128)(2,1)}) %all-gather.12.cloned.1.call-update) | async-done | bytes 5242896 | tf_op jit(solution)/shard_map/all_gather | solution.py:265
  311.1 13.3 collective-permute-done.9.refs_1_
  327.3 23.2 %attend.3 = (bf16[256,2560]{1,0:T(8,128)(2,1)S(1)}, f32[256,256]{1,0:T(8,128)S(1)}) custom-call(bf16[512,3840]{1,0:T(8,128)(2,1)} %project.1.q_ref, bf16[256,1280]{1,0:T(8,128)(2,1)S(1)} %get-tuple-element.253.refs_0_, bf16[256,1280]{1,0:T(8,128)(2,1)S(1)} %collective-permute-done.9.refs_1_, bf16[256,1280]{1,0:T(8,128)(2,1)S(1)} %collective-permute-done.10.refs_2_, ...), custom_call_target="tpu_custom_call" | custom-call | flops 6174015488 | bytes 65536 | tf_op jit(solution)/shard_map/attend/pallas_call | solution.py:97
  350.6 9.7 multiply_reduce_fusion.7
  365.9 4.7 columns_for.7
  387.1 21.9 %weave.1.wg_ref.wu_ref.refs_2_.refs_3_ = bf16[2560,3584]{1,0:T(8,128)(2,1)} custom-call(s32[9]{0:T(128)} %stack.118.place_ref, bf16[320,1792]{1,0:T(8,128)(2,1)} %copy-done.47, bf16[320,1792]{1,0:T(8,128)(2,1)} %copy-done.46, bf16[320,1792]{1,0:T(8,128)(2,1)} %collective-permute-done.refs_2_, bf16[320,1792]{1,0:T(8,128)(2,1)} %collective-permute-done.1.refs_3_, ...), custom_call_target="tpu_custom_call" | custom-call | flops 5637144576 | bytes 65536 | tf_op jit(solution)/shard_map/weave/pallas_call | solution.py:378
  409.0 4.7 constant_dynamic-update-slice_fusion.1
  413.8 4.7 constant_dynamic-update-slice_fusion.wd_ref.b_ref
  418.5 36.7 %feed_forward.2 = (bf16[1024,1792]{1,0:T(8,128)(2,1)}, bf16[1024,1792]{1,0:T(8,128)(2,1)}, bf16[1024,1792]{1,0:T(8,128)(2,1)}) custom-call(bf16[1024,2560]{1,0:T(8,128)(2,1)} %all-gather.14.cloned.1.call-done.n_ref.refs_0_, bf16[1024,2560]{1,0:T(8,128)(2,1)} %all-gather.12.cloned.1.call-done.g_ref.refs_2_, ...), custom_call_target="tpu_custom_call" | custom-call | flops 9663676416 | bytes 65536 | tf_op jit(solution)/shard_map/feed_forward/pallas_call | solution.py:531
  459.3 26.5 %sum_nt.2 = bf16[1024,2560]{1,0:T(8,128)(2,1)} custom-call(bf16[1024,1792]{1,0:T(8,128)(2,1)} %get-tuple-element.104.refs_0_.refs_2_, bf16[1024,1792]{1,0:T(8,128)(2,1)} %get-tuple-element.95.refs_1_.refs_4_, bf16[2560,3584]{1,0:T(8,128)(2,1)} %weave.1.wg_ref.wu_ref.refs_2_.refs_3_, bf16[2560,3584]{1,0:T(8,128)(2,1)} %weave.1.wg_ref.wu_ref.refs_2_.refs_3_), custom_call_target="tpu_custom_call" | custom-call | flops 6979321856 | bytes 65536 | tf_op jit(solution)/shard_map/sum_nt/pallas_call | solution.py:552
  485.9 37.2 %all-gather.16.cloned.1.call-done.n_ref.refs_1_ = bf16[1024,2560]{1,0:T(8,128)(2,1)} async-done(((bf16[256,2560]{1,0:T(8,128)(2,1)}), bf16[1024,2560]{1,0:T(8,128)(2,1)}) %all-gather.16.cloned.1.call-update) | async-done | bytes 5242896 | tf_op jit(solution)/shard_map/all_gather | solution.py:265
  523.1 36.8 %feed_forward.3 = (bf16[1024,1792]{1,0:T(8,128)(2,1)}, bf16[1024,1792]{1,0:T(8,128)(2,1)}, bf16[1024,1792]{1,0:T(8,128)(2,1)}) custom-call(bf16[1024,2560]{1,0:T(8,128)(2,1)} %all-gather.16.cloned.1.call-done.n_ref.refs_1_, bf16[1024,2560]{1,0:T(8,128)(2,1)} %all-gather.18.cloned.1.call-done.g_ref.refs_3_, ...), custom_call_target="tpu_custom_call" | custom-call | flops 9663676416 | bytes 65536 | tf_op jit(solution)/shard_map/feed_forward/pallas_call | solution.py:531
  559.9 28.3 %sum_tn.4 = bf16[4,8,80,1792]{3,2,1,0:T(8,128)(2,1)} custom-call(bf16[1024,2560]{1,0:T(8,128)(2,1)} %all-gather.14.cloned.1.call-done.n_ref.refs_0_, bf16[1024,2560]{1,0:T(8,128)(2,1)} %all-gather.16.cloned.1.call-done.n_ref.refs_1_, bf16[1024,1792]{1,0:T(8,128)(2,1)} %get-tuple-element.104.refs_0_.refs_2_, ...), custom_call_target="tpu_custom_call" | custom-call | flops 6979321856 | bytes 65536 | tf_op jit(solution)/shard_map/sum_tn/pallas_call | solution.py:502
  588.8 16.2 %sum_tn.5 = bf16[896,2560]{1,0:T(8,128)(2,1)} custom-call(bf16[1024,1792]{1,0:T(8,128)(2,1)} %get-tuple-element.107.refs_0_.a_ref, bf16[1024,1792]{1,0:T(8,128)(2,1)} %get-tuple-element.108.refs_1_.a_ref, bf16[1024,2560]{1,0:T(8,128)(2,1)} %all-gather.12.cloned.1.call-done.g_ref.refs_2_, bf16[1024,2560]{1,0:T(8,128)(2,1)} %all-gather.18.cloned.1.call-done.g_ref.refs_3_), custom_call_target="tpu_custom_call" | custom-call | flops 4294967296 | bytes 65536 | tf_op jit(solution)/shard_map/sum_tn/pallas_call | solution.py:502
  605.0 28.7 %sum_tn.6 = bf16[4,8,80,1792]{3,2,1,0:T(8,128)(2,1)} custom-call(bf16[1024,2560]{1,0:T(8,128)(2,1)} %all-gather.14.cloned.1.call-done.n_ref.refs_0_, bf16[1024,2560]{1,0:T(8,128)(2,1)} %all-gather.16.cloned.1.call-done.n_ref.refs_1_, bf16[1024,1792]{1,0:T(8,128)(2,1)} %get-tuple-element.104.refs_0_.refs_2_, ...), custom_call_target="tpu_custom_call" | custom-call | flops 6979321856 | bytes 65536 | tf_op jit(solution)/shard_map/sum_tn/pallas_call | solution.py:502
  644.3 4.9 dynamic-slice_bitcast_fusion.20
  651.9 17.0 %sum_tn.7 = bf16[896,2560]{1,0:T(8,128)(2,1)} custom-call(bf16[1024,1792]{1,0:T(8,128)(2,1)} %get-tuple-element.107.refs_0_.a_ref, bf16[1024,1792]{1,0:T(8,128)(2,1)} %get-tuple-element.108.refs_1_.a_ref, bf16[1024,2560]{1,0:T(8,128)(2,1)} %all-gather.12.cloned.1.call-done.g_ref.refs_2_, bf16[1024,2560]{1,0:T(8,128)(2,1)} %all-gather.18.cloned.1.call-done.g_ref.refs_3_, ...), custom_call_target="tpu_custom_call" | custom-call | flops 4294967296 | bytes 65536 | tf_op jit(solution)/shard_map/sum_tn/pallas_call | solution.py:502
  668.9 26.0 %sum_nt.3 = bf16[1024,2560]{1,0:T(8,128)(2,1)} custom-call(bf16[1024,1792]{1,0:T(8,128)(2,1)} %get-tuple-element.106.refs_3_.refs_0_, bf16[1024,1792]{1,0:T(8,128)(2,1)} %get-tuple-element.100.refs_5_.refs_1_, bf16[2560,3584]{1,0:T(8,128)(2,1)} %weave.1.wg_ref.wu_ref.refs_2_.refs_3_, bf16[2560,3584]{1,0:T(8,128)(2,1)} %weave.1.wg_ref.wu_ref.refs_2_.refs_3_), custom_call_target="tpu_custom_call" | custom-call | flops 6979321856 | bytes 65536 | tf_op jit(solution)/shard_map/sum_nt/pallas_call | solution.py:552
  694.9 15.9 %plain_nn.2 = bf16[1024,2560]{1,0:T(8,128)(2,1)} custom-call(bf16[1024,1792]{1,0:T(8,128)(2,1)} %get-tuple-element.107.refs_0_.a_ref, bf16[1792,2560]{1,0:T(8,128)(2,1)} %constant_dynamic-update-slice_fusion.wd_ref.b_ref), custom_call_target="tpu_custom_call" | custom-call | flops 4294967296 | bytes 65536 | tf_op jit(solution)/shard_map/plain_nn/pallas_call | solution.py:571
  710.8 15.9 %plain_nn.3 = bf16[1024,2560]{1,0:T(8,128)(2,1)} custom-call(bf16[1024,1792]{1,0:T(8,128)(2,1)} %get-tuple-element.108.refs_1_.a_ref, bf16[1792,2560]{1,0:T(8,128)(2,1)} %constant_dynamic-update-slice_fusion.wd_ref.b_ref), custom_call_target="tpu_custom_call" | custom-call | flops 4294967296 | bytes 65536 | tf_op jit(solution)/shard_map/plain_nn/pallas_call | solution.py:571
  734.8 5.5 fusion.70
  740.3 9.9 convolution_convert_fusion.4.dctx_ref
  756.6 27.4 %attend_back.4 = (bf16[256,2560]{1,0:T(8,128)(2,1)}, bf16[256,1280]{1,0:T(8,128)(2,1)S(1)}, bf16[256,1280]{1,0:T(8,128)(2,1)S(1)}, bf16[256,1280]{1,0:T(8,128)(2,1)S(1)}, bf16[256,1280]{1,0:T(8,128)(2,1)S(1)}) custom-call(bf16[512,3840]{1,0:T(8,128)(2,1)} %project.1.q_ref, bf16[256,2560]{1,0:T(8,128)(2,1)} %convolution_convert_fusion.4.dctx_ref, ...), custom_call_target="tpu_custom_call" | custom-call | flops 26843545600 | bytes 65536 | tf_op jit(solution)/shard_map/attend_back/pallas_call | solution.py:160
  783.9 26.9 %attend_back.5 = (bf16[256,2560]{1,0:T(8,128)(2,1)}, bf16[256,1280]{1,0:T(8,128)(2,1)S(1)}, bf16[256,1280]{1,0:T(8,128)(2,1)S(1)}, bf16[256,1280]{1,0:T(8,128)(2,1)S(1)}, bf16[256,1280]{1,0:T(8,128)(2,1)S(1)}) custom-call(bf16[512,3840]{1,0:T(8,128)(2,1)} %project.1.q_ref, ...), custom_call_target="tpu_custom_call", output_to_operand_aliasing={{0}: (12, {}), {1}: (13, {}), {2}: (14, {}), {3}: (15, {}),... | custom-call | flops 26843545600 | bytes 65536 | tf_op jit(solution)/shard_map/attend_back/pallas_call | solution.py:160
  821.1 5.1 fusion.69
  827.2 9.6 convolution_convert_fusion.3.dctx_ref
  836.8 9.2 convolution_convert_fusion.1
  859.5 26.8 %attend_back.6 = (bf16[256,2560]{1,0:T(8,128)(2,1)}, bf16[256,1280]{1,0:T(8,128)(2,1)S(1)}, bf16[256,1280]{1,0:T(8,128)(2,1)S(1)}, bf16[256,1280]{1,0:T(8,128)(2,1)S(1)}, bf16[256,1280]{1,0:T(8,128)(2,1)S(1)}) custom-call(bf16[512,3840]{1,0:T(8,128)(2,1)} %project.1.q_ref, bf16[256,2560]{1,0:T(8,128)(2,1)} %convolution_convert_fusion.3.dctx_ref, ...), custom_call_target="tpu_custom_call" | custom-call | flops 26843545600 | bytes 65536 | tf_op jit(solution)/shard_map/attend_back/pallas_call | solution.py:160
  888.8 34.4 %collective-permute-done.42 = bf16[320,2560]{1,0:T(8,128)(2,1)} collective-permute-done((bf16[320,2560]{1,0:T(8,128)(2,1)}, bf16[320,2560]{1,0:T(8,128)(2,1)}, u32[]{:S(2)}, u32[]{:S(2)}) %collective-permute-start.42) | collective-permute-done | bytes 1638432 | tf_op jit(solution)/shard_map/ppermute | solution.py:273
  924.4 5.0 fusion.27
  929.3 5.5 collective-permute-done.34
  936.8 11.0 collective-permute-done.36
  947.8 26.8 %attend_back.7 = (bf16[256,2560]{1,0:T(8,128)(2,1)}, bf16[256,1280]{1,0:T(8,128)(2,1)S(1)}, bf16[256,1280]{1,0:T(8,128)(2,1)S(1)}, bf16[256,1280]{1,0:T(8,128)(2,1)S(1)}, bf16[256,1280]{1,0:T(8,128)(2,1)S(1)}) custom-call(bf16[512,3840]{1,0:T(8,128)(2,1)} %project.1.q_ref, ...), custom_call_target="tpu_custom_call", output_to_operand_aliasing={{0}: (12, {}), {1}: (13, {}), {2}: (14, {}), {3}: (15, {}),... | custom-call | flops 26843545600 | bytes 65536 | tf_op jit(solution)/shard_map/attend_back/pallas_call | solution.py:160
  979.7 5.5 reshape.284
  999.2 10.1 convolution_convert_fusion
  1010.8 11.5 fusion
  1026.5 54.8 %collective-permute-done.47.other_ref = bf16[256,1280]{1,0:T(8,128)(2,1)S(1)} collective-permute-done((bf16[256,1280]{1,0:T(8,128)(2,1)S(1)}, bf16[256,1280]{1,0:T(8,128)(2,1)S(1)}, u32[]{:S(2)}, u32[]{:S(2)}) %collective-permute-start.47) | collective-permute-done | bytes 655392 | tf_op jit(solution)/shard_map/ppermute | solution.py:595
  1085.9 5.0 dynamic-slice_bitcast_fusion.21
  1096.4 5.6 dynamic-slice_bitcast_fusion.2
  1103.8 10.9 multiply_reduce_fusion
  1116.8 5.9 convolution_convert_fusion.2
  1124.7 6.2 copy.67
  1134.5 20.0 %collective-permute-done.60 = bf16[320,2560]{1,0:T(8,128)(2,1)} collective-permute-done((bf16[320,2560]{1,0:T(8,128)(2,1)}, bf16[320,2560]{1,0:T(8,128)(2,1)}, u32[]{:S(2)}, u32[]{:S(2)}) %collective-permute-start.60) | collective-permute-done | bytes 1638432 | tf_op jit(solution)/shard_map/ppermute | solution.py:273
  1155.7 6.1 fusion.18
  1161.8 4.9 convert_element_type.330
  1166.9 22.5 %collective-permute-done.62 = bf16[320,2560]{1,0:T(8,128)(2,1)} collective-permute-done((bf16[320,2560]{1,0:T(8,128)(2,1)}, bf16[320,2560]{1,0:T(8,128)(2,1)}, u32[]{:S(2)}, u32[]{:S(2)}) %collective-permute-start.62) | collective-permute-done | bytes 1638432 | tf_op jit(solution)/shard_map/ppermute | solution.py:273
  1190.8 4.9 fusion.24
  1195.7 13.2 collective-permute-done.56
  1210.4 17.7 %collective-permute-done.58 = bf16[320,1408]{1,0:T(8,128)(2,1)S(1)} collective-permute-done((bf16[320,1408]{1,0:T(8,128)(2,1)S(1)}, bf16[320,1408]{1,0:T(8,128)(2,1)S(1)}, u32[]{:S(2)}, u32[]{:S(2)}) %collective-permute-start.58) | collective-permute-done | bytes 901152 | tf_op jit(solution)/shard_map/ppermute | solution.py:273
  1232.0 19.0 %all-gather.20.cloned.1.call-done = bf16[320,14336]{1,0:T(8,128)(2,1)} async-done(((bf16[80,14336]{1,0:T(8,128)(2,1)}), bf16[320,14336]{1,0:T(8,128)(2,1)}) %all-gather.20.cloned.1.call-update) | async-done | bytes 9175056 | tf_op jit(solution)/shard_map/all_gather | solution.py:755
  1251.1 19.4 %collective-permute-done.51 = bf16[256,2560]{1,0:T(8,128)(2,1)} collective-permute-done((bf16[256,2560]{1,0:T(8,128)(2,1)}, bf16[256,2560]{1,0:T(8,128)(2,1)}, u32[]{:S(2)}, u32[]{:S(2)}) %collective-permute-start.51) | collective-permute-done | bytes 1310752 | tf_op jit(solution)/shard_map/ppermute | solution.py:273
  1273.8 10.7 collective-permute-done.53
  1284.5 42.2 %collective-permute-done.54 = bf16[256,2560]{1,0:T(8,128)(2,1)} collective-permute-done((bf16[256,2560]{1,0:T(8,128)(2,1)}, bf16[256,2560]{1,0:T(8,128)(2,1)}, u32[]{:S(2)}, u32[]{:S(2)}) %collective-permute-start.54) | collective-permute-done | bytes 1310752 | tf_op jit(solution)/shard_map/ppermute | solution.py:273
  1331.4 13.0 slice_convert_fusion
  1344.3 63.0 %all-reduce.8.cloned.1.call-done = (bf16[320,1408]{1,0:T(8,128)(2,1)}, bf16[320,2560]{1,0:T(8,128)(2,1)}, bf16[320,2560]{1,0:T(8,128)(2,1)}) async-done(((bf16[320,1408]{1,0:T(8,128)(2,1)}, bf16[320,2560]{1,0:T(8,128)(2,1)}, bf16[320,2560]{1,0:T(8,128)(2,1)}), (bf16[320,1408]{1,0:T(8,128)(2,1)}, bf16[320,2560]{1,0:T(8,128)(2,1)}, bf16[320,2560]{1,0:T(8,128)(2,1)})) %all-reduce.8.cloned.1.call-update) | async-done | bytes 4177936 | tf_op jit(solution)/shard_map/psum | solution.py:767
  (397 shorter events, 214.4 us)
Async XLA Ops:
  7.2 160.9 %all-gather.8.cloned.1.call-start = ((), (), s32[]{:S(2)}) async-start(), calls=%async_computation.1 | async-start | bytes 22855680 | tf_op jit(solution)/shard_map/all_gather | solution.py:627
  13.4 231.0 %all-gather.10.cloned.1.call-start = ((), (), s32[]{:S(2)}) async-start(), calls=%async_computation.2 | async-start | bytes 14745600 | tf_op jit(solution)/shard_map/all_gather | solution.py:628
  14.1 293.7 %all-gather.12.cloned.1.call-start = ((), (), s32[]{:S(2)}) async-start(), calls=%async_computation.3 | async-start | bytes 6553600 | tf_op jit(solution)/shard_map/all_gather | solution.py:265
  17.8 44.2 %collective-permute-start = (bf16[320,1792]{1,0:T(8,128)(2,1)}, bf16[320,1792]{1,0:T(8,128)(2,1)}, u32[]{:S(2)}, u32[]{:S(2)}) collective-permute-start(bf16[320,1792]{1,0:T(8,128)(2,1)} %columns_for.4), channel_id=1, source_target_pairs={{0,8},{4,12},{8,0},{12,4},{16,24},{20,28},{24,16},{28,20},{1,9},{5... | collective-permute-start | bytes 3440648 | tf_op jit(solution)/shard_map/ppermute | solution.py:409
  23.5 55.2 %collective-permute-start.2 = (bf16[320,1792]{1,0:T(8,128)(2,1)}, bf16[320,1792]{1,0:T(8,128)(2,1)}, u32[]{:S(2)}, u32[]{:S(2)}) collective-permute-start(bf16[320,1792]{1,0:T(8,128)(2,1)} %columns_for.5), channel_id=1, source_target_pairs={{0,16},{4,20},{8,24},{12,28},{16,0},{20,4},{24,8},{28,12},{1,17},{... | collective-permute-start | bytes 3440648 | tf_op jit(solution)/shard_map/ppermute | solution.py:409
  28.8 69.0 %collective-permute-start.4 = (bf16[320,1792]{1,0:T(8,128)(2,1)}, bf16[320,1792]{1,0:T(8,128)(2,1)}, u32[]{:S(2)}, u32[]{:S(2)}) collective-permute-start(bf16[320,1792]{1,0:T(8,128)(2,1)} %columns_for.6), channel_id=1, source_target_pairs={{0,24},{4,28},{8,16},{12,20},{16,8},{20,12},{24,0},{28,4},{1,25},{... | collective-permute-start | bytes 3440648 | tf_op jit(solution)/shard_map/ppermute | solution.py:409
  61.9 112.2 %collective-permute-start.1 = (bf16[320,1792]{1,0:T(8,128)(2,1)}, bf16[320,1792]{1,0:T(8,128)(2,1)}, u32[]{:S(2)}, u32[]{:S(2)}) collective-permute-start(bf16[320,1792]{1,0:T(8,128)(2,1)} %collective-permute-done.refs_2_), channel_id=1, source_target_pairs={{0,1},{1,0},{2,3},{3,2},{4,5},{5,4},{6,7},{7,6},{8,9},{9,8},{10,11... | collective-permute-start | bytes 3440648 | tf_op jit(solution)/shard_map/ppermute | solution.py:412
  78.6 95.5 %collective-permute-start.3 = (bf16[320,1792]{1,0:T(8,128)(2,1)}, bf16[320,1792]{1,0:T(8,128)(2,1)}, u32[]{:S(2)}, u32[]{:S(2)}) collective-permute-start(bf16[320,1792]{1,0:T(8,128)(2,1)} %collective-permute-done.2.refs_4_), channel_id=1, source_target_pairs={{0,1},{1,0},{2,3},{3,2},{4,5},{5,4},{6,7},{7,6},{8,9},{9,8},{10,11... | collective-permute-start | bytes 3440648 | tf_op jit(solution)/shard_map/ppermute | solution.py:412
  97.8 76.4 %collective-permute-start.5 = (bf16[320,1792]{1,0:T(8,128)(2,1)}, bf16[320,1792]{1,0:T(8,128)(2,1)}, u32[]{:S(2)}, u32[]{:S(2)}) collective-permute-start(bf16[320,1792]{1,0:T(8,128)(2,1)} %collective-permute-done.4.refs_6_), channel_id=1, source_target_pairs={{0,1},{1,0},{2,3},{3,2},{4,5},{5,4},{6,7},{7,6},{8,9},{9,8},{10,11... | collective-permute-start | bytes 3440648 | tf_op jit(solution)/shard_map/ppermute | solution.py:412
  193.5 225.0 %all-gather.14.cloned.1.call-start = ((), (), s32[]{:S(2)}) async-start(), calls=%async_computation.4 | async-start | bytes 6553600 | tf_op jit(solution)/shard_map/all_gather | solution.py:265
  195.1 17.1 %collective-permute-start.6 = (bf16[256,1280]{1,0:T(8,128)(2,1)S(1)}, bf16[256,1280]{1,0:T(8,128)(2,1)S(1)}, u32[]{:S(2)}, u32[]{:S(2)}) collective-permute-start(bf16[256,1280]{1,0:T(8,128)(2,1)S(1)} %get-tuple-element.254.refs_0_), channel_id=1, source_target_pairs={{0,1},{1,2},{2,3},{4,5},{5,6},{6,7},{8,9},{9,10},{10,11},{12,13},{... | collective-permute-start | bytes 1966088 | tf_op jit(solution)/shard_map/ppermute | solution.py:662
  307.9 151.5 %all-gather.18.cloned.1.call-start = ((), (), s32[]{:S(2)}) async-start(), calls=%async_computation.6 | async-start | bytes 6553600 | tf_op jit(solution)/shard_map/all_gather | solution.py:265
  307.9 16.5 %collective-permute-start.9 = (bf16[256,1280]{1,0:T(8,128)(2,1)S(1)}, bf16[256,1280]{1,0:T(8,128)(2,1)S(1)}, u32[]{:S(2)}, u32[]{:S(2)}) collective-permute-start(bf16[256,1280]{1,0:T(8,128)(2,1)S(1)} %get-tuple-element.253.refs_0_), channel_id=1, source_target_pairs={{0,1},{1,2},{2,3},{4,5},{5,6},{6,7},{8,9},{9,10},{10,11},{12,13},{... | collective-permute-start | bytes 1966088 | tf_op jit(solution)/shard_map/ppermute | solution.py:662
  363.1 160.0 %all-gather.16.cloned.1.call-start = ((), (), s32[]{:S(2)}) async-start(), calls=%async_computation.5 | async-start | bytes 6553600 | tf_op jit(solution)/shard_map/all_gather | solution.py:265
  363.7 489.3 %reduce-scatter.2.cloned.1.call-start = ((), (), s32[]{:S(2)}) async-start(), calls=%async_computation.7 | async-start | bytes 11468800 | tf_op jit(solution)/shard_map/reduce_scatter | solution.py:706
  363.7 50.0 %collective-permute-start.20 = (bf16[896,2560]{1,0:T(8,128)(2,1)}, bf16[896,2560]{1,0:T(8,128)(2,1)}, u32[]{:S(2)}, u32[]{:S(2)}) collective-permute-start(bf16[896,2560]{1,0:T(8,128)(2,1)} %param.23), channel_id=1, source_target_pairs={{0,4},{4,0},{8,12},{12,8},{16,20},{20,16},{24,28},{28,24},{1,5},{5... | collective-permute-start | bytes 13762568 | tf_op jit(solution)/shard_map/ppermute | solution.py:256
  373.5 5.3 collective-permute-start.14
  373.9 8.1 collective-permute-start.16
  375.3 8.5 collective-permute-start.18
  379.6 5.9 collective-permute-start.17
  588.2 16.9 %collective-permute-start.21 = (bf16[4,8,80,1792]{3,2,1,0:T(8,128)(2,1)}, bf16[4,8,80,1792]{3,2,1,0:T(8,128)(2,1)}, u32[]{:S(2)}, u32[]{:S(2)}) collective-permute-start(bf16[4,8,80,1792]{3,2,1,0:T(8,128)(2,1)} %sum_tn.4), channel_id=1, source_target_pairs={{0,4},{4,0},{8,12},{12,8},{16,20},{20,16},{24,28},{28,24},{1,5},{5... | collective-permute-start | bytes 27525128 | tf_op jit(solution)/shard_map/ppermute | solution.py:256
  633.7 460.0 %all-reduce.6.cloned.1.call-start = ((), (), s32[]{:S(2)}) async-start(), calls=%async_computation.9 | async-start | bytes 9175040 | tf_op jit(solution)/shard_map/psum | solution.py:708
  633.8 18.1 %collective-permute-start.22 = (bf16[896,2560]{1,0:T(8,128)(2,1)}, bf16[896,2560]{1,0:T(8,128)(2,1)}, u32[]{:S(2)}, u32[]{:S(2)}) collective-permute-start(bf16[896,2560]{1,0:T(8,128)(2,1)} %sum_tn.5), channel_id=1, source_target_pairs={{0,4},{4,0},{8,12},{12,8},{16,20},{20,16},{24,28},{28,24},{1,5},{5... | collective-permute-start | bytes 13762568 | tf_op jit(solution)/shard_map/ppermute | solution.py:256
  643.7 193.1 %collective-permute-start.37 = (bf16[512,1280]{1,0:T(8,128)(2,1)}, bf16[512,1280]{1,0:T(8,128)(2,1)}, u32[]{:S(2)}, u32[]{:S(2)}) collective-permute-start(bf16[512,1280]{1,0:T(8,128)(2,1)} %get-tuple-element.129), channel_id=1, source_target_pairs={{0,4},{4,0},{8,12},{12,8},{16,20},{20,16},{24,28},{28,24},{1,5},{5... | collective-permute-start | bytes 3932168 | tf_op jit(solution)/shard_map/ppermute | solution.py:256
  649.2 81.1 %collective-permute-start.24 = (bf16[256,2560]{1,0:T(8,128)(2,1)}, bf16[256,2560]{1,0:T(8,128)(2,1)}, u32[]{:S(2)}, u32[]{:S(2)}) collective-permute-start(bf16[256,2560]{1,0:T(8,128)(2,1)} %get-tuple-element.244), channel_id=1, source_target_pairs={{0,8},{4,12},{8,0},{12,4},{16,24},{20,28},{24,16},{28,20},{1,9},{5... | collective-permute-start | bytes 3932168 | tf_op jit(solution)/shard_map/ppermute | solution.py:273
  650.4 79.9 %collective-permute-start.25 = (bf16[256,2560]{1,0:T(8,128)(2,1)}, bf16[256,2560]{1,0:T(8,128)(2,1)}, u32[]{:S(2)}, u32[]{:S(2)}) collective-permute-start(bf16[256,2560]{1,0:T(8,128)(2,1)} %get-tuple-element.243), channel_id=1, source_target_pairs={{0,16},{4,20},{8,24},{12,28},{16,0},{20,4},{24,8},{28,12},{1,17},{... | collective-permute-start | bytes 3932168 | tf_op jit(solution)/shard_map/ppermute | solution.py:273
  651.1 79.3 %collective-permute-start.26 = (bf16[256,2560]{1,0:T(8,128)(2,1)}, bf16[256,2560]{1,0:T(8,128)(2,1)}, u32[]{:S(2)}, u32[]{:S(2)}) collective-permute-start(bf16[256,2560]{1,0:T(8,128)(2,1)} %get-tuple-element.242), channel_id=1, source_target_pairs={{0,24},{4,28},{8,16},{12,20},{16,8},{20,12},{24,0},{28,4},{1,25},{... | collective-permute-start | bytes 3932168 | tf_op jit(solution)/shard_map/ppermute | solution.py:273
  750.2 86.6 %collective-permute-start.38 = (bf16[256,2560]{1,0:T(8,128)(2,1)}, bf16[256,2560]{1,0:T(8,128)(2,1)}, u32[]{:S(2)}, u32[]{:S(2)}) collective-permute-start(bf16[256,2560]{1,0:T(8,128)(2,1)} %get-tuple-element.227), channel_id=1, source_target_pairs={{0,4},{4,0},{8,12},{12,8},{16,20},{20,16},{24,28},{28,24},{1,5},{5... | collective-permute-start | bytes 3932168 | tf_op jit(solution)/shard_map/ppermute | solution.py:256
  753.9 60.4 %collective-permute-start.30 = (bf16[256,2560]{1,0:T(8,128)(2,1)}, bf16[256,2560]{1,0:T(8,128)(2,1)}, u32[]{:S(2)}, u32[]{:S(2)}) collective-permute-start(bf16[256,2560]{1,0:T(8,128)(2,1)} %get-tuple-element.248), channel_id=1, source_target_pairs={{0,8},{4,12},{8,0},{12,4},{16,24},{20,28},{24,16},{28,20},{1,9},{5... | collective-permute-start | bytes 3932168 | tf_op jit(solution)/shard_map/ppermute | solution.py:273
  755.0 60.2 %collective-permute-start.31 = (bf16[256,2560]{1,0:T(8,128)(2,1)}, bf16[256,2560]{1,0:T(8,128)(2,1)}, u32[]{:S(2)}, u32[]{:S(2)}) collective-permute-start(bf16[256,2560]{1,0:T(8,128)(2,1)} %get-tuple-element.247), channel_id=1, source_target_pairs={{0,16},{4,20},{8,24},{12,28},{16,0},{20,4},{24,8},{28,12},{1,17},{... | collective-permute-start | bytes 3932168 | tf_op jit(solution)/shard_map/ppermute | solution.py:273
  755.8 60.7 %collective-permute-start.32 = (bf16[256,2560]{1,0:T(8,128)(2,1)}, bf16[256,2560]{1,0:T(8,128)(2,1)}, u32[]{:S(2)}, u32[]{:S(2)}) collective-permute-start(bf16[256,2560]{1,0:T(8,128)(2,1)} %get-tuple-element.246), channel_id=1, source_target_pairs={{0,24},{4,28},{8,16},{12,20},{16,8},{20,12},{24,0},{28,4},{1,25},{... | collective-permute-start | bytes 3932168 | tf_op jit(solution)/shard_map/ppermute | solution.py:273
  811.7 439.4 %all-gather.20.cloned.1.call-start = ((), (), s32[]{:S(2)}) async-start(), calls=%async_computation.8 | async-start | bytes 11468800 | tf_op jit(solution)/shard_map/all_gather | solution.py:755
  814.3 184.3 %collective-permute-start.43 = (bf16[256,2560]{1,0:T(8,128)(2,1)}, bf16[256,2560]{1,0:T(8,128)(2,1)}, u32[]{:S(2)}, u32[]{:S(2)}) collective-permute-start(bf16[256,2560]{1,0:T(8,128)(2,1)} %get-tuple-element.124), channel_id=1, source_target_pairs={{0,4},{4,0},{8,12},{12,8},{16,20},{20,16},{24,28},{28,24},{1,5},{5... | collective-permute-start | bytes 3932168 | tf_op jit(solution)/shard_map/ppermute | solution.py:256
  815.3 10.9 collective-permute-start.27
  826.2 10.6 collective-permute-start.39
  850.3 37.1 %collective-permute-start.40 = (bf16[320,2560]{1,0:T(8,128)(2,1)}, bf16[320,2560]{1,0:T(8,128)(2,1)}, u32[]{:S(2)}, u32[]{:S(2)}) collective-permute-start(bf16[320,2560]{1,0:T(8,128)(2,1)} %get-tuple-element.234), channel_id=1, source_target_pairs={{0,8},{4,12},{8,0},{12,4},{16,24},{20,28},{24,16},{28,20},{1,9},{5... | collective-permute-start | bytes 4915208 | tf_op jit(solution)/shard_map/ppermute | solution.py:273
  851.2 37.1 %collective-permute-start.41 = (bf16[320,2560]{1,0:T(8,128)(2,1)}, bf16[320,2560]{1,0:T(8,128)(2,1)}, u32[]{:S(2)}, u32[]{:S(2)}) collective-permute-start(bf16[320,2560]{1,0:T(8,128)(2,1)} %get-tuple-element.236), channel_id=1, source_target_pairs={{0,16},{4,20},{8,24},{12,28},{16,0},{20,4},{24,8},{28,12},{1,17},{... | collective-permute-start | bytes 4915208 | tf_op jit(solution)/shard_map/ppermute | solution.py:273
  851.6 71.6 %collective-permute-start.42 = (bf16[320,2560]{1,0:T(8,128)(2,1)}, bf16[320,2560]{1,0:T(8,128)(2,1)}, u32[]{:S(2)}, u32[]{:S(2)}) collective-permute-start(bf16[320,2560]{1,0:T(8,128)(2,1)} %get-tuple-element.235), channel_id=1, source_target_pairs={{0,24},{4,28},{8,16},{12,20},{16,8},{20,12},{24,0},{28,4},{1,25},{... | collective-permute-start | bytes 4915208 | tf_op jit(solution)/shard_map/ppermute | solution.py:273
  854.7 31.6 %collective-permute-start.33 = (bf16[4,80,1792]{2,1,0:T(8,128)(2,1)S(1)}, bf16[4,80,1792]{2,1,0:T(8,128)(2,1)S(1)}, u32[]{:S(2)}, u32[]{:S(2)}) collective-permute-start(bf16[4,80,1792]{2,1,0:T(8,128)(2,1)S(1)} %get-tuple-element.265), channel_id=1, source_target_pairs={{0,4},{4,0},{8,12},{12,8},{16,20},{20,16},{24,28},{28,24},{1,5},{5... | collective-permute-start | bytes 3440648 | tf_op jit(solution)/shard_map/ppermute | solution.py:256
  886.3 108.7 %collective-permute-start.23 = (bf16[512,1280]{1,0:T(8,128)(2,1)}, bf16[512,1280]{1,0:T(8,128)(2,1)}, u32[]{:S(2)}, u32[]{:S(2)}) collective-permute-start(bf16[512,1280]{1,0:T(8,128)(2,1)} %get-tuple-element.111), channel_id=1, source_target_pairs={{0,4},{4,0},{8,12},{12,8},{16,20},{20,16},{24,28},{28,24},{1,5},{5... | collective-permute-start | bytes 3932168 | tf_op jit(solution)/shard_map/ppermute | solution.py:256
  887.4 47.4 %collective-permute-start.34 = (bf16[1,2,80,1792]{3,2,1,0:T(8,128)(2,1)S(1)}, bf16[1,2,80,1792]{3,2,1,0:T(8,128)(2,1)S(1)}, u32[]{:S(2)}, u32[]{:S(2)}) collective-permute-start(bf16[1,2,80,1792]{3,2,1,0:T(8,128)(2,1)S(1)} %get-tuple-element.262), channel_id=1, source_target_pairs={{0,8},{4,12},{8,0},{12,4},{16,24},{20,28},{24,16},{28,20},{1,9},{5... | collective-permute-start | bytes 1720328 | tf_op jit(solution)/shard_map/ppermute | solution.py:300
  888.3 48.4 %collective-permute-start.35 = (bf16[1,2,80,1792]{3,2,1,0:T(8,128)(2,1)S(1)}, bf16[1,2,80,1792]{3,2,1,0:T(8,128)(2,1)S(1)}, u32[]{:S(2)}, u32[]{:S(2)}) collective-permute-start(bf16[1,2,80,1792]{3,2,1,0:T(8,128)(2,1)S(1)} %get-tuple-element.261), channel_id=1, source_target_pairs={{0,16},{4,20},{8,24},{12,28},{16,0},{20,4},{24,8},{28,12},{1,17},{... | collective-permute-start | bytes 1720328 | tf_op jit(solution)/shard_map/ppermute | solution.py:300
  923.2 24.6 %collective-permute-start.36 = (bf16[1,2,80,1792]{3,2,1,0:T(8,128)(2,1)S(1)}, bf16[1,2,80,1792]{3,2,1,0:T(8,128)(2,1)S(1)}, u32[]{:S(2)}, u32[]{:S(2)}) collective-permute-start(bf16[1,2,80,1792]{3,2,1,0:T(8,128)(2,1)S(1)} %get-tuple-element.260), channel_id=1, source_target_pairs={{0,24},{4,28},{8,16},{12,20},{16,8},{20,12},{24,0},{28,4},{1,25},{... | collective-permute-start | bytes 1720328 | tf_op jit(solution)/shard_map/ppermute | solution.py:300
  934.9 56.7 %collective-permute-start.28 = (bf16[256,1280]{1,0:T(8,128)(2,1)}, bf16[256,1280]{1,0:T(8,128)(2,1)}, u32[]{:S(2)}, u32[]{:S(2)}) collective-permute-start(bf16[256,1280]{1,0:T(8,128)(2,1)} %add_convert_fusion.5), channel_id=1, source_target_pairs={{3,2},{2,1},{7,6},{6,5},{11,10},{10,9},{15,14},{14,13},{19,18},{18... | collective-permute-start | bytes 1966088 | tf_op jit(solution)/shard_map/ppermute | solution.py:595
  990.0 8.6 collective-permute-start.44
  992.8 29.6 %collective-permute-start.29 = (bf16[256,1280]{1,0:T(8,128)(2,1)S(1)}, bf16[256,1280]{1,0:T(8,128)(2,1)S(1)}, u32[]{:S(2)}, u32[]{:S(2)}) collective-permute-start(bf16[256,1280]{1,0:T(8,128)(2,1)S(1)} %add_convert_fusion.4), channel_id=1, source_target_pairs={{3,2},{2,1},{1,0},{7,6},{6,5},{5,4},{11,10},{10,9},{9,8},{15,14},{... | collective-permute-start | bytes 1966088 | tf_op jit(solution)/shard_map/ppermute | solution.py:595
  997.8 11.5 collective-permute-start.46
  1009.5 71.8 %collective-permute-start.47 = (bf16[256,1280]{1,0:T(8,128)(2,1)S(1)}, bf16[256,1280]{1,0:T(8,128)(2,1)S(1)}, u32[]{:S(2)}, u32[]{:S(2)}) collective-permute-start(bf16[256,1280]{1,0:T(8,128)(2,1)S(1)} %add_convert_fusion.2), channel_id=1, source_target_pairs={{3,2},{2,1},{1,0},{7,6},{6,5},{5,4},{11,10},{10,9},{9,8},{15,14},{... | collective-permute-start | bytes 1966088 | tf_op jit(solution)/shard_map/ppermute | solution.py:595
  1085.4 321.9 %all-reduce.8.cloned.1.call-start = ((), (), s32[]{:S(2)}) async-start(), calls=%async_computation.10 | async-start | bytes 8355840 | tf_op jit(solution)/shard_map/psum | solution.py:767
  1091.0 43.4 %collective-permute-start.50 = (bf16[256,2560]{1,0:T(8,128)(2,1)}, bf16[256,2560]{1,0:T(8,128)(2,1)}, u32[]{:S(2)}, u32[]{:S(2)}) collective-permute-start(bf16[256,2560]{1,0:T(8,128)(2,1)} %get-tuple-element.240), channel_id=1, source_target_pairs={{0,8},{4,12},{8,0},{12,4},{16,24},{20,28},{24,16},{28,20},{1,9},{5... | collective-permute-start | bytes 3932168 | tf_op jit(solution)/shard_map/ppermute | solution.py:273
  1093.8 21.4 %collective-permute-start.48 = (bf16[256,1280]{1,0:T(8,128)(2,1)S(1)}, bf16[256,1280]{1,0:T(8,128)(2,1)}, u32[]{:S(2)}, u32[]{:S(2)}) collective-permute-start(bf16[256,1280]{1,0:T(8,128)(2,1)S(1)} %copy-done.58), channel_id=1, source_target_pairs={{0,4},{4,0},{8,12},{12,8},{16,20},{20,16},{24,28},{28,24},{1,5},{5... | collective-permute-start | bytes 1966088 | tf_op jit(solution)/shard_map/ppermute | solution.py:256
  1102.1 52.4 %collective-permute-start.60 = (bf16[320,2560]{1,0:T(8,128)(2,1)}, bf16[320,2560]{1,0:T(8,128)(2,1)}, u32[]{:S(2)}, u32[]{:S(2)}) collective-permute-start(bf16[320,2560]{1,0:T(8,128)(2,1)} %get-tuple-element.231), channel_id=1, source_target_pairs={{0,8},{4,12},{8,0},{12,4},{16,24},{20,28},{24,16},{28,20},{1,9},{5... | collective-permute-start | bytes 4915208 | tf_op jit(solution)/shard_map/ppermute | solution.py:273
  1103.3 63.4 %collective-permute-start.61 = (bf16[320,2560]{1,0:T(8,128)(2,1)}, bf16[320,2560]{1,0:T(8,128)(2,1)}, u32[]{:S(2)}, u32[]{:S(2)}) collective-permute-start(bf16[320,2560]{1,0:T(8,128)(2,1)} %get-tuple-element.233), channel_id=1, source_target_pairs={{0,16},{4,20},{8,24},{12,28},{16,0},{20,4},{24,8},{28,12},{1,17},{... | collective-permute-start | bytes 4915208 | tf_op jit(solution)/shard_map/ppermute | solution.py:273
  1103.3 13.5 collective-permute-start.49
  1115.2 74.3 %collective-permute-start.62 = (bf16[320,2560]{1,0:T(8,128)(2,1)}, bf16[320,2560]{1,0:T(8,128)(2,1)}, u32[]{:S(2)}, u32[]{:S(2)}) collective-permute-start(bf16[320,2560]{1,0:T(8,128)(2,1)} %get-tuple-element.232), channel_id=1, source_target_pairs={{0,24},{4,28},{8,16},{12,20},{16,8},{20,12},{24,0},{28,4},{1,25},{... | collective-permute-start | bytes 4915208 | tf_op jit(solution)/shard_map/ppermute | solution.py:273
  1133.1 75.9 %collective-permute-start.56 = (bf16[320,1408]{1,0:T(8,128)(2,1)S(1)}, bf16[320,1408]{1,0:T(8,128)(2,1)S(1)}, u32[]{:S(2)}, u32[]{:S(2)}) collective-permute-start(bf16[320,1408]{1,0:T(8,128)(2,1)S(1)} %get-tuple-element.255), channel_id=1, source_target_pairs={{0,8},{4,12},{8,0},{12,4},{16,24},{20,28},{24,16},{28,20},{1,9},{5... | collective-permute-start | bytes 2703368 | tf_op jit(solution)/shard_map/ppermute | solution.py:273
  1134.3 74.9 %collective-permute-start.57 = (bf16[320,1408]{1,0:T(8,128)(2,1)S(1)}, bf16[320,1408]{1,0:T(8,128)(2,1)S(1)}, u32[]{:S(2)}, u32[]{:S(2)}) collective-permute-start(bf16[320,1408]{1,0:T(8,128)(2,1)S(1)} %get-tuple-element.257), channel_id=1, source_target_pairs={{0,16},{4,20},{8,24},{12,28},{16,0},{20,4},{24,8},{28,12},{1,17},{... | collective-permute-start | bytes 2703368 | tf_op jit(solution)/shard_map/ppermute | solution.py:273
  1154.5 73.6 %collective-permute-start.58 = (bf16[320,1408]{1,0:T(8,128)(2,1)S(1)}, bf16[320,1408]{1,0:T(8,128)(2,1)S(1)}, u32[]{:S(2)}, u32[]{:S(2)}) collective-permute-start(bf16[320,1408]{1,0:T(8,128)(2,1)S(1)} %get-tuple-element.256), channel_id=1, source_target_pairs={{0,24},{4,28},{8,16},{12,20},{16,8},{20,12},{24,0},{28,4},{1,25},{... | collective-permute-start | bytes 2703368 | tf_op jit(solution)/shard_map/ppermute | solution.py:273
  1166.7 103.8 %collective-permute-start.51 = (bf16[256,2560]{1,0:T(8,128)(2,1)}, bf16[256,2560]{1,0:T(8,128)(2,1)}, u32[]{:S(2)}, u32[]{:S(2)}) collective-permute-start(bf16[256,2560]{1,0:T(8,128)(2,1)} %get-tuple-element.239), channel_id=1, source_target_pairs={{0,16},{4,20},{8,24},{12,28},{16,0},{20,4},{24,8},{28,12},{1,17},{... | collective-permute-start | bytes 3932168 | tf_op jit(solution)/shard_map/ppermute | solution.py:273
  1189.4 81.1 %collective-permute-start.52 = (bf16[256,2560]{1,0:T(8,128)(2,1)}, bf16[256,2560]{1,0:T(8,128)(2,1)}, u32[]{:S(2)}, u32[]{:S(2)}) collective-permute-start(bf16[256,2560]{1,0:T(8,128)(2,1)} %get-tuple-element.238), channel_id=1, source_target_pairs={{0,24},{4,28},{8,16},{12,20},{16,8},{20,12},{24,0},{28,4},{1,25},{... | collective-permute-start | bytes 3932168 | tf_op jit(solution)/shard_map/ppermute | solution.py:273
  1208.9 75.5 %collective-permute-start.53 = (bf16[256,2560]{1,0:T(8,128)(2,1)}, bf16[256,2560]{1,0:T(8,128)(2,1)}, u32[]{:S(2)}, u32[]{:S(2)}) collective-permute-start(bf16[256,2560]{1,0:T(8,128)(2,1)} %get-tuple-element.252), channel_id=1, source_target_pairs={{0,8},{4,12},{8,0},{12,4},{16,24},{20,28},{24,16},{28,20},{1,9},{5... | collective-permute-start | bytes 3932168 | tf_op jit(solution)/shard_map/ppermute | solution.py:273
  1209.2 117.5 %collective-permute-start.54 = (bf16[256,2560]{1,0:T(8,128)(2,1)}, bf16[256,2560]{1,0:T(8,128)(2,1)}, u32[]{:S(2)}, u32[]{:S(2)}) collective-permute-start(bf16[256,2560]{1,0:T(8,128)(2,1)} %get-tuple-element.251), channel_id=1, source_target_pairs={{0,16},{4,20},{8,24},{12,28},{16,0},{20,4},{24,8},{28,12},{1,17},{... | collective-permute-start | bytes 3932168 | tf_op jit(solution)/shard_map/ppermute | solution.py:273
  1228.1 98.6 %collective-permute-start.55 = (bf16[256,2560]{1,0:T(8,128)(2,1)}, bf16[256,2560]{1,0:T(8,128)(2,1)}, u32[]{:S(2)}, u32[]{:S(2)}) collective-permute-start(bf16[256,2560]{1,0:T(8,128)(2,1)} %get-tuple-element.250), channel_id=1, source_target_pairs={{0,24},{4,28},{8,16},{12,20},{16,8},{20,12},{24,0},{28,4},{1,25},{... | collective-permute-start | bytes 3932168 | tf_op jit(solution)/shard_map/ppermute | solution.py:273
  1408.9 7.8 collective-permute-start.59
  (87 other events, 1727.9 us)
Sparse Core Ops, SparseCore 0:
  13.5 154.5 all-gather.7
  170.0 74.3 all-gather.9
  246.8 60.9 all-gather.11
  309.5 61.4 all-gather.13
  373.3 86.0 all-gather.17
  461.6 61.4 all-gather.15
  633.9 156.2 reduce-scatter.1
  811.8 195.5 all-reduce.5
  1085.6 165.4 all-gather.19
  1254.0 153.2 all-reduce.7
